TPU v7x, 32 devices: a whole 2x2x4 slice. The times are simulated.
32 devices in a mesh: tok: 8 (over z, x), head: 4 (over y, core).
Axes of the slice: x: 2, y: 2, z: 4, core: 2. Of those that a mesh axis runs over, the one named last changes fastest.
Arguments:
- tokens_in: bfloat16 [5, 32, 14, 14, 384], P(None, ('tok', 'head')), may hold values from -6 to 6
- cotangent: bfloat16 [5, 32, 14, 14, 384], P(None, ('tok', 'head')), may hold values from -6 to 6
- route: int32 [5, 32, 4], P(None, 'tok'), may hold values from -1 to 15, as said below
- extent: int32 [5, 32, 2], P(None, 'tok'), may hold values from 7 to 14, as said below
- qkv_weight: float32 [3, 384, 384], P(None, 'tok', 'head'), may hold values from -0.15625 to 0.15625
- proj_weight: float32 [384, 384], P('head', 'tok'), may hold values from -0.875 to 0.875
- fc1_weight: float32 [384, 1536], P('tok', 'head'), may hold values from -0.15625 to 0.15625
- fc2_weight: float32 [1536, 384], P('head', 'tok'), may hold values from -0.21875 to 0.21875
- vectors: float32 [12, 384], replicated
- rel_table: float32 [169, 12], replicated, may hold values from -5 to 5
- qkv_first: float32 [3, 384, 384], P(None, 'tok', 'head'), may hold values from -6.1035156e-05 to 6.1035156e-05
- proj_first: float32 [384, 384], P('head', 'tok'), may hold values from -6.1035156e-05 to 6.1035156e-05
- fc1_first: float32 [384, 1536], P('tok', 'head'), may hold values from -6.1035156e-05 to 6.1035156e-05
- fc2_first: float32 [1536, 384], P('head', 'tok'), may hold values from -6.1035156e-05 to 6.1035156e-05
- vectors_first: float32 [12, 384], replicated, may hold values from -6.1035156e-05 to 6.1035156e-05
- table_first: float32 [169, 12], replicated, may hold values from -6.1035156e-05 to 6.1035156e-05
- qkv_second: float32 [3, 384, 384], P(None, 'tok', 'head'), may hold values from 7.064254e-13 to 1.1302807e-11
- proj_second: float32 [384, 384], P('head', 'tok'), may hold values from 7.064254e-13 to 1.1302807e-11
- fc1_second: float32 [384, 1536], P('tok', 'head'), may hold values from 7.064254e-13 to 1.1302807e-11
- fc2_second: float32 [1536, 384], P('head', 'tok'), may hold values from 7.064254e-13 to 1.1302807e-11
- vectors_second: float32 [12, 384], replicated, may hold values from 7.064254e-13 to 1.1302807e-11
- table_second: float32 [169, 12], replicated, may hold values from 7.064254e-13 to 1.1302807e-11
Outputs:
- block_out: bfloat16 [5, 32, 14, 14, 384], P(None, ('tok', 'head'))
- grad_in: bfloat16 [5, 32, 14, 14, 384], P(None, ('tok', 'head'))
- grad_norm: float32 [], replicated
- qkv_new: float32 [3, 384, 384], P(None, 'tok', 'head')
- qkv_first_new: float32 [3, 384, 384], P(None, 'tok', 'head')
- qkv_second_new: float32 [3, 384, 384], P(None, 'tok', 'head')
- proj_new: float32 [384, 384], P('head', 'tok')
- proj_first_new: float32 [384, 384], P('head', 'tok')
- proj_second_new: float32 [384, 384], P('head', 'tok')
- fc1_new: float32 [384, 1536], P('tok', 'head')
- fc1_first_new: float32 [384, 1536], P('tok', 'head')
- fc1_second_new: float32 [384, 1536], P('tok', 'head')
- fc2_new: float32 [1536, 384], P('head', 'tok')
- fc2_first_new: float32 [1536, 384], P('head', 'tok')
- fc2_second_new: float32 [1536, 384], P('head', 'tok')
- vectors_new: float32 [12, 384], replicated
- vectors_first_new: float32 [12, 384], replicated
- vectors_second_new: float32 [12, 384], replicated
- table_new: float32 [169, 12], replicated
- table_first_new: float32 [169, 12], replicated
- table_second_new: float32 [169, 12], replicated
Inputs may be any that keep to these rules, and one draw needn't show every extreme that they name: `route`: for every window of the rolled partition (images in order, windows row by row): -1 exactly when the window holds no valid patch, otherwise destination * 2 + slot with destination an index along tok and slot below 2. Among the windows of the images that share an index along tok no value repeats, so a device receives at most 2 windows from one group, and in every micro-batch each group fills all 2 slots of some device. `extent`: valid patches of an image are the rows below its first entry and the columns below its second; the rest is padding.
All inputs are finite; a program needn't handle non-finite values.
Results may differ from a plain program's by a relative error of at most 0.012.
The roundings to bfloat16 on the way count: a program that leaves them out, or rounds other values in their place, can miss the bound.
Values may be sent and summed in bfloat16 or wider, within the bound.
No kernel may reach another device: no remote copies, remote signals or barrier semaphores. Data moves between devices by JAX's collectives and lax.ppermute only.
A program may use at most 256 MiB of HBM per device.

v0:
```python
import math

import jax
import jax.numpy as jnp
from jax import lax
from jax.sharding import PartitionSpec as P

C = 384
HD = 32
FF = 1536
WS = 7
SHIFT = 3
STEP = 10
GRID = 14


EPS_NORM = 1e-05
BETA_ONE = 0.9
BETA_TWO = 0.999
ADAM_EPS = 1e-08
RATE_MATRIX = 0.08
RATE_VECTOR = 1.0
DECAY_MATRIX = 0.05
CLIP_NORM = 0.05
NEG_FILL = -1e30
HIGH = lax.Precision.HIGHEST


def layer_norm(rows, gain, shift):
    average = jnp.mean(rows, axis=-1, keepdims=True)
    centered = rows - average
    inverse = lax.rsqrt(jnp.mean(centered * centered, axis=-1, keepdims=True) + EPS_NORM)
    normed = centered * inverse
    return (normed * gain + shift, normed, inverse)


def norm_back(gradient, normed, inverse, gain):
    scaled = gradient * gain
    backward = inverse * (
        scaled
        - jnp.mean(scaled, axis=-1, keepdims=True)
        - normed * jnp.mean(scaled * normed, axis=-1, keepdims=True)
    )
    return (backward, jnp.sum(gradient * normed, axis=0), jnp.sum(gradient, axis=0))


def gelu_value(pre_act):
    return pre_act * 0.5 * (1.0 + lax.erf(pre_act * 2.0 ** (-0.5)))


def gelu_slope(pre_act):
    return 0.5 * (1.0 + lax.erf(pre_act * 2.0 ** (-0.5))) + pre_act * jnp.exp(
        -0.5 * pre_act * pre_act
    ) * (2.0 * math.pi) ** (-0.5)


def to_windows(grid):
    images = grid.shape[0]
    features = grid.shape[3]
    side = grid.shape[1] // WS
    rolled = jnp.roll(grid, (-SHIFT, -SHIFT), axis=(1, 2))
    blocks = rolled.reshape(images, side, WS, side, WS, features).transpose(0, 1, 3, 2, 4, 5)
    return blocks.reshape(images * side * side, WS * WS, features)


def from_windows(windows, images):
    side = GRID // WS
    features = windows.shape[-1]
    blocks = windows.reshape(images, side, side, WS, WS, features).transpose(0, 1, 3, 2, 4, 5)
    return jnp.roll(blocks.reshape(images, GRID, GRID, features), (SHIFT, SHIFT), axis=(1, 2))


def patch_labels(extent_rows):
    position = jnp.arange(GRID)
    source_pos = (position + SHIFT) % GRID
    region_band = jnp.where(position < GRID - WS, 0, jnp.where(position < GRID - SHIFT, 1, 2))
    region = region_band[:, None] * 3 + region_band[None, :] + 1
    rows_inside = source_pos[None, :] < extent_rows[:, 0:1]
    cols_inside = source_pos[None, :] < extent_rows[:, 1:2]
    inside = rows_inside[:, :, None] & cols_inside[:, None, :]
    return jnp.where(inside, region[None], 0).astype(jnp.float32)


def valid_patches(extent_rows):
    position = jnp.arange(GRID)
    rows_inside = position[None, :] < extent_rows[:, 0:1]
    cols_inside = position[None, :] < extent_rows[:, 1:2]
    return rows_inside[:, :, None, None] & cols_inside[:, None, :, None]


def position_lookup():
    cell_pos = jnp.arange(WS * WS)
    cell_row = cell_pos // WS
    cell_col = cell_pos % WS
    offsets = (
        (cell_row[:, None] - cell_row[None, :] + WS - 1) * (2 * WS - 1)
        + cell_col[:, None]
        - cell_col[None, :]
        + WS
        - 1
    )
    return (offsets.reshape(-1)[:, None] == jnp.arange((2 * WS - 1) ** 2)[None, :]).astype(
        jnp.float32
    )


def window_scores(packed, labels, table_cols, lookup):
    windows = packed.shape[0]
    cells = packed.shape[1]
    head_count = table_cols.shape[1]
    split_heads = packed.reshape(windows, cells, 3, head_count, HD)
    queries = split_heads[:, :, 0]
    key_part = split_heads[:, :, 1]
    values = split_heads[:, :, 2]
    bias_term = jnp.dot(lookup, table_cols, precision=HIGH).T.reshape(head_count, cells, cells)
    scores = (
        jnp.einsum("wqhd,wkhd->whqk", queries, key_part, preferred_element_type=jnp.float32)
        * HD ** (-0.5)
        + bias_term[None]
    )
    same = (labels[:, :, None] == labels[:, None, :]) & (labels[:, None, :] > 0)
    allowed = same | jnp.eye(cells, dtype=bool)[None]
    return (jnp.where(allowed[:, None], scores, NEG_FILL), queries, key_part, values)


def attend(packed, labels, table_cols, lookup):
    scores, queries, key_part, values = window_scores(packed, labels, table_cols, lookup)
    peak = jnp.max(scores, axis=-1, keepdims=True)
    exponent = jnp.exp(scores - peak)
    totals = jnp.sum(exponent, axis=-1, keepdims=True)
    weights_soft = (exponent / totals).astype(jnp.bfloat16)
    result = jnp.einsum("whqk,wkhd->wqhd", weights_soft, values, preferred_element_type=jnp.float32)
    return (
        result.reshape(packed.shape[0], packed.shape[1], -1).astype(jnp.bfloat16),
        peak + jnp.log(totals),
    )


def attend_back(packed, labels, table_cols, lookup, log_totals, gradient):
    scores, queries, key_part, values = window_scores(packed, labels, table_cols, lookup)
    windows = packed.shape[0]
    cells = packed.shape[1]
    head_count = table_cols.shape[1]
    weights_soft = jnp.exp(scores - log_totals)
    weights_low = weights_soft.astype(jnp.bfloat16)
    grad_result = gradient.reshape(windows, cells, head_count, HD)
    grad_soft = jnp.einsum(
        "wqhd,wkhd->whqk", grad_result, values, preferred_element_type=jnp.float32
    )
    grad_values = jnp.einsum(
        "whqk,wqhd->wkhd", weights_low, grad_result, preferred_element_type=jnp.float32
    )
    inner = jnp.sum(weights_soft * grad_soft, axis=-1, keepdims=True)
    grad_scores = (weights_soft * (grad_soft - inner)).astype(jnp.bfloat16)
    grad_queries = jnp.einsum(
        "whqk,wkhd->wqhd", grad_scores, key_part, preferred_element_type=jnp.float32
    ) * HD ** (-0.5)
    grad_keys = jnp.einsum(
        "whqk,wqhd->wkhd", grad_scores, queries, preferred_element_type=jnp.float32
    ) * HD ** (-0.5)
    grad_bias = jnp.sum(grad_scores, axis=0, dtype=jnp.float32).reshape(head_count, cells * cells)
    grad_table = jnp.dot(lookup.T, grad_bias.T, precision=HIGH)
    grad_packed = (
        jnp.stack([grad_queries, grad_keys, grad_values], axis=2)
        .reshape(windows, cells, -1)
        .astype(jnp.bfloat16)
    )
    return (grad_packed, grad_table)


def deal_matrix(route_rows, slots):
    return (route_rows.reshape(-1)[None, :] == jnp.arange(slots)[:, None]).astype(jnp.bfloat16)


def deal(matrix, windows):
    flat = windows.reshape(windows.shape[0], -1)
    return jnp.dot(matrix, flat, preferred_element_type=jnp.float32).astype(jnp.bfloat16)


def undeal(matrix, slot_data):
    return jnp.einsum("sw,sf->wf", matrix, slot_data, preferred_element_type=jnp.float32).astype(
        jnp.bfloat16
    )


def vector_grads(
    gain_one,
    shift_one,
    query_shift,
    value_shift,
    proj_shift,
    gain_two,
    shift_two,
    fc2_shift,
    fc1_shift,
    width_at,
    hidden_at,
):
    flat_hidden = lax.dynamic_update_slice_in_dim(
        jnp.zeros((FF,), jnp.float32), fc1_shift, hidden_at, 0
    )
    pair = lax.dynamic_update_slice_in_dim(
        jnp.zeros((2, C), jnp.float32), jnp.stack([query_shift, value_shift]), width_at, 1
    )
    return jnp.concatenate(
        [
            gain_one[None],
            shift_one[None],
            pair,
            proj_shift[None],
            gain_two[None],
            shift_two[None],
            fc2_shift[None],
            flat_hidden.reshape(-1, C),
        ],
        axis=0,
    )


def gather_group(rows, fold, initial):
    return fold(initial, lax.all_gather(rows, "head", axis=0, tiled=True), jnp.int32(0))


def sum_group(term, rows):
    return lax.psum_scatter(
        term(jnp.int32(0), rows * lax.axis_size("head")), "head", scatter_dimension=0, tiled=True
    )


def move_back(packets):
    return lax.all_to_all(packets, "tok", split_axis=0, concat_axis=0, tiled=True)


def split_pass(
    x_own,
    grad_own,
    route_rows,
    extent_rows,
    w_qkv,
    w_proj,
    w_fc1,
    w_fc2,
    vectors,
    rel_table,
    lookup,
):
    own_rows = x_own.shape[0]
    head_at = lax.axis_index("head")
    head_total = lax.axis_size("head")
    tok_total = lax.axis_size("tok")
    group_rows = own_rows * head_total
    local_width = w_qkv.shape[2]
    local_heads = local_width // HD
    local_hidden = w_fc1.shape[1]
    cells = WS * WS
    zero_low = jnp.zeros((), jnp.bfloat16)
    bias_pair = lax.dynamic_slice_in_dim(vectors[2:4], head_at * local_width, local_width, 1)
    qkv_bias = jnp.stack([bias_pair[0], jnp.zeros_like(bias_pair[0]), bias_pair[1]])
    fc1_bias = lax.dynamic_slice_in_dim(
        vectors[8:].reshape(-1), head_at * local_hidden, local_hidden, 0
    )
    table_cols = lax.dynamic_slice_in_dim(rel_table, head_at * local_heads, local_heads, 1)
    normed_one, unit_one, inverse_one = layer_norm(x_own, vectors[0], vectors[1])

    def qkv_fold(carried, portion, offset):
        made = (
            jnp.einsum("nc,wcd->nwd", portion, w_qkv, preferred_element_type=jnp.float32)
            + qkv_bias[None]
        )
        packed = made.reshape(portion.shape[0], -1).astype(jnp.bfloat16)
        return (portion, packed)

    held_one, packed = gather_group(
        normed_one.astype(jnp.bfloat16),
        qkv_fold,
        (
            jnp.zeros((group_rows, C), jnp.bfloat16),
            jnp.zeros((group_rows, 3 * local_width), jnp.bfloat16),
        ),
    )
    labels = to_windows(patch_labels(extent_rows)[..., None])[..., 0]
    windows = to_windows(packed.reshape(head_total, GRID, GRID, -1))
    window_count = windows.shape[0]
    capacity = -(-window_count // tok_total)
    slots = tok_total * capacity
    matrix = deal_matrix(route_rows, slots)
    sent = deal(matrix, windows).reshape(tok_total, capacity, cells, 3 * local_width)
    sent_labels = deal(matrix, labels.astype(jnp.bfloat16)).reshape(tok_total, capacity, cells)
    got, got_labels = (
        lax.all_to_all(sent, "tok", split_axis=0, concat_axis=0, tiled=True),
        lax.all_to_all(sent_labels, "tok", split_axis=0, concat_axis=0, tiled=True),
    )
    got = got.reshape(slots, cells, 3 * local_width)
    got_labels = got_labels.reshape(slots, cells).astype(jnp.float32)
    attended, log_totals = attend(got, got_labels, table_cols, lookup)
    returned = move_back(attended.reshape(tok_total, capacity, cells, local_width))
    mine = undeal(matrix, returned.reshape(slots, -1)).reshape(window_count, cells, local_width)
    valid = valid_patches(extent_rows)
    attn_group = jnp.where(valid, from_windows(mine, head_total), zero_low).reshape(
        group_rows, local_width
    )

    def proj_term(offset, amount):
        return jnp.dot(attn_group, w_proj, preferred_element_type=jnp.float32)

    middle = x_own + sum_group(proj_term, own_rows) + vectors[4]
    normed_two, unit_two, inverse_two = layer_norm(middle, vectors[5], vectors[6])

    def mlp_fold(carried, portion, offset):
        pre_act = jnp.dot(portion, w_fc1, preferred_element_type=jnp.float32) + fc1_bias
        hidden_out = gelu_value(pre_act).astype(jnp.bfloat16)
        return (portion, pre_act, hidden_out)

    held_two, hidden_in, hidden_out = gather_group(
        normed_two.astype(jnp.bfloat16),
        mlp_fold,
        (
            jnp.zeros((group_rows, C), jnp.bfloat16),
            jnp.zeros((group_rows, local_hidden), jnp.float32),
            jnp.zeros((group_rows, local_hidden), jnp.bfloat16),
        ),
    )

    def down_term(offset, amount):
        return jnp.dot(hidden_out, w_fc2, preferred_element_type=jnp.float32)

    result = middle + sum_group(down_term, own_rows) + vectors[7]
    grad_low = grad_own.astype(jnp.bfloat16)

    def fc2_fold(carried, portion, offset):
        grad_post = jnp.einsum("nc,fc->nf", portion, w_fc2, preferred_element_type=jnp.float32)
        grad_pre = grad_post * gelu_slope(hidden_in)
        grad_hidden = grad_pre.astype(jnp.bfloat16)
        grad_fc2 = jnp.einsum("nf,nc->fc", hidden_out, portion, preferred_element_type=jnp.float32)
        grad_shift = jnp.sum(grad_pre, axis=0)
        return (grad_hidden, grad_fc2, grad_shift)

    grad_hidden, grad_fc2, grad_fc1_shift = gather_group(
        grad_low,
        fc2_fold,
        (
            jnp.zeros((group_rows, local_hidden), jnp.bfloat16),
            jnp.zeros((local_hidden, C), jnp.float32),
            jnp.zeros((local_hidden,), jnp.float32),
        ),
    )
    grad_fc1 = jnp.einsum("nc,nf->cf", held_two, grad_hidden, preferred_element_type=jnp.float32)

    def hidden_term(offset, amount):
        return jnp.einsum("nf,cf->nc", grad_hidden, w_fc1, preferred_element_type=jnp.float32)

    back_two, gain_two, shift_two = norm_back(
        sum_group(hidden_term, own_rows), unit_two, inverse_two, vectors[5]
    )
    grad_middle = grad_own + back_two

    def proj_fold(carried, portion, offset):
        made = jnp.einsum("nc,dc->nd", portion, w_proj, preferred_element_type=jnp.float32)
        grad_attn = made.astype(jnp.bfloat16)
        grad_proj = jnp.einsum("nd,nc->dc", attn_group, portion, preferred_element_type=jnp.float32)
        return (grad_attn, grad_proj)

    grad_attn, grad_proj = gather_group(
        grad_middle.astype(jnp.bfloat16),
        proj_fold,
        (
            jnp.zeros((group_rows, local_width), jnp.bfloat16),
            jnp.zeros((local_width, C), jnp.float32),
        ),
    )
    grad_attn = jnp.where(valid, grad_attn.reshape(head_total, GRID, GRID, local_width), zero_low)
    sent_grad = deal(matrix, to_windows(grad_attn)).reshape(tok_total, capacity, cells, local_width)
    got_grad = move_back(sent_grad)
    grad_packed, grad_table = attend_back(
        got, got_labels, table_cols, lookup, log_totals, got_grad.reshape(slots, cells, local_width)
    )
    returned_grad = move_back(grad_packed.reshape(tok_total, capacity, cells, 3 * local_width))
    mine_grad = undeal(matrix, returned_grad.reshape(slots, -1)).reshape(
        window_count, cells, 3 * local_width
    )
    grad_qkv_rows = from_windows(mine_grad, head_total).reshape(group_rows, 3, local_width)
    grad_qkv = jnp.einsum(
        "nc,nwd->wcd", held_one, grad_qkv_rows, preferred_element_type=jnp.float32
    )
    grad_qkv_shift = jnp.sum(grad_qkv_rows, axis=0, dtype=jnp.float32)

    def input_term(offset, amount):
        return jnp.einsum("nwd,wcd->nc", grad_qkv_rows, w_qkv, preferred_element_type=jnp.float32)

    back_one, gain_one, shift_one = norm_back(
        sum_group(input_term, own_rows), unit_one, inverse_one, vectors[0]
    )
    grad_in = grad_middle + back_one
    vec_grad = vector_grads(
        gain_one,
        shift_one,
        grad_qkv_shift[0],
        grad_qkv_shift[2],
        jnp.sum(grad_middle, axis=0),
        gain_two,
        shift_two,
        jnp.sum(grad_own, axis=0),
        grad_fc1_shift,
        head_at * local_width,
        head_at * local_hidden,
    )
    table_grad = lax.dynamic_update_slice_in_dim(
        jnp.zeros(rel_table.shape, jnp.float32), grad_table, head_at * local_heads, 1
    )
    return (result, grad_in, (grad_qkv, grad_proj, grad_fc1, grad_fc2), vec_grad, table_grad)


def adam_update(weight, first, second, gradient, rate, decay):
    first_new = BETA_ONE * first + (1.0 - BETA_ONE) * gradient
    second_new = BETA_TWO * second + (1.0 - BETA_TWO) * gradient * gradient
    first_hat = first_new / (1.0 - BETA_ONE**STEP)
    second_hat = second_new / (1.0 - BETA_TWO**STEP)
    weight_new = weight * (1.0 - rate * decay) - rate * first_hat / (
        jnp.sqrt(second_hat) + ADAM_EPS
    )
    return (weight_new, first_new, second_new)


def body(
    tokens_in,
    cotangent,
    route,
    extent,
    qkv_weight,
    proj_weight,
    fc1_weight,
    fc2_weight,
    vectors,
    rel_table,
    qkv_first,
    proj_first,
    fc1_first,
    fc2_first,
    vectors_first,
    table_first,
    qkv_second,
    proj_second,
    fc1_second,
    fc2_second,
    vectors_second,
    table_second,
):
    lookup = position_lookup()
    micro_count = tokens_in.shape[0]
    qkv_low = qkv_weight.astype(jnp.bfloat16)
    proj_low = proj_weight.astype(jnp.bfloat16)
    fc1_low = fc1_weight.astype(jnp.bfloat16)
    fc2_low = fc2_weight.astype(jnp.bfloat16)
    matrix_totals = [
        jnp.zeros(qkv_weight.shape, jnp.float32),
        jnp.zeros(proj_weight.shape, jnp.float32),
        jnp.zeros(fc1_weight.shape, jnp.float32),
        jnp.zeros(fc2_weight.shape, jnp.float32),
    ]
    vector_total = jnp.zeros(vectors.shape, jnp.float32)
    table_total = jnp.zeros(rel_table.shape, jnp.float32)
    results = []
    grads_in = []
    for batch_index in range(micro_count):
        w_qkv, w_proj, w_fc1, w_fc2 = (
            lax.all_gather(qkv_low, "tok", axis=1, tiled=True),
            lax.all_gather(proj_low, "tok", axis=1, tiled=True),
            lax.all_gather(fc1_low, "tok", axis=0, tiled=True),
            lax.all_gather(fc2_low, "tok", axis=1, tiled=True),
        )
        x_own = tokens_in[batch_index, 0].reshape(-1, C).astype(jnp.float32)
        grad_own = cotangent[batch_index, 0].reshape(-1, C).astype(jnp.float32)
        outcome = split_pass(
            x_own,
            grad_own,
            route[batch_index],
            extent[batch_index],
            w_qkv,
            w_proj,
            w_fc1,
            w_fc2,
            vectors,
            rel_table,
            lookup,
        )
        result, grad_in, mats, vec_grad, table_grad = outcome
        reduced = (
            lax.psum_scatter(mats[0], "tok", scatter_dimension=1, tiled=True),
            lax.psum_scatter(mats[1], "tok", scatter_dimension=1, tiled=True),
            lax.psum_scatter(mats[2], "tok", scatter_dimension=0, tiled=True),
            lax.psum_scatter(mats[3], "tok", scatter_dimension=1, tiled=True),
        )
        matrix_totals = [
            total_part + new_part for total_part, new_part in zip(matrix_totals, reduced)
        ]
        vector_total = vector_total + vec_grad
        table_total = table_total + table_grad
        results.append(result.astype(jnp.bfloat16))
        grads_in.append(grad_in.astype(jnp.bfloat16))
    patches = micro_count * lax.axis_size("tok") * lax.axis_size("head") * GRID * GRID
    vector_total, table_total = lax.psum((vector_total, table_total), ("tok", "head"))
    gradients = [member / patches for member in matrix_totals] + [
        vector_total / patches,
        table_total / patches,
    ]
    matrix_squares = jnp.float32(0.0)
    for member in gradients[:4]:
        matrix_squares = matrix_squares + jnp.sum(member * member)
    matrix_squares = lax.psum(matrix_squares, ("tok", "head"))
    grad_norm = jnp.sqrt(
        matrix_squares + jnp.sum(gradients[4] * gradients[4]) + jnp.sum(gradients[5] * gradients[5])
    )
    factor = jnp.minimum(1.0, CLIP_NORM / (grad_norm + 1e-06))
    params = (qkv_weight, proj_weight, fc1_weight, fc2_weight, vectors, rel_table)
    firsts = (qkv_first, proj_first, fc1_first, fc2_first, vectors_first, table_first)
    seconds = (qkv_second, proj_second, fc1_second, fc2_second, vectors_second, table_second)
    rates = (RATE_MATRIX, RATE_MATRIX, RATE_MATRIX, RATE_MATRIX, RATE_VECTOR, RATE_VECTOR)
    decays = (DECAY_MATRIX, DECAY_MATRIX, DECAY_MATRIX, DECAY_MATRIX, 0.0, 0.0)
    updated = [
        adam_update(
            params[index],
            firsts[index],
            seconds[index],
            gradients[index] * factor,
            rates[index],
            decays[index],
        )
        for index in range(6)
    ]
    block_out = jnp.stack(results).reshape(tokens_in.shape)
    grad_block = jnp.stack(grads_in).reshape(tokens_in.shape)
    return (
        block_out,
        grad_block,
        grad_norm,
        updated[0][0],
        updated[0][1],
        updated[0][2],
        updated[1][0],
        updated[1][1],
        updated[1][2],
        updated[2][0],
        updated[2][1],
        updated[2][2],
        updated[3][0],
        updated[3][1],
        updated[3][2],
        updated[4][0],
        updated[4][1],
        updated[4][2],
        updated[5][0],
        updated[5][1],
        updated[5][2],
    )


def solution(mesh):
    return jax.shard_map(
        body,
        mesh=mesh,
        in_specs=(
            P(None, ("tok", "head"), None, None, None),
            P(None, ("tok", "head"), None, None, None),
            P(None, "tok", None),
            P(None, "tok", None),
            P(None, "tok", "head"),
            P("head", "tok"),
            P("tok", "head"),
            P("head", "tok"),
            P(),
            P(),
            P(None, "tok", "head"),
            P("head", "tok"),
            P("tok", "head"),
            P("head", "tok"),
            P(),
            P(),
            P(None, "tok", "head"),
            P("head", "tok"),
            P("tok", "head"),
            P("head", "tok"),
            P(),
            P(),
        ),
        out_specs=(
            P(None, ("tok", "head"), None, None, None),
            P(None, ("tok", "head"), None, None, None),
            P(),
            P(None, "tok", "head"),
            P(None, "tok", "head"),
            P(None, "tok", "head"),
            P("head", "tok"),
            P("head", "tok"),
            P("head", "tok"),
            P("tok", "head"),
            P("tok", "head"),
            P("tok", "head"),
            P("head", "tok"),
            P("head", "tok"),
            P("head", "tok"),
            P(),
            P(),
            P(),
            P(),
            P(),
            P(),
        ),
        check_vma=False,
    )
```

profile of v0, /device:TPU:0, one launch (start us, length us, event | category | flops | bytes accessed | tf_op | source)
XLA Modules:
  0.0 1505.2 jit_solution(13952251979229363871)
XLA Ops:
  32.2 31.4 %all_gather.89 = bf16[3,384,96]{2,1,0:T(8,128)(2,1)S(1)} all-gather(bf16[3,48,96]{2,1,0:T(8,128)(2,1)S(1)} %convert_element_type.677), channel_id=1, replica_groups=mesh['tok'=8,'head'=4] {'tok'}, dimensions={1}, use_global_device_ids=true | all-gather | bytes 248832 | tf_op jit(solution)/shard_map/all_gather | solution.py:466
  88.3 7.8 all-gather.4
  101.8 7.8 all-gather.6
  115.5 8.0 all-gather
  153.9 7.9 all-gather.16
  169.6 7.8 all-gather.10
  185.2 8.8 all-gather.14
  227.3 31.0 %all_gather.90 = bf16[96,384]{0,1:T(8,128)(2,1)S(1)} all-gather(bf16[96,48]{0,1:T(8,128)(2,1)S(1)} %convert_element_type.693), channel_id=1, replica_groups=mesh['tok'=8,'head'=4] {'tok'}, dimensions={1}, use_global_device_ids=true | all-gather | bytes 82944 | tf_op jit(solution)/shard_map/all_gather | solution.py:467
  314.3 37.8 %all_gather.93 = bf16[384,384]{0,1:T(8,128)(2,1)} all-gather(bf16[384,48]{0,1:T(8,128)(2,1)S(1)} %convert_element_type.697), channel_id=1, replica_groups=mesh['tok'=8,'head'=4] {'tok'}, dimensions={1}, use_global_device_ids=true | all-gather | bytes 331776 | tf_op jit(solution)/shard_map/all_gather | solution.py:469
  352.1 33.5 %all_gather.92 = bf16[384,384]{1,0:T(8,128)(2,1)} all-gather(bf16[48,384]{1,0:T(8,128)(2,1)S(1)} %convert_element_type.695), channel_id=1, replica_groups=mesh['tok'=8,'head'=4] {'tok'}, dimensions={0}, use_global_device_ids=true | all-gather | bytes 331776 | tf_op jit(solution)/shard_map/all_gather | solution.py:468
  553.2 58.0 %fusion.234 = (f32[208,384]{1,0:T(8,128)S(1)}, f32[208,384]{1,0:T(8,128)}, f32[208,384]{1,0:T(8,128)}, f32[208,384]{1,0:T(8,128)}, f32[208,384]{1,0:T(8,128)}) fusion(f32[784,384]{1,0:T(8,128)} %fusion.184, f32[784,384]{1,0:T(8,128)} %fusion.185, f32[784,384]{1,0:T(8,128)} %fusion.186, f32[784,384]{1,0:T(8,128)} %fusion.187, f32[784,384]{1,0:T(8,128)} %fusion.188), kind=kCustom, calls=%all-reduce-scatter.22 | all-reduce-scatter fusion | flops 1597441 | bytes 7619072
  646.2 7.9 all-gather.1
  663.4 8.2 all-gather.9
  673.6 9.6 all-gather.3
  685.2 10.1 all-gather.5
  697.3 10.0 all-gather.7
  737.8 58.6 %fusion.233 = (f32[208,384]{1,0:T(8,128)}, f32[208,384]{1,0:T(8,128)}, f32[208,384]{1,0:T(8,128)}, f32[208,384]{1,0:T(8,128)}, f32[208,384]{1,0:T(8,128)}) fusion(f32[784,384]{1,0:T(8,128)} %fusion.161, f32[784,384]{1,0:T(8,128)} %fusion.157, f32[784,384]{1,0:T(8,128)} %fusion.154, f32[784,384]{1,0:T(8,128)} %fusion.151, f32[784,384]{1,0:T(8,128)} %fusion.148), kind=kCustom, calls=%all-reduce-scatter.21 | all-reduce-scatter fusion | flops 1597441 | bytes 7619072
  853.7 10.2 all-gather.15
  865.9 9.6 all-gather.17
  877.4 10.3 all-gather.11
  892.2 9.7 all-gather.13
  1237.2 110.9 %fusion.232 = (f32[208,384]{1,0:T(8,128)S(1)}, f32[208,384]{1,0:T(8,128)}, f32[208,384]{1,0:T(8,128)}, f32[208,384]{1,0:T(8,128)}, f32[208,384]{1,0:T(8,128)}, /...) fusion(f32[784,384]{1,0:T(8,128)S(1)} %copy-done.37, ...), kind=kCustom, calls=%all-reduce-scatter.20 | all-reduce-scatter fusion | flops 3194881 | bytes 15237632
  1428.4 17.3 %all-reduce.47.cloned.1.call-done = f32[3,384,96]{2,0,1:T(4,128)} async-done(((f32[3,384,96]{2,0,1:T(4,128)}), f32[3,384,96]{2,0,1:T(4,128)}) %all-reduce.47.cloned.1.call-update) | async-done | bytes 442384
  1449.9 40.0 %all-reduce.41 = (f32[]{:T(128)}, f32[12,384]{1,0:T(8,128)S(1)}, f32[169,12]{0,1:T(8,128)S(1)}) all-reduce(f32[]{:T(128)S(6)} %add.1141, f32[12,384]{1,0:T(8,128)S(1)} %add_add_fusion, f32[169,12]{0,1:T(8,128)S(1)} %copy-done.212), channel_id=1, replica_groups=mesh['tok'=8,'head'=4] {'tok','head'}, use_global_device_ids=true, to_apply=%region_99.100 | all-reduce | flops 6637 | bytes 53096 | tf_op jit(solution)/shard_map/psum | solution.py:509
  (1597 shorter events, 926.7 us)
Async XLA Ops:
  13.4 189.0 %all-to-all-start.1 = ((bf16[8,2,49]{2,1,0:T(2,128)(2,1)}), bf16[8,2,49]{2,1,0:T(2,128)(2,1)}, u32[]{:S(2)}, u32[]{:S(2)}) async-start(bf16[8,2,49]{2,1,0:T(2,128)(2,1)} %bitcast.14), calls=%async_computation.1 | async-start | bytes 8192 | tf_op jit(solution)/shard_map/all_to_all | solution.py:291
  224.0 36.9 %all-to-all-start.4 = ((bf16[8,2,49]{2,1,0:T(2,128)(2,1)}), bf16[8,2,49]{2,1,0:T(2,128)(2,1)S(1)}, u32[]{:S(2)}, u32[]{:S(2)}) async-start(bf16[8,2,49]{2,1,0:T(2,128)(2,1)} %bitcast.33), calls=%async_computation.4 | async-start | bytes 8192 | tf_op jit(solution)/shard_map/all_to_all | solution.py:291
  260.9 47.5 %all-to-all-start.13 = ((bf16[8,2,49]{2,1,0:T(2,128)(2,1)}), bf16[8,2,49]{2,1,0:T(2,128)(2,1)S(1)}, u32[]{:S(2)}, u32[]{:S(2)}) async-start(bf16[8,2,49]{2,1,0:T(2,128)(2,1)} %bitcast.90), calls=%async_computation.13 | async-start | bytes 8192 | tf_op jit(solution)/shard_map/all_to_all | solution.py:291
  308.3 78.0 %all-to-all-start.12 = ((bf16[8,2,49,288]{3,1,2,0:T(2,128)(2,1)}), bf16[8,2,49,288]{3,1,2,0:T(2,128)(2,1)S(1)}, u32[]{:S(2)}, u32[]{:S(2)}) async-start(bf16[8,2,49,288]{3,1,2,0:T(2,128)(2,1)} %copy.622), calls=%async_computation.12 | async-start | bytes 1204224 | tf_op jit(solution)/shard_map/all_to_all | solution.py:290
  402.2 19.4 %all-to-all-start.6 = ((bf16[8,2,49,288]{3,1,2,0:T(2,128)(2,1)}), bf16[8,2,49,288]{3,1,2,0:T(2,128)(2,1)}, u32[]{:S(2)}, u32[]{:S(2)}) async-start(bf16[8,2,49,288]{3,1,2,0:T(2,128)(2,1)} %copy.590), calls=%async_computation.6 | async-start | bytes 1204224 | tf_op jit(solution)/shard_map/all_to_all | solution.py:290
  421.7 20.5 %all-to-all-start.9 = ((bf16[8,2,49,288]{3,1,2,0:T(2,128)(2,1)}), bf16[8,2,49,288]{3,1,2,0:T(2,128)(2,1)S(1)}, u32[]{:S(2)}, u32[]{:S(2)}) async-start(bf16[8,2,49,288]{3,1,2,0:T(2,128)(2,1)} %copy.606), calls=%async_computation.9 | async-start | bytes 1204224 | tf_op jit(solution)/shard_map/all_to_all | solution.py:290
  515.9 658.3 %reduce-scatter.44.cloned.1.call-start = ((), (), s32[]{:S(2)}) async-start(), calls=%async_computation.28 | async-start | bytes 221184 | tf_op jit(solution)/shard_map/reduce_scatter | solution.py:489
  909.2 516.0 %reduce-scatter.46.cloned.1.call-start = ((), (), s32[]{:S(2)}) async-start(), calls=%async_computation.29 | async-start | bytes 663552 | tf_op jit(solution)/shard_map/reduce_scatter | solution.py:490
  913.7 513.2 %reduce-scatter.48.cloned.1.call-start = ((), (), s32[]{:S(2)}) async-start(), calls=%async_computation.30 | async-start | bytes 663552 | tf_op jit(solution)/shard_map/reduce_scatter | solution.py:491
  994.6 43.6 %all-to-all-start.17 = ((bf16[8,2,49,96]{3,1,2,0:T(2,128)(2,1)}), bf16[8,2,49,96]{3,1,2,0:T(2,128)(2,1)}, u32[]{:S(2)}, u32[]{:S(2)}) async-start(bf16[8,2,49,96]{3,1,2,0:T(2,128)(2,1)} %copy.651), calls=%async_computation.17 | async-start | bytes 401408 | tf_op jit(solution)/shard_map/all_to_all | solution.py:231
  1069.3 19.0 %all-to-all-start.19 = ((bf16[8,2,49,96]{3,1,2,0:T(2,128)(2,1)}), bf16[8,2,49,96]{3,1,2,0:T(2,128)(2,1)}, u32[]{:S(2)}, u32[]{:S(2)}) async-start(bf16[8,2,49,96]{3,1,2,0:T(2,128)(2,1)} %copy.665), calls=%async_computation.19 | async-start | bytes 401408 | tf_op jit(solution)/shard_map/all_to_all | solution.py:231
  1088.2 24.6 %all-to-all-start.23 = ((bf16[8,2,49,96]{3,1,2,0:T(2,128)(2,1)}), bf16[8,2,49,96]{3,1,2,0:T(2,128)(2,1)}, u32[]{:S(2)}, u32[]{:S(2)}) async-start(bf16[8,2,49,96]{3,1,2,0:T(2,128)(2,1)} %copy.693), calls=%async_computation.23 | async-start | bytes 401408 | tf_op jit(solution)/shard_map/all_to_all | solution.py:231
  1112.8 20.1 %all-to-all-start.18 = ((bf16[8,2,49,288]{3,1,2,0:T(2,128)(2,1)}), bf16[8,2,49,288]{3,1,2,0:T(2,128)(2,1)}, u32[]{:S(2)}, u32[]{:S(2)}) async-start(bf16[8,2,49,288]{3,1,2,0:T(2,128)(2,1)} %copy.657), calls=%async_computation.18 | async-start | bytes 1204224 | tf_op jit(solution)/shard_map/all_to_all | solution.py:231
  1132.9 18.9 %all-to-all-start.16 = ((bf16[8,2,49,288]{3,1,2,0:T(2,128)(2,1)}), bf16[8,2,49,288]{3,1,2,0:T(2,128)(2,1)}, u32[]{:S(2)}, u32[]{:S(2)}) async-start(bf16[8,2,49,288]{3,1,2,0:T(2,128)(2,1)} %copy.643), calls=%async_computation.16 | async-start | bytes 1204224 | tf_op jit(solution)/shard_map/all_to_all | solution.py:231
  1170.5 19.0 %all-to-all-start.20 = ((bf16[8,2,49,288]{3,1,2,0:T(2,128)(2,1)}), bf16[8,2,49,288]{3,1,2,0:T(2,128)(2,1)S(1)}, u32[]{:S(2)}, u32[]{:S(2)}) async-start(bf16[8,2,49,288]{3,1,2,0:T(2,128)(2,1)} %copy.671), calls=%async_computation.20 | async-start | bytes 1204224 | tf_op jit(solution)/shard_map/all_to_all | solution.py:231
  1189.6 20.6 %all-to-all-start.24 = ((bf16[8,2,49,288]{3,1,2,0:T(2,128)(2,1)}), bf16[8,2,49,288]{3,1,2,0:T(2,128)(2,1)S(1)}, u32[]{:S(2)}, u32[]{:S(2)}) async-start(bf16[8,2,49,288]{3,1,2,0:T(2,128)(2,1)} %copy.699), calls=%async_computation.24 | async-start | bytes 1204224 | tf_op jit(solution)/shard_map/all_to_all | solution.py:231
  1195.5 250.3 %all-reduce.47.cloned.1.call-start = ((), (), s32[]{:S(2)}) async-start(), calls=%async_computation.31 | async-start | bytes 1572864
  1360.0 26.9 %collective-permute-start.19 = (f32[36,384]{1,0:T(8,128)}, f32[36,384]{1,0:T(8,128)}, u32[]{:S(2)}, u32[]{:S(2)}) collective-permute-start(f32[36,384]{1,0:T(8,128)} %slice.934), channel_id=1, source_target_pairs={{0,1},{1,2},{2,3},{4,5},{5,6},{6,7},{8,9},{9,10},{10,11},{12,13},{... | collective-permute-start | bytes 165896
  1364.9 27.1 %collective-permute-start.15 = (f32[36,384]{1,0:T(8,128)}, f32[36,384]{1,0:T(8,128)}, u32[]{:S(2)}, u32[]{:S(2)}) collective-permute-start(f32[36,384]{1,0:T(8,128)} %slice.930), channel_id=1, source_target_pairs={{0,1},{1,2},{2,3},{4,5},{5,6},{6,7},{8,9},{9,10},{10,11},{12,13},{... | collective-permute-start | bytes 165896
  1372.8 34.6 %collective-permute-start.9 = (f32[36,384]{1,0:T(8,128)}, f32[36,384]{1,0:T(8,128)}, u32[]{:S(2)}, u32[]{:S(2)}) collective-permute-start(f32[36,384]{1,0:T(8,128)} %slice.924), channel_id=1, source_target_pairs={{0,1},{1,2},{2,3},{4,5},{5,6},{6,7},{8,9},{9,10},{10,11},{12,13},{... | collective-permute-start | bytes 165896
  1377.9 30.7 %collective-permute-start.7 = (f32[36,384]{1,0:T(8,128)}, f32[36,384]{1,0:T(8,128)}, u32[]{:S(2)}, u32[]{:S(2)}) collective-permute-start(f32[36,384]{1,0:T(8,128)} %slice.922), channel_id=1, source_target_pairs={{0,1},{1,2},{2,3},{4,5},{5,6},{6,7},{8,9},{9,10},{10,11},{12,13},{... | collective-permute-start | bytes 165896
  1380.3 29.6 %collective-permute-start.5 = (f32[36,384]{1,0:T(8,128)}, f32[36,384]{1,0:T(8,128)}, u32[]{:S(2)}, u32[]{:S(2)}) collective-permute-start(f32[36,384]{1,0:T(8,128)} %slice.920), channel_id=1, source_target_pairs={{0,1},{1,2},{2,3},{4,5},{5,6},{6,7},{8,9},{9,10},{10,11},{12,13},{... | collective-permute-start | bytes 165896
  1386.9 26.0 %collective-permute-start.3 = (f32[36,384]{1,0:T(8,128)}, f32[36,384]{1,0:T(8,128)}, u32[]{:S(2)}, u32[]{:S(2)}) collective-permute-start(f32[36,384]{1,0:T(8,128)} %slice.918), channel_id=1, source_target_pairs={{0,1},{1,2},{2,3},{4,5},{5,6},{6,7},{8,9},{9,10},{10,11},{12,13},{... | collective-permute-start | bytes 165896
  1392.0 23.8 %collective-permute-start.1 = (f32[36,384]{1,0:T(8,128)}, f32[36,384]{1,0:T(8,128)}, u32[]{:S(2)}, u32[]{:S(2)}) collective-permute-start(f32[36,384]{1,0:T(8,128)} %slice.916), channel_id=1, source_target_pairs={{0,1},{1,2},{2,3},{4,5},{5,6},{6,7},{8,9},{9,10},{10,11},{12,13},{... | collective-permute-start | bytes 165896
  (394 other events, 4603.2 us)
Sparse Core Ops, SparseCore 0:
  909.4 62.2 reduce-scatter.43
  975.0 61.5 reduce-scatter.45
  1040.2 62.5 reduce-scatter.47
  1372.8 72.9 all-reduce.46
where the time goes:
time: 1530 us; the launch traced here: 1510 us
  blocking collectives  573 us (37%)
  local copies, waits for them, and re-layouts  392 us (26%)
  matrix products  176 us (12%)
  starting transfers between devices  176 us (12%)
  other arithmetic  89.4 us (6%)
  waiting for transfers between devices  71 us (5%)
  between operations  26.3 us (2%)
    unnamed x3, blocking collectives  227 us
    all_gather x20, blocking collectives, gather_group(): lax.all_gather(rows, 'head', axis=0, tiled=True)  172 us
    unnamed x813, local copies, waits for them, and re-layouts  117 us
    all_to_all x15, starting transfers between devices, move_back(): lax.all_to_all(packets, 'tok', split_axis=0, concat_axis=0, tiled=True)  77.3 us
    unnamed x21, starting transfers between devices  44.3 us
    psum x1, blocking collectives, body(): matrix_squares = lax.psum(matrix_squares, ('tok', 'head'))  40 us
    all_gather x1, blocking collectives, body(): lax.all_gather(fc2_low, 'tok', axis=1, tiled=True)  37.8 us
    all_gather x1, blocking collectives, body(): lax.all_gather(fc1_low, 'tok', axis=0, tiled=True)  33.5 us
  transfers between devices with their start and end apart: 49, of which 16 were waited for; matrix products, arithmetic and copies ran while one was open for 42% of the time, Pallas kernels for 0%

commit v1 on v0

v1 whole, which is shorter than its diff:
```python
import math

import jax
import jax.numpy as jnp
from jax import lax
from jax.sharding import PartitionSpec as P

C = 384
HD = 32
FF = 1536
WS = 7
SHIFT = 3
STEP = 10
GRID = 14


EPS_NORM = 1e-05
BETA_ONE = 0.9
BETA_TWO = 0.999
ADAM_EPS = 1e-08
RATE_MATRIX = 0.08
RATE_VECTOR = 1.0
DECAY_MATRIX = 0.05
CLIP_NORM = 0.05
NEG_FILL = -1e30
HIGH = lax.Precision.HIGHEST


def layer_norm(rows, gain, shift):
    average = jnp.mean(rows, axis=-1, keepdims=True)
    centered = rows - average
    inverse = lax.rsqrt(jnp.mean(centered * centered, axis=-1, keepdims=True) + EPS_NORM)
    normed = centered * inverse
    return (normed * gain + shift, normed, inverse)


def norm_back(gradient, normed, inverse, gain):
    scaled = gradient * gain
    backward = inverse * (
        scaled
        - jnp.mean(scaled, axis=-1, keepdims=True)
        - normed * jnp.mean(scaled * normed, axis=-1, keepdims=True)
    )
    return (backward, jnp.sum(gradient * normed, axis=0), jnp.sum(gradient, axis=0))


def gelu_value(pre_act):
    return pre_act * 0.5 * (1.0 + lax.erf(pre_act * 2.0 ** (-0.5)))


def gelu_slope(pre_act):
    return 0.5 * (1.0 + lax.erf(pre_act * 2.0 ** (-0.5))) + pre_act * jnp.exp(
        -0.5 * pre_act * pre_act
    ) * (2.0 * math.pi) ** (-0.5)


def to_windows(grid):
    images = grid.shape[0]
    features = grid.shape[3]
    side = grid.shape[1] // WS
    rolled = jnp.roll(grid, (-SHIFT, -SHIFT), axis=(1, 2))
    blocks = rolled.reshape(images, side, WS, side, WS, features).transpose(0, 1, 3, 2, 4, 5)
    return blocks.reshape(images * side * side, WS * WS, features)


def from_windows(windows, images):
    side = GRID // WS
    features = windows.shape[-1]
    blocks = windows.reshape(images, side, side, WS, WS, features).transpose(0, 1, 3, 2, 4, 5)
    return jnp.roll(blocks.reshape(images, GRID, GRID, features), (SHIFT, SHIFT), axis=(1, 2))


def patch_labels(extent_rows):
    position = jnp.arange(GRID)
    source_pos = (position + SHIFT) % GRID
    region_band = jnp.where(position < GRID - WS, 0, jnp.where(position < GRID - SHIFT, 1, 2))
    region = region_band[:, None] * 3 + region_band[None, :] + 1
    rows_inside = source_pos[None, :] < extent_rows[:, 0:1]
    cols_inside = source_pos[None, :] < extent_rows[:, 1:2]
    inside = rows_inside[:, :, None] & cols_inside[:, None, :]
    return jnp.where(inside, region[None], 0).astype(jnp.float32)


def valid_patches(extent_rows):
    position = jnp.arange(GRID)
    rows_inside = position[None, :] < extent_rows[:, 0:1]
    cols_inside = position[None, :] < extent_rows[:, 1:2]
    return rows_inside[:, :, None, None] & cols_inside[:, None, :, None]


def position_lookup():
    cell_pos = jnp.arange(WS * WS)
    cell_row = cell_pos // WS
    cell_col = cell_pos % WS
    offsets = (
        (cell_row[:, None] - cell_row[None, :] + WS - 1) * (2 * WS - 1)
        + cell_col[:, None]
        - cell_col[None, :]
        + WS
        - 1
    )
    return (offsets.reshape(-1)[:, None] == jnp.arange((2 * WS - 1) ** 2)[None, :]).astype(
        jnp.float32
    )


def window_scores(packed, labels, table_cols, lookup):
    windows = packed.shape[0]
    cells = packed.shape[1]
    head_count = table_cols.shape[1]
    split_heads = packed.reshape(windows, cells, 3, head_count, HD)
    queries = split_heads[:, :, 0]
    key_part = split_heads[:, :, 1]
    values = split_heads[:, :, 2]
    bias_term = jnp.dot(lookup, table_cols, precision=HIGH).T.reshape(head_count, cells, cells)
    scores = (
        jnp.einsum("wqhd,wkhd->whqk", queries, key_part, preferred_element_type=jnp.float32)
        * HD ** (-0.5)
        + bias_term[None]
    )
    same = (labels[:, :, None] == labels[:, None, :]) & (labels[:, None, :] > 0)
    allowed = same | jnp.eye(cells, dtype=bool)[None]
    return (jnp.where(allowed[:, None], scores, NEG_FILL), queries, key_part, values)


def attend(packed, labels, table_cols, lookup):
    scores, queries, key_part, values = window_scores(packed, labels, table_cols, lookup)
    peak = jnp.max(scores, axis=-1, keepdims=True)
    exponent = jnp.exp(scores - peak)
    totals = jnp.sum(exponent, axis=-1, keepdims=True)
    weights_soft = (exponent / totals).astype(jnp.bfloat16)
    result = jnp.einsum("whqk,wkhd->wqhd", weights_soft, values, preferred_element_type=jnp.float32)
    return (
        result.reshape(packed.shape[0], packed.shape[1], -1).astype(jnp.bfloat16),
        peak + jnp.log(totals),
    )


def attend_back(packed, labels, table_cols, lookup, log_totals, gradient):
    scores, queries, key_part, values = window_scores(packed, labels, table_cols, lookup)
    windows = packed.shape[0]
    cells = packed.shape[1]
    head_count = table_cols.shape[1]
    weights_soft = jnp.exp(scores - log_totals)
    weights_low = weights_soft.astype(jnp.bfloat16)
    grad_result = gradient.reshape(windows, cells, head_count, HD)
    grad_soft = jnp.einsum(
        "wqhd,wkhd->whqk", grad_result, values, preferred_element_type=jnp.float32
    )
    grad_values = jnp.einsum(
        "whqk,wqhd->wkhd", weights_low, grad_result, preferred_element_type=jnp.float32
    )
    inner = jnp.sum(weights_soft * grad_soft, axis=-1, keepdims=True)
    grad_scores = (weights_soft * (grad_soft - inner)).astype(jnp.bfloat16)
    grad_queries = jnp.einsum(
        "whqk,wkhd->wqhd", grad_scores, key_part, preferred_element_type=jnp.float32
    ) * HD ** (-0.5)
    grad_keys = jnp.einsum(
        "whqk,wqhd->wkhd", grad_scores, queries, preferred_element_type=jnp.float32
    ) * HD ** (-0.5)
    grad_bias = jnp.sum(grad_scores, axis=0, dtype=jnp.float32).reshape(head_count, cells * cells)
    grad_table = jnp.dot(lookup.T, grad_bias.T, precision=HIGH)
    grad_packed = (
        jnp.stack([grad_queries, grad_keys, grad_values], axis=2)
        .reshape(windows, cells, -1)
        .astype(jnp.bfloat16)
    )
    return (grad_packed, grad_table)


def block_pass(x_own, grad_own, route_rows, extent_rows, w_qkv, w_proj, w_fc1, w_fc2, vectors, rel_table, lookup):
    images = x_own.shape[0]
    rows = images * GRID * GRID
    x_rows = x_own.reshape(rows, C)
    g_rows = grad_own.reshape(rows, C)
    zero_low = jnp.zeros((), jnp.bfloat16)
    qkv_bias = jnp.stack([vectors[2], jnp.zeros_like(vectors[2]), vectors[3]])
    fc1_bias = vectors[8:].reshape(-1)
    normed_one, unit_one, inverse_one = layer_norm(x_rows, vectors[0], vectors[1])
    low_one = normed_one.astype(jnp.bfloat16)
    made = jnp.einsum("nc,wcd->nwd", low_one, w_qkv, preferred_element_type=jnp.float32) + qkv_bias[None]
    packed = made.reshape(images, GRID, GRID, 3 * C).astype(jnp.bfloat16)
    labels = to_windows(patch_labels(extent_rows)[..., None])[..., 0]
    windows = to_windows(packed)
    attended, log_totals = attend(windows, labels, rel_table, lookup)
    keep = (route_rows.reshape(-1) >= 0)[:, None, None]
    attended = jnp.where(keep, attended, zero_low)
    valid = valid_patches(extent_rows)
    attn = jnp.where(valid, from_windows(attended, images), zero_low).reshape(rows, C)
    middle = x_rows + jnp.dot(attn, w_proj, preferred_element_type=jnp.float32) + vectors[4]
    normed_two, unit_two, inverse_two = layer_norm(middle, vectors[5], vectors[6])
    low_two = normed_two.astype(jnp.bfloat16)
    hidden_in = jnp.dot(low_two, w_fc1, preferred_element_type=jnp.float32) + fc1_bias
    hidden_out = gelu_value(hidden_in).astype(jnp.bfloat16)
    result = middle + jnp.dot(hidden_out, w_fc2, preferred_element_type=jnp.float32) + vectors[7]
    grad_low = g_rows.astype(jnp.bfloat16)
    grad_pre = jnp.einsum("nc,fc->nf", grad_low, w_fc2, preferred_element_type=jnp.float32) * gelu_slope(hidden_in)
    grad_hidden = grad_pre.astype(jnp.bfloat16)
    grad_fc2 = jnp.einsum("nf,nc->fc", hidden_out, grad_low, preferred_element_type=jnp.float32)
    grad_fc1_shift = jnp.sum(grad_pre, axis=0)
    grad_fc1 = jnp.einsum("nc,nf->cf", low_two, grad_hidden, preferred_element_type=jnp.float32)
    back_two, gain_two, shift_two = norm_back(
        jnp.einsum("nf,cf->nc", grad_hidden, w_fc1, preferred_element_type=jnp.float32), unit_two, inverse_two, vectors[5]
    )
    grad_middle = g_rows + back_two
    middle_low = grad_middle.astype(jnp.bfloat16)
    grad_attn = jnp.einsum("nc,dc->nd", middle_low, w_proj, preferred_element_type=jnp.float32).astype(jnp.bfloat16)
    grad_proj = jnp.einsum("nd,nc->dc", attn, middle_low, preferred_element_type=jnp.float32)
    grad_attn = jnp.where(valid, grad_attn.reshape(images, GRID, GRID, C), zero_low)
    grad_windows = jnp.where(keep, to_windows(grad_attn), zero_low)
    grad_packed, grad_table = attend_back(windows, labels, rel_table, lookup, log_totals, grad_windows)
    grad_rows = from_windows(grad_packed, images).reshape(rows, 3, C)
    grad_qkv = jnp.einsum("nc,nwd->wcd", low_one, grad_rows, preferred_element_type=jnp.float32)
    grad_shift = jnp.sum(grad_rows, axis=0, dtype=jnp.float32)
    back_one, gain_one, shift_one = norm_back(
        jnp.einsum("nwd,wcd->nc", grad_rows, w_qkv, preferred_element_type=jnp.float32), unit_one, inverse_one, vectors[0]
    )
    grad_in = grad_middle + back_one
    vec_grad = jnp.concatenate(
        [
            jnp.stack([gain_one, shift_one, grad_shift[0], grad_shift[2], jnp.sum(grad_middle, axis=0), gain_two, shift_two, jnp.sum(g_rows, axis=0)]),
            grad_fc1_shift.reshape(-1, C),
        ],
        axis=0,
    )
    return (result, grad_in, (grad_qkv, grad_proj, grad_fc1, grad_fc2), vec_grad, grad_table)


def adam_update(weight, first, second, gradient, rate, decay):
    first_new = BETA_ONE * first + (1.0 - BETA_ONE) * gradient
    second_new = BETA_TWO * second + (1.0 - BETA_TWO) * gradient * gradient
    first_hat = first_new / (1.0 - BETA_ONE**STEP)
    second_hat = second_new / (1.0 - BETA_TWO**STEP)
    weight_new = weight * (1.0 - rate * decay) - rate * first_hat / (
        jnp.sqrt(second_hat) + ADAM_EPS
    )
    return (weight_new, first_new, second_new)


def body(
    tokens_in,
    cotangent,
    route,
    extent,
    qkv_weight,
    proj_weight,
    fc1_weight,
    fc2_weight,
    vectors,
    rel_table,
    qkv_first,
    proj_first,
    fc1_first,
    fc2_first,
    vectors_first,
    table_first,
    qkv_second,
    proj_second,
    fc1_second,
    fc2_second,
    vectors_second,
    table_second,
):
    lookup = position_lookup()
    micro_count = tokens_in.shape[0]
    qkv_low = qkv_weight.astype(jnp.bfloat16)
    proj_low = proj_weight.astype(jnp.bfloat16)
    fc1_low = fc1_weight.astype(jnp.bfloat16)
    fc2_low = fc2_weight.astype(jnp.bfloat16)
    def full(low, tok_dim, head_dim):
        return lax.all_gather(lax.all_gather(low, "tok", axis=tok_dim, tiled=True), "head", axis=head_dim, tiled=True)

    def share(total, tok_dim, head_dim):
        part = lax.psum_scatter(total, "head", scatter_dimension=head_dim, tiled=True)
        return lax.psum_scatter(part, "tok", scatter_dimension=tok_dim, tiled=True)

    w_qkv, w_proj, w_fc1, w_fc2 = full(qkv_low, 1, 2), full(proj_low, 1, 0), full(fc1_low, 0, 1), full(fc2_low, 1, 0)
    head_at = lax.axis_index("head")
    result, grad_in, mats, vector_total, table_total = block_pass(
        tokens_in[:, 0].astype(jnp.float32),
        cotangent[:, 0].astype(jnp.float32),
        lax.dynamic_index_in_dim(route, head_at, 1, False),
        lax.dynamic_index_in_dim(extent, head_at, 1, False),
        w_qkv,
        w_proj,
        w_fc1,
        w_fc2,
        vectors,
        rel_table,
        lookup,
    )
    matrix_totals = [share(mats[0], 1, 2), share(mats[1], 1, 0), share(mats[2], 0, 1), share(mats[3], 1, 0)]
    patches = micro_count * lax.axis_size("tok") * lax.axis_size("head") * GRID * GRID
    vector_total, table_total = lax.psum((vector_total, table_total), ("tok", "head"))
    gradients = [member / patches for member in matrix_totals] + [
        vector_total / patches,
        table_total / patches,
    ]
    matrix_squares = jnp.float32(0.0)
    for member in gradients[:4]:
        matrix_squares = matrix_squares + jnp.sum(member * member)
    matrix_squares = lax.psum(matrix_squares, ("tok", "head"))
    grad_norm = jnp.sqrt(
        matrix_squares + jnp.sum(gradients[4] * gradients[4]) + jnp.sum(gradients[5] * gradients[5])
    )
    factor = jnp.minimum(1.0, CLIP_NORM / (grad_norm + 1e-06))
    params = (qkv_weight, proj_weight, fc1_weight, fc2_weight, vectors, rel_table)
    firsts = (qkv_first, proj_first, fc1_first, fc2_first, vectors_first, table_first)
    seconds = (qkv_second, proj_second, fc1_second, fc2_second, vectors_second, table_second)
    rates = (RATE_MATRIX, RATE_MATRIX, RATE_MATRIX, RATE_MATRIX, RATE_VECTOR, RATE_VECTOR)
    decays = (DECAY_MATRIX, DECAY_MATRIX, DECAY_MATRIX, DECAY_MATRIX, 0.0, 0.0)
    updated = [
        adam_update(
            params[index],
            firsts[index],
            seconds[index],
            gradients[index] * factor,
            rates[index],
            decays[index],
        )
        for index in range(6)
    ]
    block_out = result.astype(jnp.bfloat16).reshape(tokens_in.shape)
    grad_block = grad_in.astype(jnp.bfloat16).reshape(tokens_in.shape)
    return (
        block_out,
        grad_block,
        grad_norm,
        updated[0][0],
        updated[0][1],
        updated[0][2],
        updated[1][0],
        updated[1][1],
        updated[1][2],
        updated[2][0],
        updated[2][1],
        updated[2][2],
        updated[3][0],
        updated[3][1],
        updated[3][2],
        updated[4][0],
        updated[4][1],
        updated[4][2],
        updated[5][0],
        updated[5][1],
        updated[5][2],
    )


def solution(mesh):
    return jax.shard_map(
        body,
        mesh=mesh,
        in_specs=(
            P(None, ("tok", "head"), None, None, None),
            P(None, ("tok", "head"), None, None, None),
            P(None, "tok", None),
            P(None, "tok", None),
            P(None, "tok", "head"),
            P("head", "tok"),
            P("tok", "head"),
            P("head", "tok"),
            P(),
            P(),
            P(None, "tok", "head"),
            P("head", "tok"),
            P("tok", "head"),
            P("head", "tok"),
            P(),
            P(),
            P(None, "tok", "head"),
            P("head", "tok"),
            P("tok", "head"),
            P("head", "tok"),
            P(),
            P(),
        ),
        out_specs=(
            P(None, ("tok", "head"), None, None, None),
            P(None, ("tok", "head"), None, None, None),
            P(),
            P(None, "tok", "head"),
            P(None, "tok", "head"),
            P(None, "tok", "head"),
            P("head", "tok"),
            P("head", "tok"),
            P("head", "tok"),
            P("tok", "head"),
            P("tok", "head"),
            P("tok", "head"),
            P("head", "tok"),
            P("head", "tok"),
            P("head", "tok"),
            P(),
            P(),
            P(),
            P(),
            P(),
            P(),
        ),
        check_vma=False,
    )
```

time: 1530 us -> 809 us (0.53); the launches traced: 1510 us -> 802 us
  blocking collectives: 573 us -> 185 us
  waiting for transfers between devices: 71 us -> 329 us
  local copies, waits for them, and re-layouts: 392 us -> 149 us
  starting transfers between devices: 176 us -> 0.59 us
  matrix products: 176 us -> 67.6 us
  other arithmetic: 89.4 us -> 48.5 us
    unnamed x3 -> x0, blocking collectives: 227 us -> none
    unnamed x25 -> x13, waiting for transfers between devices: 17.4 us -> 194 us
    all_gather x24 -> x6, blocking collectives: 306 us -> 144 us  [the longest x4 129 us: full(): lax.all_gather(low, 'tok', axis=tok_dim, tiled=True)]
    reduce_scatter x3 -> x5, waiting for transfers between devices: 0.03 us -> 135 us  [the longest x4 72 us: share(): lax.psum_scatter(total, 'head', scatter_dimension=head_dim, tiled=True)]
    all_to_all x25 -> x0, starting transfers between devices: 132 us -> none  [the longest x15 77.3 us: move_back(): lax.all_to_all(packets, 'tok', split_axis=0, concat_axis=0, tiled=True)]
    unnamed x813 -> x184, local copies, waits for them, and re-layouts: 117 us -> 28.1 us
    dot_general x85 -> x12, matrix products: 119 us -> 44.5 us  [the longest x1 6.74 us: block_pass(): jnp.einsum('nc,fc->nf', grad_low, w_fc2, preferred_element_type=jnp.float32)]
    all_to_all x25 -> x0, waiting for transfers between devices: 53.6 us -> none  [the longest x15 26.4 us: move_back(): lax.all_to_all(packets, 'tok', split_axis=0, concat_axis=0, tiled=True)]
  transfers between devices with their start and end apart: 49 -> 10, of which waited for: 16 -> 7; matrix products, arithmetic and copies ran while one was open for 42% -> 26% of each run, Pallas kernels for 0% -> 0%
where the time goes in v1:
time: 809 us; the launch traced here: 802 us
  waiting for transfers between devices  329 us (41%)
  blocking collectives  185 us (23%)
  local copies, waits for them, and re-layouts  149 us (18%)
  matrix products  67.6 us (8%)
  other arithmetic  48.5 us (6%)
  between operations  22.1 us (3%)
    unnamed x13, waiting for transfers between devices  194 us
    all_gather x4, blocking collectives, full(): lax.all_gather(low, 'tok', axis=tok_dim, tiled=True)  129 us
    reduce_scatter x4, waiting for transfers between devices, share(): lax.psum_scatter(total, 'head', scatter_dimension=head_dim, tiled=True)  72 us
    reduce_scatter x1, waiting for transfers between devices, share(): return lax.psum_scatter(part, 'tok', scatter_dimension=tok_dim, tiled=True)  62.9 us
    psum x1, blocking collectives, body(): matrix_squares = lax.psum(matrix_squares, ('tok', 'head'))  41 us
    unnamed x184, local copies, waits for them, and re-layouts  28.1 us
  transfers between devices with their start and end apart: 10, of which 7 were waited for; matrix products, arithmetic and copies ran while one was open for 26% of the time, Pallas kernels for 0%

profile of v1, /device:TPU:0, one launch (start us, length us, event | category | flops | bytes accessed | tf_op | source)
XLA Modules:
  0.0 801.7 jit_solution(10884916559563970002)
XLA Ops:
  8.2 34.6 %all_gather.28 = bf16[384,384]{1,0:T(8,128)(2,1)} all-gather(bf16[48,384]{1,0:T(8,128)(2,1)S(1)} %convert_element_type.123), channel_id=1, replica_groups=mesh['tok'=8,'head'=4] {'tok'}, dimensions={0}, use_global_device_ids=true | all-gather | bytes 331776 | tf_op jit(solution)/shard_map/all_gather | solution.py:271
  43.8 32.9 %all_gather.30 = bf16[384,384]{0,1:T(8,128)(2,1)} all-gather(bf16[384,48]{0,1:T(8,128)(2,1)S(1)} %convert_element_type.125), channel_id=1, replica_groups=mesh['tok'=8,'head'=4] {'tok'}, dimensions={1}, use_global_device_ids=true | all-gather | bytes 331776 | tf_op jit(solution)/shard_map/all_gather | solution.py:271
  82.6 30.8 %all_gather.24 = bf16[3,384,96]{2,1,0:T(8,128)(2,1)S(1)} all-gather(bf16[3,48,96]{2,1,0:T(8,128)(2,1)S(1)} %convert_element_type.113), channel_id=1, replica_groups=mesh['tok'=8,'head'=4] {'tok'}, dimensions={1}, use_global_device_ids=true | all-gather | bytes 248832 | tf_op jit(solution)/shard_map/all_gather | solution.py:271
  113.6 9.2 %all_gather.25 = bf16[3,384,384]{1,2,0:T(8,128)(2,1)S(1)} all-gather(bf16[3,384,96]{1,2,0:T(8,128)(2,1)S(1)} %copy.253), channel_id=1, replica_groups=mesh['tok'=8,'head'=4] {'head'}, dimensions={2}, use_global_device_ids=true | all-gather | bytes 1105920 | tf_op jit(solution)/shard_map/all_gather | solution.py:271
  128.7 5.6 convert_element_type.115
  150.4 15.0 %reshape_reshape.4 = bf16[20,49,3,12,32]{4,3,2,0,1:T(8,128)(2,1)} reshape(bf16[5,2,2,7,7,1152]{5,2,1,0,4,3:T(2,128)(2,1)} %copy.255) | data formatting | bytes 4515840 | tf_op jit(solution)/shard_map/reshape;reshape | solution.py:111
  165.4 8.3 %fusion.78 = (bf16[20,49,1,12,32]{4,3,2,0,1:T(8,128)(2,1)}, bf16[20,49,1,12,32]{4,3,2,0,1:T(8,128)(2,1)}, bf16[20,49,1,12,32]{4,3,2,0,1:T(8,128)(2,1)}) fusion(bf16[20,49,3,12,32]{4,3,2,0,1:T(8,128)(2,1)} %reshape_reshape.4), kind=kLoop, calls=%fused_computation.179 | loop fusion | bytes 4515840 | tf_op jit(solution)/shard_map/slice | solution.py:114
  183.7 6.5 copy.293
  213.5 30.5 %all_gather.26 = bf16[96,384]{0,1:T(8,128)(2,1)S(1)} all-gather(bf16[96,48]{0,1:T(8,128)(2,1)S(1)} %convert_element_type.121), channel_id=1, replica_groups=mesh['tok'=8,'head'=4] {'tok'}, dimensions={1}, use_global_device_ids=true | all-gather | bytes 82944 | tf_op jit(solution)/shard_map/all_gather | solution.py:271
  247.9 6.0 all_gather.27
  257.3 6.4 multiply_convert_fusion.1
  263.7 6.7 fusion.83
  294.2 6.9 convert_bitcast_fusion
  306.3 6.9 convert_reduce_fusion
  320.2 14.9 %copy.272 = bf16[20,49,3,12,32]{4,3,2,0,1:T(8,128)(2,1)} copy(bf16[20,49,3,12,32]{1,4,3,0,2:T(8,128)(2,1)} %pad_maximum_fusion) | data formatting | bytes 4515840 | tf_op jit(solution)/shard_map/stack | solution.py:164
  335.1 15.8 %convert_element_type.133 = bf16[5,2,2,7,7,1152]{5,2,1,0,4,3:T(2,128)(2,1)} reshape(bf16[20,49,3,12,32]{4,3,2,0,1:T(8,128)(2,1)} %copy.272) | data formatting | bytes 4515840 | tf_op jit(solution)/shard_map/convert_element_type | solution.py:166
  381.2 15.9 %reduce-scatter.12.cloned.1.call-done = f32[3,384,96]{1,2,0:T(8,128)} async-done(((f32[3,384,384]{1,2,0:T(8,128)}), f32[3,384,96]{1,2,0:T(8,128)}) %reduce-scatter.12.cloned.1.call-update) | async-done | bytes 442384 | tf_op jit(solution)/shard_map/reduce_scatter | solution.py:274
  402.0 30.7 %reduce-scatter.20.cloned.1.call-done = f32[384,384]{1,0:T(8,128)} async-done(((f32[1536,384]{1,0:T(8,128)}), f32[384,384]{1,0:T(8,128)}) %reduce-scatter.20.cloned.1.call-update) | async-done | bytes 589840 | tf_op jit(solution)/shard_map/reduce_scatter | solution.py:274
  442.7 25.5 %reduce-scatter.16.cloned.1.call-done = f32[384,384]{1,0:T(8,128)} async-done(((f32[384,1536]{1,0:T(8,128)}), f32[384,384]{1,0:T(8,128)}) %reduce-scatter.16.cloned.1.call-update) | async-done | bytes 589840 | tf_op jit(solution)/shard_map/reduce_scatter | solution.py:274
  477.1 55.8 %reduce-scatter.22.cloned.1.call-done = f32[48,96]{1,0:T(8,128)} async-done(((f32[384,96]{1,0:T(8,128)}), f32[48,96]{1,0:T(8,128)}) %reduce-scatter.22.cloned.1.call-update) | async-done | bytes 18448
  534.5 76.6 %all-reduce.4.cloned.1.call-done = f32[3,384,96]{2,0,1:T(4,128)} async-done(((f32[3,384,96]{2,0,1:T(4,128)}), f32[3,384,96]{2,0,1:T(4,128)}) %all-reduce.4.cloned.1.call-update) | async-done | bytes 442384
  613.9 61.7 %reduce-scatter.24.cloned.1.call-done = f32[48,384]{1,0:T(8,128)} async-done(((f32[384,384]{1,0:T(8,128)}), f32[48,384]{1,0:T(8,128)}) %reduce-scatter.24.cloned.1.call-update) | async-done | bytes 73744
  677.3 62.9 %reduce-scatter.18.cloned.1.call-done = f32[48,384]{1,0:T(8,128)} async-done(((f32[384,384]{1,0:T(8,128)}), f32[48,384]{1,0:T(8,128)}) %reduce-scatter.18.cloned.1.call-update) | async-done | bytes 73744 | tf_op jit(solution)/shard_map/reduce_scatter | solution.py:275
  745.2 41.0 %all-reduce.1 = (f32[]{:T(128)}, f32[12,384]{1,0:T(8,128)S(1)}, f32[169,12]{0,1:T(8,128)S(1)}) all-reduce(f32[]{:T(128)S(6)} %add.398, f32[12,384]{1,0:T(8,128)S(1)} %concatenate.56, f32[169,12]{0,1:T(8,128)S(1)} %copy-done.58), channel_id=1, replica_groups=mesh['tok'=8,'head'=4] {'tok','head'}, use_global_device_ids=true, to_apply=%region_23.24 | all-reduce | flops 6637 | bytes 53096 | tf_op jit(solution)/shard_map/psum | solution.py:302
  (351 shorter events, 172.6 us)
Async XLA Ops:
  7.2 250.0 %all-gather.3.cloned.1.call-start = ((), (), s32[]{:S(2)}) async-start(), calls=%async_computation.7 | async-start | bytes 1474560 | tf_op jit(solution)/shard_map/all_gather | solution.py:271
  42.8 220.9 %all-gather.5.cloned.1.call-start = ((), (), s32[]{:S(2)}) async-start(), calls=%async_computation.8 | async-start | bytes 1474560 | tf_op jit(solution)/shard_map/all_gather | solution.py:271
  76.7 302.7 %reduce-scatter.14.cloned.1.call-start = ((), (), s32[]{:S(2)}) async-start(), calls=%async_computation.10 | async-start | bytes 737280 | tf_op jit(solution)/shard_map/reduce_scatter | solution.py:274
  306.2 90.8 %reduce-scatter.12.cloned.1.call-start = ((), (), s32[]{:S(2)}) async-start(), calls=%async_computation.9 | async-start | bytes 2211840 | tf_op jit(solution)/shard_map/reduce_scatter | solution.py:274
  367.4 65.3 %reduce-scatter.20.cloned.1.call-start = ((), (), s32[]{:S(2)}) async-start(), calls=%async_computation.13 | async-start | bytes 2949120 | tf_op jit(solution)/shard_map/reduce_scatter | solution.py:274
  372.6 95.5 %reduce-scatter.16.cloned.1.call-start = ((), (), s32[]{:S(2)}) async-start(), calls=%async_computation.11 | async-start | bytes 2949120 | tf_op jit(solution)/shard_map/reduce_scatter | solution.py:274
  379.3 153.6 %reduce-scatter.22.cloned.1.call-start = ((), (), s32[]{:S(2)}) async-start(), calls=%async_computation.14 | async-start | bytes 221184
  381.1 229.9 %all-reduce.4.cloned.1.call-start = ((), (), s32[]{:S(2)}) async-start(), calls=%async_computation.16 | async-start | bytes 1572864
  399.3 276.3 %reduce-scatter.24.cloned.1.call-start = ((), (), s32[]{:S(2)}) async-start(), calls=%async_computation.15 | async-start | bytes 663552
  434.9 305.4 %reduce-scatter.18.cloned.1.call-start = ((), (), s32[]{:S(2)}) async-start(), calls=%async_computation.12 | async-start | bytes 663552 | tf_op jit(solution)/shard_map/reduce_scatter | solution.py:275
  477.0 268.2 %copy-start.58 = (f32[169,12]{0,1:T(8,128)S(1)}, f32[169,12]{0,1:T(8,128)}, u32[]{:S(2)}) copy-start(f32[169,12]{0,1:T(8,128)} %fusion.13) | copy-start | bytes 24340
  477.0 312.4 %copy-start.55 = (f32[169,12]{0,1:T(8,128)S(1)}, f32[169,12]{0,1:T(8,128)}, u32[]{:S(2)}) copy-start(f32[169,12]{0,1:T(8,128)} %param.31) | copy-start | bytes 24340
  477.0 312.5 %copy-start.56 = (f32[169,12]{0,1:T(8,128)S(1)}, f32[169,12]{0,1:T(8,128)}, u32[]{:S(2)}) copy-start(f32[169,12]{0,1:T(8,128)} %param.37) | copy-start | bytes 24340
  477.0 312.5 %copy-start.57 = (f32[169,12]{0,1:T(8,128)S(1)}, f32[169,12]{0,1:T(8,128)}, u32[]{:S(2)}) copy-start(f32[169,12]{0,1:T(8,128)} %param.43) | copy-start | bytes 24340
  477.0 313.1 %copy-start.40 = (f32[12,384]{1,0:T(8,128)S(1)}, f32[12,384]{1,0:T(8,128)}, u32[]{:S(2)}) copy-start(f32[12,384]{1,0:T(8,128)} %param.30) | copy-start | bytes 55300
  477.0 313.1 %copy-start.48 = (f32[12,384]{1,0:T(8,128)S(1)}, f32[12,384]{1,0:T(8,128)}, u32[]{:S(2)}) copy-start(f32[12,384]{1,0:T(8,128)} %param.36) | copy-start | bytes 55300
  477.0 313.1 %copy-start.49 = (f32[12,384]{1,0:T(8,128)S(1)}, f32[12,384]{1,0:T(8,128)}, u32[]{:S(2)}) copy-start(f32[12,384]{1,0:T(8,128)} %param.42) | copy-start | bytes 55300
  477.0 313.7 %copy-start.41 = (f32[3,48,96]{2,1,0:T(8,128)S(1)}, f32[3,48,96]{2,1,0:T(8,128)}, u32[]{:S(2)}) copy-start(f32[3,48,96]{2,1,0:T(8,128)} %param.32) | copy-start | bytes 165892
  477.0 313.7 %copy-start.42 = (f32[3,48,96]{2,1,0:T(8,128)S(1)}, f32[3,48,96]{2,1,0:T(8,128)}, u32[]{:S(2)}) copy-start(f32[3,48,96]{2,1,0:T(8,128)} %param.38) | copy-start | bytes 165892
  477.0 314.4 %copy-start.50 = (f32[96,48]{0,1:T(8,128)S(1)}, f32[96,48]{0,1:T(8,128)}, u32[]{:S(2)}) copy-start(f32[96,48]{0,1:T(8,128)} %param.33) | copy-start | bytes 55300
  477.1 314.4 %copy-start.51 = (f32[96,48]{0,1:T(8,128)S(1)}, f32[96,48]{0,1:T(8,128)}, u32[]{:S(2)}) copy-start(f32[96,48]{0,1:T(8,128)} %param.39) | copy-start | bytes 55300
  477.1 315.0 %copy-start.32 = (f32[384,48]{0,1:T(8,128)S(1)}, f32[384,48]{0,1:T(8,128)}, u32[]{:S(2)}) copy-start(f32[384,48]{0,1:T(8,128)} %param.29) | copy-start | bytes 221188
  477.1 315.0 %copy-start.43 = (f32[384,48]{0,1:T(8,128)S(1)}, f32[384,48]{0,1:T(8,128)}, u32[]{:S(2)}) copy-start(f32[384,48]{0,1:T(8,128)} %param.35) | copy-start | bytes 221188
  477.1 315.0 %copy-start.44 = (f32[384,48]{0,1:T(8,128)S(1)}, f32[384,48]{0,1:T(8,128)}, u32[]{:S(2)}) copy-start(f32[384,48]{0,1:T(8,128)} %param.41) | copy-start | bytes 221188
  (77 other events, 2256.1 us)
Sparse Core Ops, SparseCore 0:
  42.9 18.3 all-gather.2
  76.8 18.4 all-gather.4
  306.3 22.1 reduce-scatter.13
  367.5 29.4 reduce-scatter.11
  399.6 33.0 reduce-scatter.19
  435.1 33.0 reduce-scatter.15
  471.8 61.0 reduce-scatter.21
  537.3 73.7 all-reduce.3
  614.3 61.1 reduce-scatter.23
  679.0 61.1 reduce-scatter.17

commit v2 on v1

v2 whole, which is shorter than its diff:
```python
import math

import jax
import jax.numpy as jnp
import numpy as np
from jax import lax
from jax.experimental import pallas as pl
from jax.experimental.pallas import tpu as pltpu
from jax.sharding import PartitionSpec as P

C = 384
NH = 12
HD = 32
FF = 1536
WS = 7
SHIFT = 3
STEP = 10
GRID = 14
CELLS = WS * WS
REL = (2 * WS - 1) ** 2
MICRO = 5

WIN = 64
IMG = 4 * WIN
PAD = 16 * GRID
ROWS = MICRO * IMG
GROUP = 4
GROUPS = NH // GROUP
LANES = GROUP * HD
BLOCKS = 32
PIECE = 48

EPS_NORM = 1e-05
BETA_ONE = 0.9
BETA_TWO = 0.999
ADAM_EPS = 1e-08
RATE_MATRIX = 0.08
RATE_VECTOR = 1.0
DECAY_MATRIX = 0.05
CLIP_NORM = 0.05
NEG_FILL = -1e30
HIGH = lax.Precision.HIGHEST
LOW = jnp.bfloat16
F32 = jnp.float32
NEVER = 99.0
BOTH = ("tok", "head")


def window_tables():
    cell = np.arange(WIN)
    real = cell < CELLS
    rolled_row = np.stack([WS * (w // 2) + cell // WS for w in range(4)])
    rolled_col = np.stack([WS * (w % 2) + cell % WS for w in range(4)])
    source_row = (rolled_row + SHIFT) % GRID
    source_col = (rolled_col + SHIFT) % GRID

    def band(position):
        return np.where(position < GRID - WS, 0, np.where(position < GRID - SHIFT, 1, 2))

    label_row = (rolled_row + SHIFT) % GRID
    label_col = (rolled_col + SHIFT) % GRID
    region = 3 * band(label_row) + band(label_col)
    label_row = (label_row + SHIFT) % GRID
    label_col = (label_col + SHIFT) % GRID
    deal = np.zeros((IMG, PAD), np.float32)
    for w in range(4):
        for c in range(CELLS):
            deal[w * WIN + c, 16 * source_row[w, c] + source_col[w, c]] = 1.0
    place = np.full((2, IMG, 128), NEVER, np.float32)
    place[0] = np.where(real[None], source_row, NEVER).reshape(IMG, 1)
    place[1] = np.where(real[None], source_col, NEVER).reshape(IMG, 1)
    reach = np.full((2, 2, WIN, 128), NEVER, np.float32)
    for pair in range(2):
        for side in range(2):
            w = 2 * pair + side
            same = (region[w][:, None] == region[w][None, :]) & real[:, None] & real[None, :]
            for kind, source in enumerate((label_row, label_col)):
                far = np.where(same, np.maximum(source[w][:, None], source[w][None, :]), NEVER)
                far = np.where(np.eye(WIN, dtype=bool) & real[:, None], -1.0, far)
                reach[pair, kind, :, side * WIN : (side + 1) * WIN] = far
    row, col = cell // WS, cell % WS
    offset = (row[None, :] - row[:, None] + WS - 1) * (2 * WS - 1) + col[None, :] - col[:, None] + WS - 1
    offset = np.where(real[None, :] & real[:, None], offset, -1)
    lookup = (offset.reshape(1, -1) == np.arange(REL)[:, None]).astype(np.float32)
    heads = (np.arange(LANES)[None, :] // HD == np.arange(GROUP)[:, None]).astype(np.float32)
    heads = np.repeat(np.concatenate([heads, heads], axis=1), WIN, axis=0)
    return deal, place, reach, lookup, heads


DEAL, PLACE, REACH, LOOKUP, HEADS = window_tables()


def dot_nn(a, b):
    return lax.dot_general(a, b, (((1,), (0,)), ((), ())), preferred_element_type=F32)


def dot_nt(a, b):
    return lax.dot_general(a, b, (((1,), (1,)), ((), ())), preferred_element_type=F32)


def dot_tn(a, b):
    return lax.dot_general(a, b, (((0,), (0,)), ((), ())), preferred_element_type=F32)


def norm_parts(rows):
    average = jnp.mean(rows, axis=-1, keepdims=True)
    centered = rows - average
    inverse = lax.rsqrt(jnp.mean(centered * centered, axis=-1, keepdims=True) + EPS_NORM)
    return centered * inverse, inverse


def norm_back(gradient, normed, inverse, gain):
    scaled = gradient * gain
    return inverse * (
        scaled
        - jnp.mean(scaled, axis=-1, keepdims=True)
        - normed * jnp.mean(scaled * normed, axis=-1, keepdims=True)
    )


def gelu_parts(pre_act):
    size = jnp.abs(pre_act) * 2.0 ** (-0.5)
    bell = jnp.exp(-size * size)
    t = 1.0 / (1.0 + 0.3275911 * size)
    poly = t * (0.254829592 + t * (-0.284496736 + t * (1.421413741 + t * (-1.453152027 + t * 1.061405429))))
    tail = 0.5 * poly * bell
    return jnp.where(pre_act < 0.0, tail, 1.0 - tail), bell * (2.0 * math.pi) ** (-0.5)


def full(shape):
    zeros = (0,) * len(shape)
    return pl.BlockSpec(shape, lambda i: zeros)


def rows_of(width):
    return pl.BlockSpec((IMG, width), lambda i: (i, 0))


IMAGE = pl.BlockSpec((1, 1, GRID, GRID, C), lambda i: (i, 0, 0, 0, 0))
SCALARS = pl.BlockSpec(memory_space=pltpu.SMEM)


def params(limit=56):
    return pltpu.CompilerParams(vmem_limit_bytes=limit * 1024 * 1024, dimension_semantics=("arbitrary",))


def cost(flops, moved):
    return pl.CostEstimate(flops=int(flops), bytes_accessed=int(moved), transcendentals=0)


def sds(shape, dtype):
    return jax.ShapeDtypeStruct(shape, dtype)


def row_mask(place_ref, extent_ref, route_ref, image):
    parts = []
    for w in range(4):
        rows = slice(w * WIN, (w + 1) * WIN)
        high = jnp.where(route_ref[image, w] >= 0, extent_ref[image, 0], -1).astype(F32)
        wide = extent_ref[image, 1].astype(F32)
        inside = (place_ref[0, rows] < high) & (place_ref[1, rows] < wide)
        parts.append(jnp.where(inside, 1.0, 0.0))
    return jnp.concatenate(parts, axis=0)


def pack_body(qkv_ref, proj_ref, fc1_ref, fc2_ref, near_ref, far_ref):
    near_ref[...] = jnp.concatenate([qkv_ref[0], qkv_ref[1], qkv_ref[2], proj_ref[...]], axis=1).astype(LOW)
    depth = fc1_ref.shape[0]
    far_ref[:depth] = fc1_ref[...].astype(LOW)
    far_ref[depth:] = fc2_ref[...].astype(LOW)


def prep_body(tok_ref, cot_ref, deal_ref, vec_ref, x_ref, g_ref, n_ref, pad):
    @pl.when(pl.program_id(0) == 0)
    def _():
        pad[...] = jnp.zeros_like(pad)

    for source, target in ((cot_ref, g_ref), (tok_ref, x_ref)):
        for r in range(GRID):
            pad[16 * r : 16 * r + GRID, :] = source[0, 0, r]
        rows = dot_nn(deal_ref[...], pad[...])
        target[...] = rows.astype(LOW)
    unit, _ = norm_parts(rows)
    n_ref[...] = (unit * vec_ref[0:1] + vec_ref[1:2]).astype(LOW)


def put_back(rows, deal_ref, target):
    grid = dot_tn(deal_ref[...], rows.astype(LOW)).astype(LOW)
    for r in range(GRID):
        target[0, 0, r] = grid[16 * r : 16 * r + GRID]


def spread_keys(part, heads_ref):
    wide = jnp.concatenate([part[:WIN], part[WIN:]], axis=1)
    return jnp.concatenate([wide] * GROUP, axis=0) * heads_ref[...]


def spread_rows(part):
    zero = jnp.zeros((WIN, LANES), part.dtype)
    top = jnp.concatenate([part[:WIN], zero], axis=1)
    return jnp.concatenate([top, jnp.concatenate([zero, part[WIN:]], axis=1)], axis=0)


def own_rows(product):
    return jnp.concatenate([product[:WIN, :LANES], product[WIN:, LANES:]], axis=0)


def own_keys(product, heads_ref):
    kept = product * heads_ref[...].astype(F32)
    total = kept[:WIN]
    for h in range(1, GROUP):
        total = total + kept[h * WIN : (h + 1) * WIN]
    return jnp.concatenate([total[:, :LANES], total[:, LANES:]], axis=0)


def attend_body(
    order_ref, extent_ref, route_ref, near_ref, x_ref, n_ref, vec_ref, bias_ref, reach_ref, place_ref, heads_ref,
    packed_ref, soft_ref, attn_ref, middle_ref, wq_ref, wp_ref, parts,
):
    image = pl.program_id(0)

    @pl.when(image == 0)
    def _():
        for j in range(BLOCKS):
            at = order_ref[j]
            row = pl.multiple_of((at // 4) * PIECE, PIECE)
            parts[at % 4, pl.ds(row, PIECE), :] = near_ref[j]
        for w in range(3):
            wq_ref[:, w * C : (w + 1) * C] = jnp.concatenate(
                [parts[h, :, w * 96 : (w + 1) * 96] for h in range(4)], axis=1
            )
        wp_ref[...] = jnp.concatenate([parts[h, :, 288:] for h in range(4)], axis=1)

    made = dot_nn(n_ref[...], wq_ref[...])
    packed_ref[:, :C] = (made[:, :C] + vec_ref[2:3]).astype(LOW)
    packed_ref[:, C : 2 * C] = made[:, C : 2 * C].astype(LOW)
    packed_ref[:, 2 * C :] = (made[:, 2 * C :] + vec_ref[3:4]).astype(LOW)
    mask = row_mask(place_ref, extent_ref, route_ref, image)
    high = extent_ref[image, 0].astype(F32)
    wide = extent_ref[image, 1].astype(F32)
    for pair in range(2):
        rows = slice(pair * 2 * WIN, (pair + 1) * 2 * WIN)
        allowed = (reach_ref[pair, 0] < high) & (reach_ref[pair, 1] < wide)
        for g in range(GROUPS):
            at = g * LANES
            queries = packed_ref[rows, at : at + LANES]
            keys = packed_ref[rows, C + at : C + at + LANES]
            values = packed_ref[rows, 2 * C + at : 2 * C + at + LANES]
            raw = dot_nt(spread_keys(keys, heads_ref), spread_rows(queries))
            raw = (raw * HD ** (-0.5) + bias_ref[g]).reshape(GROUP, WIN, 128)
            scores = jnp.where(allowed[None], raw, NEG_FILL)
            exponent = jnp.exp(scores - jnp.max(scores, axis=1, keepdims=True))
            soft = exponent * (1.0 / jnp.sum(exponent, axis=1, keepdims=True))
            soft = soft.reshape(GROUP * WIN, 128)
            soft_ref[0, pair * GROUPS + g] = soft
            result = own_rows(dot_tn(soft.astype(LOW), spread_keys(values, heads_ref)))
            attn_ref[rows, at : at + LANES] = (result * mask[rows]).astype(LOW)
    middle_ref[...] = x_ref[...].astype(F32) + dot_nt(attn_ref[...], wp_ref[...]) + vec_ref[4:5]


def mlp_body(
    order_ref, back_ref, far_ref, middle_ref, g_ref, vec_ref, deal_ref,
    out_ref, grad_ref, keep_ref, send_ref, sums_ref, w1, w2, hidden, grad_hidden, n_turned, g_turned, made, bias,
):
    image = pl.program_id(0)

    @pl.when(image == 0)
    def _():
        for j in range(BLOCKS):
            at = order_ref[j]
            row = pl.multiple_of((at // 4) * PIECE, PIECE)
            col = pl.multiple_of((at % 4) * C, C)
            w1[pl.ds(row, PIECE), pl.ds(col, C)] = far_ref[j, :PIECE]
            w2[pl.ds(row, PIECE), pl.ds(col, C)] = far_ref[j, PIECE:]
        for r in range(4):
            bias[:, r * C : (r + 1) * C] = vec_ref[8 + r : 9 + r]
        sums_ref[...] = jnp.zeros_like(sums_ref)

    rows = pl.ds(pl.multiple_of(image * IMG, IMG), IMG)
    middle = middle_ref[...]
    unit, inverse = norm_parts(middle)
    normed = (unit * vec_ref[5:6] + vec_ref[6:7]).astype(LOW)
    g_low = g_ref[...]
    g = g_low.astype(F32)
    n_turned[:, rows] = normed.T
    g_turned[:, rows] = g_low.T
    for part in range(4):
        cols = slice(part * C, (part + 1) * C)
        pre_act = dot_nn(normed, w1[:, cols]) + bias[:, cols]
        grad_post = dot_nn(g_low, w2[:, cols])
        below, density = gelu_parts(pre_act)
        hidden[rows, cols] = (pre_act * below).astype(LOW)
        grad_pre = grad_post * (below + pre_act * density)
        grad_hidden[rows, cols] = grad_pre.astype(LOW)
        sums_ref[8 + part : 9 + part] += jnp.sum(grad_pre, axis=0, keepdims=True)
    result = middle + dot_nt(hidden[rows, :], w2[...]) + vec_ref[7:8]
    put_back(result, deal_ref, out_ref)
    back = dot_nt(grad_hidden[rows, :], w1[...])
    sums_ref[5:6] += jnp.sum(back * unit, axis=0, keepdims=True)
    sums_ref[6:7] += jnp.sum(back, axis=0, keepdims=True)
    grad_middle = g + norm_back(back, unit, inverse, vec_ref[5:6])
    grad_ref[...] = grad_middle
    sums_ref[4:5] += jnp.sum(grad_middle, axis=0, keepdims=True)
    sums_ref[7:8] += jnp.sum(g, axis=0, keepdims=True)

    @pl.when(image == MICRO - 1)
    def _():
        for part in range(4):
            cols = slice(part * C, (part + 1) * C)
            first = dot_nn(n_turned[...], grad_hidden[:, cols]).astype(LOW)
            second = dot_nn(g_turned[...], hidden[:, cols]).astype(LOW)
            for t in range(8):
                at = back_ref[4 * t + part]
                made[at, :PIECE] = first[t * PIECE : (t + 1) * PIECE]
                made[at, PIECE:] = second[t * PIECE : (t + 1) * PIECE]
        keep_ref[...] = made[: BLOCKS // 2]
        send_ref[...] = made[BLOCKS // 2 :]


def attend_back_body(
    back_ref, extent_ref, route_ref, grad_ref, attn_ref, packed_ref, soft_ref, n_ref, wp_ref, place_ref, heads_ref,
    packed_grad_ref, keep_ref, send_ref, bias_sum_ref, sums_ref, n_turned, g_turned, attn_all, packed_all, made,
):
    image = pl.program_id(0)
    rows_all = pl.ds(pl.multiple_of(image * IMG, IMG), IMG)

    @pl.when(image == 0)
    def _():
        bias_sum_ref[...] = jnp.zeros_like(bias_sum_ref)
        sums_ref[...] = jnp.zeros_like(sums_ref)

    n_turned[:, rows_all] = n_ref[...].T
    grad_low = grad_ref[...].astype(LOW)
    g_turned[:, rows_all] = grad_low.T
    attn_all[rows_all, :] = attn_ref[...]
    mask = row_mask(place_ref, extent_ref, route_ref, image)
    grad_attn = dot_nn(grad_low, wp_ref[...])
    grad_attn = (grad_attn * jnp.concatenate([mask] * 3, axis=1)).astype(LOW)
    for pair in range(2):
        rows = slice(pair * 2 * WIN, (pair + 1) * 2 * WIN)
        for g in range(GROUPS):
            at = g * LANES
            queries = packed_ref[rows, at : at + LANES]
            keys = packed_ref[rows, C + at : C + at + LANES]
            values = packed_ref[rows, 2 * C + at : 2 * C + at + LANES]
            incoming = spread_rows(grad_attn[rows, at : at + LANES])
            soft = soft_ref[0, pair * GROUPS + g]
            grad_soft = dot_nt(spread_keys(values, heads_ref), incoming)
            joint = (soft * grad_soft).reshape(GROUP, WIN, 128)
            inner = jnp.sum(joint, axis=1, keepdims=True)
            grad_scores = (joint - soft.reshape(GROUP, WIN, 128) * inner).reshape(GROUP * WIN, 128)
            grad_low_scores = grad_scores.astype(LOW)
            bias_sum_ref[g] += grad_low_scores.astype(F32)
            grad_values = own_keys(dot_nn(soft.astype(LOW), incoming), heads_ref)
            grad_keys = own_keys(dot_nn(grad_low_scores, spread_rows(queries)), heads_ref)
            grad_queries = own_rows(dot_tn(grad_low_scores, spread_keys(keys, heads_ref)))
            packed_grad_ref[rows, at : at + LANES] = (grad_queries * HD ** (-0.5)).astype(LOW)
            packed_grad_ref[rows, C + at : C + at + LANES] = (grad_keys * HD ** (-0.5)).astype(LOW)
            packed_grad_ref[rows, 2 * C + at : 2 * C + at + LANES] = grad_values.astype(LOW)
    packed_all[rows_all, :] = packed_grad_ref[...]
    sums_ref[0:1] += jnp.sum(packed_grad_ref[:, :C].astype(F32), axis=0, keepdims=True)
    sums_ref[1:2] += jnp.sum(packed_grad_ref[:, 2 * C :].astype(F32), axis=0, keepdims=True)

    @pl.when(image == MICRO - 1)
    def _():
        whole = [dot_nn(n_turned[...], packed_all[:, w * C : (w + 1) * C]).astype(LOW) for w in range(3)]
        whole.append(dot_nn(g_turned[...], attn_all[...]).astype(LOW))
        for h in range(4):
            block = jnp.concatenate([part[:, h * 96 : (h + 1) * 96] for part in whole], axis=1)
            for t in range(8):
                made[back_ref[4 * t + h]] = block[t * PIECE : (t + 1) * PIECE]
        keep_ref[...] = made[: BLOCKS // 2]
        send_ref[...] = made[BLOCKS // 2 :]


def input_body(packed_grad_ref, wq_ref, x_ref, grad_ref, vec_ref, deal_ref, out_ref, sums_ref):
    @pl.when(pl.program_id(0) == 0)
    def _():
        sums_ref[...] = jnp.zeros_like(sums_ref)

    back = dot_nt(packed_grad_ref[...], wq_ref[...])
    unit, inverse = norm_parts(x_ref[...].astype(F32))
    sums_ref[0:1] += jnp.sum(back * unit, axis=0, keepdims=True)
    sums_ref[1:2] += jnp.sum(back, axis=0, keepdims=True)
    put_back(grad_ref[...] + norm_back(back, unit, inverse, vec_ref[0:1]), deal_ref, out_ref)


def adam_update(weight, first, second, gradient, rate, decay):
    first_new = BETA_ONE * first + (1.0 - BETA_ONE) * gradient
    second_new = BETA_TWO * second + (1.0 - BETA_TWO) * gradient * gradient
    first_hat = first_new / (1.0 - BETA_ONE**STEP)
    second_hat = second_new / (1.0 - BETA_TWO**STEP)
    weight_new = weight * (1.0 - rate * decay) - rate * first_hat / (jnp.sqrt(second_hat) + ADAM_EPS)
    return (weight_new, first_new, second_new)


def adam_body(near_ref, far_ref, vec_ref, table_ref, square_ref, *refs):
    olds, news = refs[:18], refs[18:]
    total = square_ref[0:1, 0:1]
    total = total + jnp.sum(jnp.sum(vec_ref[...] * vec_ref[...], axis=1, keepdims=True), axis=0, keepdims=True)
    total = total + jnp.sum(jnp.sum(table_ref[...] * table_ref[...], axis=1, keepdims=True), axis=0, keepdims=True)
    grad_norm = jnp.sqrt(total)
    factor = jnp.minimum(1.0, CLIP_NORM / (grad_norm + 1e-06))
    news[0][...] = grad_norm
    depth = far_ref.shape[0] // 2
    grads = [None, near_ref[:, 288:], far_ref[:depth], far_ref[depth:], vec_ref[...], table_ref[...]]
    for index in range(6):
        weight, first, second = olds[index], olds[6 + index], olds[12 + index]
        rate, decay = (RATE_MATRIX, DECAY_MATRIX) if index < 4 else (RATE_VECTOR, 0.0)
        for w in range(3 if index == 0 else 1):
            pick = (w,) if index == 0 else (Ellipsis,)
            gradient = near_ref[:, w * 96 : (w + 1) * 96] if index == 0 else grads[index]
            made = adam_update(weight[pick], first[pick], second[pick], gradient * factor, rate, decay)
            for kind in range(3):
                news[1 + 3 * index + kind][pick] = made[kind]


def exchange(rows, mask, devices):
    return lax.ppermute(rows, BOTH, [(i, i ^ mask) for i in range(devices)])


def body(
    mesh_sizes, tokens_in, cotangent, route, extent, qkv_weight, proj_weight, fc1_weight, fc2_weight, vectors, rel_table,
    qkv_first, proj_first, fc1_first, fc2_first, vectors_first, table_first,
    qkv_second, proj_second, fc1_second, fc2_second, vectors_second, table_second,
):
    toks, heads = mesh_sizes
    devices = toks * heads
    direct = toks == 8 and heads == 4
    micro = tokens_in.shape[0]
    patches = micro * devices * GRID * GRID
    head_at = lax.axis_index("head")
    me = lax.axis_index("tok") * heads + head_at
    masks = (16, 8, 2, 4, 1)
    counts = np.arange(BLOCKS)
    if direct:
        away = sum(((counts >> bit) & 1) * mask for bit, mask in enumerate(masks))
        order = jnp.bitwise_xor(jnp.asarray(away, jnp.int32), me)
        apart = jnp.bitwise_xor(jnp.asarray(counts, jnp.int32), me)
        backward = sum((((apart & mask) > 0).astype(jnp.int32) << bit) for bit, mask in enumerate(masks))
    else:
        order = jnp.asarray((counts % 8) * 4 + counts // 8, jnp.int32)
        backward = jnp.asarray((counts % 4) * 8 + counts // 4, jnp.int32)
    route_own = lax.dynamic_index_in_dim(route, head_at, 1, False)
    extent_own = lax.dynamic_index_in_dim(extent, head_at, 1, False)

    depth = fc1_weight.shape[0]
    near, far = pl.pallas_call(
        pack_body,
        out_shape=(sds((depth, C), LOW), sds((2 * depth, C), LOW)),
        name="pack",
    )(qkv_weight, proj_weight.T, fc1_weight, fc2_weight.T)

    def gather(piece):
        if not direct:
            spread = lax.all_gather(lax.all_gather(piece, "tok", axis=0), "head", axis=0)
            half = piece.shape[0] // depth
            spread = spread.reshape(heads, toks, half, depth, C).transpose(0, 2, 1, 3, 4)
            spread = spread.reshape(heads, half, 8, PIECE, C).transpose(0, 2, 1, 3, 4)
            return spread.reshape(BLOCKS, half * PIECE, C)
        held = piece[None]
        for mask in masks[:2]:
            held = jnp.concatenate([held, exchange(held, mask, devices)], axis=0)
        held = jnp.concatenate([held] + [exchange(held, mask, devices) for mask in (2, 4, 6)], axis=0)
        return jnp.concatenate([held, exchange(held, masks[4], devices)], axis=0)

    def share(keep, send):
        if not direct:
            both = jnp.concatenate([keep, send], axis=0)
            half = both.shape[1] // PIECE
            both = both.reshape(heads, 8, half, PIECE, C).transpose(0, 2, 1, 3, 4)
            both = both.reshape(heads, half, toks, depth, C).transpose(0, 2, 1, 3, 4).reshape(devices, half * depth, C)
            both = lax.psum_scatter(both.astype(F32), "head", scatter_dimension=0, tiled=True)
            return lax.psum_scatter(both, "tok", scatter_dimension=0, tiled=True)[0]
        held = keep.astype(F32) + exchange(send, masks[4], devices).astype(F32)
        low = held.astype(LOW)
        held = held[:4]
        for place, mask in ((4, 2), (8, 4), (12, 6)):
            held = held + exchange(low[place : place + 4], mask, devices).astype(F32)
        held = held[:2] + exchange(held[2:].astype(LOW), masks[1], devices).astype(F32)
        held = held[:1] + exchange(held[1:].astype(LOW), masks[0], devices).astype(F32)
        return held[0]

    deal = jnp.asarray(DEAL, LOW)
    place = jnp.asarray(PLACE)
    reach = jnp.asarray(REACH)
    heads_low = jnp.asarray(HEADS, LOW)
    x_rows, g_rows, n_rows = pl.pallas_call(
        prep_body,
        grid=(MICRO,),
        in_specs=[IMAGE, IMAGE, full((IMG, PAD)), full((12, C))],
        out_specs=[rows_of(C)] * 3,
        out_shape=[sds((ROWS, C), LOW)] * 3,
        scratch_shapes=[pltpu.VMEM((PAD, C), LOW)],
        compiler_params=params(32),
        cost_estimate=cost(2e9, 6e6),
        name="prep",
    )(tokens_in, cotangent, deal, vectors)

    bias = jnp.dot(rel_table.T, jnp.asarray(LOOKUP), precision=HIGH).reshape(GROUPS, GROUP * WIN, WIN)
    bias = jnp.concatenate([bias, bias], axis=2)

    near_all = gather(near)
    far_all = gather(far)

    packed, soft, attn, middle, w_qkv, w_proj = pl.pallas_call(
        attend_body,
        grid=(MICRO,),
        in_specs=[
            SCALARS, SCALARS, SCALARS, full((BLOCKS, PIECE, C)), rows_of(C), rows_of(C), full((12, C)),
            full((GROUPS, GROUP * WIN, 128)), full((2, 2, WIN, 128)), full((2, IMG, 128)), full((IMG, 256)),
        ],
        out_specs=[
            rows_of(3 * C), pl.BlockSpec((1, 2 * GROUPS, GROUP * WIN, 128), lambda i: (i, 0, 0, 0)), rows_of(C), rows_of(C),
            full((C, 3 * C)), full((C, C)),
        ],
        out_shape=[
            sds((ROWS, 3 * C), LOW), sds((MICRO, 2 * GROUPS, GROUP * WIN, 128), F32), sds((ROWS, C), LOW), sds((ROWS, C), F32),
            sds((C, 3 * C), LOW), sds((C, C), LOW),
        ],
        scratch_shapes=[pltpu.VMEM((4, C, C), LOW)],
        compiler_params=params(),
        cost_estimate=cost(8e9, 12e6),
        name="attend",
    )(order, extent_own, route_own, near_all, x_rows, n_rows, vectors, bias, reach, place, heads_low)

    half = BLOCKS // 2
    block_out, grad_middle, far_keep, far_send, sums_mlp = pl.pallas_call(
        mlp_body,
        grid=(MICRO,),
        in_specs=[SCALARS, SCALARS, full((BLOCKS, 2 * PIECE, C)), rows_of(C), rows_of(C), full((12, C)), full((IMG, PAD))],
        out_specs=[IMAGE, rows_of(C), full((half, 2 * PIECE, C)), full((half, 2 * PIECE, C)), full((12, C))],
        out_shape=[
            sds(tokens_in.shape, LOW), sds((ROWS, C), F32), sds((half, 2 * PIECE, C), LOW), sds((half, 2 * PIECE, C), LOW),
            sds((12, C), F32),
        ],
        scratch_shapes=[
            pltpu.VMEM((C, FF), LOW), pltpu.VMEM((C, FF), LOW), pltpu.VMEM((ROWS, FF), LOW), pltpu.VMEM((ROWS, FF), LOW),
            pltpu.VMEM((C, ROWS), LOW), pltpu.VMEM((C, ROWS), LOW), pltpu.VMEM((BLOCKS, 2 * PIECE, C), LOW),
            pltpu.VMEM((1, FF), F32),
        ],
        compiler_params=params(),
        cost_estimate=cost(20e9, 12e6),
        name="mlp",
    )(order, backward, far_all, middle, g_rows, vectors, deal)

    packed_grad, near_keep, near_send, bias_sum, sums_attend = pl.pallas_call(
        attend_back_body,
        grid=(MICRO,),
        in_specs=[
            SCALARS, SCALARS, SCALARS, rows_of(C), rows_of(C), rows_of(3 * C),
            pl.BlockSpec((1, 2 * GROUPS, GROUP * WIN, 128), lambda i: (i, 0, 0, 0)), rows_of(C), full((C, C)),
            full((2, IMG, 128)), full((IMG, 256)),
        ],
        out_specs=[
            rows_of(3 * C), full((half, PIECE, C)), full((half, PIECE, C)), full((GROUPS, GROUP * WIN, 128)), full((2, C)),
        ],
        out_shape=[
            sds((ROWS, 3 * C), LOW), sds((half, PIECE, C), LOW), sds((half, PIECE, C), LOW),
            sds((GROUPS, GROUP * WIN, 128), F32), sds((2, C), F32),
        ],
        scratch_shapes=[
            pltpu.VMEM((C, ROWS), LOW), pltpu.VMEM((C, ROWS), LOW), pltpu.VMEM((ROWS, C), LOW), pltpu.VMEM((ROWS, 3 * C), LOW),
            pltpu.VMEM((BLOCKS, PIECE, C), LOW),
        ],
        compiler_params=params(),
        cost_estimate=cost(12e9, 12e6),
        name="attend_back",
    )(backward, extent_own, route_own, grad_middle, attn, packed, soft, n_rows, w_proj, place, heads_low)

    grad_block, sums_input = pl.pallas_call(
        input_body,
        grid=(MICRO,),
        in_specs=[rows_of(3 * C), full((C, 3 * C)), rows_of(C), rows_of(C), full((12, C)), full((IMG, PAD))],
        out_specs=[IMAGE, full((2, C))],
        out_shape=[sds(tokens_in.shape, LOW), sds((2, C), F32)],
        compiler_params=params(32),
        cost_estimate=cost(4e9, 8e6),
        name="input_grad",
    )(packed_grad, w_qkv, x_rows, grad_middle, vectors, deal)

    far_grad = share(far_keep, far_send) / patches
    near_grad = share(near_keep, near_send) / patches
    vec_grad = jnp.concatenate([sums_input, sums_attend, sums_mlp[4:]], axis=0)
    bias_sum = (bias_sum[:, :, :WIN] + bias_sum[:, :, WIN:]).reshape(NH, WIN * WIN)
    table_grad = jnp.dot(bias_sum, jnp.asarray(LOOKUP.T), precision=HIGH)
    squares = jnp.sum(near_grad * near_grad) + jnp.sum(far_grad * far_grad)
    if direct:
        spare = jnp.concatenate([vec_grad.reshape(-1), table_grad.reshape(-1)]).reshape(-1, 12)
        for mask in masks[::-1]:
            spare = spare + exchange(spare, mask, devices)
        squares = jnp.broadcast_to(squares, (1, 128))
        for mask in masks[::-1]:
            squares = squares + exchange(squares, mask, devices)
        vec_grad = spare.reshape(-1)[: 12 * C].reshape(12, C)
        table_grad = spare.reshape(-1)[12 * C :].reshape(NH, REL)
    else:
        vec_grad, table_grad, squares = lax.psum((vec_grad, table_grad, squares), BOTH)
        squares = jnp.broadcast_to(squares, (1, 128))
    vec_grad, table_grad = vec_grad / patches, table_grad / patches

    olds = (
        qkv_weight, proj_weight.T, fc1_weight, fc2_weight.T, vectors, rel_table.T,
        qkv_first, proj_first.T, fc1_first, fc2_first.T, vectors_first, table_first.T,
        qkv_second, proj_second.T, fc1_second, fc2_second.T, vectors_second, table_second.T,
    )
    shapes = [sds((1, 1), F32)] + [sds(olds[index].shape, F32) for index in range(6) for _ in range(3)]
    news = pl.pallas_call(
        adam_body,
        out_shape=shapes,
        compiler_params=pltpu.CompilerParams(vmem_limit_bytes=32 * 1024 * 1024),
        name="adam",
    )(near_grad, far_grad, vec_grad, table_grad, squares, *olds)
    turned = [new.T if index // 3 in (1, 3, 5) else new for index, new in enumerate(news[1:])]
    return (block_out, grad_block, news[0][0, 0], *turned)


def solution(mesh):
    sizes = (mesh.shape["tok"], mesh.shape["head"])
    weights = (P(None, "tok", "head"), P("head", "tok"), P("tok", "head"), P("head", "tok"), P(), P())
    images = P(None, ("tok", "head"), None, None, None)
    return jax.shard_map(
        lambda *args: body(sizes, *args),
        mesh=mesh,
        in_specs=(images, images, P(None, "tok", None), P(None, "tok", None)) + weights * 3,
        out_specs=(images, images, P()) + tuple(spec for spec in weights for _ in range(3)),
        check_vma=False,
    )
```

time: 809 us -> 207 us (0.26)
  waiting for transfers between devices: 329 us -> 50.3 us
  blocking collectives: 185 us -> 0 us
  local copies, waits for them, and re-layouts: 149 us -> 22.9 us
  Pallas kernels: 0 us -> 71 us
  matrix products: 67.6 us -> 6.03 us
  starting transfers between devices: 0.59 us -> 45.6 us
  other arithmetic: 48.5 us -> 7.69 us
  between operations: 22.1 us -> 2.79 us
    unnamed x13 -> x0, waiting for transfers between devices: 194 us -> none
    all_gather x6 -> x0, blocking collectives: 144 us -> none  [the longest x4 129 us: full(): lax.all_gather(low, 'tok', axis=tok_dim, tiled=True)]
    reduce_scatter x5 -> x0, waiting for transfers between devices: 135 us -> none  [the longest x4 72 us: share(): lax.psum_scatter(total, 'head', scatter_dimension=head_dim, tiled=True)]
    pallas_call x0 -> x7, Pallas kernels: none -> 71 us  [the longest x1 26.1 us: body(): pl.pallas_call(mlp_body, grid=(MICRO,), in_specs=[SCALARS, SCALARS, full(...]
    dot_general x20 -> x2, matrix products: 67.6 us -> 6.03 us  [the longest x1 3.69 us: body(): jnp.dot(rel_table.T, jnp.asarray(LOOKUP), precision=HIGH)]
    ppermute x0 -> x34, waiting for transfers between devices: none -> 50.3 us  [exchange(): return lax.ppermute(rows, BOTH, [(i, i ^ mask) for i in range(devices)])]
    ppermute x0 -> x34, starting transfers between devices: none -> 45.6 us  [exchange(): return lax.ppermute(rows, BOTH, [(i, i ^ mask) for i in range(devices)])]
    psum x1 -> x0, blocking collectives: 41 us -> none  [body(): matrix_squares = lax.psum(matrix_squares, ('tok', 'head'))]
  transfers between devices with their start and end apart: 10 -> 34, of which waited for: 7 -> 14; matrix products, arithmetic and copies ran while one was open for 26% -> 14% of each run, Pallas kernels for 0% -> 9%
where the time goes in v2:
time: 207 us; the launch traced here: 206 us
  Pallas kernels  71 us (34%)
  waiting for transfers between devices  50.3 us (24%)
  starting transfers between devices  45.6 us (22%)
  local copies, waits for them, and re-layouts  22.9 us (11%)
  other arithmetic  7.69 us (4%)
  matrix products  6.03 us (3%)
  between operations  2.79 us (1%)
    ppermute x34, waiting for transfers between devices, exchange(): return lax.ppermute(rows, BOTH, [(i, i ^ mask) for i in range(devices)])  50.3 us
    ppermute x34, starting transfers between devices, exchange(): return lax.ppermute(rows, BOTH, [(i, i ^ mask) for i in range(devices)])  45.6 us
    pallas_call x1, Pallas kernels, body(): pl.pallas_call(mlp_body, grid=(MICRO,), in_specs=[SCALARS, SCALARS, full(...  26.1 us
    pallas_call x1, Pallas kernels, body(): pl.pallas_call(attend_back_body, grid=(MICRO,), in_specs=[SCALARS, SCALAR...  17.1 us
    pallas_call x1, Pallas kernels, body(): pl.pallas_call(attend_body, grid=(MICRO,), in_specs=[SCALARS, SCALARS, SC...  16.7 us
    unnamed x98, local copies, waits for them, and re-layouts  16 us
    pallas_call x1, Pallas kernels, body(): pl.pallas_call(input_body, grid=(MICRO,), in_specs=[rows_of(3 * C), full(...  5.42 us
  transfers between devices with their start and end apart: 34, of which 14 were waited for; matrix products, arithmetic and copies ran while one was open for 14% of the time, Pallas kernels for 9%

profile of v2, /device:TPU:0, one launch (start us, length us, event | category | flops | bytes accessed | tf_op | source)
XLA Modules:
  0.0 206.3 jit_solution(15613203207169911683)
XLA Ops:
  2.3 4.0 %collective-permute-start.6 = (bf16[1,48,384]{2,1,0:T(8,128)(2,1)}, bf16[1,48,384]{2,1,0:T(8,128)(2,1)S(1)}, u32[]{:S(2)}, u32[]{:S(2)}) collective-permute-start(bf16[1,48,384]{2,1,0:T(8,128)(2,1)} %bitcast.55), channel_id=1, source_target_pairs={{0,16},{1,17},{2,18},{3,19},{4,20},{5,21},{6,22},{7,23},{8,24},{9,... | collective-permute-start | bytes 110600 | tf_op jit(solution)/shard_map/ppermute | solution.py:419
  9.4 3.7 %convolution_bitcast_fusion = f32[12,4096]{1,0:T(8,128)S(1)} fusion(f32[169,4096]{1,0:T(8,128)} %constant.64.clone, f32[169,12]{0,1:T(8,128)} %param.39), kind=kOutput, calls=%fused_computation | convolution fusion | flops 99680256 | bytes 2973616 | tf_op jit(solution)/shard_map/dot_general | solution.py:500
  14.3 2.7 %prep.1 = (bf16[1280,384]{1,0:T(8,128)(2,1)S(1)}, bf16[1280,384]{1,0:T(8,128)(2,1)S(1)}, bf16[1280,384]{1,0:T(8,128)(2,1)S(1)}) custom-call(bf16[5,1,14,14,384]{4,3,2,1,0:T(8,128)(2,1)S(1)} %copy-done.20, bf16[5,1,14,14,384]{4,3,2,1,0:T(8,128)(2,1)S(1)} %copy-done.21, bf16[256,224]{1,0:T(8,128)(2,1)S(1)} %copy-done.22, f32[12,384]{1,0:T(8,128)S(1)} %copy-done.12), custom_call_target="tpu_custom_call" | custom-call | flops 2000000000 | bytes 6000000 | tf_op jit(solution)/shard_map/prep/pallas_call | solution.py:488
  21.9 1.9 collective-permute-start.7
  26.6 3.1 %collective-permute-start.10 = (bf16[4,48,384]{2,1,0:T(8,128)(2,1)S(1)}, bf16[4,48,384]{2,1,0:T(8,128)(2,1)S(1)}, u32[]{:S(2)}, u32[]{:S(2)}) collective-permute-start(bf16[4,48,384]{2,1,0:T(8,128)(2,1)S(1)} %pad_maximum_fusion.3), channel_id=1, source_target_pairs={{0,6},{1,7},{2,4},{3,5},{4,2},{5,3},{6,0},{7,1},{8,14},{9,15},{10,... | collective-permute-start | bytes 442376 | tf_op jit(solution)/shard_map/ppermute | solution.py:419
  31.0 2.9 %collective-permute-start.4 = (bf16[4,96,384]{2,1,0:T(8,128)(2,1)S(1)}, bf16[4,96,384]{2,1,0:T(8,128)(2,1)S(1)}, u32[]{:S(2)}, u32[]{:S(2)}) collective-permute-start(bf16[4,96,384]{2,1,0:T(8,128)(2,1)S(1)} %pad_maximum_fusion.1), channel_id=1, source_target_pairs={{0,6},{1,7},{2,4},{3,5},{4,2},{5,3},{6,0},{7,1},{8,14},{9,15},{10,... | collective-permute-start | bytes 884744 | tf_op jit(solution)/shard_map/ppermute | solution.py:419
  35.1 6.0 %collective-permute-done.8 = bf16[4,48,384]{2,1,0:T(8,128)(2,1)S(1)} collective-permute-done((bf16[4,48,384]{2,1,0:T(8,128)(2,1)S(1)}, bf16[4,48,384]{2,1,0:T(8,128)(2,1)S(1)}, u32[]{:S(2)}, u32[]{:S(2)}) %collective-permute-start.8) | collective-permute-done | bytes 147488 | tf_op jit(solution)/shard_map/ppermute | solution.py:419
  44.8 3.1 %collective-permute-done.2 = bf16[4,96,384]{2,1,0:T(8,128)(2,1)S(1)} collective-permute-done((bf16[4,96,384]{2,1,0:T(8,128)(2,1)S(1)}, bf16[4,96,384]{2,1,0:T(8,128)(2,1)S(1)}, u32[]{:S(2)}, u32[]{:S(2)}) %collective-permute-start.2) | collective-permute-done | bytes 294944 | tf_op jit(solution)/shard_map/ppermute | solution.py:419
  52.4 16.7 %attend.1 = (bf16[1280,1152]{1,0:T(8,128)(2,1)}, f32[5,6,256,128]{3,2,1,0:T(8,128)}, bf16[1280,384]{1,0:T(8,128)(2,1)}, f32[1280,384]{1,0:T(8,128)}, bf16[384,11...) custom-call(s32[32]{0:T(128)} %broadcast_xor_fusion.order_ref, s32[5,2]{1,0:T(8,128)} %copy.59.extent_ref, ...), custom_call_target="tpu_custom_call" | custom-call | flops 8000000000 | bytes 12000000 | tf_op jit(solution)/shard_map/attend/pallas_call | solution.py:506
  70.8 26.1 %mlp.1 = (bf16[5,1,14,14,384]{4,3,2,1,0:T(8,128)(2,1)}, f32[1280,384]{1,0:T(8,128)}, bf16[16,96,384]{2,1,0:T(8,128)(2,1)}, bf16[16,96,384]{2,1,0:T(8,128)(2,1)}, f32[12,384]{1,0:T(8,128)}) custom-call(s32[32]{0:T(128)} %broadcast_xor_fusion.order_ref, s32[32]{0:T(128)} %fusion.15.back_ref, bf16[32,96,384]{2,1,0:T(8,128)(2,1)} %copy-done.40, ...), custom_call_target="tpu_custom_call" | custom-call | flops 20000000000 | bytes 12000000 | tf_op jit(solution)/shard_map/mlp/pallas_call | solution.py:528
  97.7 17.1 %attend_back.1 = (bf16[1280,1152]{1,0:T(8,128)(2,1)}, bf16[16,48,384]{2,1,0:T(8,128)(2,1)}, bf16[16,48,384]{2,1,0:T(8,128)(2,1)}, f32[3,256,128]{2,1,0:T(8,128)}, f32[2,384]{1,0:T(2,128)}) custom-call(s32[32]{0:T(128)} %fusion.15.back_ref, s32[5,2]{1,0:T(8,128)} %copy.59.extent_ref, s32[5,4]{1,0:T(8,128)} %copy.60.route_ref, ...), custom_call_target="tpu_custom_call" | custom-call | flops 12000000000 | bytes 12000000 | tf_op jit(solution)/shard_map/attend_back/pallas_call | solution.py:547
  116.7 5.4 %input_grad.1 = (bf16[5,1,14,14,384]{4,3,2,1,0:T(8,128)(2,1)}, f32[2,384]{1,0:T(2,128)S(1)}) custom-call(bf16[1280,1152]{1,0:T(8,128)(2,1)S(1)} %copy-done.24, bf16[384,1152]{1,0:T(8,128)(2,1)S(1)} %copy-done.30, bf16[1280,384]{1,0:T(8,128)(2,1)S(1)} %copy-done.26, f32[1280,384]{1,0:T(8,128)S(1)} %copy-done.29, f32[12,384]{1,0:T(8,128)S(1)} %copy-done.13, ...), custom_call_target="tpu_custom_call" | custom-call | flops 4000000000 | bytes 8000000 | tf_op jit(solution)/shard_map/input_grad/pallas_call | solution.py:571
  124.9 2.3 %fusion.23 = f32[12,169]{1,0:T(8,128)S(1)} fusion(f32[12,4096]{1,0:T(8,128)S(1)} %reshape.75, f32[4096,169]{0,1:T(8,128)S(1)} %copy-done.31), kind=kOutput, calls=%fused_computation.81 | convolution fusion | flops 99680256 | bytes 2973616 | tf_op jit(solution)/shard_map/dot_general | solution.py:586
  139.3 2.3 %collective-permute-start.21 = (bf16[4,96,384]{2,1,0:T(8,128)(2,1)S(1)}, bf16[4,96,384]{2,1,0:T(8,128)(2,1)S(1)}, u32[]{:S(2)}, u32[]{:S(2)}) collective-permute-start(bf16[4,96,384]{2,1,0:T(8,128)(2,1)S(1)} %get-tuple-element.112), channel_id=1, source_target_pairs={{0,6},{1,7},{2,4},{3,5},{4,2},{5,3},{6,0},{7,1},{8,14},{9,15},{10,... | collective-permute-start | bytes 884744 | tf_op jit(solution)/shard_map/ppermute | solution.py:419
  147.2 8.1 %collective-permute-done.19 = bf16[4,96,384]{2,1,0:T(8,128)(2,1)S(1)} collective-permute-done((bf16[4,96,384]{2,1,0:T(8,128)(2,1)S(1)}, bf16[4,96,384]{2,1,0:T(8,128)(2,1)S(1)}, u32[]{:S(2)}, u32[]{:S(2)}) %collective-permute-start.19) | collective-permute-done | bytes 294944 | tf_op jit(solution)/shard_map/ppermute | solution.py:419
  155.4 2.2 %collective-permute-done.20 = bf16[4,96,384]{2,1,0:T(8,128)(2,1)S(1)} collective-permute-done((bf16[4,96,384]{2,1,0:T(8,128)(2,1)S(1)}, bf16[4,96,384]{2,1,0:T(8,128)(2,1)S(1)}, u32[]{:S(2)}, u32[]{:S(2)}) %collective-permute-start.20) | collective-permute-done | bytes 294944 | tf_op jit(solution)/shard_map/ppermute | solution.py:419
  159.4 2.6 %collective-permute-start.17 = (bf16[1,48,384]{2,1,0:T(8,128)(2,1)S(1)}, bf16[1,48,384]{2,1,0:T(8,128)(2,1)S(1)}, u32[]{:S(2)}, u32[]{:S(2)}) collective-permute-start(bf16[1,48,384]{2,1,0:T(8,128)(2,1)S(1)} %slice.141), channel_id=1, source_target_pairs={{0,16},{1,17},{2,18},{3,19},{4,20},{5,21},{6,22},{7,23},{8,24},{9,... | collective-permute-start | bytes 110600 | tf_op jit(solution)/shard_map/ppermute | solution.py:419
  163.6 2.8 %collective-permute-start.23 = (bf16[1,96,384]{2,1,0:T(8,128)(2,1)S(1)}, bf16[1,96,384]{2,1,0:T(8,128)(2,1)S(1)}, u32[]{:S(2)}, u32[]{:S(2)}) collective-permute-start(bf16[1,96,384]{2,1,0:T(8,128)(2,1)S(1)} %slice.139), channel_id=1, source_target_pairs={{0,16},{1,17},{2,18},{3,19},{4,20},{5,21},{6,22},{7,23},{8,24},{9,... | collective-permute-start | bytes 221192 | tf_op jit(solution)/shard_map/ppermute | solution.py:419
  174.4 5.8 %collective-permute-done.27 = f32[553,12]{1,0:T(8,128)S(1)} collective-permute-done((f32[553,12]{1,0:T(8,128)S(1)}, f32[553,12]{1,0:T(8,128)S(1)}, u32[]{:S(2)}, u32[]{:S(2)}) %collective-permute-start.27) | collective-permute-done | bytes 26576 | tf_op jit(solution)/shard_map/ppermute | solution.py:419
  180.3 3.3 %collective-permute-start.28 = (f32[553,12]{1,0:T(8,128)S(1)}, f32[553,12]{1,0:T(8,128)S(1)}, u32[]{:S(2)}, u32[]{:S(2)}) collective-permute-start(f32[553,12]{1,0:T(8,128)S(1)} %add.115), channel_id=1, source_target_pairs={{0,16},{1,17},{2,18},{3,19},{4,20},{5,21},{6,22},{7,23},{8,24},{9,... | collective-permute-start | bytes 79640 | tf_op jit(solution)/shard_map/ppermute | solution.py:419
  184.9 11.7 %collective-permute-done.28 = f32[553,12]{1,0:T(8,128)S(1)} collective-permute-done((f32[553,12]{1,0:T(8,128)S(1)}, f32[553,12]{1,0:T(8,128)S(1)}, u32[]{:S(2)}, u32[]{:S(2)}) %collective-permute-start.28) | collective-permute-done | bytes 26576 | tf_op jit(solution)/shard_map/ppermute | solution.py:419
  197.5 2.8 %collective-permute-done.32 = f32[1,128]{1,0:T(1,128)S(1)} collective-permute-done((f32[1,128]{1,0:T(1,128)S(1)}, f32[1,128]{1,0:T(1,128)S(1)}, u32[]{:S(2)}, u32[]{:S(2)}) %collective-permute-start.32) | collective-permute-done | bytes 544 | tf_op jit(solution)/shard_map/ppermute | solution.py:419
  200.3 2.1 %collective-permute-start.33 = (f32[1,128]{1,0:T(1,128)S(1)}, f32[1,128]{1,0:T(1,128)S(1)}, u32[]{:S(2)}, u32[]{:S(2)}) collective-permute-start(f32[1,128]{1,0:T(1,128)S(1)} %add.121), channel_id=1, source_target_pairs={{0,16},{1,17},{2,18},{3,19},{4,20},{5,21},{6,22},{7,23},{8,24},{9,... | collective-permute-start | bytes 1544 | tf_op jit(solution)/shard_map/ppermute | solution.py:419
  202.8 2.0 collective-permute-done.33
  (204 shorter events, 62.7 us)
Async XLA Ops:
  2.3 19.6 %collective-permute-start.6 = (bf16[1,48,384]{2,1,0:T(8,128)(2,1)}, bf16[1,48,384]{2,1,0:T(8,128)(2,1)S(1)}, u32[]{:S(2)}, u32[]{:S(2)}) collective-permute-start(bf16[1,48,384]{2,1,0:T(8,128)(2,1)} %bitcast.55), channel_id=1, source_target_pairs={{0,16},{1,17},{2,18},{3,19},{4,20},{5,21},{6,22},{7,23},{8,24},{9,... | collective-permute-start | bytes 110600 | tf_op jit(solution)/shard_map/ppermute | solution.py:419
  6.4 18.1 %collective-permute-start = (bf16[1,96,384]{2,1,0:T(8,128)(2,1)}, bf16[1,96,384]{2,1,0:T(8,128)(2,1)S(1)}, u32[]{:S(2)}, u32[]{:S(2)}) collective-permute-start(bf16[1,96,384]{2,1,0:T(8,128)(2,1)} %bitcast.52), channel_id=1, source_target_pairs={{0,16},{1,17},{2,18},{3,19},{4,20},{5,21},{6,22},{7,23},{8,24},{9,... | collective-permute-start | bytes 221192 | tf_op jit(solution)/shard_map/ppermute | solution.py:419
  26.6 17.5 %collective-permute-start.10 = (bf16[4,48,384]{2,1,0:T(8,128)(2,1)S(1)}, bf16[4,48,384]{2,1,0:T(8,128)(2,1)S(1)}, u32[]{:S(2)}, u32[]{:S(2)}) collective-permute-start(bf16[4,48,384]{2,1,0:T(8,128)(2,1)S(1)} %pad_maximum_fusion.3), channel_id=1, source_target_pairs={{0,6},{1,7},{2,4},{3,5},{4,2},{5,3},{6,0},{7,1},{8,14},{9,15},{10,... | collective-permute-start | bytes 442376 | tf_op jit(solution)/shard_map/ppermute | solution.py:419
  29.6 13.6 %collective-permute-start.9 = (bf16[4,48,384]{2,1,0:T(8,128)(2,1)S(1)}, bf16[4,48,384]{2,1,0:T(8,128)(2,1)S(1)}, u32[]{:S(2)}, u32[]{:S(2)}) collective-permute-start(bf16[4,48,384]{2,1,0:T(8,128)(2,1)S(1)} %pad_maximum_fusion.3), channel_id=1, source_target_pairs={{0,4},{1,5},{2,6},{3,7},{4,0},{5,1},{6,2},{7,3},{8,12},{9,13},{10,... | collective-permute-start | bytes 442376 | tf_op jit(solution)/shard_map/ppermute | solution.py:419
  30.2 10.9 %collective-permute-start.8 = (bf16[4,48,384]{2,1,0:T(8,128)(2,1)S(1)}, bf16[4,48,384]{2,1,0:T(8,128)(2,1)S(1)}, u32[]{:S(2)}, u32[]{:S(2)}) collective-permute-start(bf16[4,48,384]{2,1,0:T(8,128)(2,1)S(1)} %pad_maximum_fusion.3), channel_id=1, source_target_pairs={{0,2},{1,3},{2,0},{3,1},{4,6},{5,7},{6,4},{7,5},{8,10},{9,11},{10,... | collective-permute-start | bytes 442376 | tf_op jit(solution)/shard_map/ppermute | solution.py:419
  31.0 18.4 %collective-permute-start.4 = (bf16[4,96,384]{2,1,0:T(8,128)(2,1)S(1)}, bf16[4,96,384]{2,1,0:T(8,128)(2,1)S(1)}, u32[]{:S(2)}, u32[]{:S(2)}) collective-permute-start(bf16[4,96,384]{2,1,0:T(8,128)(2,1)S(1)} %pad_maximum_fusion.1), channel_id=1, source_target_pairs={{0,6},{1,7},{2,4},{3,5},{4,2},{5,3},{6,0},{7,1},{8,14},{9,15},{10,... | collective-permute-start | bytes 884744 | tf_op jit(solution)/shard_map/ppermute | solution.py:419
  33.9 14.7 %collective-permute-start.3 = (bf16[4,96,384]{2,1,0:T(8,128)(2,1)S(1)}, bf16[4,96,384]{2,1,0:T(8,128)(2,1)S(1)}, u32[]{:S(2)}, u32[]{:S(2)}) collective-permute-start(bf16[4,96,384]{2,1,0:T(8,128)(2,1)S(1)} %pad_maximum_fusion.1), channel_id=1, source_target_pairs={{0,4},{1,5},{2,6},{3,7},{4,0},{5,1},{6,2},{7,3},{8,12},{9,13},{10,... | collective-permute-start | bytes 884744 | tf_op jit(solution)/shard_map/ppermute | solution.py:419
  50.2 18.9 %collective-permute-start.5 = (bf16[16,96,384]{2,1,0:T(8,128)(2,1)S(1)}, bf16[16,96,384]{2,1,0:T(8,128)(2,1)S(1)}, u32[]{:S(2)}, u32[]{:S(2)}) collective-permute-start(bf16[16,96,384]{2,1,0:T(8,128)(2,1)S(1)} %get-tuple-element.119), channel_id=1, source_target_pairs={{0,1},{1,0},{2,3},{3,2},{4,5},{5,4},{6,7},{7,6},{8,9},{9,8},{10,11... | collective-permute-start | bytes 3538952 | tf_op jit(solution)/shard_map/ppermute | solution.py:419
  122.2 8.9 %collective-permute-start.12 = (bf16[16,48,384]{2,1,0:T(8,128)(2,1)}, bf16[16,48,384]{2,1,0:T(8,128)(2,1)}, u32[]{:S(2)}, u32[]{:S(2)}) collective-permute-start(bf16[16,48,384]{2,1,0:T(8,128)(2,1)} %get-tuple-element.79), channel_id=1, source_target_pairs={{0,1},{1,0},{2,3},{3,2},{4,5},{5,4},{6,7},{7,6},{8,9},{9,8},{10,11... | collective-permute-start | bytes 1769480 | tf_op jit(solution)/shard_map/ppermute | solution.py:419
  122.7 13.3 %collective-permute-start.18 = (bf16[16,96,384]{2,1,0:T(8,128)(2,1)}, bf16[16,96,384]{2,1,0:T(8,128)(2,1)}, u32[]{:S(2)}, u32[]{:S(2)}) collective-permute-start(bf16[16,96,384]{2,1,0:T(8,128)(2,1)} %get-tuple-element.81), channel_id=1, source_target_pairs={{0,1},{1,0},{2,3},{3,2},{4,5},{5,4},{6,7},{7,6},{8,9},{9,8},{10,11... | collective-permute-start | bytes 3538952 | tf_op jit(solution)/shard_map/ppermute | solution.py:419
  129.4 10.0 %collective-permute-start.25 = (f32[553,12]{1,0:T(8,128)S(1)}, f32[553,12]{1,0:T(8,128)S(1)}, u32[]{:S(2)}, u32[]{:S(2)}) collective-permute-start(f32[553,12]{1,0:T(8,128)S(1)} %add.112), channel_id=1, source_target_pairs={{0,4},{1,5},{2,6},{3,7},{4,0},{5,1},{6,2},{7,3},{8,12},{9,13},{10,... | collective-permute-start | bytes 79640 | tf_op jit(solution)/shard_map/ppermute | solution.py:419
  132.5 9.2 %collective-permute-start.13 = (bf16[4,48,384]{2,1,0:T(8,128)(2,1)S(1)}, bf16[4,48,384]{2,1,0:T(8,128)(2,1)S(1)}, u32[]{:S(2)}, u32[]{:S(2)}) collective-permute-start(bf16[4,48,384]{2,1,0:T(8,128)(2,1)S(1)} %get-tuple-element.116), channel_id=1, source_target_pairs={{0,2},{1,3},{2,0},{3,1},{4,6},{5,7},{6,4},{7,5},{8,10},{9,11},{10,... | collective-permute-start | bytes 442376 | tf_op jit(solution)/shard_map/ppermute | solution.py:419
  134.0 9.2 %collective-permute-start.15 = (bf16[4,48,384]{2,1,0:T(8,128)(2,1)S(1)}, bf16[4,48,384]{2,1,0:T(8,128)(2,1)S(1)}, u32[]{:S(2)}, u32[]{:S(2)}) collective-permute-start(bf16[4,48,384]{2,1,0:T(8,128)(2,1)S(1)} %get-tuple-element.117), channel_id=1, source_target_pairs={{0,6},{1,7},{2,4},{3,5},{4,2},{5,3},{6,0},{7,1},{8,14},{9,15},{10,... | collective-permute-start | bytes 442376 | tf_op jit(solution)/shard_map/ppermute | solution.py:419
  134.4 11.0 %collective-permute-start.14 = (bf16[4,48,384]{2,1,0:T(8,128)(2,1)S(1)}, bf16[4,48,384]{2,1,0:T(8,128)(2,1)S(1)}, u32[]{:S(2)}, u32[]{:S(2)}) collective-permute-start(bf16[4,48,384]{2,1,0:T(8,128)(2,1)S(1)} %get-tuple-element.118), channel_id=1, source_target_pairs={{0,4},{1,5},{2,6},{3,7},{4,0},{5,1},{6,2},{7,3},{8,12},{9,13},{10,... | collective-permute-start | bytes 442376 | tf_op jit(solution)/shard_map/ppermute | solution.py:419
  137.8 17.6 %collective-permute-start.19 = (bf16[4,96,384]{2,1,0:T(8,128)(2,1)S(1)}, bf16[4,96,384]{2,1,0:T(8,128)(2,1)S(1)}, u32[]{:S(2)}, u32[]{:S(2)}) collective-permute-start(bf16[4,96,384]{2,1,0:T(8,128)(2,1)S(1)} %get-tuple-element.111), channel_id=1, source_target_pairs={{0,2},{1,3},{2,0},{3,1},{4,6},{5,7},{6,4},{7,5},{8,10},{9,11},{10,... | collective-permute-start | bytes 884744 | tf_op jit(solution)/shard_map/ppermute | solution.py:419
  139.3 16.0 %collective-permute-start.21 = (bf16[4,96,384]{2,1,0:T(8,128)(2,1)S(1)}, bf16[4,96,384]{2,1,0:T(8,128)(2,1)S(1)}, u32[]{:S(2)}, u32[]{:S(2)}) collective-permute-start(bf16[4,96,384]{2,1,0:T(8,128)(2,1)S(1)} %get-tuple-element.112), channel_id=1, source_target_pairs={{0,6},{1,7},{2,4},{3,5},{4,2},{5,3},{6,0},{7,1},{8,14},{9,15},{10,... | collective-permute-start | bytes 884744 | tf_op jit(solution)/shard_map/ppermute | solution.py:419
  141.7 15.9 %collective-permute-start.20 = (bf16[4,96,384]{2,1,0:T(8,128)(2,1)S(1)}, bf16[4,96,384]{2,1,0:T(8,128)(2,1)S(1)}, u32[]{:S(2)}, u32[]{:S(2)}) collective-permute-start(bf16[4,96,384]{2,1,0:T(8,128)(2,1)S(1)} %get-tuple-element.113), channel_id=1, source_target_pairs={{0,4},{1,5},{2,6},{3,7},{4,0},{5,1},{6,2},{7,3},{8,12},{9,13},{10,... | collective-permute-start | bytes 884744 | tf_op jit(solution)/shard_map/ppermute | solution.py:419
  143.2 27.7 %collective-permute-start.26 = (f32[553,12]{1,0:T(8,128)S(1)}, f32[553,12]{1,0:T(8,128)S(1)}, u32[]{:S(2)}, u32[]{:S(2)}) collective-permute-start(f32[553,12]{1,0:T(8,128)S(1)} %add.113), channel_id=1, source_target_pairs={{0,2},{1,3},{2,0},{3,1},{4,6},{5,7},{6,4},{7,5},{8,10},{9,11},{10,... | collective-permute-start | bytes 79640 | tf_op jit(solution)/shard_map/ppermute | solution.py:419
  145.5 13.9 %collective-permute-start.16 = (bf16[2,48,384]{2,1,0:T(8,128)(2,1)S(1)}, bf16[2,48,384]{2,1,0:T(8,128)(2,1)S(1)}, u32[]{:S(2)}, u32[]{:S(2)}) collective-permute-start(bf16[2,48,384]{2,1,0:T(8,128)(2,1)S(1)} %slice.140), channel_id=1, source_target_pairs={{0,8},{1,9},{2,10},{3,11},{4,12},{5,13},{6,14},{7,15},{8,0},{9,1},... | collective-permute-start | bytes 221192 | tf_op jit(solution)/shard_map/ppermute | solution.py:419
  159.4 6.9 %collective-permute-start.17 = (bf16[1,48,384]{2,1,0:T(8,128)(2,1)S(1)}, bf16[1,48,384]{2,1,0:T(8,128)(2,1)S(1)}, u32[]{:S(2)}, u32[]{:S(2)}) collective-permute-start(bf16[1,48,384]{2,1,0:T(8,128)(2,1)S(1)} %slice.141), channel_id=1, source_target_pairs={{0,16},{1,17},{2,18},{3,19},{4,20},{5,21},{6,22},{7,23},{8,24},{9,... | collective-permute-start | bytes 110600 | tf_op jit(solution)/shard_map/ppermute | solution.py:419
  171.0 9.3 %collective-permute-start.27 = (f32[553,12]{1,0:T(8,128)S(1)}, f32[553,12]{1,0:T(8,128)S(1)}, u32[]{:S(2)}, u32[]{:S(2)}) collective-permute-start(f32[553,12]{1,0:T(8,128)S(1)} %add.114), channel_id=1, source_target_pairs={{0,8},{1,9},{2,10},{3,11},{4,12},{5,13},{6,14},{7,15},{8,0},{9,1},... | collective-permute-start | bytes 79640 | tf_op jit(solution)/shard_map/ppermute | solution.py:419
  172.8 10.7 %collective-permute-start.30 = (f32[1,128]{1,0:T(1,128)S(1)}, f32[1,128]{1,0:T(1,128)S(1)}, u32[]{:S(2)}, u32[]{:S(2)}) collective-permute-start(f32[1,128]{1,0:T(1,128)S(1)} %broadcast_add_fusion), channel_id=1, source_target_pairs={{0,4},{1,5},{2,6},{3,7},{4,0},{5,1},{6,2},{7,3},{8,12},{9,13},{10,... | collective-permute-start | bytes 1544 | tf_op jit(solution)/shard_map/ppermute | solution.py:419
  180.3 16.3 %collective-permute-start.28 = (f32[553,12]{1,0:T(8,128)S(1)}, f32[553,12]{1,0:T(8,128)S(1)}, u32[]{:S(2)}, u32[]{:S(2)}) collective-permute-start(f32[553,12]{1,0:T(8,128)S(1)} %add.115), channel_id=1, source_target_pairs={{0,16},{1,17},{2,18},{3,19},{4,20},{5,21},{6,22},{7,23},{8,24},{9,... | collective-permute-start | bytes 79640 | tf_op jit(solution)/shard_map/ppermute | solution.py:419
  183.6 13.1 %collective-permute-start.31 = (f32[1,128]{1,0:T(1,128)S(1)}, f32[1,128]{1,0:T(1,128)S(1)}, u32[]{:S(2)}, u32[]{:S(2)}) collective-permute-start(f32[1,128]{1,0:T(1,128)S(1)} %fusion.28), channel_id=1, source_target_pairs={{0,2},{1,3},{2,0},{3,1},{4,6},{5,7},{6,4},{7,5},{8,10},{9,11},{10,... | collective-permute-start | bytes 1544 | tf_op jit(solution)/shard_map/ppermute | solution.py:419
  (54 other events, 786.8 us)

commit v3 on v2

--- a/solution.py
+++ b/solution.py
@@ -1,3 +1,4 @@
+import functools
 import math
 
 import jax
@@ -44,6 +45,16 @@
 F32 = jnp.float32
 NEVER = 99.0
 BOTH = ("tok", "head")
+MASKS = (16, 8, 2, 4, 1)
+ME, SLOT, EXTENT, ROUTE = 0, 1, 2, 12
+
+
+def swap_bits(position):
+    return sum((position & mask) // mask << bit for bit, mask in enumerate(MASKS))
+
+
+def block_at(place):
+    return sum(((place >> bit) & 1) * mask for bit, mask in enumerate(MASKS))
 
 
 def window_tables():
@@ -152,12 +163,12 @@
     return jax.ShapeDtypeStruct(shape, dtype)
 
 
-def row_mask(place_ref, extent_ref, route_ref, image):
+def row_mask(place_ref, table_ref, image):
     parts = []
     for w in range(4):
         rows = slice(w * WIN, (w + 1) * WIN)
-        high = jnp.where(route_ref[image, w] >= 0, extent_ref[image, 0], -1).astype(F32)
-        wide = extent_ref[image, 1].astype(F32)
+        high = jnp.where(table_ref[ROUTE + 4 * image + w] >= 0, table_ref[EXTENT + 2 * image], -1).astype(F32)
+        wide = table_ref[EXTENT + 2 * image + 1].astype(F32)
         inside = (place_ref[0, rows] < high) & (place_ref[1, rows] < wide)
         parts.append(jnp.where(inside, 1.0, 0.0))
     return jnp.concatenate(parts, axis=0)
@@ -214,17 +225,17 @@
 
 
 def attend_body(
-    order_ref, extent_ref, route_ref, near_ref, x_ref, n_ref, vec_ref, bias_ref, reach_ref, place_ref, heads_ref,
-    packed_ref, soft_ref, attn_ref, middle_ref, wq_ref, wp_ref, parts,
+    direct, table_ref, near_ref, n_ref, vec_ref, bias_ref, reach_ref, place_ref, heads_ref,
+    packed_ref, soft_ref, attn_ref, wq_ref, wp_ref, parts,
 ):
     image = pl.program_id(0)
 
     @pl.when(image == 0)
     def _():
         for j in range(BLOCKS):
-            at = order_ref[j]
-            row = pl.multiple_of((at // 4) * PIECE, PIECE)
-            parts[at % 4, pl.ds(row, PIECE), :] = near_ref[j]
+            at = table_ref[ME] ^ block_at(j) if direct else (j % 8) * 4 + j // 8
+            row = at // 4 * PIECE if not direct else pl.multiple_of((at >> 2) * PIECE, PIECE)
+            parts[at & 3, pl.ds(row, PIECE), :] = near_ref[j]
         for w in range(3):
             wq_ref[:, w * C : (w + 1) * C] = jnp.concatenate(
                 [parts[h, :, w * 96 : (w + 1) * 96] for h in range(4)], axis=1
@@ -235,9 +246,9 @@
     packed_ref[:, :C] = (made[:, :C] + vec_ref[2:3]).astype(LOW)
     packed_ref[:, C : 2 * C] = made[:, C : 2 * C].astype(LOW)
     packed_ref[:, 2 * C :] = (made[:, 2 * C :] + vec_ref[3:4]).astype(LOW)
-    mask = row_mask(place_ref, extent_ref, route_ref, image)
-    high = extent_ref[image, 0].astype(F32)
-    wide = extent_ref[image, 1].astype(F32)
+    mask = row_mask(place_ref, table_ref, image)
+    high = table_ref[EXTENT + 2 * image].astype(F32)
+    wide = table_ref[EXTENT + 2 * image + 1].astype(F32)
     for pair in range(2):
         rows = slice(pair * 2 * WIN, (pair + 1) * 2 * WIN)
         allowed = (reach_ref[pair, 0] < high) & (reach_ref[pair, 1] < wide)
@@ -255,47 +266,47 @@
             soft_ref[0, pair * GROUPS + g] = soft
             result = own_rows(dot_tn(soft.astype(LOW), spread_keys(values, heads_ref)))
             attn_ref[rows, at : at + LANES] = (result * mask[rows]).astype(LOW)
-    middle_ref[...] = x_ref[...].astype(F32) + dot_nt(attn_ref[...], wp_ref[...]) + vec_ref[4:5]
+
+
+def middle_body(attn_ref, x_ref, wp_ref, vec_ref, middle_ref, n_ref):
+    middle = x_ref[...].astype(F32) + dot_nt(attn_ref[...], wp_ref[...]) + vec_ref[4:5]
+    middle_ref[...] = middle
+    unit, _ = norm_parts(middle)
+    n_ref[...] = (unit * vec_ref[5:6] + vec_ref[6:7]).astype(LOW)
 
 
 def mlp_body(
-    order_ref, back_ref, far_ref, middle_ref, g_ref, vec_ref, deal_ref,
-    out_ref, grad_ref, keep_ref, send_ref, sums_ref, w1, w2, hidden, grad_hidden, n_turned, g_turned, made, bias,
+    direct, table_ref, far_ref, middle_ref, n_ref, g_ref, vec_ref,
+    hidden_ref, grad_hidden_ref, grad_ref, sums_ref, w2_ref, w1, bias,
 ):
     image = pl.program_id(0)
 
     @pl.when(image == 0)
     def _():
         for j in range(BLOCKS):
-            at = order_ref[j]
-            row = pl.multiple_of((at // 4) * PIECE, PIECE)
-            col = pl.multiple_of((at % 4) * C, C)
+            at = table_ref[ME] ^ block_at(j) if direct else (j % 8) * 4 + j // 8
+            row = at // 4 * PIECE if not direct else pl.multiple_of((at >> 2) * PIECE, PIECE)
+            col = at % 4 * C if not direct else pl.multiple_of((at & 3) * C, C)
             w1[pl.ds(row, PIECE), pl.ds(col, C)] = far_ref[j, :PIECE]
-            w2[pl.ds(row, PIECE), pl.ds(col, C)] = far_ref[j, PIECE:]
+            w2_ref[pl.ds(row, PIECE), pl.ds(col, C)] = far_ref[j, PIECE:]
         for r in range(4):
             bias[:, r * C : (r + 1) * C] = vec_ref[8 + r : 9 + r]
         sums_ref[...] = jnp.zeros_like(sums_ref)
 
-    rows = pl.ds(pl.multiple_of(image * IMG, IMG), IMG)
-    middle = middle_ref[...]
-    unit, inverse = norm_parts(middle)
-    normed = (unit * vec_ref[5:6] + vec_ref[6:7]).astype(LOW)
+    unit, inverse = norm_parts(middle_ref[...])
+    normed = n_ref[...]
     g_low = g_ref[...]
     g = g_low.astype(F32)
-    n_turned[:, rows] = normed.T
-    g_turned[:, rows] = g_low.T
     for part in range(4):
         cols = slice(part * C, (part + 1) * C)
         pre_act = dot_nn(normed, w1[:, cols]) + bias[:, cols]
-        grad_post = dot_nn(g_low, w2[:, cols])
+        grad_post = dot_nn(g_low, w2_ref[:, cols])
         below, density = gelu_parts(pre_act)
-        hidden[rows, cols] = (pre_act * below).astype(LOW)
+        hidden_ref[:, cols] = (pre_act * below).astype(LOW)
         grad_pre = grad_post * (below + pre_act * density)
-        grad_hidden[rows, cols] = grad_pre.astype(LOW)
+        grad_hidden_ref[:, cols] = grad_pre.astype(LOW)
         sums_ref[8 + part : 9 + part] += jnp.sum(grad_pre, axis=0, keepdims=True)
-    result = middle + dot_nt(hidden[rows, :], w2[...]) + vec_ref[7:8]
-    put_back(result, deal_ref, out_ref)
-    back = dot_nt(grad_hidden[rows, :], w1[...])
+    back = dot_nt(grad_hidden_ref[...], w1[...])
     sums_ref[5:6] += jnp.sum(back * unit, axis=0, keepdims=True)
     sums_ref[6:7] += jnp.sum(back, axis=0, keepdims=True)
     grad_middle = g + norm_back(back, unit, inverse, vec_ref[5:6])
@@ -303,37 +314,52 @@
     sums_ref[4:5] += jnp.sum(grad_middle, axis=0, keepdims=True)
     sums_ref[7:8] += jnp.sum(g, axis=0, keepdims=True)
 
-    @pl.when(image == MICRO - 1)
+
+def place_of(direct, table_ref, t, h):
+    if not direct:
+        return h * 8 + t
+    return table_ref[SLOT] ^ swap_bits(4 * t) ^ ((h & 1) * 16 + (h >> 1) * 4)
+
+
+def mlp_weights_body(direct, table_ref, n_ref, g_ref, hidden_ref, grad_hidden_ref, keep_ref, send_ref, n_turned, g_turned, made):
+    part = pl.program_id(0)
+
+    @pl.when(part == 0)
     def _():
-        for part in range(4):
-            cols = slice(part * C, (part + 1) * C)
-            first = dot_nn(n_turned[...], grad_hidden[:, cols]).astype(LOW)
-            second = dot_nn(g_turned[...], hidden[:, cols]).astype(LOW)
-            for t in range(8):
-                at = back_ref[4 * t + part]
-                made[at, :PIECE] = first[t * PIECE : (t + 1) * PIECE]
-                made[at, PIECE:] = second[t * PIECE : (t + 1) * PIECE]
+        n_turned[...] = n_ref[...].T
+        g_turned[...] = g_ref[...].T
+
+    first = dot_nn(n_turned[...], grad_hidden_ref[...]).astype(LOW)
+    second = dot_nn(g_turned[...], hidden_ref[...]).astype(LOW)
+    for t in range(8):
+        at = place_of(direct, table_ref, t, part)
+        made[at, :PIECE] = first[t * PIECE : (t + 1) * PIECE]
+        made[at, PIECE:] = second[t * PIECE : (t + 1) * PIECE]
+
+    @pl.when(part == 3)
+    def _():
         keep_ref[...] = made[: BLOCKS // 2]
         send_ref[...] = made[BLOCKS // 2 :]
 
 
+def output_body(hidden_ref, w2_ref, middle_ref, vec_ref, deal_ref, out_ref):
+    put_back(middle_ref[...] + dot_nt(hidden_ref[...], w2_ref[...]) + vec_ref[7:8], deal_ref, out_ref)
+
+
 def attend_back_body(
-    back_ref, extent_ref, route_ref, grad_ref, attn_ref, packed_ref, soft_ref, n_ref, wp_ref, place_ref, heads_ref,
-    packed_grad_ref, keep_ref, send_ref, bias_sum_ref, sums_ref, n_turned, g_turned, attn_all, packed_all, made,
+    table_ref, grad_ref, packed_ref, soft_ref, wp_ref, place_ref, heads_ref,
+    packed_grad_ref, grad_low_ref, bias_sum_ref, sums_ref,
 ):
     image = pl.program_id(0)
-    rows_all = pl.ds(pl.multiple_of(image * IMG, IMG), IMG)
 
     @pl.when(image == 0)
     def _():
         bias_sum_ref[...] = jnp.zeros_like(bias_sum_ref)
         sums_ref[...] = jnp.zeros_like(sums_ref)
 
-    n_turned[:, rows_all] = n_ref[...].T
     grad_low = grad_ref[...].astype(LOW)
-    g_turned[:, rows_all] = grad_low.T
-    attn_all[rows_all, :] = attn_ref[...]
-    mask = row_mask(place_ref, extent_ref, route_ref, image)
+    grad_low_ref[...] = grad_low
+    mask = row_mask(place_ref, table_ref, image)
     grad_attn = dot_nn(grad_low, wp_ref[...])
     grad_attn = (grad_attn * jnp.concatenate([mask] * 3, axis=1)).astype(LOW)
     for pair in range(2):
@@ -357,20 +383,20 @@
             packed_grad_ref[rows, at : at + LANES] = (grad_queries * HD ** (-0.5)).astype(LOW)
             packed_grad_ref[rows, C + at : C + at + LANES] = (grad_keys * HD ** (-0.5)).astype(LOW)
             packed_grad_ref[rows, 2 * C + at : 2 * C + at + LANES] = grad_values.astype(LOW)
-    packed_all[rows_all, :] = packed_grad_ref[...]
     sums_ref[0:1] += jnp.sum(packed_grad_ref[:, :C].astype(F32), axis=0, keepdims=True)
     sums_ref[1:2] += jnp.sum(packed_grad_ref[:, 2 * C :].astype(F32), axis=0, keepdims=True)
 
-    @pl.when(image == MICRO - 1)
-    def _():
-        whole = [dot_nn(n_turned[...], packed_all[:, w * C : (w + 1) * C]).astype(LOW) for w in range(3)]
-        whole.append(dot_nn(g_turned[...], attn_all[...]).astype(LOW))
-        for h in range(4):
-            block = jnp.concatenate([part[:, h * 96 : (h + 1) * 96] for part in whole], axis=1)
-            for t in range(8):
-                made[back_ref[4 * t + h]] = block[t * PIECE : (t + 1) * PIECE]
-        keep_ref[...] = made[: BLOCKS // 2]
-        send_ref[...] = made[BLOCKS // 2 :]
+
+def attend_weights_body(direct, table_ref, n_ref, grad_low_ref, packed_grad_ref, attn_ref, keep_ref, send_ref, made):
+    n_turned = n_ref[...].T
+    whole = [dot_nn(n_turned, packed_grad_ref[:, w * C : (w + 1) * C]).astype(LOW) for w in range(3)]
+    whole.append(dot_nn(grad_low_ref[...].T, attn_ref[...]).astype(LOW))
+    for h in range(4):
+        block = jnp.concatenate([part[:, h * 96 : (h + 1) * 96] for part in whole], axis=1)
+        for t in range(8):
+            made[place_of(direct, table_ref, t, h)] = block[t * PIECE : (t + 1) * PIECE]
+    keep_ref[...] = made[: BLOCKS // 2]
+    send_ref[...] = made[BLOCKS // 2 :]
 
 
 def input_body(packed_grad_ref, wq_ref, x_ref, grad_ref, vec_ref, deal_ref, out_ref, sums_ref):
@@ -415,10 +441,6 @@
                 news[1 + 3 * index + kind][pick] = made[kind]
 
 
-def exchange(rows, mask, devices):
-    return lax.ppermute(rows, BOTH, [(i, i ^ mask) for i in range(devices)])
-
-
 def body(
     mesh_sizes, tokens_in, cotangent, route, extent, qkv_weight, proj_weight, fc1_weight, fc2_weight, vectors, rel_table,
     qkv_first, proj_first, fc1_first, fc2_first, vectors_first, table_first,
@@ -431,18 +453,19 @@
     patches = micro * devices * GRID * GRID
     head_at = lax.axis_index("head")
     me = lax.axis_index("tok") * heads + head_at
-    masks = (16, 8, 2, 4, 1)
-    counts = np.arange(BLOCKS)
-    if direct:
-        away = sum(((counts >> bit) & 1) * mask for bit, mask in enumerate(masks))
-        order = jnp.bitwise_xor(jnp.asarray(away, jnp.int32), me)
-        apart = jnp.bitwise_xor(jnp.asarray(counts, jnp.int32), me)
-        backward = sum((((apart & mask) > 0).astype(jnp.int32) << bit) for bit, mask in enumerate(masks))
-    else:
-        order = jnp.asarray((counts % 8) * 4 + counts // 8, jnp.int32)
-        backward = jnp.asarray((counts % 4) * 8 + counts // 4, jnp.int32)
-    route_own = lax.dynamic_index_in_dim(route, head_at, 1, False)
-    extent_own = lax.dynamic_index_in_dim(extent, head_at, 1, False)
+    table = jnp.concatenate(
+        [
+            jnp.stack([me, swap_bits(me)]).astype(jnp.int32),
+            lax.dynamic_index_in_dim(extent, head_at, 1, False).reshape(-1),
+            lax.dynamic_index_in_dim(route, head_at, 1, False).reshape(-1),
+        ]
+    )
+
+    def tie(*arrays):
+        return lax.optimization_barrier(arrays)
+
+    def passed(rows, mask):
+        return lax.ppermute(rows, BOTH, [(i, i ^ mask) for i in range(devices)])
 
     depth = fc1_weight.shape[0]
     near, far = pl.pallas_call(
@@ -451,36 +474,38 @@
         name="pack",
     )(qkv_weight, proj_weight.T, fc1_weight, fc2_weight.T)
 
-    def gather(piece):
-        if not direct:
-            spread = lax.all_gather(lax.all_gather(piece, "tok", axis=0), "head", axis=0)
-            half = piece.shape[0] // depth
-            spread = spread.reshape(heads, toks, half, depth, C).transpose(0, 2, 1, 3, 4)
-            spread = spread.reshape(heads, half, 8, PIECE, C).transpose(0, 2, 1, 3, 4)
-            return spread.reshape(BLOCKS, half * PIECE, C)
-        held = piece[None]
-        for mask in masks[:2]:
-            held = jnp.concatenate([held, exchange(held, mask, devices)], axis=0)
-        held = jnp.concatenate([held] + [exchange(held, mask, devices) for mask in (2, 4, 6)], axis=0)
-        return jnp.concatenate([held, exchange(held, masks[4], devices)], axis=0)
-
-    def share(keep, send):
-        if not direct:
-            both = jnp.concatenate([keep, send], axis=0)
-            half = both.shape[1] // PIECE
-            both = both.reshape(heads, 8, half, PIECE, C).transpose(0, 2, 1, 3, 4)
-            both = both.reshape(heads, half, toks, depth, C).transpose(0, 2, 1, 3, 4).reshape(devices, half * depth, C)
-            both = lax.psum_scatter(both.astype(F32), "head", scatter_dimension=0, tiled=True)
-            return lax.psum_scatter(both, "tok", scatter_dimension=0, tiled=True)[0]
-        held = keep.astype(F32) + exchange(send, masks[4], devices).astype(F32)
-        low = held.astype(LOW)
-        held = held[:4]
-        for place, mask in ((4, 2), (8, 4), (12, 6)):
-            held = held + exchange(low[place : place + 4], mask, devices).astype(F32)
-        held = held[:2] + exchange(held[2:].astype(LOW), masks[1], devices).astype(F32)
-        held = held[:1] + exchange(held[1:].astype(LOW), masks[0], devices).astype(F32)
-        return held[0]
-
+    def gather_plain(piece):
+        spread = lax.all_gather(lax.all_gather(piece, "tok", axis=0), "head", axis=0)
+        half = piece.shape[0] // depth
+        spread = spread.reshape(heads, toks, half, depth, C).transpose(0, 2, 1, 3, 4)
+        spread = spread.reshape(heads, half, 8, PIECE, C).transpose(0, 2, 1, 3, 4)
+        return spread.reshape(BLOCKS, half * PIECE, C)
+
+    def share_plain(keep, send):
+        both = jnp.concatenate([keep, send], axis=0)
+        half = both.shape[1] // PIECE
+        both = both.reshape(heads, 8, half, PIECE, C).transpose(0, 2, 1, 3, 4)
+        both = both.reshape(heads, half, toks, depth, C).transpose(0, 2, 1, 3, 4).reshape(devices, half * depth, C)
+        both = lax.psum_scatter(both.astype(F32), "head", scatter_dimension=0, tiled=True)
+        return lax.psum_scatter(both, "tok", scatter_dimension=0, tiled=True)[0]
+
+    def join(*arrays):
+        return jnp.concatenate(arrays, axis=0)
+
+    def first_sum(keep, got):
+        total = keep.astype(F32) + got.astype(F32)
+        return total[:4], [total[at : at + 4].astype(LOW) for at in (4, 8, 12)]
+
+    def plane_sum(stays, got):
+        for part in got:
+            stays = stays + part.astype(F32)
+        return stays[:2], stays[2:].astype(LOW)
+
+    def line_sum(stays, got):
+        total = stays + got.astype(F32)
+        return total[:1], total[1:].astype(LOW)
+
+    plane = (2, 4, 6)
     deal = jnp.asarray(DEAL, LOW)
     place = jnp.asarray(PLACE)
     reach = jnp.asarray(REACH)
@@ -492,81 +517,150 @@
         out_specs=[rows_of(C)] * 3,
         out_shape=[sds((ROWS, C), LOW)] * 3,
         scratch_shapes=[pltpu.VMEM((PAD, C), LOW)],
-        compiler_params=params(32),
+        compiler_params=params(16),
         cost_estimate=cost(2e9, 6e6),
         name="prep",
     )(tokens_in, cotangent, deal, vectors)
-
     bias = jnp.dot(rel_table.T, jnp.asarray(LOOKUP), precision=HIGH).reshape(GROUPS, GROUP * WIN, WIN)
     bias = jnp.concatenate([bias, bias], axis=2)
 
-    near_all = gather(near)
-    far_all = gather(far)
-
-    packed, soft, attn, middle, w_qkv, w_proj = pl.pallas_call(
-        attend_body,
+    if direct:
+        near_all, far_all = near[None], far[None]
+        for mask in MASKS[:2]:
+            near_all, far_all = join(near_all, passed(near_all, mask)), join(far_all, passed(far_all, mask))
+        near_all = join(near_all, *[passed(near_all, mask) for mask in plane])
+        near_all, far_all = tie(near_all, far_all)
+        far_got = [passed(far_all, mask) for mask in plane]
+        near_all = join(near_all, passed(near_all, MASKS[4]))
+        near_all, x_rows, g_rows, n_rows, bias, table = tie(near_all, x_rows, g_rows, n_rows, bias, table)
+    else:
+        near_all, far_all = gather_plain(near), gather_plain(far)
+
+    packed, soft, attn, w_qkv, w_proj = pl.pallas_call(
+        functools.partial(attend_body, direct),
         grid=(MICRO,),
         in_specs=[
-            SCALARS, SCALARS, SCALARS, full((BLOCKS, PIECE, C)), rows_of(C), rows_of(C), full((12, C)),
+            SCALARS, full((BLOCKS, PIECE, C)), rows_of(C), full((12, C)),
             full((GROUPS, GROUP * WIN, 128)), full((2, 2, WIN, 128)), full((2, IMG, 128)), full((IMG, 256)),
         ],
         out_specs=[
-            rows_of(3 * C), pl.BlockSpec((1, 2 * GROUPS, GROUP * WIN, 128), lambda i: (i, 0, 0, 0)), rows_of(C), rows_of(C),
+            rows_of(3 * C), pl.BlockSpec((1, 2 * GROUPS, GROUP * WIN, 128), lambda i: (i, 0, 0, 0)), rows_of(C),
             full((C, 3 * C)), full((C, C)),
         ],
         out_shape=[
-            sds((ROWS, 3 * C), LOW), sds((MICRO, 2 * GROUPS, GROUP * WIN, 128), F32), sds((ROWS, C), LOW), sds((ROWS, C), F32),
+            sds((ROWS, 3 * C), LOW), sds((MICRO, 2 * GROUPS, GROUP * WIN, 128), F32), sds((ROWS, C), LOW),
             sds((C, 3 * C), LOW), sds((C, C), LOW),
         ],
         scratch_shapes=[pltpu.VMEM((4, C, C), LOW)],
-        compiler_params=params(),
+        compiler_params=params(32),
         cost_estimate=cost(8e9, 12e6),
         name="attend",
-    )(order, extent_own, route_own, near_all, x_rows, n_rows, vectors, bias, reach, place, heads_low)
+    )(table, near_all, n_rows, vectors, bias, reach, place, heads_low)
+
+    if direct:
+        attn, *far_got = tie(attn, *far_got)
+        far_all = join(far_all, *far_got)
+        far_core = passed(far_all, MASKS[4])
+
+    middle, n_two = pl.pallas_call(
+        middle_body,
+        grid=(MICRO,),
+        in_specs=[rows_of(C), rows_of(C), full((C, C)), full((12, C))],
+        out_specs=[rows_of(C), rows_of(C)],
+        out_shape=[sds((ROWS, C), F32), sds((ROWS, C), LOW)],
+        compiler_params=params(16),
+        cost_estimate=cost(1e9, 6e6),
+        name="middle",
+    )(attn, x_rows, w_proj, vectors)
+
+    if direct:
+        far_core, middle = tie(far_core, middle)
+        far_all = join(far_all, far_core)
+
+    hidden, grad_hidden, grad_middle, sums_mlp, w_fc2 = pl.pallas_call(
+        functools.partial(mlp_body, direct),
+        grid=(MICRO,),
+        in_specs=[SCALARS, full((BLOCKS, 2 * PIECE, C)), rows_of(C), rows_of(C), rows_of(C), full((12, C))],
+        out_specs=[rows_of(FF), rows_of(FF), rows_of(C), full((12, C)), full((C, FF))],
+        out_shape=[sds((ROWS, FF), LOW), sds((ROWS, FF), LOW), sds((ROWS, C), F32), sds((12, C), F32), sds((C, FF), LOW)],
+        scratch_shapes=[pltpu.VMEM((C, FF), LOW), pltpu.VMEM((1, FF), F32)],
+        compiler_params=params(32),
+        cost_estimate=cost(10e9, 16e6),
+        name="mlp",
+    )(table, far_all, middle, n_two, g_rows, vectors)
 
     half = BLOCKS // 2
-    block_out, grad_middle, far_keep, far_send, sums_mlp = pl.pallas_call(
-        mlp_body,
+    columns = pl.BlockSpec((ROWS, C), lambda i: (0, i))
+    far_keep, far_send = pl.pallas_call(
+        functools.partial(mlp_weights_body, direct),
+        grid=(4,),
+        in_specs=[SCALARS, full((ROWS, C)), full((ROWS, C)), columns, columns],
+        out_specs=[full((half, 2 * PIECE, C)), full((half, 2 * PIECE, C))],
+        out_shape=[sds((half, 2 * PIECE, C), LOW), sds((half, 2 * PIECE, C), LOW)],
+        scratch_shapes=[pltpu.VMEM((C, ROWS), LOW), pltpu.VMEM((C, ROWS), LOW), pltpu.VMEM((BLOCKS, 2 * PIECE, C), LOW)],
+        compiler_params=params(32),
+        cost_estimate=cost(4e9, 12e6),
+        name="mlp_weights",
+    )(table, n_two, g_rows, hidden, grad_hidden)
+
+    if direct:
+        far_got = passed(far_send, MASKS[4])
+
+    block_out = pl.pallas_call(
+        output_body,
         grid=(MICRO,),
-        in_specs=[SCALARS, SCALARS, full((BLOCKS, 2 * PIECE, C)), rows_of(C), rows_of(C), full((12, C)), full((IMG, PAD))],
-        out_specs=[IMAGE, rows_of(C), full((half, 2 * PIECE, C)), full((half, 2 * PIECE, C)), full((12, C))],
-        out_shape=[
-            sds(tokens_in.shape, LOW), sds((ROWS, C), F32), sds((half, 2 * PIECE, C), LOW), sds((half, 2 * PIECE, C), LOW),
-            sds((12, C), F32),
-        ],
-        scratch_shapes=[
-            pltpu.VMEM((C, FF), LOW), pltpu.VMEM((C, FF), LOW), pltpu.VMEM((ROWS, FF), LOW), pltpu.VMEM((ROWS, FF), LOW),
-            pltpu.VMEM((C, ROWS), LOW), pltpu.VMEM((C, ROWS), LOW), pltpu.VMEM((BLOCKS, 2 * PIECE, C), LOW),
-            pltpu.VMEM((1, FF), F32),
-        ],
-        compiler_params=params(),
-        cost_estimate=cost(20e9, 12e6),
-        name="mlp",
-    )(order, backward, far_all, middle, g_rows, vectors, deal)
-
-    packed_grad, near_keep, near_send, bias_sum, sums_attend = pl.pallas_call(
+        in_specs=[rows_of(FF), full((C, FF)), rows_of(C), full((12, C)), full((IMG, PAD))],
+        out_specs=IMAGE,
+        out_shape=sds(tokens_in.shape, LOW),
+        compiler_params=params(16),
+        cost_estimate=cost(2e9, 8e6),
+        name="output",
+    )(hidden, w_fc2, middle, vectors, deal)
+
+    if direct:
+        block_out, far_got, grad_middle = tie(block_out, far_got, grad_middle)
+        far_stays, far_goes = first_sum(far_keep, far_got)
+        far_got = [passed(part, mask) for part, mask in zip(far_goes, plane)]
+
+    packed_grad, grad_low, bias_sum, sums_attend = pl.pallas_call(
         attend_back_body,
         grid=(MICRO,),
         in_specs=[
-            SCALARS, SCALARS, SCALARS, rows_of(C), rows_of(C), rows_of(3 * C),
-            pl.BlockSpec((1, 2 * GROUPS, GROUP * WIN, 128), lambda i: (i, 0, 0, 0)), rows_of(C), full((C, C)),
-            full((2, IMG, 128)), full((IMG, 256)),
+            SCALARS, rows_of(C), rows_of(3 * C), pl.BlockSpec((1, 2 * GROUPS, GROUP * WIN, 128), lambda i: (i, 0, 0, 0)),
+            full((C, C)), full((2, IMG, 128)), full((IMG, 256)),
         ],
-        out_specs=[
-            rows_of(3 * C), full((half, PIECE, C)), full((half, PIECE, C)), full((GROUPS, GROUP * WIN, 128)), full((2, C)),
+        out_specs=[rows_of(3 * C), rows_of(C), full((GROUPS, GROUP * WIN, 128)), full((2, C))],
+        out_shape=[
+            sds((ROWS, 3 * C), LOW), sds((ROWS, C), LOW), sds((GROUPS, GROUP * WIN, 128), F32), sds((2, C), F32),
         ],
-        out_shape=[
-            sds((ROWS, 3 * C), LOW), sds((half, PIECE, C), LOW), sds((half, PIECE, C), LOW),
-            sds((GROUPS, GROUP * WIN, 128), F32), sds((2, C), F32),
-        ],
-        scratch_shapes=[
-            pltpu.VMEM((C, ROWS), LOW), pltpu.VMEM((C, ROWS), LOW), pltpu.VMEM((ROWS, C), LOW), pltpu.VMEM((ROWS, 3 * C), LOW),
-            pltpu.VMEM((BLOCKS, PIECE, C), LOW),
-        ],
-        compiler_params=params(),
-        cost_estimate=cost(12e9, 12e6),
+        compiler_params=params(32),
+        cost_estimate=cost(10e9, 12e6),
         name="attend_back",
-    )(backward, extent_own, route_own, grad_middle, attn, packed, soft, n_rows, w_proj, place, heads_low)
+    )(table, grad_middle, packed, soft, w_proj, place, heads_low)
+
+    if direct:
+        packed_grad, *far_got = tie(packed_grad, *far_got)
+        far_stays, far_goes = plane_sum(far_stays, far_got)
+        far_got = passed(far_goes, MASKS[1])
+
+    near_keep, near_send = pl.pallas_call(
+        functools.partial(attend_weights_body, direct),
+        in_specs=[SCALARS] + [pl.BlockSpec(memory_space=pltpu.VMEM)] * 4,
+        out_shape=[sds((half, PIECE, C), LOW), sds((half, PIECE, C), LOW)],
+        scratch_shapes=[pltpu.VMEM((BLOCKS, PIECE, C), LOW)],
+        compiler_params=pltpu.CompilerParams(vmem_limit_bytes=32 * 1024 * 1024),
+        cost_estimate=cost(2e9, 8e6),
+        name="attend_weights",
+    )(table, n_rows, grad_low, packed_grad, attn)
+
+    if direct:
+        near_send, far_got = tie(near_send, far_got)
+        near_got = passed(near_send, MASKS[4])
+        far_stays, far_goes = line_sum(far_stays, far_got)
+        near_keep, near_got, packed_grad = tie(near_keep, near_got, packed_grad)
+        near_stays, near_goes = first_sum(near_keep, near_got)
+        near_got = [passed(part, mask) for part, mask in zip(near_goes, plane)]
+        far_got = passed(far_goes, MASKS[0])
 
     grad_block, sums_input = pl.pallas_call(
         input_body,
@@ -574,30 +668,35 @@
         in_specs=[rows_of(3 * C), full((C, 3 * C)), rows_of(C), rows_of(C), full((12, C)), full((IMG, PAD))],
         out_specs=[IMAGE, full((2, C))],
         out_shape=[sds(tokens_in.shape, LOW), sds((2, C), F32)],
-        compiler_params=params(32),
+        compiler_params=params(16),
         cost_estimate=cost(4e9, 8e6),
         name="input_grad",
     )(packed_grad, w_qkv, x_rows, grad_middle, vectors, deal)
 
-    far_grad = share(far_keep, far_send) / patches
-    near_grad = share(near_keep, near_send) / patches
     vec_grad = jnp.concatenate([sums_input, sums_attend, sums_mlp[4:]], axis=0)
     bias_sum = (bias_sum[:, :, :WIN] + bias_sum[:, :, WIN:]).reshape(NH, WIN * WIN)
     table_grad = jnp.dot(bias_sum, jnp.asarray(LOOKUP.T), precision=HIGH)
-    squares = jnp.sum(near_grad * near_grad) + jnp.sum(far_grad * far_grad)
     if direct:
-        spare = jnp.concatenate([vec_grad.reshape(-1), table_grad.reshape(-1)]).reshape(-1, 12)
-        for mask in masks[::-1]:
-            spare = spare + exchange(spare, mask, devices)
-        squares = jnp.broadcast_to(squares, (1, 128))
-        for mask in masks[::-1]:
-            squares = squares + exchange(squares, mask, devices)
-        vec_grad = spare.reshape(-1)[: 12 * C].reshape(12, C)
-        table_grad = spare.reshape(-1)[12 * C :].reshape(NH, REL)
+        spare = jnp.concatenate([vec_grad.reshape(-1), table_grad.reshape(-1), jnp.zeros((20,), F32)]).reshape(52, 128)
+        grad_block, spare, *near_got = tie(grad_block, spare, *near_got)
+        near_stays, near_goes = plane_sum(near_stays, near_got)
+        near_stays, near_goes = line_sum(near_stays, passed(near_goes, MASKS[1]))
+        near_grad = (near_stays + passed(near_goes, MASKS[0]).astype(F32))[0] / patches
+        far_grad = (far_stays + far_got.astype(F32))[0] / patches
+        squares = jnp.sum(near_grad * near_grad) + jnp.sum(far_grad * far_grad)
+        spare = join(spare, jnp.broadcast_to(squares, (4, 128)))
+        for mask in MASKS[::-1]:
+            spare = spare + passed(spare, mask)
+        squares = spare[52:53]
+        spare = spare[:52].reshape(-1) / patches
+        vec_grad = spare[: 12 * C].reshape(12, C)
+        table_grad = spare[12 * C : 12 * C + NH * REL].reshape(NH, REL)
     else:
+        near_grad, far_grad = share_plain(near_keep, near_send) / patches, share_plain(far_keep, far_send) / patches
+        squares = jnp.sum(near_grad * near_grad) + jnp.sum(far_grad * far_grad)
         vec_grad, table_grad, squares = lax.psum((vec_grad, table_grad, squares), BOTH)
         squares = jnp.broadcast_to(squares, (1, 128))
-    vec_grad, table_grad = vec_grad / patches, table_grad / patches
+        vec_grad, table_grad = vec_grad / patches, table_grad / patches
 
     olds = (
         qkv_weight, proj_weight.T, fc1_weight, fc2_weight.T, vectors, rel_table.T,

time: 207 us -> 151 us (0.73)
  waiting for transfers between devices: 50.3 us -> 22.6 us
  local copies, waits for them, and re-layouts: 22.9 us -> 8.55 us
  starting transfers between devices: 45.6 us -> 35.1 us
  Pallas kernels: 71 us -> 66 us
    ppermute x34 -> x29, waiting for transfers between devices: 50.3 us -> 22.6 us  [passed(): return lax.ppermute(rows, BOTH, [(i, i ^ mask) for i in range(devices)])]
    ppermute x34 -> x29, starting transfers between devices: 45.6 us -> 35.1 us  [passed(): return lax.ppermute(rows, BOTH, [(i, i ^ mask) for i in range(devices)])]
    unnamed x98 -> x89, local copies, waits for them, and re-layouts: 16 us -> 5.83 us
    pallas_call x3 -> x7, Pallas kernels: 59.9 us -> 55.1 us  [the longest x1 14.1 us: body(): pl.pallas_call(functools.partial(mlp_body, direct), grid=(MICRO,), in_spe...]
    add x15 -> x11, other arithmetic: 0.96 us -> 4.22 us  [the longest x2 2.86 us: first_sum(): total = keep.astype(F32) + got.astype(F32)]
    convert_element_type x2 -> x0, other arithmetic: 2.98 us -> none  [share(): low = held.astype(LOW)]
  transfers between devices with their start and end apart: 34 -> 29, of which waited for: 14 -> 14; matrix products, arithmetic and copies ran while one was open for 14% -> 10% of each run, Pallas kernels for 9% -> 28%
where the time goes in v3:
time: 151 us
  Pallas kernels  66 us (44%)
  starting transfers between devices  35.1 us (23%)
  waiting for transfers between devices  22.6 us (15%)
  local copies, waits for them, and re-layouts  8.55 us (6%)
  matrix products  7.76 us (5%)
  other arithmetic  7.58 us (5%)
  between operations  2.98 us (2%)
    ppermute x29, starting transfers between devices, passed(): return lax.ppermute(rows, BOTH, [(i, i ^ mask) for i in range(devices)])  35.1 us
    ppermute x29, waiting for transfers between devices, passed(): return lax.ppermute(rows, BOTH, [(i, i ^ mask) for i in range(devices)])  22.6 us
    pallas_call x1, Pallas kernels, body(): pl.pallas_call(functools.partial(mlp_body, direct), grid=(MICRO,), in_spe...  14.1 us
    pallas_call x1, Pallas kernels, body(): pl.pallas_call(functools.partial(attend_body, direct), grid=(MICRO,), in_...  12.9 us
    pallas_call x1, Pallas kernels, body(): pl.pallas_call(attend_back_body, grid=(MICRO,), in_specs=[SCALARS, rows_o...  11.1 us
    pallas_call x1, Pallas kernels, body(): pl.pallas_call(functools.partial(mlp_weights_body, direct), grid=(4,), in...  6.74 us
    unnamed x89, local copies, waits for them, and re-layouts  5.83 us
    pallas_call x1, Pallas kernels, body(): pl.pallas_call(input_body, grid=(MICRO,), in_specs=[rows_of(3 * C), full(...  5.29 us
  transfers between devices with their start and end apart: 29, of which 14 were waited for; matrix products, arithmetic and copies ran while one was open for 10% of the time, Pallas kernels for 28%

profile of v3, /device:TPU:0, one launch (start us, length us, event | category | flops | bytes accessed | tf_op | source)
XLA Modules:
  0.0 150.7 jit_solution(13161404196366312732)
XLA Ops:
  2.4 4.0 %collective-permute-start = (bf16[1,48,384]{2,1,0:T(8,128)(2,1)}, bf16[1,48,384]{2,1,0:T(8,128)(2,1)S(1)}, u32[]{:S(2)}, u32[]{:S(2)}) collective-permute-start(bf16[1,48,384]{2,1,0:T(8,128)(2,1)} %bitcast.54), channel_id=1, source_target_pairs={{0,16},{1,17},{2,18},{3,19},{4,20},{5,21},{6,22},{7,23},{8,24},{9,... | collective-permute-start | bytes 110600 | tf_op jit(solution)/shard_map/ppermute | solution.py:468
  6.5 3.6 %convolution_bitcast_fusion = f32[12,4096]{1,0:T(8,128)S(1)} fusion(f32[169,4096]{1,0:T(8,128)} %constant.102.clone, f32[169,12]{0,1:T(8,128)} %param.37), kind=kOutput, calls=%fused_computation | convolution fusion | flops 99680256 | bytes 2973616 | tf_op jit(solution)/shard_map/dot_general | solution.py:524
  15.5 2.0 %collective-permute-start.2 = (bf16[4,48,384]{2,1,0:T(8,128)(2,1)S(1)}, bf16[4,48,384]{2,1,0:T(8,128)(2,1)S(1)}, u32[]{:S(2)}, u32[]{:S(2)}) collective-permute-start(bf16[4,48,384]{2,1,0:T(8,128)(2,1)S(1)} %pad_maximum_fusion.4), channel_id=1, source_target_pairs={{0,2},{1,3},{2,0},{3,1},{4,6},{5,7},{6,4},{7,5},{8,10},{9,11},{10,... | collective-permute-start | bytes 442376 | tf_op jit(solution)/shard_map/ppermute | solution.py:468
  19.7 2.5 %collective-permute-done.2 = bf16[4,48,384]{2,1,0:T(8,128)(2,1)S(1)} collective-permute-done((bf16[4,48,384]{2,1,0:T(8,128)(2,1)S(1)}, bf16[4,48,384]{2,1,0:T(8,128)(2,1)S(1)}, u32[]{:S(2)}, u32[]{:S(2)}) %collective-permute-start.2) | collective-permute-done | bytes 147488 | tf_op jit(solution)/shard_map/ppermute | solution.py:468
  27.2 2.7 %prep.1 = (bf16[1280,384]{1,0:T(8,128)(2,1)S(1)}, bf16[1280,384]{1,0:T(8,128)(2,1)S(1)}, bf16[1280,384]{1,0:T(8,128)(2,1)S(1)}) custom-call(bf16[5,1,14,14,384]{4,3,2,1,0:T(8,128)(2,1)S(1)} %copy-done.21, bf16[5,1,14,14,384]{4,3,2,1,0:T(8,128)(2,1)S(1)} %copy-done.22, bf16[256,224]{1,0:T(8,128)(2,1)S(1)} %copy-done.5, f32[12,384]{1,0:T(8,128)S(1)} %copy-done.7), custom_call_target="tpu_custom_call" | custom-call | flops 2000000000 | bytes 6000000 | tf_op jit(solution)/shard_map/prep/pallas_call | solution.py:513
  35.0 12.9 %attend.1 = (bf16[1280,1152]{1,0:T(8,128)(2,1)S(1)}, f32[5,6,256,128]{3,2,1,0:T(8,128)S(1)}, bf16[1280,384]{1,0:T(8,128)(2,1)S(1)}, bf16[384,1152]{1,0:T(8,128)(2,1)S(1)}, bf16[384,384]{1,0:T(8,128)(2,1)S(1)}) custom-call(s32[32]{0:T(128)S(1)} %pad_add_fusion.table_ref, bf16[32,48,384]{2,1,0:T(8,128)(2,1)S(1)} %pad_maximum_fusion.near_ref, ...), custom_call_target="tpu_custom_call" | custom-call | flops 8000000000 | bytes 12000000 | tf_op jit(solution)/shard_map/attend/pallas_call | solution.py:539
  48.2 2.5 %middle.1 = (f32[1280,384]{1,0:T(8,128)S(1)}, bf16[1280,384]{1,0:T(8,128)(2,1)S(1)}) custom-call(bf16[1280,384]{1,0:T(8,128)(2,1)S(1)} %get-tuple-element.113.attn_ref, bf16[1280,384]{1,0:T(8,128)(2,1)S(1)} %get-tuple-element.114.x_ref, bf16[384,384]{1,0:T(8,128)(2,1)S(1)} %get-tuple-element.115.wp_ref, f32[12,384]{1,0:T(8,128)S(1)} %copy-done.7), custom_call_target="tpu_custom_call" | custom-call | flops 1000000000 | bytes 6000000 | tf_op jit(solution)/shard_map/middle/pallas_call | solution.py:565
  51.3 14.1 %mlp.1 = (bf16[1280,1536]{1,0:T(8,128)(2,1)S(1)}, bf16[1280,1536]{1,0:T(8,128)(2,1)S(1)}, f32[1280,384]{1,0:T(8,128)S(1)}, f32[12,384]{1,0:T(8,128)S(1)}, bf16[384,1536]{1,0:T(8,128)(2,1)S(1)}) custom-call(s32[32]{0:T(128)S(1)} %pad_add_fusion.table_ref, bf16[32,96,384]{2,1,0:T(8,128)(2,1)S(1)} %constant_dynamic-update-slice_fusion.6.far_ref, ...), custom_call_target="tpu_custom_call" | custom-call | flops 10000000000 | bytes 16000000 | tf_op jit(solution)/shard_map/mlp/pallas_call | solution.py:580
  65.4 6.7 %mlp_weights.1 = (bf16[16,96,384]{2,1,0:T(8,128)(2,1)S(1)}, bf16[16,96,384]{2,1,0:T(8,128)(2,1)S(1)}) custom-call(s32[32]{0:T(128)S(1)} %pad_add_fusion.table_ref, bf16[1280,384]{1,0:T(8,128)(2,1)S(1)} %get-tuple-element.119.n_ref, bf16[1280,384]{1,0:T(8,128)(2,1)S(1)} %get-tuple-element.120.g_ref, bf16[1280,1536]{1,0:T(8,128)(2,1)S(1)} %get-tuple-element.121.hidden_ref, ...), custom_call_target="tpu_custom_call" | custom-call | flops 4000000000 | bytes 12000000 | tf_op jit(solution)/shard_map/mlp_weights/pallas_call | solution.py:594
  72.6 4.7 %output.1 = bf16[5,1,14,14,384]{4,3,2,1,0:T(8,128)(2,1)} custom-call(bf16[1280,1536]{1,0:T(8,128)(2,1)S(1)} %get-tuple-element.121.hidden_ref, bf16[384,1536]{1,0:T(8,128)(2,1)S(1)} %get-tuple-element.122.w2_ref, f32[1280,384]{1,0:T(8,128)S(1)} %get-tuple-element.118.middle_ref, f32[12,384]{1,0:T(8,128)S(1)} %copy-done.7, bf16[256,224]{1,0:T(8,128)(2,1)S(1)} %copy-done.5), custom_call_target="tpu_custom_call" | custom-call | flops 2000000000 | bytes 8000000 | tf_op jit(solution)/shard_map/output/pallas_call | solution.py:609
  81.3 11.1 %attend_back.1 = (bf16[1280,1152]{1,0:T(8,128)(2,1)S(1)}, bf16[1280,384]{1,0:T(8,128)(2,1)S(1)}, f32[3,256,128]{2,1,0:T(8,128)S(1)}, f32[2,384]{1,0:T(2,128)S(1)}) custom-call(s32[32]{0:T(128)S(1)} %pad_add_fusion.table_ref, f32[1280,384]{1,0:T(8,128)S(1)} %get-tuple-element.127.grad_ref, bf16[1280,1152]{1,0:T(8,128)(2,1)S(1)} %get-tuple-element.128.packed_ref, ...), custom_call_target="tpu_custom_call" | custom-call | flops 10000000000 | bytes 12000000 | tf_op jit(solution)/shard_map/attend_back/pallas_call | solution.py:625
  94.5 1.9 %collective-permute-start.16 = (bf16[2,96,384]{2,1,0:T(8,128)(2,1)S(1)}, bf16[2,96,384]{2,1,0:T(8,128)(2,1)S(1)}, u32[]{:S(2)}, u32[]{:S(2)}) collective-permute-start(bf16[2,96,384]{2,1,0:T(8,128)(2,1)S(1)} %slice.154), channel_id=1, source_target_pairs={{0,8},{1,9},{2,10},{3,11},{4,12},{5,13},{6,14},{7,15},{8,0},{9,1},... | collective-permute-start | bytes 442376 | tf_op jit(solution)/shard_map/ppermute | solution.py:468
  96.4 3.1 %attend_weights.1 = (bf16[16,48,384]{2,1,0:T(8,128)(2,1)S(1)}, bf16[16,48,384]{2,1,0:T(8,128)(2,1)S(1)}) custom-call(s32[32]{0:T(128)S(1)} %pad_add_fusion.table_ref, bf16[1280,384]{1,0:T(8,128)(2,1)S(1)} %get-tuple-element.107.n_ref, bf16[1280,384]{1,0:T(8,128)(2,1)S(1)} %get-tuple-element.130.grad_low_ref, ...), custom_call_target="tpu_custom_call" | custom-call | flops 2000000000 | bytes 8000000 | tf_op jit(solution)/shard_map/attend_weights/pallas_call | solution.py:646
  100.7 4.1 %fusion.15 = f32[12,169]{1,0:T(8,128)S(1)} fusion(f32[12,4096]{1,0:T(8,128)S(1)} %reshape.84, f32[4096,169]{0,1:T(8,128)} %constant.103.clone), kind=kOutput, calls=%fused_computation.52 | convolution fusion | flops 99680256 | bytes 2973616 | tf_op jit(solution)/shard_map/dot_general | solution.py:678
  105.0 2.5 %convert_add_fusion.1 = (f32[16,48,384]{2,1,0:T(8,128)}, bf16[16,48,384]{2,1,0:T(8,128)(2,1)S(1)}) fusion(bf16[16,48,384]{2,1,0:T(8,128)(2,1)} %collective-permute-done.17, bf16[16,48,384]{2,1,0:T(8,128)(2,1)S(1)} %get-tuple-element.148), kind=kLoop, calls=%fused_computation.4 | loop fusion | flops 1179648 | bytes 2949120 | tf_op jit(solution)/shard_map/add | solution.py:496
  112.6 5.3 %input_grad.1 = (bf16[5,1,14,14,384]{4,3,2,1,0:T(8,128)(2,1)}, f32[2,384]{1,0:T(2,128)S(1)}) custom-call(bf16[1280,1152]{1,0:T(8,128)(2,1)S(1)} %copy-done.27, bf16[384,1152]{1,0:T(8,128)(2,1)S(1)} %copy-done.31, bf16[1280,384]{1,0:T(8,128)(2,1)S(1)} %get-tuple-element.114.x_ref, f32[1280,384]{1,0:T(8,128)S(1)} %copy-done.29, f32[12,384]{1,0:T(8,128)S(1)} %copy-done.7, ...), custom_call_target="tpu_custom_call" | custom-call | flops 4000000000 | bytes 8000000 | tf_op jit(solution)/shard_map/input_grad/pallas_call | solution.py:665
  119.4 1.9 %collective-permute-start.21 = (bf16[2,48,384]{2,1,0:T(8,128)(2,1)S(1)}, bf16[2,48,384]{2,1,0:T(8,128)(2,1)S(1)}, u32[]{:S(2)}, u32[]{:S(2)}) collective-permute-start(bf16[2,48,384]{2,1,0:T(8,128)(2,1)S(1)} %slice.156), channel_id=1, source_target_pairs={{0,8},{1,9},{2,10},{3,11},{4,12},{5,13},{6,14},{7,15},{8,0},{9,1},... | collective-permute-start | bytes 221192 | tf_op jit(solution)/shard_map/ppermute | solution.py:468
  121.4 2.7 %collective-permute-start.23 = (bf16[1,96,384]{2,1,0:T(8,128)(2,1)S(1)}, bf16[1,96,384]{2,1,0:T(8,128)(2,1)S(1)}, u32[]{:S(2)}, u32[]{:S(2)}) collective-permute-start(bf16[1,96,384]{2,1,0:T(8,128)(2,1)S(1)} %slice.155), channel_id=1, source_target_pairs={{0,16},{1,17},{2,18},{3,19},{4,20},{5,21},{6,22},{7,23},{8,24},{9,... | collective-permute-start | bytes 221192 | tf_op jit(solution)/shard_map/ppermute | solution.py:468
  124.4 2.2 %collective-permute-start.22 = (bf16[1,48,384]{2,1,0:T(8,128)(2,1)S(1)}, bf16[1,48,384]{2,1,0:T(8,128)(2,1)S(1)}, u32[]{:S(2)}, u32[]{:S(2)}) collective-permute-start(bf16[1,48,384]{2,1,0:T(8,128)(2,1)S(1)} %slice.157), channel_id=1, source_target_pairs={{0,16},{1,17},{2,18},{3,19},{4,20},{5,21},{6,22},{7,23},{8,24},{9,... | collective-permute-start | bytes 110600 | tf_op jit(solution)/shard_map/ppermute | solution.py:468
  133.1 3.2 %collective-permute-done.25 = f32[56,128]{1,0:T(8,128)S(1)} collective-permute-done((f32[56,128]{1,0:T(8,128)S(1)}, f32[56,128]{1,0:T(8,128)S(1)}, u32[]{:S(2)}, u32[]{:S(2)}) %collective-permute-start.25) | collective-permute-done | bytes 28704 | tf_op jit(solution)/shard_map/ppermute | solution.py:468
  137.0 3.2 %collective-permute-done.26 = f32[56,128]{1,0:T(8,128)S(1)} collective-permute-done((f32[56,128]{1,0:T(8,128)S(1)}, f32[56,128]{1,0:T(8,128)S(1)}, u32[]{:S(2)}, u32[]{:S(2)}) %collective-permute-start.26) | collective-permute-done | bytes 28704 | tf_op jit(solution)/shard_map/ppermute | solution.py:468
  142.0 2.1 %collective-permute-done.27 = f32[56,128]{1,0:T(8,128)S(1)} collective-permute-done((f32[56,128]{1,0:T(8,128)S(1)}, f32[56,128]{1,0:T(8,128)S(1)}, u32[]{:S(2)}, u32[]{:S(2)}) %collective-permute-start.27) | collective-permute-done | bytes 28704 | tf_op jit(solution)/shard_map/ppermute | solution.py:468
  144.1 2.2 %collective-permute-start.28 = (f32[56,128]{1,0:T(8,128)S(1)}, f32[56,128]{1,0:T(8,128)S(1)}, u32[]{:S(2)}, u32[]{:S(2)}) collective-permute-start(f32[56,128]{1,0:T(8,128)S(1)} %add.108), channel_id=1, source_target_pairs={{0,16},{1,17},{2,18},{3,19},{4,20},{5,21},{6,22},{7,23},{8,24},{9,... | collective-permute-start | bytes 86024 | tf_op jit(solution)/shard_map/ppermute | solution.py:468
  146.4 2.5 %collective-permute-done.28 = f32[56,128]{1,0:T(8,128)S(1)} collective-permute-done((f32[56,128]{1,0:T(8,128)S(1)}, f32[56,128]{1,0:T(8,128)S(1)}, u32[]{:S(2)}, u32[]{:S(2)}) %collective-permute-start.28) | collective-permute-done | bytes 28704 | tf_op jit(solution)/shard_map/ppermute | solution.py:468
  (187 shorter events, 43.7 us)
Async XLA Ops:
  2.4 8.4 %collective-permute-start = (bf16[1,48,384]{2,1,0:T(8,128)(2,1)}, bf16[1,48,384]{2,1,0:T(8,128)(2,1)S(1)}, u32[]{:S(2)}, u32[]{:S(2)}) collective-permute-start(bf16[1,48,384]{2,1,0:T(8,128)(2,1)} %bitcast.54), channel_id=1, source_target_pairs={{0,16},{1,17},{2,18},{3,19},{4,20},{5,21},{6,22},{7,23},{8,24},{9,... | collective-permute-start | bytes 110600 | tf_op jit(solution)/shard_map/ppermute | solution.py:468
  6.4 6.9 %collective-permute-start.5 = (bf16[1,96,384]{2,1,0:T(8,128)(2,1)}, bf16[1,96,384]{2,1,0:T(8,128)(2,1)S(1)}, u32[]{:S(2)}, u32[]{:S(2)}) collective-permute-start(bf16[1,96,384]{2,1,0:T(8,128)(2,1)} %bitcast.57), channel_id=1, source_target_pairs={{0,16},{1,17},{2,18},{3,19},{4,20},{5,21},{6,22},{7,23},{8,24},{9,... | collective-permute-start | bytes 221192 | tf_op jit(solution)/shard_map/ppermute | solution.py:468
  10.8 4.7 %collective-permute-start.1 = (bf16[2,48,384]{2,1,0:T(8,128)(2,1)S(1)}, bf16[2,48,384]{2,1,0:T(8,128)(2,1)S(1)}, u32[]{:S(2)}, u32[]{:S(2)}) collective-permute-start(bf16[2,48,384]{2,1,0:T(8,128)(2,1)S(1)} %pad_maximum_fusion.6), channel_id=1, source_target_pairs={{0,8},{1,9},{2,10},{3,11},{4,12},{5,13},{6,14},{7,15},{8,0},{9,1},... | collective-permute-start | bytes 221192 | tf_op jit(solution)/shard_map/ppermute | solution.py:468
  13.3 6.4 %collective-permute-start.6 = (bf16[2,96,384]{2,1,0:T(8,128)(2,1)S(1)}, bf16[2,96,384]{2,1,0:T(8,128)(2,1)S(1)}, u32[]{:S(2)}, u32[]{:S(2)}) collective-permute-start(bf16[2,96,384]{2,1,0:T(8,128)(2,1)S(1)} %pad_maximum_fusion.5), channel_id=1, source_target_pairs={{0,8},{1,9},{2,10},{3,11},{4,12},{5,13},{6,14},{7,15},{8,0},{9,1},... | collective-permute-start | bytes 442376 | tf_op jit(solution)/shard_map/ppermute | solution.py:468
  15.5 6.8 %collective-permute-start.2 = (bf16[4,48,384]{2,1,0:T(8,128)(2,1)S(1)}, bf16[4,48,384]{2,1,0:T(8,128)(2,1)S(1)}, u32[]{:S(2)}, u32[]{:S(2)}) collective-permute-start(bf16[4,48,384]{2,1,0:T(8,128)(2,1)S(1)} %pad_maximum_fusion.4), channel_id=1, source_target_pairs={{0,2},{1,3},{2,0},{3,1},{4,6},{5,7},{6,4},{7,5},{8,10},{9,11},{10,... | collective-permute-start | bytes 442376 | tf_op jit(solution)/shard_map/ppermute | solution.py:468
  17.5 5.4 %collective-permute-start.3 = (bf16[4,48,384]{2,1,0:T(8,128)(2,1)S(1)}, bf16[4,48,384]{2,1,0:T(8,128)(2,1)S(1)}, u32[]{:S(2)}, u32[]{:S(2)}) collective-permute-start(bf16[4,48,384]{2,1,0:T(8,128)(2,1)S(1)} %pad_maximum_fusion.4), channel_id=1, source_target_pairs={{0,4},{1,5},{2,6},{3,7},{4,0},{5,1},{6,2},{7,3},{8,12},{9,13},{10,... | collective-permute-start | bytes 442376 | tf_op jit(solution)/shard_map/ppermute | solution.py:468
  19.0 6.0 %collective-permute-start.4 = (bf16[4,48,384]{2,1,0:T(8,128)(2,1)S(1)}, bf16[4,48,384]{2,1,0:T(8,128)(2,1)S(1)}, u32[]{:S(2)}, u32[]{:S(2)}) collective-permute-start(bf16[4,48,384]{2,1,0:T(8,128)(2,1)S(1)} %pad_maximum_fusion.4), channel_id=1, source_target_pairs={{0,6},{1,7},{2,4},{3,5},{4,2},{5,3},{6,0},{7,1},{8,14},{9,15},{10,... | collective-permute-start | bytes 442376 | tf_op jit(solution)/shard_map/ppermute | solution.py:468
  25.7 7.8 %collective-permute-start.7 = (bf16[16,48,384]{2,1,0:T(8,128)(2,1)}, bf16[16,48,384]{2,1,0:T(8,128)(2,1)}, u32[]{:S(2)}, u32[]{:S(2)}) collective-permute-start(bf16[16,48,384]{2,1,0:T(8,128)(2,1)} %constant_dynamic-update-slice_fusion), channel_id=1, source_target_pairs={{0,1},{1,0},{2,3},{3,2},{4,5},{5,4},{6,7},{7,6},{8,9},{9,8},{10,11... | collective-permute-start | bytes 1769480 | tf_op jit(solution)/shard_map/ppermute | solution.py:468
  30.0 17.9 %collective-permute-start.8 = (bf16[4,96,384]{2,1,0:T(8,128)(2,1)S(1)}, bf16[4,96,384]{2,1,0:T(8,128)(2,1)S(1)}, u32[]{:S(2)}, u32[]{:S(2)}) collective-permute-start(bf16[4,96,384]{2,1,0:T(8,128)(2,1)S(1)} %pad_maximum_fusion.3), channel_id=1, source_target_pairs={{0,2},{1,3},{2,0},{3,1},{4,6},{5,7},{6,4},{7,5},{8,10},{9,11},{10,... | collective-permute-start | bytes 884744 | tf_op jit(solution)/shard_map/ppermute | solution.py:468
  30.7 17.2 %collective-permute-start.9 = (bf16[4,96,384]{2,1,0:T(8,128)(2,1)S(1)}, bf16[4,96,384]{2,1,0:T(8,128)(2,1)S(1)}, u32[]{:S(2)}, u32[]{:S(2)}) collective-permute-start(bf16[4,96,384]{2,1,0:T(8,128)(2,1)S(1)} %pad_maximum_fusion.3), channel_id=1, source_target_pairs={{0,4},{1,5},{2,6},{3,7},{4,0},{5,1},{6,2},{7,3},{8,12},{9,13},{10,... | collective-permute-start | bytes 884744 | tf_op jit(solution)/shard_map/ppermute | solution.py:468
  32.2 15.7 %collective-permute-start.10 = (bf16[4,96,384]{2,1,0:T(8,128)(2,1)S(1)}, bf16[4,96,384]{2,1,0:T(8,128)(2,1)S(1)}, u32[]{:S(2)}, u32[]{:S(2)}) collective-permute-start(bf16[4,96,384]{2,1,0:T(8,128)(2,1)S(1)} %pad_maximum_fusion.3), channel_id=1, source_target_pairs={{0,6},{1,7},{2,4},{3,5},{4,2},{5,3},{6,0},{7,1},{8,14},{9,15},{10,... | collective-permute-start | bytes 884744 | tf_op jit(solution)/shard_map/ppermute | solution.py:468
  72.1 5.1 %collective-permute-start.12 = (bf16[16,96,384]{2,1,0:T(8,128)(2,1)S(1)}, bf16[16,96,384]{2,1,0:T(8,128)(2,1)S(1)}, u32[]{:S(2)}, u32[]{:S(2)}) collective-permute-start(bf16[16,96,384]{2,1,0:T(8,128)(2,1)S(1)} %get-tuple-element.124), channel_id=1, source_target_pairs={{0,1},{1,0},{2,3},{3,2},{4,5},{5,4},{6,7},{7,6},{8,9},{9,8},{10,11... | collective-permute-start | bytes 3538952 | tf_op jit(solution)/shard_map/ppermute | solution.py:468
  77.8 14.6 %collective-permute-start.13 = (bf16[4,96,384]{2,1,0:T(8,128)(2,1)S(1)}, bf16[4,96,384]{2,1,0:T(8,128)(2,1)S(1)}, u32[]{:S(2)}, u32[]{:S(2)}) collective-permute-start(bf16[4,96,384]{2,1,0:T(8,128)(2,1)S(1)} %get-tuple-element.185), channel_id=1, source_target_pairs={{0,2},{1,3},{2,0},{3,1},{4,6},{5,7},{6,4},{7,5},{8,10},{9,11},{10,... | collective-permute-start | bytes 884744 | tf_op jit(solution)/shard_map/ppermute | solution.py:468
  78.5 13.9 %collective-permute-start.14 = (bf16[4,96,384]{2,1,0:T(8,128)(2,1)S(1)}, bf16[4,96,384]{2,1,0:T(8,128)(2,1)S(1)}, u32[]{:S(2)}, u32[]{:S(2)}) collective-permute-start(bf16[4,96,384]{2,1,0:T(8,128)(2,1)S(1)} %get-tuple-element.184), channel_id=1, source_target_pairs={{0,4},{1,5},{2,6},{3,7},{4,0},{5,1},{6,2},{7,3},{8,12},{9,13},{10,... | collective-permute-start | bytes 884744 | tf_op jit(solution)/shard_map/ppermute | solution.py:468
  80.0 14.4 %collective-permute-start.15 = (bf16[4,96,384]{2,1,0:T(8,128)(2,1)S(1)}, bf16[4,96,384]{2,1,0:T(8,128)(2,1)S(1)}, u32[]{:S(2)}, u32[]{:S(2)}) collective-permute-start(bf16[4,96,384]{2,1,0:T(8,128)(2,1)S(1)} %get-tuple-element.183), channel_id=1, source_target_pairs={{0,6},{1,7},{2,4},{3,5},{4,2},{5,3},{6,0},{7,1},{8,14},{9,15},{10,... | collective-permute-start | bytes 884744 | tf_op jit(solution)/shard_map/ppermute | solution.py:468
  94.5 5.2 %collective-permute-start.16 = (bf16[2,96,384]{2,1,0:T(8,128)(2,1)S(1)}, bf16[2,96,384]{2,1,0:T(8,128)(2,1)S(1)}, u32[]{:S(2)}, u32[]{:S(2)}) collective-permute-start(bf16[2,96,384]{2,1,0:T(8,128)(2,1)S(1)} %slice.154), channel_id=1, source_target_pairs={{0,8},{1,9},{2,10},{3,11},{4,12},{5,13},{6,14},{7,15},{8,0},{9,1},... | collective-permute-start | bytes 442376 | tf_op jit(solution)/shard_map/ppermute | solution.py:468
  99.7 5.3 %collective-permute-start.17 = (bf16[16,48,384]{2,1,0:T(8,128)(2,1)S(1)}, bf16[16,48,384]{2,1,0:T(8,128)(2,1)}, u32[]{:S(2)}, u32[]{:S(2)}) collective-permute-start(bf16[16,48,384]{2,1,0:T(8,128)(2,1)S(1)} %get-tuple-element.140), channel_id=1, source_target_pairs={{0,1},{1,0},{2,3},{3,2},{4,5},{5,4},{6,7},{7,6},{8,9},{9,8},{10,11... | collective-permute-start | bytes 1769480 | tf_op jit(solution)/shard_map/ppermute | solution.py:468
  107.5 10.7 %collective-permute-start.18 = (bf16[4,48,384]{2,1,0:T(8,128)(2,1)S(1)}, bf16[4,48,384]{2,1,0:T(8,128)(2,1)S(1)}, u32[]{:S(2)}, u32[]{:S(2)}) collective-permute-start(bf16[4,48,384]{2,1,0:T(8,128)(2,1)S(1)} %get-tuple-element.188), channel_id=1, source_target_pairs={{0,2},{1,3},{2,0},{3,1},{4,6},{5,7},{6,4},{7,5},{8,10},{9,11},{10,... | collective-permute-start | bytes 442376 | tf_op jit(solution)/shard_map/ppermute | solution.py:468
  108.2 10.0 %collective-permute-start.19 = (bf16[4,48,384]{2,1,0:T(8,128)(2,1)S(1)}, bf16[4,48,384]{2,1,0:T(8,128)(2,1)}, u32[]{:S(2)}, u32[]{:S(2)}) collective-permute-start(bf16[4,48,384]{2,1,0:T(8,128)(2,1)S(1)} %get-tuple-element.187), channel_id=1, source_target_pairs={{0,4},{1,5},{2,6},{3,7},{4,0},{5,1},{6,2},{7,3},{8,12},{9,13},{10,... | collective-permute-start | bytes 442376 | tf_op jit(solution)/shard_map/ppermute | solution.py:468
  109.7 8.5 %collective-permute-start.20 = (bf16[4,48,384]{2,1,0:T(8,128)(2,1)S(1)}, bf16[4,48,384]{2,1,0:T(8,128)(2,1)}, u32[]{:S(2)}, u32[]{:S(2)}) collective-permute-start(bf16[4,48,384]{2,1,0:T(8,128)(2,1)S(1)} %get-tuple-element.186), channel_id=1, source_target_pairs={{0,6},{1,7},{2,4},{3,5},{4,2},{5,3},{6,0},{7,1},{8,14},{9,15},{10,... | collective-permute-start | bytes 442376 | tf_op jit(solution)/shard_map/ppermute | solution.py:468
  119.4 4.9 %collective-permute-start.21 = (bf16[2,48,384]{2,1,0:T(8,128)(2,1)S(1)}, bf16[2,48,384]{2,1,0:T(8,128)(2,1)S(1)}, u32[]{:S(2)}, u32[]{:S(2)}) collective-permute-start(bf16[2,48,384]{2,1,0:T(8,128)(2,1)S(1)} %slice.156), channel_id=1, source_target_pairs={{0,8},{1,9},{2,10},{3,11},{4,12},{5,13},{6,14},{7,15},{8,0},{9,1},... | collective-permute-start | bytes 221192 | tf_op jit(solution)/shard_map/ppermute | solution.py:468
  121.4 6.8 %collective-permute-start.23 = (bf16[1,96,384]{2,1,0:T(8,128)(2,1)S(1)}, bf16[1,96,384]{2,1,0:T(8,128)(2,1)S(1)}, u32[]{:S(2)}, u32[]{:S(2)}) collective-permute-start(bf16[1,96,384]{2,1,0:T(8,128)(2,1)S(1)} %slice.155), channel_id=1, source_target_pairs={{0,16},{1,17},{2,18},{3,19},{4,20},{5,21},{6,22},{7,23},{8,24},{9,... | collective-permute-start | bytes 221192 | tf_op jit(solution)/shard_map/ppermute | solution.py:468
  124.4 4.9 %collective-permute-start.22 = (bf16[1,48,384]{2,1,0:T(8,128)(2,1)S(1)}, bf16[1,48,384]{2,1,0:T(8,128)(2,1)S(1)}, u32[]{:S(2)}, u32[]{:S(2)}) collective-permute-start(bf16[1,48,384]{2,1,0:T(8,128)(2,1)S(1)} %slice.157), channel_id=1, source_target_pairs={{0,16},{1,17},{2,18},{3,19},{4,20},{5,21},{6,22},{7,23},{8,24},{9,... | collective-permute-start | bytes 110600 | tf_op jit(solution)/shard_map/ppermute | solution.py:468
  144.1 4.8 %collective-permute-start.28 = (f32[56,128]{1,0:T(8,128)S(1)}, f32[56,128]{1,0:T(8,128)S(1)}, u32[]{:S(2)}, u32[]{:S(2)}) collective-permute-start(f32[56,128]{1,0:T(8,128)S(1)} %add.108), channel_id=1, source_target_pairs={{0,16},{1,17},{2,18},{3,19},{4,20},{5,21},{6,22},{7,23},{8,24},{9,... | collective-permute-start | bytes 86024 | tf_op jit(solution)/shard_map/ppermute | solution.py:468
  (45 other events, 774.7 us)

commit v4 on v3

v4 whole, which is shorter than its diff:
```python
import functools
import math

import jax
import jax.numpy as jnp
import numpy as np
from jax import lax
from jax.experimental import pallas as pl
from jax.experimental.pallas import tpu as pltpu
from jax.sharding import PartitionSpec as P

C = 384
NH = 12
HD = 32
FF = 1536
WS = 7
SHIFT = 3
STEP = 10
GRID = 14
CELLS = WS * WS
REL = (2 * WS - 1) ** 2
MICRO = 5

WIN = 64
IMG = 4 * WIN
PAD = 16 * GRID
ROWS = MICRO * IMG
GROUP = 4
GROUPS = NH // GROUP
LANES = GROUP * HD
BLOCKS = 32
PIECE = 48

EPS_NORM = 1e-05
BETA_ONE = 0.9
BETA_TWO = 0.999
ADAM_EPS = 1e-08
RATE_MATRIX = 0.08
RATE_VECTOR = 1.0
DECAY_MATRIX = 0.05
CLIP_NORM = 0.05
NEG_FILL = -1e30
HIGH = lax.Precision.HIGHEST
LOW = jnp.bfloat16
F32 = jnp.float32
NEVER = 99.0
BOTH = ("tok", "head")
MASKS = (16, 8, 2, 4, 1)
CORE, PLANE, LINE = 1, (2, 4, 6), (16, 8, 24)
PIECES = 8
ME, SLOT, EXTENT, ROUTE = 0, 1, 2, 12


def swap_bits(position):
    return sum((position & mask) // mask << bit for bit, mask in enumerate(MASKS))


def block_at(place):
    return sum(((place >> bit) & 1) * mask for bit, mask in enumerate(MASKS))


def window_tables():
    cell = np.arange(WIN)
    real = cell < CELLS
    rolled_row = np.stack([WS * (w // 2) + cell // WS for w in range(4)])
    rolled_col = np.stack([WS * (w % 2) + cell % WS for w in range(4)])
    source_row = (rolled_row + SHIFT) % GRID
    source_col = (rolled_col + SHIFT) % GRID

    def band(position):
        return np.where(position < GRID - WS, 0, np.where(position < GRID - SHIFT, 1, 2))

    label_row = (rolled_row + SHIFT) % GRID
    label_col = (rolled_col + SHIFT) % GRID
    region = 3 * band(label_row) + band(label_col)
    label_row = (label_row + SHIFT) % GRID
    label_col = (label_col + SHIFT) % GRID
    deal = np.zeros((IMG, PAD), np.float32)
    for w in range(4):
        for c in range(CELLS):
            deal[w * WIN + c, 16 * source_row[w, c] + source_col[w, c]] = 1.0
    place = np.full((2, IMG, 128), NEVER, np.float32)
    place[0] = np.where(real[None], source_row, NEVER).reshape(IMG, 1)
    place[1] = np.where(real[None], source_col, NEVER).reshape(IMG, 1)
    reach = np.full((2, 2, WIN, 128), NEVER, np.float32)
    for pair in range(2):
        for side in range(2):
            w = 2 * pair + side
            same = (region[w][:, None] == region[w][None, :]) & real[:, None] & real[None, :]
            for kind, source in enumerate((label_row, label_col)):
                far = np.where(same, np.maximum(source[w][:, None], source[w][None, :]), NEVER)
                far = np.where(np.eye(WIN, dtype=bool) & real[:, None], -1.0, far)
                reach[pair, kind, :, side * WIN : (side + 1) * WIN] = far
    row, col = cell // WS, cell % WS
    offset = (row[None, :] - row[:, None] + WS - 1) * (2 * WS - 1) + col[None, :] - col[:, None] + WS - 1
    offset = np.where(real[None, :] & real[:, None], offset, -1)
    lookup = (offset.reshape(1, -1) == np.arange(REL)[:, None]).astype(np.float32)
    heads = (np.arange(LANES)[None, :] // HD == np.arange(GROUP)[:, None]).astype(np.float32)
    heads = np.repeat(np.concatenate([heads, heads], axis=1), WIN, axis=0)
    return deal, place, reach, lookup, heads


DEAL, PLACE, REACH, LOOKUP, HEADS = window_tables()


def dot_nn(a, b):
    return lax.dot_general(a, b, (((1,), (0,)), ((), ())), preferred_element_type=F32)


def dot_nt(a, b):
    return lax.dot_general(a, b, (((1,), (1,)), ((), ())), preferred_element_type=F32)


def dot_tn(a, b):
    return lax.dot_general(a, b, (((0,), (0,)), ((), ())), preferred_element_type=F32)


def norm_parts(rows):
    average = jnp.mean(rows, axis=-1, keepdims=True)
    centered = rows - average
    inverse = lax.rsqrt(jnp.mean(centered * centered, axis=-1, keepdims=True) + EPS_NORM)
    return centered * inverse, inverse


def norm_back(gradient, normed, inverse, gain):
    scaled = gradient * gain
    return inverse * (
        scaled
        - jnp.mean(scaled, axis=-1, keepdims=True)
        - normed * jnp.mean(scaled * normed, axis=-1, keepdims=True)
    )


def gelu_parts(pre_act):
    size = jnp.abs(pre_act) * 2.0 ** (-0.5)
    bell = jnp.exp(-size * size)
    t = 1.0 / (1.0 + 0.3275911 * size)
    poly = t * (0.254829592 + t * (-0.284496736 + t * (1.421413741 + t * (-1.453152027 + t * 1.061405429))))
    tail = 0.5 * poly * bell
    return jnp.where(pre_act < 0.0, tail, 1.0 - tail), bell * (2.0 * math.pi) ** (-0.5)


SCALARS = pl.BlockSpec(memory_space=pltpu.SMEM)
HELD = pl.BlockSpec(memory_space=pltpu.VMEM)


def call(body, outs, inputs, name, limit=16, scratch=(), flops=1e9, scalars=0):
    return pl.pallas_call(
        body,
        in_specs=[SCALARS] * scalars + [HELD] * (len(inputs) - scalars),
        out_specs=[HELD] * len(outs),
        out_shape=[jax.ShapeDtypeStruct(shape, dtype) for shape, dtype in outs],
        scratch_shapes=list(scratch),
        compiler_params=whole(limit),
        cost_estimate=pl.CostEstimate(flops=int(flops), bytes_accessed=4000000, transcendentals=0),
        name=name,
    )(*inputs)


def image_rows(image):
    return pl.ds(pl.multiple_of(image * IMG, IMG), IMG)


def whole(limit):
    return pltpu.CompilerParams(vmem_limit_bytes=limit * 1024 * 1024)


def sds(shape, dtype):
    return jax.ShapeDtypeStruct(shape, dtype)


def streamed(*arrays):
    return [pltpu.with_memory_space_constraint(array, pltpu.HBM) for array in arrays]


def row_mask(place_ref, table_ref, image):
    parts = []
    for w in range(4):
        rows = slice(w * WIN, (w + 1) * WIN)
        high = jnp.where(table_ref[ROUTE + 4 * image + w] >= 0, table_ref[EXTENT + 2 * image], -1).astype(F32)
        wide = table_ref[EXTENT + 2 * image + 1].astype(F32)
        inside = (place_ref[0, rows] < high) & (place_ref[1, rows] < wide)
        parts.append(jnp.where(inside, 1.0, 0.0))
    return jnp.concatenate(parts, axis=0)


def pack_body(qkv_ref, proj_ref, fc1_ref, fc2_ref, near_ref, far_ref):
    near_ref[...] = jnp.concatenate([qkv_ref[0], qkv_ref[1], qkv_ref[2], proj_ref[...]], axis=1).astype(LOW)
    depth = fc1_ref.shape[0]
    far_ref[:depth] = fc1_ref[...].astype(LOW)
    far_ref[depth:] = fc2_ref[...].astype(LOW)


def first_sum_body(keep_ref, got_ref, stays_ref, *goes_refs):
    stays_ref[...] = keep_ref[:4].astype(F32) + got_ref[:4].astype(F32)
    for index, goes in enumerate(goes_refs):
        at = 4 * (index + 1)
        goes[...] = (keep_ref[at : at + 4].astype(F32) + got_ref[at : at + 4].astype(F32)).astype(LOW)


def plane_sum_body(stays_ref, *refs):
    got, (rest, *goes) = refs[:3], refs[3:]
    for at in range(4):
        total = stays_ref[at : at + 1] + got[0][at : at + 1].astype(F32)
        total = total + (got[1][at : at + 1].astype(F32) + got[2][at : at + 1].astype(F32))
        if at == 0:
            rest[...] = total
        else:
            goes[at - 1][...] = total.astype(LOW)


def finish_body(patches, near_ref, far_ref, vec_ref, table_ref, *refs):
    near_got, far_got, (near_grad, far_grad, spare) = refs[:3], refs[3:6], refs[6:]
    squares = jnp.zeros((1, 1), F32)
    for stays, got, target in ((near_ref, near_got, near_grad), (far_ref, far_got, far_grad)):
        total = stays[0] + got[0][0].astype(F32) + (got[1][0].astype(F32) + got[2][0].astype(F32))
        total = total * (1.0 / patches)
        target[...] = total
        squares = squares + jnp.sum(jnp.sum(total * total, axis=1, keepdims=True), axis=0, keepdims=True)
    spare[0:12] = vec_ref[...] * (1.0 / patches)
    spare[12:24] = jnp.zeros((12, C), F32)
    spare[12:24, :REL] = table_ref[...] * (1.0 / patches)
    spare[24:32] = jnp.broadcast_to(squares, (8, C))


def prep_body(tok_ref, cot_ref, deal_ref, vec_ref, x_ref, g_ref, n_ref, pad):
    pad[...] = jnp.zeros_like(pad)

    @pl.loop(0, MICRO)
    def _(image):
        at = image_rows(image)
        for source, target in ((cot_ref, g_ref), (tok_ref, x_ref)):
            for r in range(GRID):
                pad[16 * r : 16 * r + GRID, :] = source[image, 0, r]
            rows = dot_nn(deal_ref[...], pad[...])
            target[at, :] = rows.astype(LOW)
        unit, _ = norm_parts(rows)
        n_ref[at, :] = (unit * vec_ref[0:1] + vec_ref[1:2]).astype(LOW)


def put_back(rows, back_ref, target, image):
    grid = dot_nn(back_ref[...], rows.astype(LOW)).astype(LOW)
    for r in range(GRID):
        target[image, 0, r] = grid[16 * r : 16 * r + GRID]


def spread_keys(part, heads_ref):
    wide = jnp.concatenate([part[:WIN], part[WIN:]], axis=1)
    return jnp.concatenate([wide] * GROUP, axis=0) * heads_ref[...]


def spread_rows(part):
    zero = jnp.zeros((WIN, LANES), part.dtype)
    top = jnp.concatenate([part[:WIN], zero], axis=1)
    return jnp.concatenate([top, jnp.concatenate([zero, part[WIN:]], axis=1)], axis=0)


def own_rows(product):
    return jnp.concatenate([product[:WIN, :LANES], product[WIN:, LANES:]], axis=0)


def own_keys(product, heads_ref):
    kept = product * heads_ref[...].astype(F32)
    total = kept[:WIN]
    for h in range(1, GROUP):
        total = total + kept[h * WIN : (h + 1) * WIN]
    return jnp.concatenate([total[:, :LANES], total[:, LANES:]], axis=0)


def attend_body(
    direct, table_ref, n_ref, vec_ref, bias_ref, reach_ref, place_ref, heads_ref, *refs,
):
    near_refs, (packed_ref, soft_ref, attn_ref, wq_ref, wp_ref, parts) = refs[:PIECES], refs[PIECES:]
    for j in range(BLOCKS):
        at = table_ref[ME] ^ block_at(j) if direct else (j % 8) * 4 + j // 8
        row = at // 4 * PIECE if not direct else pl.multiple_of((at >> 2) * PIECE, PIECE)
        parts[at & 3, pl.ds(row, PIECE), :] = near_refs[j // 4][j % 4]
    for w in range(3):
        wq_ref[:, w * C : (w + 1) * C] = jnp.concatenate([parts[h, :, w * 96 : (w + 1) * 96] for h in range(4)], axis=1)
    wp_ref[...] = jnp.concatenate([parts[h, :, 288:] for h in range(4)], axis=1)

    @pl.loop(0, MICRO)
    def _(image):
        at_image = image_rows(image)
        made = dot_nn(n_ref[at_image, :], wq_ref[...])
        packed_ref[at_image, :C] = (made[:, :C] + vec_ref[2:3]).astype(LOW)
        packed_ref[at_image, C : 2 * C] = made[:, C : 2 * C].astype(LOW)
        packed_ref[at_image, 2 * C :] = (made[:, 2 * C :] + vec_ref[3:4]).astype(LOW)
        mask = row_mask(place_ref, table_ref, image)
        high = table_ref[EXTENT + 2 * image].astype(F32)
        wide = table_ref[EXTENT + 2 * image + 1].astype(F32)
        for pair in range(2):
            rows = slice(pair * 2 * WIN, (pair + 1) * 2 * WIN)
            at_pair = pl.ds(pl.multiple_of(image * IMG + pair * 2 * WIN, 2 * WIN), 2 * WIN)
            allowed = (reach_ref[pair, 0] < high) & (reach_ref[pair, 1] < wide)
            for g in range(GROUPS):
                at = g * LANES
                queries = packed_ref[at_pair, at : at + LANES]
                keys = packed_ref[at_pair, C + at : C + at + LANES]
                values = packed_ref[at_pair, 2 * C + at : 2 * C + at + LANES]
                raw = dot_nt(spread_keys(keys, heads_ref), spread_rows(queries))
                raw = (raw * HD ** (-0.5) + bias_ref[g]).reshape(GROUP, WIN, 128)
                scores = jnp.where(allowed[None], raw, NEG_FILL)
                exponent = jnp.exp(scores - jnp.max(scores, axis=1, keepdims=True))
                soft = exponent * (1.0 / jnp.sum(exponent, axis=1, keepdims=True))
                soft = soft.reshape(GROUP * WIN, 128)
                soft_ref[image, pair * GROUPS + g] = soft
                result = own_rows(dot_tn(soft.astype(LOW), spread_keys(values, heads_ref)))
                attn_ref[at_pair, at : at + LANES] = (result * mask[rows]).astype(LOW)


def middle_body(attn_ref, x_ref, wp_ref, vec_ref, middle_ref, n_ref):
    @pl.loop(0, MICRO)
    def _(image):
        at = image_rows(image)
        middle = x_ref[at, :].astype(F32) + dot_nt(attn_ref[at, :], wp_ref[...]) + vec_ref[4:5]
        middle_ref[at, :] = middle
        unit, _ = norm_parts(middle)
        n_ref[at, :] = (unit * vec_ref[5:6] + vec_ref[6:7]).astype(LOW)


def mlp_body(
    direct, table_ref, middle_ref, n_ref, g_ref, vec_ref, *refs,
):
    far_refs, (hidden_ref, grad_hidden_ref, grad_ref, sums_ref, w2_ref, w1, bias) = refs[:PIECES], refs[PIECES:]
    for j in range(BLOCKS):
        at = table_ref[ME] ^ block_at(j) if direct else (j % 8) * 4 + j // 8
        row = at // 4 * PIECE if not direct else pl.multiple_of((at >> 2) * PIECE, PIECE)
        col = at % 4 * C if not direct else pl.multiple_of((at & 3) * C, C)
        w1[pl.ds(row, PIECE), pl.ds(col, C)] = far_refs[j // 4][j % 4, :PIECE]
        w2_ref[pl.ds(row, PIECE), pl.ds(col, C)] = far_refs[j // 4][j % 4, PIECE:]
    for r in range(4):
        bias[:, r * C : (r + 1) * C] = vec_ref[8 + r : 9 + r]
    sums_ref[...] = jnp.zeros_like(sums_ref)

    @pl.loop(0, MICRO)
    def _(image):
        at = image_rows(image)
        unit, inverse = norm_parts(middle_ref[at, :])
        normed = n_ref[at, :]
        g_low = g_ref[at, :]
        g = g_low.astype(F32)
        for part in range(4):
            cols = slice(part * C, (part + 1) * C)
            pre_act = dot_nn(normed, w1[:, cols]) + bias[:, cols]
            grad_post = dot_nn(g_low, w2_ref[:, cols])
            below, density = gelu_parts(pre_act)
            hidden_ref[at, cols] = (pre_act * below).astype(LOW)
            grad_pre = grad_post * (below + pre_act * density)
            grad_hidden_ref[at, cols] = grad_pre.astype(LOW)
            sums_ref[8 + part : 9 + part] += jnp.sum(grad_pre, axis=0, keepdims=True)
        back = dot_nt(grad_hidden_ref[at, :], w1[...])
        sums_ref[5:6] += jnp.sum(back * unit, axis=0, keepdims=True)
        sums_ref[6:7] += jnp.sum(back, axis=0, keepdims=True)
        grad_middle = g + norm_back(back, unit, inverse, vec_ref[5:6])
        grad_ref[at, :] = grad_middle
        sums_ref[4:5] += jnp.sum(grad_middle, axis=0, keepdims=True)
        sums_ref[7:8] += jnp.sum(g, axis=0, keepdims=True)


def place_of(direct, table_ref, t, h):
    if not direct:
        return h * 8 + t
    return table_ref[SLOT] ^ swap_bits(4 * t) ^ ((h & 1) * 16 + (h >> 1) * 4)


def mlp_weights_body(direct, table_ref, n_ref, g_ref, hidden_ref, grad_hidden_ref, keep_ref, send_ref, n_turned, g_turned, made):
    n_turned[...] = n_ref[...].T
    g_turned[...] = g_ref[...].T
    for part in range(4):
        cols = slice(part * C, (part + 1) * C)
        first = dot_nn(n_turned[...], grad_hidden_ref[:, cols]).astype(LOW)
        second = dot_nn(g_turned[...], hidden_ref[:, cols]).astype(LOW)
        for t in range(8):
            at = place_of(direct, table_ref, t, part)
            made[at, :PIECE] = first[t * PIECE : (t + 1) * PIECE]
            made[at, PIECE:] = second[t * PIECE : (t + 1) * PIECE]
    keep_ref[...] = made[: BLOCKS // 2]
    send_ref[...] = made[BLOCKS // 2 :]


def output_body(hidden_ref, w2_ref, middle_ref, vec_ref, back_ref, out_ref):
    @pl.loop(0, MICRO)
    def _(image):
        at = image_rows(image)
        put_back(middle_ref[at, :] + dot_nt(hidden_ref[at, :], w2_ref[...]) + vec_ref[7:8], back_ref, out_ref, image)


def attend_back_body(
    table_ref, grad_ref, packed_ref, soft_ref, wp_ref, place_ref, heads_ref,
    packed_grad_ref, grad_low_ref, bias_sum_ref, sums_ref,
):
    bias_sum_ref[...] = jnp.zeros_like(bias_sum_ref)
    sums_ref[...] = jnp.zeros_like(sums_ref)

    @pl.loop(0, MICRO)
    def _(image):
        at_image = image_rows(image)
        grad_low = grad_ref[at_image, :].astype(LOW)
        grad_low_ref[at_image, :] = grad_low
        mask = row_mask(place_ref, table_ref, image)
        grad_attn = dot_nn(grad_low, wp_ref[...])
        grad_attn = (grad_attn * jnp.concatenate([mask] * 3, axis=1)).astype(LOW)
        for pair in range(2):
            rows = slice(pair * 2 * WIN, (pair + 1) * 2 * WIN)
            at_pair = pl.ds(pl.multiple_of(image * IMG + pair * 2 * WIN, 2 * WIN), 2 * WIN)
            for g in range(GROUPS):
                at = g * LANES
                queries = packed_ref[at_pair, at : at + LANES]
                keys = packed_ref[at_pair, C + at : C + at + LANES]
                values = packed_ref[at_pair, 2 * C + at : 2 * C + at + LANES]
                incoming = spread_rows(grad_attn[rows, at : at + LANES])
                soft = soft_ref[image, pair * GROUPS + g]
                grad_soft = dot_nt(spread_keys(values, heads_ref), incoming)
                joint = (soft * grad_soft).reshape(GROUP, WIN, 128)
                inner = jnp.sum(joint, axis=1, keepdims=True)
                grad_scores = (joint - soft.reshape(GROUP, WIN, 128) * inner).reshape(GROUP * WIN, 128)
                grad_low_scores = grad_scores.astype(LOW)
                bias_sum_ref[g] += grad_low_scores.astype(F32)
                grad_values = own_keys(dot_nn(soft.astype(LOW), incoming), heads_ref)
                grad_keys = own_keys(dot_nn(grad_low_scores, spread_rows(queries)), heads_ref)
                grad_queries = own_rows(dot_tn(grad_low_scores, spread_keys(keys, heads_ref)))
                packed_grad_ref[at_pair, at : at + LANES] = (grad_queries * HD ** (-0.5)).astype(LOW)
                packed_grad_ref[at_pair, C + at : C + at + LANES] = (grad_keys * HD ** (-0.5)).astype(LOW)
                packed_grad_ref[at_pair, 2 * C + at : 2 * C + at + LANES] = grad_values.astype(LOW)
        sums_ref[0:1] += jnp.sum(packed_grad_ref[at_image, :C].astype(F32), axis=0, keepdims=True)
        sums_ref[1:2] += jnp.sum(packed_grad_ref[at_image, 2 * C :].astype(F32), axis=0, keepdims=True)


def attend_weights_body(direct, table_ref, n_ref, grad_low_ref, packed_grad_ref, attn_ref, keep_ref, send_ref, made):
    n_turned = n_ref[...].T
    parts = [dot_nn(n_turned, packed_grad_ref[:, w * C : (w + 1) * C]).astype(LOW) for w in range(3)]
    parts.append(dot_nn(grad_low_ref[...].T, attn_ref[...]).astype(LOW))
    for h in range(4):
        block = jnp.concatenate([part[:, h * 96 : (h + 1) * 96] for part in parts], axis=1)
        for t in range(8):
            made[place_of(direct, table_ref, t, h)] = block[t * PIECE : (t + 1) * PIECE]
    keep_ref[...] = made[: BLOCKS // 2]
    send_ref[...] = made[BLOCKS // 2 :]


def input_body(packed_grad_ref, wq_ref, x_ref, grad_ref, vec_ref, back_ref, out_ref, sums_ref):
    sums_ref[...] = jnp.zeros_like(sums_ref)

    @pl.loop(0, MICRO)
    def _(image):
        at = image_rows(image)
        back = dot_nt(packed_grad_ref[at, :], wq_ref[...])
        unit, inverse = norm_parts(x_ref[at, :].astype(F32))
        sums_ref[0:1] += jnp.sum(back * unit, axis=0, keepdims=True)
        sums_ref[1:2] += jnp.sum(back, axis=0, keepdims=True)
        put_back(grad_ref[at, :] + norm_back(back, unit, inverse, vec_ref[0:1]), back_ref, out_ref, image)


def adam_update(weight, first, second, gradient, rate, decay):
    first_new = BETA_ONE * first + (1.0 - BETA_ONE) * gradient
    second_new = BETA_TWO * second + (1.0 - BETA_TWO) * gradient * gradient
    first_hat = first_new / (1.0 - BETA_ONE**STEP)
    second_hat = second_new / (1.0 - BETA_TWO**STEP)
    weight_new = weight * (1.0 - rate * decay) - rate * first_hat / (jnp.sqrt(second_hat) + ADAM_EPS)
    return (weight_new, first_new, second_new)


def adam_body(near_ref, far_ref, spare_ref, *refs):
    olds, news = refs[:18], refs[18:]
    vec, table = spare_ref[0:12], spare_ref[12:24, :REL]
    total = spare_ref[24:25, 0:1]
    total = total + jnp.sum(jnp.sum(vec * vec, axis=1, keepdims=True), axis=0, keepdims=True)
    total = total + jnp.sum(jnp.sum(table * table, axis=1, keepdims=True), axis=0, keepdims=True)
    grad_norm = jnp.sqrt(total)
    factor = jnp.minimum(1.0, CLIP_NORM / (grad_norm + 1e-06))
    news[0][...] = grad_norm
    depth = far_ref.shape[0] // 2
    grads = [None, near_ref[:, 288:], far_ref[:depth], far_ref[depth:], vec, table]
    for index in range(6):
        weight, first, second = olds[index], olds[6 + index], olds[12 + index]
        rate, decay = (RATE_MATRIX, DECAY_MATRIX) if index < 4 else (RATE_VECTOR, 0.0)
        for w in range(3 if index == 0 else 1):
            pick = (w,) if index == 0 else (Ellipsis,)
            gradient = near_ref[:, w * 96 : (w + 1) * 96] if index == 0 else grads[index]
            made = adam_update(weight[pick], first[pick], second[pick], gradient * factor, rate, decay)
            for kind in range(3):
                news[1 + 3 * index + kind][pick] = made[kind]


def body(
    mesh_sizes, tokens_in, cotangent, route, extent, qkv_weight, proj_weight, fc1_weight, fc2_weight, vectors, rel_table,
    qkv_first, proj_first, fc1_first, fc2_first, vectors_first, table_first,
    qkv_second, proj_second, fc1_second, fc2_second, vectors_second, table_second,
):
    toks, heads = mesh_sizes
    devices = toks * heads
    direct = toks == 8 and heads == 4
    micro = tokens_in.shape[0]
    patches = micro * devices * GRID * GRID
    head_at = lax.axis_index("head")
    me = lax.axis_index("tok") * heads + head_at
    def tie(*arrays):
        return lax.optimization_barrier(arrays)

    def passed(rows, mask):
        return lax.ppermute(rows, BOTH, [(i, i ^ mask) for i in range(devices)])

    depth = fc1_weight.shape[0]
    near, far = pl.pallas_call(
        pack_body, out_shape=(sds((depth, C), LOW), sds((2 * depth, C), LOW)), compiler_params=whole(8), name="pack"
    )(*streamed(qkv_weight, proj_weight.T, fc1_weight, fc2_weight.T))

    def gather_plain(piece):
        spread = lax.all_gather(lax.all_gather(piece, "tok", axis=0), "head", axis=0)
        half = piece.shape[0] // depth
        spread = spread.reshape(heads, toks, half, depth, C).transpose(0, 2, 1, 3, 4)
        spread = spread.reshape(heads, half, 8, PIECE, C).transpose(0, 2, 1, 3, 4)
        spread = spread.reshape(BLOCKS, half * PIECE, C)
        return [spread[at : at + 4] for at in range(0, BLOCKS, 4)]

    def share_plain(keep, send):
        both = jnp.concatenate([keep, send], axis=0)
        half = both.shape[1] // PIECE
        both = both.reshape(heads, 8, half, PIECE, C).transpose(0, 2, 1, 3, 4)
        both = both.reshape(heads, half, toks, depth, C).transpose(0, 2, 1, 3, 4).reshape(devices, half * depth, C)
        both = lax.psum_scatter(both.astype(F32), "head", scatter_dimension=0, tiled=True)
        return lax.psum_scatter(both, "tok", scatter_dimension=0, tiled=True)[0]

    def join(*arrays):
        return jnp.concatenate(arrays, axis=0)

    def first_sum(keep, got):
        shape = (4,) + keep.shape[1:]
        stays, *goes = pl.pallas_call(
            first_sum_body, out_shape=[sds(shape, F32)] + [sds(shape, LOW)] * 3, compiler_params=whole(2), name="first_sum"
        )(keep, got)
        return stays, goes

    def plane_sum(stays, got):
        shape = (1,) + stays.shape[1:]
        rest, *goes = pl.pallas_call(
            plane_sum_body, out_shape=[sds(shape, F32)] + [sds(shape, LOW)] * 3, compiler_params=whole(2), name="plane_sum"
        )(stays, *got)
        return rest, goes

    def spread(rows, masks):
        return [passed(rows, mask) for mask in masks]

    def sent(parts, masks):
        return [passed(part, mask) for part, mask in zip(parts, masks)]

    def total_of(rows, masks):
        one, two, three = spread(rows, masks)
        return (rows + one) + (two + three)

    back = jnp.asarray(DEAL.T, LOW)
    deal = jnp.asarray(DEAL, LOW)
    place = jnp.asarray(PLACE)
    reach = jnp.asarray(REACH)
    heads_low = jnp.asarray(HEADS, LOW)
    x_rows, g_rows, n_rows = call(
        prep_body,
        [((ROWS, C), LOW)] * 3,
        (tokens_in, cotangent, deal, vectors),
        "prep",
        limit=4,
        scratch=[pltpu.VMEM((PAD, C), LOW)],
    )

    def product_of(values, lookup):
        first = lax.reduce_precision(values, 8, 7)
        second = lax.reduce_precision(values - first, 8, 7)
        parts = jnp.concatenate([first, second, values - first - second], axis=0).astype(LOW)
        made = jnp.dot(parts, jnp.asarray(lookup, LOW), preferred_element_type=F32).reshape(3, values.shape[0], -1)
        return made[0] + (made[1] + made[2])

    def make_bias(values):
        made = product_of(values.T, LOOKUP).reshape(GROUPS, GROUP * WIN, WIN)
        return jnp.concatenate([made, made], axis=2)

    if direct:
        near, extent, route, rel_bias = tie(near[None], extent, route, rel_table)
        near_got, far_got = spread(near, LINE), spread(far[None], LINE)
        near_all = join(near, *near_got)
        near_all, x_rows, g_rows, n_rows, rel_bias = tie(near_all, x_rows, g_rows, n_rows, rel_bias)
        near_all = [near_all] + spread(near_all, PLANE)
        table = jnp.concatenate(
            [
                jnp.stack([me, swap_bits(me)]).astype(jnp.int32),
                lax.dynamic_index_in_dim(extent, head_at, 1, False).reshape(-1),
                lax.dynamic_index_in_dim(route, head_at, 1, False).reshape(-1),
            ]
        )
        bias = make_bias(rel_bias)
        far_got[0], bias, table, *near_all = tie(far_got[0], bias, table, *near_all)
        far_all = join(far[None], *far_got)
        near_all = near_all + [passed(piece, CORE) for piece in near_all]
        far_got = [far_all] + spread(far_all, PLANE)
    else:
        table = jnp.concatenate(
            [
                jnp.stack([me, swap_bits(me)]).astype(jnp.int32),
                lax.dynamic_index_in_dim(extent, head_at, 1, False).reshape(-1),
                lax.dynamic_index_in_dim(route, head_at, 1, False).reshape(-1),
            ]
        )
        bias = make_bias(rel_table)
        near_all, far_all = gather_plain(near), gather_plain(far)

    packed, soft, attn, w_qkv, w_proj = call(
        functools.partial(attend_body, direct),
        [
            ((ROWS, 3 * C), LOW), ((MICRO, 2 * GROUPS, GROUP * WIN, 128), F32), ((ROWS, C), LOW), ((C, 3 * C), LOW), ((C, C), LOW),
        ],
        (table, n_rows, vectors, bias, reach, place, heads_low, *near_all),
        "attend",
        limit=8,
        scratch=[pltpu.VMEM((4, C, C), LOW)],
        flops=8e9,
        scalars=1,
    )

    if direct:
        attn, *far_got = tie(attn, *far_got)
        far_core = [passed(piece, CORE) for piece in far_got]

    middle, n_two = call(middle_body, [((ROWS, C), F32), ((ROWS, C), LOW)], (attn, x_rows, w_proj, vectors), "middle",
        limit=4)

    if direct:
        middle, *far_core = tie(middle, *far_core)
        far_all = far_got + far_core

    hidden, grad_hidden, grad_middle, sums_mlp, w_fc2 = call(
        functools.partial(mlp_body, direct),
        [((ROWS, FF), LOW), ((ROWS, FF), LOW), ((ROWS, C), F32), ((12, C), F32), ((C, FF), LOW)],
        (table, middle, n_two, g_rows, vectors, *far_all),
        "mlp",
        limit=8,
        scratch=[pltpu.VMEM((C, FF), LOW), pltpu.VMEM((1, FF), F32)],
        flops=10e9,
        scalars=1,
    )

    half = BLOCKS // 2
    far_keep, far_send = call(
        functools.partial(mlp_weights_body, direct),
        [((half, 2 * PIECE, C), LOW)] * 2,
        (table, n_two, g_rows, hidden, grad_hidden),
        "mlp_weights",
        limit=10,
        scratch=[pltpu.VMEM((C, ROWS), LOW), pltpu.VMEM((C, ROWS), LOW), pltpu.VMEM((BLOCKS, 2 * PIECE, C), LOW)],
        flops=4e9,
        scalars=1,
    )

    if direct:
        far_got = passed(far_send, CORE)

    (block_out,) = call(output_body, [(tokens_in.shape, LOW)], (hidden, w_fc2, middle, vectors, back), "output",
        limit=5, flops=2e9)

    if direct:
        block_out, far_got, grad_middle = tie(block_out, far_got, grad_middle)
        far_stays, far_goes = first_sum(far_keep, far_got)
        far_got = sent(far_goes, PLANE)

    packed_grad, grad_low, bias_sum, sums_attend = call(
        attend_back_body,
        [((ROWS, 3 * C), LOW), ((ROWS, C), LOW), ((GROUPS, GROUP * WIN, 128), F32), ((2, C), F32)],
        (table, grad_middle, packed, soft, w_proj, place, heads_low),
        "attend_back",
        limit=6,
        flops=8e9,
        scalars=1,
    )

    near_keep, near_send = call(
        functools.partial(attend_weights_body, direct),
        [((half, PIECE, C), LOW)] * 2,
        (table, n_rows, grad_low, packed_grad, attn),
        "attend_weights",
        limit=8,
        scratch=[pltpu.VMEM((BLOCKS, PIECE, C), LOW)],
        flops=2e9,
        scalars=1,
    )

    if direct:
        near_send, *far_got = tie(near_send, *far_got)
        near_got = passed(near_send, CORE)
        near_stays, near_goes = first_sum(near_keep, near_got)
        near_goes[0], packed_grad, bias_sum, *far_got = tie(near_goes[0], packed_grad, bias_sum, *far_got)
        near_got = sent(near_goes, PLANE)
        far_stays, far_goes = plane_sum(far_stays, far_got)
        far_got = sent(far_goes, LINE)

    grad_block, sums_input = call(
        input_body,
        [(tokens_in.shape, LOW), ((2, C), F32)],
        (packed_grad, w_qkv, x_rows, grad_middle, vectors, back),
        "input_grad",
        limit=5,
        flops=4e9,
    )

    vec_grad = jnp.concatenate([sums_input, sums_attend, sums_mlp[4:]], axis=0)
    bias_sum = (bias_sum[:, :, :WIN] + bias_sum[:, :, WIN:]).reshape(NH, WIN * WIN)
    table_grad = product_of(bias_sum, LOOKUP.T)
    if direct:
        grad_block, vec_grad, table_grad, *near_got = tie(grad_block, vec_grad, table_grad, *near_got)
        near_stays, near_goes = plane_sum(near_stays, near_got)
        near_got = sent(near_goes, LINE)
        near_grad, far_grad, spare = pl.pallas_call(
            functools.partial(finish_body, patches),
            out_shape=[sds((depth, C), F32), sds((2 * depth, C), F32), sds((32, C), F32)],
            compiler_params=whole(2),
            name="finish",
        )(near_stays, far_stays, vec_grad, table_grad, *near_got, *far_got)
        spare = spare + passed(spare, CORE)
        spare = total_of(spare, PLANE)
        spare = total_of(spare, LINE)
    else:
        near_grad, far_grad = share_plain(near_keep, near_send) / patches, share_plain(far_keep, far_send) / patches
        squares = jnp.sum(near_grad * near_grad) + jnp.sum(far_grad * far_grad)
        vec_grad, table_grad, squares = lax.psum((vec_grad, table_grad, squares), BOTH)
        table_grad = jnp.concatenate([table_grad, jnp.zeros((12, C - REL), F32)], axis=1)
        spare = jnp.concatenate([vec_grad / patches, table_grad / patches, jnp.broadcast_to(squares, (8, C))], axis=0)

    olds = (
        qkv_weight, proj_weight.T, fc1_weight, fc2_weight.T, vectors, rel_table.T,
        qkv_first, proj_first.T, fc1_first, fc2_first.T, vectors_first, table_first.T,
        qkv_second, proj_second.T, fc1_second, fc2_second.T, vectors_second, table_second.T,
    )
    shapes = [sds((1, 1), F32)] + [sds(olds[index].shape, F32) for index in range(6) for _ in range(3)]
    news = pl.pallas_call(
        adam_body,
        out_shape=shapes,
        compiler_params=whole(8),
        name="adam",
    )(near_grad, far_grad, spare, *olds)
    turned = [new.T if index // 3 in (1, 3, 5) else new for index, new in enumerate(news[1:])]
    return (block_out, grad_block, news[0][0, 0], *turned)


def solution(mesh):
    sizes = (mesh.shape["tok"], mesh.shape["head"])
    weights = (P(None, "tok", "head"), P("head", "tok"), P("tok", "head"), P("head", "tok"), P(), P())
    images = P(None, ("tok", "head"), None, None, None)
    return jax.shard_map(
        lambda *args: body(sizes, *args),
        mesh=mesh,
        in_specs=(images, images, P(None, "tok", None), P(None, "tok", None)) + weights * 3,
        out_specs=(images, images, P()) + tuple(spec for spec in weights for _ in range(3)),
        check_vma=False,
    )
```

time: 151 us -> 142 us (0.940)
  starting transfers between devices: 35.1 us -> 43.7 us
  matrix products: 7.76 us -> 0.79 us
  other arithmetic: 7.58 us -> 0.64 us
  waiting for transfers between devices: 22.6 us -> 16.9 us
  local copies, waits for them, and re-layouts: 8.55 us -> 13.1 us
    ppermute x29 -> x41, starting transfers between devices: 35.1 us -> 43.7 us  [passed(): return lax.ppermute(rows, BOTH, [(i, i ^ mask) for i in range(devices)])]
    dot_general x2, matrix products: 7.76 us -> 0.79 us  [product_of(): jnp.dot(parts, jnp.asarray(lookup, LOW), preferred_element_type=F32)]
    unnamed x89 -> x80, local copies, waits for them, and re-layouts: 5.83 us -> 11.8 us
    ppermute x29 -> x41, waiting for transfers between devices: 22.6 us -> 16.9 us  [passed(): return lax.ppermute(rows, BOTH, [(i, i ^ mask) for i in range(devices)])]
    add x11 -> x5, other arithmetic: 4.22 us -> 0.08 us  [the longest x2 0.05 us: product_of(): return made[0] + (made[1] + made[2])]
    concatenate x6 -> x2, other arithmetic: 1.66 us -> 0.08 us  [join(): return jnp.concatenate(arrays, axis=0)]
    pallas_call x10 -> x15, Pallas kernels: 64.4 us -> 63.8 us  [the longest x9 61.8 us: call(): pl.pallas_call(body, in_specs=[SCALARS] * scalars + [HELD] * (len(inputs)...]
  transfers between devices with their start and end apart: 29 -> 41, of which waited for: 14 -> 12; matrix products, arithmetic and copies ran while one was open for 10% -> 2% of each run, Pallas kernels for 28% -> 30%
where the time goes in v4:
time: 142 us
  Pallas kernels  64.9 us (46%)
  starting transfers between devices  43.7 us (31%)
  waiting for transfers between devices  16.9 us (12%)
  local copies, waits for them, and re-layouts  13.1 us (9%)
  between operations  1.55 us (1%)
    pallas_call x9, Pallas kernels, call(): pl.pallas_call(body, in_specs=[SCALARS] * scalars + [HELD] * (len(inputs)...  61.8 us
    ppermute x41, starting transfers between devices, passed(): return lax.ppermute(rows, BOTH, [(i, i ^ mask) for i in range(devices)])  43.7 us
    ppermute x41, waiting for transfers between devices, passed(): return lax.ppermute(rows, BOTH, [(i, i ^ mask) for i in range(devices)])  16.9 us
    unnamed x80, local copies, waits for them, and re-layouts  11.8 us
  transfers between devices with their start and end apart: 41, of which 12 were waited for; matrix products, arithmetic and copies ran while one was open for 2% of the time, Pallas kernels for 30%

profile of v4, /device:TPU:0, one launch (start us, length us, event | category | flops | bytes accessed | tf_op | source)
XLA Modules:
  0.0 141.6 jit_solution(10399081723942051536)
XLA Ops:
  1.7 5.1 %collective-permute-start.3 = (bf16[1,48,384]{2,1,0:T(8,128)(2,1)S(1)}, bf16[1,48,384]{2,1,0:T(8,128)(2,1)S(1)}, u32[]{:S(2)}, u32[]{:S(2)}) collective-permute-start(bf16[1,48,384]{2,1,0:T(8,128)(2,1)S(1)} %bitcast.47), channel_id=1, source_target_pairs={{0,24},{1,25},{2,26},{3,27},{4,28},{5,29},{6,30},{7,31},{8,16},{9,... | collective-permute-start | bytes 110600 | tf_op jit(solution)/shard_map/ppermute | solution.py:502
  7.5 3.7 %collective-permute-start.12 = (bf16[1,96,384]{2,1,0:T(8,128)(2,1)S(1)}, bf16[1,96,384]{2,1,0:T(8,128)(2,1)S(1)}, u32[]{:S(2)}, u32[]{:S(2)}) collective-permute-start(bf16[1,96,384]{2,1,0:T(8,128)(2,1)S(1)} %bitcast.42), channel_id=1, source_target_pairs={{0,24},{1,25},{2,26},{3,27},{4,28},{5,29},{6,30},{7,31},{8,16},{9,... | collective-permute-start | bytes 221192 | tf_op jit(solution)/shard_map/ppermute | solution.py:502
  16.3 2.5 %prep.1 = (bf16[1280,384]{1,0:T(8,128)(2,1)S(1)}, bf16[1280,384]{1,0:T(8,128)(2,1)S(1)}, bf16[1280,384]{1,0:T(8,128)(2,1)S(1)}) custom-call(bf16[5,1,14,14,384]{4,3,2,1,0:T(8,128)(2,1)S(1)} %copy-done.21, bf16[5,1,14,14,384]{4,3,2,1,0:T(8,128)(2,1)S(1)} %copy-done.22, bf16[256,224]{1,0:T(8,128)(2,1)S(1)} %copy-done.26, f32[12,384]{1,0:T(8,128)S(1)} %copy-done.6), custom_call_target="tpu_custom_call" | custom-call | flops 1000000000 | bytes 4000000 | tf_op jit(solution)/shard_map/prep/pallas_call | solution.py:148
  20.8 2.5 %collective-permute-start.6 = (bf16[4,48,384]{2,1,0:T(8,128)(2,1)S(1)}, bf16[4,48,384]{2,1,0:T(8,128)(2,1)S(1)}, u32[]{:S(2)}, u32[]{:S(2)}) collective-permute-start(bf16[4,48,384]{2,1,0:T(8,128)(2,1)S(1)} %pad_maximum_fusion.4.refs_0_), channel_id=1, source_target_pairs={{0,6},{1,7},{2,4},{3,5},{4,2},{5,3},{6,0},{7,1},{8,14},{9,15},{10,... | collective-permute-start | bytes 442376 | tf_op jit(solution)/shard_map/ppermute | solution.py:502
  25.9 2.0 %collective-permute-done.6.refs_3_ = bf16[4,48,384]{2,1,0:T(8,128)(2,1)S(1)} collective-permute-done((bf16[4,48,384]{2,1,0:T(8,128)(2,1)S(1)}, bf16[4,48,384]{2,1,0:T(8,128)(2,1)S(1)}, u32[]{:S(2)}, u32[]{:S(2)}) %collective-permute-start.6) | collective-permute-done | bytes 147488 | tf_op jit(solution)/shard_map/ppermute | solution.py:502
  30.5 2.4 %collective-permute-start.15 = (bf16[4,96,384]{2,1,0:T(8,128)(2,1)S(1)}, bf16[4,96,384]{2,1,0:T(8,128)(2,1)S(1)}, u32[]{:S(2)}, u32[]{:S(2)}) collective-permute-start(bf16[4,96,384]{2,1,0:T(8,128)(2,1)S(1)} %pad_maximum_fusion.3.refs_0_), channel_id=1, source_target_pairs={{0,6},{1,7},{2,4},{3,5},{4,2},{5,3},{6,0},{7,1},{8,14},{9,15},{10,... | collective-permute-start | bytes 884744 | tf_op jit(solution)/shard_map/ppermute | solution.py:502
  35.3 12.8 %attend.1 = (bf16[1280,1152]{1,0:T(8,128)(2,1)S(1)}, f32[5,6,256,128]{3,2,1,0:T(8,128)S(1)}, bf16[1280,384]{1,0:T(8,128)(2,1)S(1)}, bf16[384,1152]{1,0:T(8,128)(2,1)S(1)}, bf16[384,384]{1,0:T(8,128)(2,1)S(1)}) custom-call(s32[32]{0:T(128)S(1)} %pad_add_fusion.table_ref, bf16[1280,384]{1,0:T(8,128)(2,1)S(1)} %copy-done.30, f32[12,384]{1,0:T(8,128)S(1)} %copy-done.7, ...), custom_call_target="tpu_custom_call" | custom-call | flops 8000000000 | bytes 4000000 | tf_op jit(solution)/shard_map/attend/pallas_call | solution.py:148
  49.3 2.5 %middle.1 = (f32[1280,384]{1,0:T(8,128)S(1)}, bf16[1280,384]{1,0:T(8,128)(2,1)S(1)}) custom-call(bf16[1280,384]{1,0:T(8,128)(2,1)S(1)} %get-tuple-element.151.attn_ref, bf16[1280,384]{1,0:T(8,128)(2,1)S(1)} %get-tuple-element.152.x_ref, bf16[384,384]{1,0:T(8,128)(2,1)S(1)} %get-tuple-element.153.wp_ref, f32[12,384]{1,0:T(8,128)S(1)} %copy-done.7), custom_call_target="tpu_custom_call" | custom-call | flops 1000000000 | bytes 4000000 | tf_op jit(solution)/shard_map/middle/pallas_call | solution.py:148
  51.8 14.3 %mlp.1 = (bf16[1280,1536]{1,0:T(8,128)(2,1)S(1)}, bf16[1280,1536]{1,0:T(8,128)(2,1)S(1)}, f32[1280,384]{1,0:T(8,128)S(1)}, f32[12,384]{1,0:T(8,128)S(1)}, bf16[384,1536]{1,0:T(8,128)(2,1)S(1)}) custom-call(s32[32]{0:T(128)S(1)} %pad_add_fusion.table_ref, f32[1280,384]{1,0:T(8,128)S(1)} %get-tuple-element.159.middle_ref, ...), custom_call_target="tpu_custom_call" | custom-call | flops 10000000000 | bytes 4000000 | tf_op jit(solution)/shard_map/mlp/pallas_call | solution.py:148
  66.1 5.1 %mlp_weights.1 = (bf16[16,96,384]{2,1,0:T(8,128)(2,1)S(1)}, bf16[16,96,384]{2,1,0:T(8,128)(2,1)S(1)}) custom-call(s32[32]{0:T(128)S(1)} %pad_add_fusion.table_ref, bf16[1280,384]{1,0:T(8,128)(2,1)S(1)} %get-tuple-element.160.n_ref, bf16[1280,384]{1,0:T(8,128)(2,1)S(1)} %copy-done.33, bf16[1280,1536]{1,0:T(8,128)(2,1)S(1)} %get-tuple-element.166.hidden_ref, ...), custom_call_target="tpu_custom_call" | custom-call | flops 4000000000 | bytes 4000000 | tf_op jit(solution)/shard_map/mlp_weights/pallas_call | solution.py:148
  71.3 4.9 %output.1 = bf16[5,1,14,14,384]{4,3,2,1,0:T(8,128)(2,1)} custom-call(bf16[1280,1536]{1,0:T(8,128)(2,1)S(1)} %get-tuple-element.166.hidden_ref, bf16[384,1536]{1,0:T(8,128)(2,1)S(1)} %get-tuple-element.167.w2_ref, f32[1280,384]{1,0:T(8,128)S(1)} %get-tuple-element.159.middle_ref, f32[12,384]{1,0:T(8,128)S(1)} %copy-done.7, bf16[224,256]{1,0:T(8,128)(2,1)S(1)} %copy-done.4), custom_call_target="tpu_custom_call" | custom-call | flops 2000000000 | bytes 4000000 | tf_op jit(solution)/shard_map/output/pallas_call | solution.py:148
  80.0 11.1 %attend_back.1 = (bf16[1280,1152]{1,0:T(8,128)(2,1)S(1)}, bf16[1280,384]{1,0:T(8,128)(2,1)S(1)}, f32[3,256,128]{2,1,0:T(8,128)S(1)}, f32[2,384]{1,0:T(2,128)S(1)}) custom-call(s32[32]{0:T(128)S(1)} %pad_add_fusion.table_ref, f32[1280,384]{1,0:T(8,128)S(1)} %get-tuple-element.172.grad_ref, bf16[1280,1152]{1,0:T(8,128)(2,1)S(1)} %get-tuple-element.173.packed_ref, ...), custom_call_target="tpu_custom_call" | custom-call | flops 8000000000 | bytes 4000000 | tf_op jit(solution)/shard_map/attend_back/pallas_call | solution.py:148
  91.2 3.1 %attend_weights.1 = (bf16[16,48,384]{2,1,0:T(8,128)(2,1)S(1)}, bf16[16,48,384]{2,1,0:T(8,128)(2,1)S(1)}) custom-call(s32[32]{0:T(128)S(1)} %pad_add_fusion.table_ref, bf16[1280,384]{1,0:T(8,128)(2,1)S(1)} %copy-done.31, bf16[1280,384]{1,0:T(8,128)(2,1)S(1)} %get-tuple-element.175.grad_low_ref, bf16[1280,1152]{1,0:T(8,128)(2,1)S(1)} %get-tuple-element.190.packed_grad_ref, ...), custom_call_target="tpu_custom_call" | custom-call | flops 2000000000 | bytes 4000000 | tf_op jit(solution)/shard_map/attend_weights/pallas_call | solution.py:148
  94.4 2.0 %collective-permute-done.24.got_ref = bf16[16,48,384]{2,1,0:T(8,128)(2,1)S(1)} collective-permute-done((bf16[16,48,384]{2,1,0:T(8,128)(2,1)S(1)}, bf16[16,48,384]{2,1,0:T(8,128)(2,1)S(1)}, u32[]{:S(2)}, u32[]{:S(2)}) %collective-permute-start.24) | collective-permute-done | bytes 589856 | tf_op jit(solution)/shard_map/ppermute | solution.py:502
  96.7 2.7 %collective-permute-start.31 = (bf16[1,96,384]{2,1,0:T(8,128)(2,1)S(1)}, bf16[1,96,384]{2,1,0:T(8,128)(2,1)S(1)}, u32[]{:S(2)}, u32[]{:S(2)}) collective-permute-start(bf16[1,96,384]{2,1,0:T(8,128)(2,1)S(1)} %get-tuple-element.216), channel_id=1, source_target_pairs={{0,16},{1,17},{2,18},{3,19},{4,20},{5,21},{6,22},{7,23},{8,24},{9,... | collective-permute-start | bytes 221192 | tf_op jit(solution)/shard_map/ppermute | solution.py:502
  103.3 1.8 %copy-done.28 = bf16[1280,1152]{1,0:T(8,128)(2,1)S(1)} copy-done((bf16[1280,1152]{1,0:T(8,128)(2,1)S(1)}, bf16[1280,1152]{1,0:T(8,128)(2,1)}, u32[]{:S(2)}) %copy-start.28) | copy-done | bytes 2949144
  107.8 5.6 %input_grad.1 = (bf16[5,1,14,14,384]{4,3,2,1,0:T(8,128)(2,1)}, f32[2,384]{1,0:T(2,128)S(1)}) custom-call(bf16[1280,1152]{1,0:T(8,128)(2,1)S(1)} %copy-done.28, bf16[384,1152]{1,0:T(8,128)(2,1)S(1)} %copy-done.37, bf16[1280,384]{1,0:T(8,128)(2,1)S(1)} %get-tuple-element.152.x_ref, f32[1280,384]{1,0:T(8,128)S(1)} %copy-done.35, f32[12,384]{1,0:T(8,128)S(1)} %copy-done.7, ...), custom_call_target="tpu_custom_call" | custom-call | flops 4000000000 | bytes 4000000 | tf_op jit(solution)/shard_map/input_grad/pallas_call | solution.py:148
  114.1 1.8 %collective-permute-start.33 = (bf16[1,96,384]{2,1,0:T(8,128)(2,1)S(1)}, bf16[1,96,384]{2,1,0:T(8,128)(2,1)S(1)}, u32[]{:S(2)}, u32[]{:S(2)}) collective-permute-start(bf16[1,96,384]{2,1,0:T(8,128)(2,1)S(1)} %get-tuple-element.218), channel_id=1, source_target_pairs={{0,24},{1,25},{2,26},{3,27},{4,28},{5,29},{6,30},{7,31},{8,16},{9,... | collective-permute-start | bytes 221192 | tf_op jit(solution)/shard_map/ppermute | solution.py:502
  116.0 1.8 %collective-permute-start.28 = (bf16[1,48,384]{2,1,0:T(8,128)(2,1)S(1)}, bf16[1,48,384]{2,1,0:T(8,128)(2,1)S(1)}, u32[]{:S(2)}, u32[]{:S(2)}) collective-permute-start(bf16[1,48,384]{2,1,0:T(8,128)(2,1)S(1)} %get-tuple-element.213), channel_id=1, source_target_pairs={{0,16},{1,17},{2,18},{3,19},{4,20},{5,21},{6,22},{7,23},{8,24},{9,... | collective-permute-start | bytes 110600 | tf_op jit(solution)/shard_map/ppermute | solution.py:502
  120.5 1.9 %collective-permute-done.28.refs_0_ = bf16[1,48,384]{2,1,0:T(8,128)(2,1)S(1)} collective-permute-done((bf16[1,48,384]{2,1,0:T(8,128)(2,1)S(1)}, bf16[1,48,384]{2,1,0:T(8,128)(2,1)S(1)}, u32[]{:S(2)}, u32[]{:S(2)}) %collective-permute-start.28) | collective-permute-done | bytes 36896 | tf_op jit(solution)/shard_map/ppermute | solution.py:502
  122.5 2.0 %collective-permute-done.30.refs_2_ = bf16[1,48,384]{2,1,0:T(8,128)(2,1)S(1)} collective-permute-done((bf16[1,48,384]{2,1,0:T(8,128)(2,1)S(1)}, bf16[1,48,384]{2,1,0:T(8,128)(2,1)S(1)}, u32[]{:S(2)}, u32[]{:S(2)}) %collective-permute-start.30) | collective-permute-done | bytes 36896 | tf_op jit(solution)/shard_map/ppermute | solution.py:502
  125.9 2.5 %collective-permute-start.37 = (f32[32,384]{1,0:T(8,128)S(1)}, f32[32,384]{1,0:T(8,128)S(1)}, u32[]{:S(2)}, u32[]{:S(2)}) collective-permute-start(f32[32,384]{1,0:T(8,128)S(1)} %add.80), channel_id=1, source_target_pairs={{0,6},{1,7},{2,4},{3,5},{4,2},{5,3},{6,0},{7,1},{8,14},{9,15},{10,... | collective-permute-start | bytes 147464 | tf_op jit(solution)/shard_map/ppermute | solution.py:502
  133.0 1.8 %collective-permute-start.40 = (f32[32,384]{1,0:T(8,128)S(1)}, f32[32,384]{1,0:T(8,128)S(1)}, u32[]{:S(2)}, u32[]{:S(2)}) collective-permute-start(f32[32,384]{1,0:T(8,128)S(1)} %add_add_fusion.1), channel_id=1, source_target_pairs={{0,24},{1,25},{2,26},{3,27},{4,28},{5,29},{6,30},{7,31},{8,16},{9,... | collective-permute-start | bytes 147464 | tf_op jit(solution)/shard_map/ppermute | solution.py:502
  134.8 2.6 %collective-permute-start.38 = (f32[32,384]{1,0:T(8,128)S(1)}, f32[32,384]{1,0:T(8,128)S(1)}, u32[]{:S(2)}, u32[]{:S(2)}) collective-permute-start(f32[32,384]{1,0:T(8,128)S(1)} %add_add_fusion.1), channel_id=1, source_target_pairs={{0,16},{1,17},{2,18},{3,19},{4,20},{5,21},{6,22},{7,23},{8,24},{9,... | collective-permute-start | bytes 147464 | tf_op jit(solution)/shard_map/ppermute | solution.py:502
  (178 shorter events, 41.5 us)
Async XLA Ops:
  1.7 19.0 %collective-permute-start.3 = (bf16[1,48,384]{2,1,0:T(8,128)(2,1)S(1)}, bf16[1,48,384]{2,1,0:T(8,128)(2,1)S(1)}, u32[]{:S(2)}, u32[]{:S(2)}) collective-permute-start(bf16[1,48,384]{2,1,0:T(8,128)(2,1)S(1)} %bitcast.47), channel_id=1, source_target_pairs={{0,24},{1,25},{2,26},{3,27},{4,28},{5,29},{6,30},{7,31},{8,16},{9,... | collective-permute-start | bytes 110600 | tf_op jit(solution)/shard_map/ppermute | solution.py:502
  6.9 13.9 %collective-permute-start.2 = (bf16[1,48,384]{2,1,0:T(8,128)(2,1)S(1)}, bf16[1,48,384]{2,1,0:T(8,128)(2,1)S(1)}, u32[]{:S(2)}, u32[]{:S(2)}) collective-permute-start(bf16[1,48,384]{2,1,0:T(8,128)(2,1)S(1)} %bitcast.48), channel_id=1, source_target_pairs={{0,8},{1,9},{2,10},{3,11},{4,12},{5,13},{6,14},{7,15},{8,0},{9,1},... | collective-permute-start | bytes 110600 | tf_op jit(solution)/shard_map/ppermute | solution.py:502
  6.9 13.9 %collective-permute-start.1 = (bf16[1,48,384]{2,1,0:T(8,128)(2,1)S(1)}, bf16[1,48,384]{2,1,0:T(8,128)(2,1)S(1)}, u32[]{:S(2)}, u32[]{:S(2)}) collective-permute-start(bf16[1,48,384]{2,1,0:T(8,128)(2,1)S(1)} %bitcast.49), channel_id=1, source_target_pairs={{0,16},{1,17},{2,18},{3,19},{4,20},{5,21},{6,22},{7,23},{8,24},{9,... | collective-permute-start | bytes 110600 | tf_op jit(solution)/shard_map/ppermute | solution.py:502
  7.5 22.4 %collective-permute-start.12 = (bf16[1,96,384]{2,1,0:T(8,128)(2,1)S(1)}, bf16[1,96,384]{2,1,0:T(8,128)(2,1)S(1)}, u32[]{:S(2)}, u32[]{:S(2)}) collective-permute-start(bf16[1,96,384]{2,1,0:T(8,128)(2,1)S(1)} %bitcast.42), channel_id=1, source_target_pairs={{0,24},{1,25},{2,26},{3,27},{4,28},{5,29},{6,30},{7,31},{8,16},{9,... | collective-permute-start | bytes 221192 | tf_op jit(solution)/shard_map/ppermute | solution.py:502
  11.2 13.7 %collective-permute-start = (bf16[1,96,384]{2,1,0:T(8,128)(2,1)S(1)}, bf16[1,96,384]{2,1,0:T(8,128)(2,1)S(1)}, u32[]{:S(2)}, u32[]{:S(2)}) collective-permute-start(bf16[1,96,384]{2,1,0:T(8,128)(2,1)S(1)} %bitcast.43), channel_id=1, source_target_pairs={{0,16},{1,17},{2,18},{3,19},{4,20},{5,21},{6,22},{7,23},{8,24},{9,... | collective-permute-start | bytes 221192 | tf_op jit(solution)/shard_map/ppermute | solution.py:502
  20.8 7.1 %collective-permute-start.6 = (bf16[4,48,384]{2,1,0:T(8,128)(2,1)S(1)}, bf16[4,48,384]{2,1,0:T(8,128)(2,1)S(1)}, u32[]{:S(2)}, u32[]{:S(2)}) collective-permute-start(bf16[4,48,384]{2,1,0:T(8,128)(2,1)S(1)} %pad_maximum_fusion.4.refs_0_), channel_id=1, source_target_pairs={{0,6},{1,7},{2,4},{3,5},{4,2},{5,3},{6,0},{7,1},{8,14},{9,15},{10,... | collective-permute-start | bytes 442376 | tf_op jit(solution)/shard_map/ppermute | solution.py:502
  23.3 6.1 %collective-permute-start.5 = (bf16[4,48,384]{2,1,0:T(8,128)(2,1)S(1)}, bf16[4,48,384]{2,1,0:T(8,128)(2,1)S(1)}, u32[]{:S(2)}, u32[]{:S(2)}) collective-permute-start(bf16[4,48,384]{2,1,0:T(8,128)(2,1)S(1)} %pad_maximum_fusion.4.refs_0_), channel_id=1, source_target_pairs={{0,4},{1,5},{2,6},{3,7},{4,0},{5,1},{6,2},{7,3},{8,12},{9,13},{10,... | collective-permute-start | bytes 442376 | tf_op jit(solution)/shard_map/ppermute | solution.py:502
  23.8 5.6 %collective-permute-start.4 = (bf16[4,48,384]{2,1,0:T(8,128)(2,1)S(1)}, bf16[4,48,384]{2,1,0:T(8,128)(2,1)S(1)}, u32[]{:S(2)}, u32[]{:S(2)}) collective-permute-start(bf16[4,48,384]{2,1,0:T(8,128)(2,1)S(1)} %pad_maximum_fusion.4.refs_0_), channel_id=1, source_target_pairs={{0,2},{1,3},{2,0},{3,1},{4,6},{5,7},{6,4},{7,5},{8,10},{9,11},{10,... | collective-permute-start | bytes 442376 | tf_op jit(solution)/shard_map/ppermute | solution.py:502
  25.0 5.5 %collective-permute-start.11 = (bf16[1,96,384]{2,1,0:T(8,128)(2,1)S(1)}, bf16[1,96,384]{2,1,0:T(8,128)(2,1)S(1)}, u32[]{:S(2)}, u32[]{:S(2)}) collective-permute-start(bf16[1,96,384]{2,1,0:T(8,128)(2,1)S(1)} %bitcast.44), channel_id=1, source_target_pairs={{0,8},{1,9},{2,10},{3,11},{4,12},{5,13},{6,14},{7,15},{8,0},{9,1},... | collective-permute-start | bytes 221192 | tf_op jit(solution)/shard_map/ppermute | solution.py:502
  30.5 17.6 %collective-permute-start.15 = (bf16[4,96,384]{2,1,0:T(8,128)(2,1)S(1)}, bf16[4,96,384]{2,1,0:T(8,128)(2,1)S(1)}, u32[]{:S(2)}, u32[]{:S(2)}) collective-permute-start(bf16[4,96,384]{2,1,0:T(8,128)(2,1)S(1)} %pad_maximum_fusion.3.refs_0_), channel_id=1, source_target_pairs={{0,6},{1,7},{2,4},{3,5},{4,2},{5,3},{6,0},{7,1},{8,14},{9,15},{10,... | collective-permute-start | bytes 884744 | tf_op jit(solution)/shard_map/ppermute | solution.py:502
  33.0 15.2 %collective-permute-start.14 = (bf16[4,96,384]{2,1,0:T(8,128)(2,1)S(1)}, bf16[4,96,384]{2,1,0:T(8,128)(2,1)S(1)}, u32[]{:S(2)}, u32[]{:S(2)}) collective-permute-start(bf16[4,96,384]{2,1,0:T(8,128)(2,1)S(1)} %pad_maximum_fusion.3.refs_0_), channel_id=1, source_target_pairs={{0,4},{1,5},{2,6},{3,7},{4,0},{5,1},{6,2},{7,3},{8,12},{9,13},{10,... | collective-permute-start | bytes 884744 | tf_op jit(solution)/shard_map/ppermute | solution.py:502
  33.5 14.7 %collective-permute-start.13 = (bf16[4,96,384]{2,1,0:T(8,128)(2,1)S(1)}, bf16[4,96,384]{2,1,0:T(8,128)(2,1)S(1)}, u32[]{:S(2)}, u32[]{:S(2)}) collective-permute-start(bf16[4,96,384]{2,1,0:T(8,128)(2,1)S(1)} %pad_maximum_fusion.3.refs_0_), channel_id=1, source_target_pairs={{0,2},{1,3},{2,0},{3,1},{4,6},{5,7},{6,4},{7,5},{8,10},{9,11},{10,... | collective-permute-start | bytes 884744 | tf_op jit(solution)/shard_map/ppermute | solution.py:502
  76.5 17.8 %collective-permute-start.21 = (bf16[4,96,384]{2,1,0:T(8,128)(2,1)S(1)}, bf16[4,96,384]{2,1,0:T(8,128)(2,1)S(1)}, u32[]{:S(2)}, u32[]{:S(2)}) collective-permute-start(bf16[4,96,384]{2,1,0:T(8,128)(2,1)S(1)} %get-tuple-element.181), channel_id=1, source_target_pairs={{0,2},{1,3},{2,0},{3,1},{4,6},{5,7},{6,4},{7,5},{8,10},{9,11},{10,... | collective-permute-start | bytes 884744 | tf_op jit(solution)/shard_map/ppermute | solution.py:502
  78.0 16.3 %collective-permute-start.22 = (bf16[4,96,384]{2,1,0:T(8,128)(2,1)S(1)}, bf16[4,96,384]{2,1,0:T(8,128)(2,1)S(1)}, u32[]{:S(2)}, u32[]{:S(2)}) collective-permute-start(bf16[4,96,384]{2,1,0:T(8,128)(2,1)S(1)} %get-tuple-element.182), channel_id=1, source_target_pairs={{0,4},{1,5},{2,6},{3,7},{4,0},{5,1},{6,2},{7,3},{8,12},{9,13},{10,... | collective-permute-start | bytes 884744 | tf_op jit(solution)/shard_map/ppermute | solution.py:502
  79.5 14.8 %collective-permute-start.23 = (bf16[4,96,384]{2,1,0:T(8,128)(2,1)S(1)}, bf16[4,96,384]{2,1,0:T(8,128)(2,1)S(1)}, u32[]{:S(2)}, u32[]{:S(2)}) collective-permute-start(bf16[4,96,384]{2,1,0:T(8,128)(2,1)S(1)} %get-tuple-element.183), channel_id=1, source_target_pairs={{0,6},{1,7},{2,4},{3,5},{4,2},{5,3},{6,0},{7,1},{8,14},{9,15},{10,... | collective-permute-start | bytes 884744 | tf_op jit(solution)/shard_map/ppermute | solution.py:502
  96.7 22.0 %collective-permute-start.31 = (bf16[1,96,384]{2,1,0:T(8,128)(2,1)S(1)}, bf16[1,96,384]{2,1,0:T(8,128)(2,1)S(1)}, u32[]{:S(2)}, u32[]{:S(2)}) collective-permute-start(bf16[1,96,384]{2,1,0:T(8,128)(2,1)S(1)} %get-tuple-element.216), channel_id=1, source_target_pairs={{0,16},{1,17},{2,18},{3,19},{4,20},{5,21},{6,22},{7,23},{8,24},{9,... | collective-permute-start | bytes 221192 | tf_op jit(solution)/shard_map/ppermute | solution.py:502
  99.4 21.0 %collective-permute-start.32 = (bf16[1,96,384]{2,1,0:T(8,128)(2,1)S(1)}, bf16[1,96,384]{2,1,0:T(8,128)(2,1)S(1)}, u32[]{:S(2)}, u32[]{:S(2)}) collective-permute-start(bf16[1,96,384]{2,1,0:T(8,128)(2,1)S(1)} %get-tuple-element.217), channel_id=1, source_target_pairs={{0,8},{1,9},{2,10},{3,11},{4,12},{5,13},{6,14},{7,15},{8,0},{9,1},... | collective-permute-start | bytes 221192 | tf_op jit(solution)/shard_map/ppermute | solution.py:502
  99.4 14.7 %collective-permute-start.25 = (bf16[4,48,384]{2,1,0:T(8,128)(2,1)S(1)}, bf16[4,48,384]{2,1,0:T(8,128)(2,1)S(1)}, u32[]{:S(2)}, u32[]{:S(2)}) collective-permute-start(bf16[4,48,384]{2,1,0:T(8,128)(2,1)S(1)} %get-tuple-element.197), channel_id=1, source_target_pairs={{0,2},{1,3},{2,0},{3,1},{4,6},{5,7},{6,4},{7,5},{8,10},{9,11},{10,... | collective-permute-start | bytes 442376 | tf_op jit(solution)/shard_map/ppermute | solution.py:502
  100.9 15.0 %collective-permute-start.26 = (bf16[4,48,384]{2,1,0:T(8,128)(2,1)S(1)}, bf16[4,48,384]{2,1,0:T(8,128)(2,1)S(1)}, u32[]{:S(2)}, u32[]{:S(2)}) collective-permute-start(bf16[4,48,384]{2,1,0:T(8,128)(2,1)S(1)} %get-tuple-element.198), channel_id=1, source_target_pairs={{0,4},{1,5},{2,6},{3,7},{4,0},{5,1},{6,2},{7,3},{8,12},{9,13},{10,... | collective-permute-start | bytes 442376 | tf_op jit(solution)/shard_map/ppermute | solution.py:502
  102.3 13.5 %collective-permute-start.27 = (bf16[4,48,384]{2,1,0:T(8,128)(2,1)S(1)}, bf16[4,48,384]{2,1,0:T(8,128)(2,1)S(1)}, u32[]{:S(2)}, u32[]{:S(2)}) collective-permute-start(bf16[4,48,384]{2,1,0:T(8,128)(2,1)S(1)} %get-tuple-element.199), channel_id=1, source_target_pairs={{0,6},{1,7},{2,4},{3,5},{4,2},{5,3},{6,0},{7,1},{8,14},{9,15},{10,... | collective-permute-start | bytes 442376 | tf_op jit(solution)/shard_map/ppermute | solution.py:502
  114.1 6.5 %collective-permute-start.33 = (bf16[1,96,384]{2,1,0:T(8,128)(2,1)S(1)}, bf16[1,96,384]{2,1,0:T(8,128)(2,1)S(1)}, u32[]{:S(2)}, u32[]{:S(2)}) collective-permute-start(bf16[1,96,384]{2,1,0:T(8,128)(2,1)S(1)} %get-tuple-element.218), channel_id=1, source_target_pairs={{0,24},{1,25},{2,26},{3,27},{4,28},{5,29},{6,30},{7,31},{8,16},{9,... | collective-permute-start | bytes 221192 | tf_op jit(solution)/shard_map/ppermute | solution.py:502
  116.0 6.5 %collective-permute-start.28 = (bf16[1,48,384]{2,1,0:T(8,128)(2,1)S(1)}, bf16[1,48,384]{2,1,0:T(8,128)(2,1)S(1)}, u32[]{:S(2)}, u32[]{:S(2)}) collective-permute-start(bf16[1,48,384]{2,1,0:T(8,128)(2,1)S(1)} %get-tuple-element.213), channel_id=1, source_target_pairs={{0,16},{1,17},{2,18},{3,19},{4,20},{5,21},{6,22},{7,23},{8,24},{9,... | collective-permute-start | bytes 110600 | tf_op jit(solution)/shard_map/ppermute | solution.py:502
  118.7 5.8 %collective-permute-start.30 = (bf16[1,48,384]{2,1,0:T(8,128)(2,1)S(1)}, bf16[1,48,384]{2,1,0:T(8,128)(2,1)S(1)}, u32[]{:S(2)}, u32[]{:S(2)}) collective-permute-start(bf16[1,48,384]{2,1,0:T(8,128)(2,1)S(1)} %get-tuple-element.215), channel_id=1, source_target_pairs={{0,24},{1,25},{2,26},{3,27},{4,28},{5,29},{6,30},{7,31},{8,16},{9,... | collective-permute-start | bytes 110600 | tf_op jit(solution)/shard_map/ppermute | solution.py:502
  133.0 6.1 %collective-permute-start.40 = (f32[32,384]{1,0:T(8,128)S(1)}, f32[32,384]{1,0:T(8,128)S(1)}, u32[]{:S(2)}, u32[]{:S(2)}) collective-permute-start(f32[32,384]{1,0:T(8,128)S(1)} %add_add_fusion.1), channel_id=1, source_target_pairs={{0,24},{1,25},{2,26},{3,27},{4,28},{5,29},{6,30},{7,31},{8,16},{9,... | collective-permute-start | bytes 147464 | tf_op jit(solution)/shard_map/ppermute | solution.py:502
  (57 other events, 627.6 us)

commit v5 on v4

--- a/solution.py
+++ b/solution.py
@@ -30,6 +30,7 @@
 LANES = GROUP * HD
 BLOCKS = 32
 PIECE = 48
+TALL, WIDE = 320, 256
 
 EPS_NORM = 1e-05
 BETA_ONE = 0.9
@@ -115,6 +116,15 @@
     return lax.dot_general(a, b, (((0,), (0,)), ((), ())), preferred_element_type=F32)
 
 
+def turned(a, eye):
+    return dot_nt(eye, a).astype(LOW)
+
+
+def identity():
+    row = lax.broadcasted_iota(jnp.int32, (128, 128), 0)
+    return jnp.where(row == lax.broadcasted_iota(jnp.int32, (128, 128), 1), 1.0, 0.0).astype(LOW)
+
+
 def norm_parts(rows):
     average = jnp.mean(rows, axis=-1, keepdims=True)
     centered = rows - average
@@ -132,24 +142,27 @@
 
 
 def gelu_parts(pre_act):
-    size = jnp.abs(pre_act) * 2.0 ** (-0.5)
-    bell = jnp.exp(-size * size)
-    t = 1.0 / (1.0 + 0.3275911 * size)
-    poly = t * (0.254829592 + t * (-0.284496736 + t * (1.421413741 + t * (-1.453152027 + t * 1.061405429))))
-    tail = 0.5 * poly * bell
-    return jnp.where(pre_act < 0.0, tail, 1.0 - tail), bell * (2.0 * math.pi) ** (-0.5)
+    below = 0.5 + 0.5 * lax.erf(pre_act * 2.0 ** (-0.5))
+    return below, jnp.exp(-0.5 * pre_act * pre_act) * (2.0 * math.pi) ** (-0.5)
 
 
 SCALARS = pl.BlockSpec(memory_space=pltpu.SMEM)
 HELD = pl.BlockSpec(memory_space=pltpu.VMEM)
 
 
-def call(body, outs, inputs, name, limit=16, scratch=(), flops=1e9, scalars=0):
+def call(body, outs, inputs, name, limit=16, scratch=(), flops=1e9, scalars=0, fetched=0, stored=0):
+    inputs = list(inputs)
+    remote = slice(scalars, scalars + fetched)
+    inputs[remote] = [pltpu.with_memory_space_constraint(array, pltpu.HBM) for array in inputs[remote]]
+    far = pl.BlockSpec(memory_space=pltpu.HBM)
     return pl.pallas_call(
         body,
-        in_specs=[SCALARS] * scalars + [HELD] * (len(inputs) - scalars),
-        out_specs=[HELD] * len(outs),
-        out_shape=[jax.ShapeDtypeStruct(shape, dtype) for shape, dtype in outs],
+        in_specs=[SCALARS] * scalars + [far] * fetched + [HELD] * (len(inputs) - scalars - fetched),
+        out_specs=[far] * stored + [HELD] * (len(outs) - stored),
+        out_shape=[
+            pltpu.HBM(shape, dtype) if index < stored else jax.ShapeDtypeStruct(shape, dtype)
+            for index, (shape, dtype) in enumerate(outs)
+        ],
         scratch_shapes=list(scratch),
         compiler_params=whole(limit),
         cost_estimate=pl.CostEstimate(flops=int(flops), bytes_accessed=4000000, transcendentals=0),
@@ -223,19 +236,36 @@
     spare[24:32] = jnp.broadcast_to(squares, (8, C))
 
 
-def prep_body(tok_ref, cot_ref, deal_ref, vec_ref, x_ref, g_ref, n_ref, pad):
+def prep_body(
+    tok_hbm, cot_hbm, deal_hbm, vec_hbm, x_hbm, g_hbm, n_ref, tok, cot, deal, vec, x_all, g_all, pad, sems, out_sems
+):
+    copies = [
+        pltpu.make_async_copy(source, target, sems.at[index])
+        for index, (source, target) in enumerate(((vec_hbm, vec), (deal_hbm, deal), (tok_hbm, tok), (cot_hbm, cot)))
+    ]
+    for copy in copies:
+        copy.start()
     pad[...] = jnp.zeros_like(pad)
-
-    @pl.loop(0, MICRO)
-    def _(image):
-        at = image_rows(image)
-        for source, target in ((cot_ref, g_ref), (tok_ref, x_ref)):
-            for r in range(GRID):
-                pad[16 * r : 16 * r + GRID, :] = source[image, 0, r]
-            rows = dot_nn(deal_ref[...], pad[...])
-            target[at, :] = rows.astype(LOW)
-        unit, _ = norm_parts(rows)
-        n_ref[at, :] = (unit * vec_ref[0:1] + vec_ref[1:2]).astype(LOW)
+    for copy in copies:
+        copy.wait()
+    for image in range(MICRO):
+        for r in range(GRID):
+            pad[image, 0, 16 * r : 16 * r + GRID, :] = tok[image, 0, r]
+            pad[image, 1, 16 * r : 16 * r + GRID, :] = cot[image, 0, r]
+    stores, made = [], []
+    for image in range(MICRO):
+        at = slice(image * IMG, (image + 1) * IMG)
+        made.append(dot_nn(deal[...], pad[image, 0]))
+        x_all[at, :] = made[-1].astype(LOW)
+        g_all[at, :] = dot_nn(deal[...], pad[image, 1]).astype(LOW)
+        for index, (source, target) in enumerate(((x_all, x_hbm), (g_all, g_hbm))):
+            stores.append(pltpu.make_async_copy(source.at[at], target.at[at], out_sems.at[image, index]))
+            stores[-1].start()
+    for image in range(MICRO):
+        unit, _ = norm_parts(made[image])
+        n_ref[image * IMG : (image + 1) * IMG, :] = (unit * vec[0:1] + vec[1:2]).astype(LOW)
+    for store in stores:
+        store.wait()
 
 
 def put_back(rows, back_ref, target, image):
@@ -289,30 +319,37 @@
         mask = row_mask(place_ref, table_ref, image)
         high = table_ref[EXTENT + 2 * image].astype(F32)
         wide = table_ref[EXTENT + 2 * image + 1].astype(F32)
-        for pair in range(2):
+        eye = identity()
+        units = [(pair, g) for pair in range(2) for g in range(GROUPS)]
+        at_pair = [pl.ds(pl.multiple_of(image * IMG + pair * 2 * WIN, 2 * WIN), 2 * WIN) for pair in range(2)]
+        raws = []
+        for pair, g in units:
+            at = g * LANES
+            queries = packed_ref[at_pair[pair], at : at + LANES]
+            keys = packed_ref[at_pair[pair], C + at : C + at + LANES]
+            raws.append(dot_nt(spread_keys(keys, heads_ref), spread_rows(queries)))
+        softs = []
+        for (pair, g), raw in zip(units, raws):
+            allowed = (reach_ref[pair, 0] < high) & (reach_ref[pair, 1] < wide)
+            raw = (raw * HD ** (-0.5) + bias_ref[g]).reshape(GROUP, WIN, 128)
+            scores = jnp.where(allowed[None], raw, NEG_FILL)
+            exponent = jnp.exp(scores - jnp.max(scores, axis=1, keepdims=True))
+            soft = exponent * (1.0 / jnp.sum(exponent, axis=1, keepdims=True))
+            soft = soft.reshape(GROUP * WIN, 128).astype(LOW)
+            soft_ref[image, pair * GROUPS + g] = soft
+            softs.append(soft)
+        softs = [turned(soft, eye) for soft in softs]
+        for (pair, g), soft in zip(units, softs):
+            at = g * LANES
+            values = packed_ref[at_pair[pair], 2 * C + at : 2 * C + at + LANES]
+            result = own_rows(dot_nn(soft, spread_keys(values, heads_ref)))
             rows = slice(pair * 2 * WIN, (pair + 1) * 2 * WIN)
-            at_pair = pl.ds(pl.multiple_of(image * IMG + pair * 2 * WIN, 2 * WIN), 2 * WIN)
-            allowed = (reach_ref[pair, 0] < high) & (reach_ref[pair, 1] < wide)
-            for g in range(GROUPS):
-                at = g * LANES
-                queries = packed_ref[at_pair, at : at + LANES]
-                keys = packed_ref[at_pair, C + at : C + at + LANES]
-                values = packed_ref[at_pair, 2 * C + at : 2 * C + at + LANES]
-                raw = dot_nt(spread_keys(keys, heads_ref), spread_rows(queries))
-                raw = (raw * HD ** (-0.5) + bias_ref[g]).reshape(GROUP, WIN, 128)
-                scores = jnp.where(allowed[None], raw, NEG_FILL)
-                exponent = jnp.exp(scores - jnp.max(scores, axis=1, keepdims=True))
-                soft = exponent * (1.0 / jnp.sum(exponent, axis=1, keepdims=True))
-                soft = soft.reshape(GROUP * WIN, 128)
-                soft_ref[image, pair * GROUPS + g] = soft
-                result = own_rows(dot_tn(soft.astype(LOW), spread_keys(values, heads_ref)))
-                attn_ref[at_pair, at : at + LANES] = (result * mask[rows]).astype(LOW)
+            attn_ref[at_pair[pair], at : at + LANES] = (result * mask[rows]).astype(LOW)
 
 
 def middle_body(attn_ref, x_ref, wp_ref, vec_ref, middle_ref, n_ref):
-    @pl.loop(0, MICRO)
-    def _(image):
-        at = image_rows(image)
+    for image in range(MICRO):
+        at = slice(image * IMG, (image + 1) * IMG)
         middle = x_ref[at, :].astype(F32) + dot_nt(attn_ref[at, :], wp_ref[...]) + vec_ref[4:5]
         middle_ref[at, :] = middle
         unit, _ = norm_parts(middle)
@@ -322,7 +359,7 @@
 def mlp_body(
     direct, table_ref, middle_ref, n_ref, g_ref, vec_ref, *refs,
 ):
-    far_refs, (hidden_ref, grad_hidden_ref, grad_ref, sums_ref, w2_ref, w1, bias) = refs[:PIECES], refs[PIECES:]
+    far_refs, (hidden_ref, grad_hidden_ref, grad_ref, sums_ref, w2_ref, w1, bias, bias_sum) = refs[:PIECES], refs[PIECES:]
     for j in range(BLOCKS):
         at = table_ref[ME] ^ block_at(j) if direct else (j % 8) * 4 + j // 8
         row = at // 4 * PIECE if not direct else pl.multiple_of((at >> 2) * PIECE, PIECE)
@@ -333,29 +370,31 @@
         bias[:, r * C : (r + 1) * C] = vec_ref[8 + r : 9 + r]
     sums_ref[...] = jnp.zeros_like(sums_ref)
 
-    @pl.loop(0, MICRO)
-    def _(image):
-        at = image_rows(image)
-        unit, inverse = norm_parts(middle_ref[at, :])
-        normed = n_ref[at, :]
-        g_low = g_ref[at, :]
-        g = g_low.astype(F32)
-        for part in range(4):
-            cols = slice(part * C, (part + 1) * C)
-            pre_act = dot_nn(normed, w1[:, cols]) + bias[:, cols]
-            grad_post = dot_nn(g_low, w2_ref[:, cols])
+    bias_sum[...] = jnp.zeros_like(bias_sum)
+    for part in range(FF // WIDE):
+        cols = slice(part * WIDE, (part + 1) * WIDE)
+        for block in range(ROWS // TALL):
+            at = slice(block * TALL, (block + 1) * TALL)
+            pre_act = dot_nn(n_ref[at, :], w1[:, cols]) + bias[:, cols]
+            grad_post = dot_nn(g_ref[at, :], w2_ref[:, cols])
             below, density = gelu_parts(pre_act)
             hidden_ref[at, cols] = (pre_act * below).astype(LOW)
             grad_pre = grad_post * (below + pre_act * density)
             grad_hidden_ref[at, cols] = grad_pre.astype(LOW)
-            sums_ref[8 + part : 9 + part] += jnp.sum(grad_pre, axis=0, keepdims=True)
+            bias_sum[:, cols] += jnp.sum(grad_pre, axis=0, keepdims=True)
+    for block in range(ROWS // TALL):
+        at = slice(block * TALL, (block + 1) * TALL)
         back = dot_nt(grad_hidden_ref[at, :], w1[...])
-        sums_ref[5:6] += jnp.sum(back * unit, axis=0, keepdims=True)
-        sums_ref[6:7] += jnp.sum(back, axis=0, keepdims=True)
+        unit, inverse = norm_parts(middle_ref[at, :])
+        g = g_ref[at, :].astype(F32)
         grad_middle = g + norm_back(back, unit, inverse, vec_ref[5:6])
         grad_ref[at, :] = grad_middle
         sums_ref[4:5] += jnp.sum(grad_middle, axis=0, keepdims=True)
+        sums_ref[5:6] += jnp.sum(back * unit, axis=0, keepdims=True)
+        sums_ref[6:7] += jnp.sum(back, axis=0, keepdims=True)
         sums_ref[7:8] += jnp.sum(g, axis=0, keepdims=True)
+    for r in range(4):
+        sums_ref[8 + r : 9 + r] = bias_sum[:, r * C : (r + 1) * C]
 
 
 def place_of(direct, table_ref, t, h):
@@ -364,26 +403,30 @@
     return table_ref[SLOT] ^ swap_bits(4 * t) ^ ((h & 1) * 16 + (h >> 1) * 4)
 
 
-def mlp_weights_body(direct, table_ref, n_ref, g_ref, hidden_ref, grad_hidden_ref, keep_ref, send_ref, n_turned, g_turned, made):
+def mlp_weights_body(direct, table_ref, n_ref, g_ref, hidden_ref, grad_hidden_ref, keep_ref, send_ref, n_turned, g_turned, made, first, second):
     n_turned[...] = n_ref[...].T
     g_turned[...] = g_ref[...].T
-    for part in range(4):
-        cols = slice(part * C, (part + 1) * C)
-        first = dot_nn(n_turned[...], grad_hidden_ref[:, cols]).astype(LOW)
-        second = dot_nn(g_turned[...], hidden_ref[:, cols]).astype(LOW)
+    for part in range(3):
+        cols = slice(part * 2 * WIDE, (part + 1) * 2 * WIDE)
+        first[:, cols] = dot_nn(n_turned[...], grad_hidden_ref[:, cols]).astype(LOW)
+        second[:, cols] = dot_nn(g_turned[...], hidden_ref[:, cols]).astype(LOW)
+    for h in range(4):
+        cols = slice(h * C, (h + 1) * C)
         for t in range(8):
-            at = place_of(direct, table_ref, t, part)
-            made[at, :PIECE] = first[t * PIECE : (t + 1) * PIECE]
-            made[at, PIECE:] = second[t * PIECE : (t + 1) * PIECE]
+            at = place_of(direct, table_ref, t, h)
+            made[at, :PIECE] = first[t * PIECE : (t + 1) * PIECE, cols]
+            made[at, PIECE:] = second[t * PIECE : (t + 1) * PIECE, cols]
     keep_ref[...] = made[: BLOCKS // 2]
     send_ref[...] = made[BLOCKS // 2 :]
 
 
 def output_body(hidden_ref, w2_ref, middle_ref, vec_ref, back_ref, out_ref):
-    @pl.loop(0, MICRO)
-    def _(image):
-        at = image_rows(image)
-        put_back(middle_ref[at, :] + dot_nt(hidden_ref[at, :], w2_ref[...]) + vec_ref[7:8], back_ref, out_ref, image)
+    made = []
+    for image in range(MICRO):
+        at = slice(image * IMG, (image + 1) * IMG)
+        made.append((middle_ref[at, :] + dot_nt(hidden_ref[at, :], w2_ref[...]) + vec_ref[7:8]).astype(LOW))
+    for image in range(MICRO):
+        put_back(made[image], back_ref, out_ref, image)
 
 
 def attend_back_body(
@@ -401,28 +444,38 @@
         mask = row_mask(place_ref, table_ref, image)
         grad_attn = dot_nn(grad_low, wp_ref[...])
         grad_attn = (grad_attn * jnp.concatenate([mask] * 3, axis=1)).astype(LOW)
-        for pair in range(2):
-            rows = slice(pair * 2 * WIN, (pair + 1) * 2 * WIN)
-            at_pair = pl.ds(pl.multiple_of(image * IMG + pair * 2 * WIN, 2 * WIN), 2 * WIN)
-            for g in range(GROUPS):
-                at = g * LANES
-                queries = packed_ref[at_pair, at : at + LANES]
-                keys = packed_ref[at_pair, C + at : C + at + LANES]
-                values = packed_ref[at_pair, 2 * C + at : 2 * C + at + LANES]
-                incoming = spread_rows(grad_attn[rows, at : at + LANES])
-                soft = soft_ref[image, pair * GROUPS + g]
-                grad_soft = dot_nt(spread_keys(values, heads_ref), incoming)
-                joint = (soft * grad_soft).reshape(GROUP, WIN, 128)
-                inner = jnp.sum(joint, axis=1, keepdims=True)
-                grad_scores = (joint - soft.reshape(GROUP, WIN, 128) * inner).reshape(GROUP * WIN, 128)
-                grad_low_scores = grad_scores.astype(LOW)
-                bias_sum_ref[g] += grad_low_scores.astype(F32)
-                grad_values = own_keys(dot_nn(soft.astype(LOW), incoming), heads_ref)
-                grad_keys = own_keys(dot_nn(grad_low_scores, spread_rows(queries)), heads_ref)
-                grad_queries = own_rows(dot_tn(grad_low_scores, spread_keys(keys, heads_ref)))
-                packed_grad_ref[at_pair, at : at + LANES] = (grad_queries * HD ** (-0.5)).astype(LOW)
-                packed_grad_ref[at_pair, C + at : C + at + LANES] = (grad_keys * HD ** (-0.5)).astype(LOW)
-                packed_grad_ref[at_pair, 2 * C + at : 2 * C + at + LANES] = grad_values.astype(LOW)
+        eye = identity()
+        units = [(pair, g) for pair in range(2) for g in range(GROUPS)]
+        at_pair = [pl.ds(pl.multiple_of(image * IMG + pair * 2 * WIN, 2 * WIN), 2 * WIN) for pair in range(2)]
+        incomings, grad_softs = [], []
+        for pair, g in units:
+            at = g * LANES
+            values = packed_ref[at_pair[pair], 2 * C + at : 2 * C + at + LANES]
+            incomings.append(spread_rows(grad_attn[pair * 2 * WIN : (pair + 1) * 2 * WIN, at : at + LANES]))
+            grad_softs.append(dot_nt(spread_keys(values, heads_ref), incomings[-1]))
+        grads = []
+        for (pair, g), grad_soft in zip(units, grad_softs):
+            soft = soft_ref[image, pair * GROUPS + g].astype(F32)
+            joint = (soft * grad_soft).reshape(GROUP, WIN, 128)
+            inner = jnp.sum(joint, axis=1, keepdims=True)
+            grad_scores = (joint - soft.reshape(GROUP, WIN, 128) * inner).reshape(GROUP * WIN, 128)
+            grads.append(grad_scores.astype(LOW))
+            bias_sum_ref[g] += grads[-1].astype(F32)
+        values_made = [dot_nn(soft_ref[image, pair * GROUPS + g], incoming) for (pair, g), incoming in zip(units, incomings)]
+        turns = [turned(grad, eye) for grad in grads]
+        keys_made, queries_made = [], []
+        for (pair, g), grad, turn in zip(units, grads, turns):
+            at = g * LANES
+            queries = packed_ref[at_pair[pair], at : at + LANES]
+            keys = packed_ref[at_pair[pair], C + at : C + at + LANES]
+            keys_made.append(dot_nn(grad, spread_rows(queries)))
+            queries_made.append(dot_nn(turn, spread_keys(keys, heads_ref)))
+        for (pair, g), grad_values, grad_keys, grad_queries in zip(units, values_made, keys_made, queries_made):
+            at = g * LANES
+            rows = at_pair[pair]
+            packed_grad_ref[rows, at : at + LANES] = (own_rows(grad_queries) * HD ** (-0.5)).astype(LOW)
+            packed_grad_ref[rows, C + at : C + at + LANES] = (own_keys(grad_keys, heads_ref) * HD ** (-0.5)).astype(LOW)
+            packed_grad_ref[rows, 2 * C + at : 2 * C + at + LANES] = own_keys(grad_values, heads_ref).astype(LOW)
         sums_ref[0:1] += jnp.sum(packed_grad_ref[at_image, :C].astype(F32), axis=0, keepdims=True)
         sums_ref[1:2] += jnp.sum(packed_grad_ref[at_image, 2 * C :].astype(F32), axis=0, keepdims=True)
 
@@ -439,17 +492,33 @@
     send_ref[...] = made[BLOCKS // 2 :]
 
 
-def input_body(packed_grad_ref, wq_ref, x_ref, grad_ref, vec_ref, back_ref, out_ref, sums_ref):
+def input_body(
+    wq_hbm, packed_grad_hbm, x_hbm, grad_hbm, vec_ref, back_ref, out_ref, sums_ref, wq, packed_grad, x_all, grad_all, wq_sem, sems
+):
     sums_ref[...] = jnp.zeros_like(sums_ref)
-
-    @pl.loop(0, MICRO)
-    def _(image):
-        at = image_rows(image)
-        back = dot_nt(packed_grad_ref[at, :], wq_ref[...])
-        unit, inverse = norm_parts(x_ref[at, :].astype(F32))
+    whole_copy = pltpu.make_async_copy(wq_hbm, wq, wq_sem)
+    whole_copy.start()
+    copies = []
+    for image in range(MICRO):
+        at = slice(image * IMG, (image + 1) * IMG)
+        for index, (source, target) in enumerate(((packed_grad_hbm, packed_grad), (x_hbm, x_all), (grad_hbm, grad_all))):
+            copies.append(pltpu.make_async_copy(source.at[at], target.at[at], sems.at[image, index]))
+            copies[-1].start()
+    whole_copy.wait()
+    backs = []
+    for image in range(MICRO):
+        for copy in copies[3 * image : 3 * image + 3]:
+            copy.wait()
+        backs.append(dot_nt(packed_grad[image * IMG : (image + 1) * IMG, :], wq[...]))
+    made = []
+    for image, back in enumerate(backs):
+        at = slice(image * IMG, (image + 1) * IMG)
+        unit, inverse = norm_parts(x_all[at, :].astype(F32))
         sums_ref[0:1] += jnp.sum(back * unit, axis=0, keepdims=True)
         sums_ref[1:2] += jnp.sum(back, axis=0, keepdims=True)
-        put_back(grad_ref[at, :] + norm_back(back, unit, inverse, vec_ref[0:1]), back_ref, out_ref, image)
+        made.append((grad_all[at, :] + norm_back(back, unit, inverse, vec_ref[0:1])).astype(LOW))
+    for image in range(MICRO):
+        put_back(made[image], back_ref, out_ref, image)
 
 
 def adam_update(weight, first, second, gradient, rate, decay):
@@ -554,14 +623,21 @@
     place = jnp.asarray(PLACE)
     reach = jnp.asarray(REACH)
     heads_low = jnp.asarray(HEADS, LOW)
-    x_rows, g_rows, n_rows = call(
-        prep_body,
-        [((ROWS, C), LOW)] * 3,
-        (tokens_in, cotangent, deal, vectors),
-        "prep",
-        limit=4,
-        scratch=[pltpu.VMEM((PAD, C), LOW)],
-    )
+    def prepare(tokens, cotangents):
+        image = (MICRO, 1, GRID, GRID, C)
+        return call(
+            prep_body,
+            [((ROWS, C), LOW)] * 3,
+            (tokens, cotangents, deal, vectors),
+            "prep",
+            scratch=[
+                pltpu.VMEM(image, LOW), pltpu.VMEM(image, LOW), pltpu.VMEM((IMG, PAD), LOW), pltpu.VMEM((12, C), F32),
+                pltpu.VMEM((ROWS, C), LOW), pltpu.VMEM((ROWS, C), LOW), pltpu.VMEM((MICRO, 2, PAD, C), LOW),
+                pltpu.SemaphoreType.DMA((4,)), pltpu.SemaphoreType.DMA((MICRO, 2)),
+            ],
+            fetched=4,
+            stored=2,
+        )
 
     def product_of(values, lookup):
         first = lax.reduce_precision(values, 8, 7)
@@ -575,11 +651,12 @@
         return jnp.concatenate([made, made], axis=2)
 
     if direct:
-        near, extent, route, rel_bias = tie(near[None], extent, route, rel_table)
+        near = near[None]
         near_got, far_got = spread(near, LINE), spread(far[None], LINE)
         near_all = join(near, *near_got)
-        near_all, x_rows, g_rows, n_rows, rel_bias = tie(near_all, x_rows, g_rows, n_rows, rel_bias)
+        near_all, tokens, cotangents, extent, route, rel_bias = tie(near_all, tokens_in, cotangent, extent, route, rel_table)
         near_all = [near_all] + spread(near_all, PLANE)
+        x_rows, g_rows, n_rows = prepare(tokens, cotangents)
         table = jnp.concatenate(
             [
                 jnp.stack([me, swap_bits(me)]).astype(jnp.int32),
@@ -588,11 +665,13 @@
             ]
         )
         bias = make_bias(rel_bias)
-        far_got[0], bias, table, *near_all = tie(far_got[0], bias, table, *near_all)
+        bias, table, n_rows, *near_all = tie(bias, table, n_rows, *near_all)
+        far_got[0], near_all[0] = tie(far_got[0], near_all[0])
         far_all = join(far[None], *far_got)
         near_all = near_all + [passed(piece, CORE) for piece in near_all]
         far_got = [far_all] + spread(far_all, PLANE)
     else:
+        x_rows, g_rows, n_rows = prepare(tokens_in, cotangent)
         table = jnp.concatenate(
             [
                 jnp.stack([me, swap_bits(me)]).astype(jnp.int32),
@@ -606,7 +685,7 @@
     packed, soft, attn, w_qkv, w_proj = call(
         functools.partial(attend_body, direct),
         [
-            ((ROWS, 3 * C), LOW), ((MICRO, 2 * GROUPS, GROUP * WIN, 128), F32), ((ROWS, C), LOW), ((C, 3 * C), LOW), ((C, C), LOW),
+            ((ROWS, 3 * C), LOW), ((MICRO, 2 * GROUPS, GROUP * WIN, 128), LOW), ((ROWS, C), LOW), ((C, 3 * C), LOW), ((C, C), LOW),
         ],
         (table, n_rows, vectors, bias, reach, place, heads_low, *near_all),
         "attend",
@@ -633,7 +712,7 @@
         (table, middle, n_two, g_rows, vectors, *far_all),
         "mlp",
         limit=8,
-        scratch=[pltpu.VMEM((C, FF), LOW), pltpu.VMEM((1, FF), F32)],
+        scratch=[pltpu.VMEM((C, FF), LOW), pltpu.VMEM((1, FF), F32), pltpu.VMEM((1, FF), F32)],
         flops=10e9,
         scalars=1,
     )
@@ -644,8 +723,11 @@
         [((half, 2 * PIECE, C), LOW)] * 2,
         (table, n_two, g_rows, hidden, grad_hidden),
         "mlp_weights",
-        limit=10,
-        scratch=[pltpu.VMEM((C, ROWS), LOW), pltpu.VMEM((C, ROWS), LOW), pltpu.VMEM((BLOCKS, 2 * PIECE, C), LOW)],
+        limit=14,
+        scratch=[
+            pltpu.VMEM((C, ROWS), LOW), pltpu.VMEM((C, ROWS), LOW), pltpu.VMEM((BLOCKS, 2 * PIECE, C), LOW),
+            pltpu.VMEM((C, FF), LOW), pltpu.VMEM((C, FF), LOW),
+        ],
         flops=4e9,
         scalars=1,
     )
@@ -686,23 +768,30 @@
         near_send, *far_got = tie(near_send, *far_got)
         near_got = passed(near_send, CORE)
         near_stays, near_goes = first_sum(near_keep, near_got)
-        near_goes[0], packed_grad, bias_sum, *far_got = tie(near_goes[0], packed_grad, bias_sum, *far_got)
+        near_goes[0], packed_grad, bias_sum = tie(near_goes[0], packed_grad, bias_sum)
         near_got = sent(near_goes, PLANE)
+
+    bias_sum = (bias_sum[:, :, :WIN] + bias_sum[:, :, WIN:]).reshape(NH, WIN * WIN)
+    table_grad = product_of(bias_sum, LOOKUP.T)
+    if direct:
+        table_grad, *far_got = tie(table_grad, *far_got)
         far_stays, far_goes = plane_sum(far_stays, far_got)
         far_got = sent(far_goes, LINE)
 
     grad_block, sums_input = call(
         input_body,
         [(tokens_in.shape, LOW), ((2, C), F32)],
-        (packed_grad, w_qkv, x_rows, grad_middle, vectors, back),
+        (w_qkv, packed_grad, x_rows, grad_middle, vectors, back),
         "input_grad",
-        limit=5,
+        scratch=[
+            pltpu.VMEM((C, 3 * C), LOW), pltpu.VMEM((ROWS, 3 * C), LOW), pltpu.VMEM((ROWS, C), LOW), pltpu.VMEM((ROWS, C), F32),
+            pltpu.SemaphoreType.DMA, pltpu.SemaphoreType.DMA((MICRO, 3)),
+        ],
         flops=4e9,
+        fetched=4,
     )
 
     vec_grad = jnp.concatenate([sums_input, sums_attend, sums_mlp[4:]], axis=0)
-    bias_sum = (bias_sum[:, :, :WIN] + bias_sum[:, :, WIN:]).reshape(NH, WIN * WIN)
-    table_grad = product_of(bias_sum, LOOKUP.T)
     if direct:
         grad_block, vec_grad, table_grad, *near_got = tie(grad_block, vec_grad, table_grad, *near_got)
         near_stays, near_goes = plane_sum(near_stays, near_got)

time: 142 us -> 126 us (0.89)
  Pallas kernels: 64.9 us -> 49.9 us
  local copies, waits for them, and re-layouts: 13.1 us -> 1.5 us
  waiting for transfers between devices: 16.9 us -> 24.7 us
  matrix products: 0.79 us -> 3.74 us
    pallas_call x9, Pallas kernels: 61.8 us -> 46.7 us  [call(): pl.pallas_call(body, in_specs=[SCALARS] * scalars + [far] * fetched + [HE...]
    unnamed x80 -> x56, local copies, waits for them, and re-layouts: 11.8 us -> 0.16 us
    ppermute x41, waiting for transfers between devices: 16.9 us -> 24.7 us  [passed(): return lax.ppermute(rows, BOTH, [(i, i ^ mask) for i in range(devices)])]
    dot_general x2, matrix products: 0.79 us -> 3.74 us  [product_of(): jnp.dot(parts, jnp.asarray(lookup, LOW), preferred_element_type=F32)]
  transfers between devices with their start and end apart: 41 -> 41, of which waited for: 12 -> 15; matrix products, arithmetic and copies ran while one was open for 2% -> 5% of each run, Pallas kernels for 30% -> 27%
where the time goes in v5:
time: 126 us
  Pallas kernels  49.9 us (40%)
  starting transfers between devices  43.1 us (34%)
  waiting for transfers between devices  24.7 us (20%)
  matrix products  3.74 us (3%)
  between operations  1.52 us (1%)
  local copies, waits for them, and re-layouts  1.5 us (1%)
  other arithmetic  1.36 us (1%)
    pallas_call x9, Pallas kernels, call(): pl.pallas_call(body, in_specs=[SCALARS] * scalars + [far] * fetched + [HE...  46.7 us
    ppermute x41, starting transfers between devices, passed(): return lax.ppermute(rows, BOTH, [(i, i ^ mask) for i in range(devices)])  43.1 us
    ppermute x41, waiting for transfers between devices, passed(): return lax.ppermute(rows, BOTH, [(i, i ^ mask) for i in range(devices)])  24.7 us
    dot_general x2, matrix products, product_of(): jnp.dot(parts, jnp.asarray(lookup, LOW), preferred_element_type=F32)  3.74 us
  transfers between devices with their start and end apart: 41, of which 15 were waited for; matrix products, arithmetic and copies ran while one was open for 5% of the time, Pallas kernels for 27%

profile of v5, /device:TPU:0, one launch (start us, length us, event | category | flops | bytes accessed | tf_op | source)
XLA Modules:
  0.0 125.8 jit_solution(17120419917729075536)
XLA Ops:
  1.7 5.1 %collective-permute-start.2 = (bf16[1,48,384]{2,1,0:T(8,128)(2,1)S(1)}, bf16[1,48,384]{2,1,0:T(8,128)(2,1)S(1)}, u32[]{:S(2)}, u32[]{:S(2)}) collective-permute-start(bf16[1,48,384]{2,1,0:T(8,128)(2,1)S(1)} %bitcast.47), channel_id=1, source_target_pairs={{0,24},{1,25},{2,26},{3,27},{4,28},{5,29},{6,30},{7,31},{8,16},{9,... | collective-permute-start | bytes 110600 | tf_op jit(solution)/shard_map/ppermute | solution.py:571
  7.5 3.7 %collective-permute-start.12 = (bf16[1,96,384]{2,1,0:T(8,128)(2,1)S(1)}, bf16[1,96,384]{2,1,0:T(8,128)(2,1)S(1)}, u32[]{:S(2)}, u32[]{:S(2)}) collective-permute-start(bf16[1,96,384]{2,1,0:T(8,128)(2,1)S(1)} %bitcast.42), channel_id=1, source_target_pairs={{0,24},{1,25},{2,26},{3,27},{4,28},{5,29},{6,30},{7,31},{8,16},{9,... | collective-permute-start | bytes 221192 | tf_op jit(solution)/shard_map/ppermute | solution.py:571
  12.7 2.5 %collective-permute-start.5 = (bf16[4,48,384]{2,1,0:T(8,128)(2,1)S(1)}, bf16[4,48,384]{2,1,0:T(8,128)(2,1)S(1)}, u32[]{:S(2)}, u32[]{:S(2)}) collective-permute-start(bf16[4,48,384]{2,1,0:T(8,128)(2,1)S(1)} %pad_maximum_fusion.4.refs_0_), channel_id=1, source_target_pairs={{0,6},{1,7},{2,4},{3,5},{4,2},{5,3},{6,0},{7,1},{8,14},{9,15},{10,... | collective-permute-start | bytes 442376 | tf_op jit(solution)/shard_map/ppermute | solution.py:571
  17.0 1.7 %fusion.3 = f32[36,4096]{1,0:T(8,128)S(1)} fusion(bf16[169,4096]{1,0:T(8,128)(2,1)} %constant.95.clone, bf16[12,169]{1,0:T(8,128)(2,1)S(1)} %get-tuple-element.245, bf16[12,169]{1,0:T(8,128)(2,1)S(1)} %get-tuple-element.246, bf16[12,169]{1,0:T(8,128)(2,1)S(1)} %get-tuple-element.244), kind=kOutput, calls=%fused_computation.21 | convolution fusion | flops 49876632 | bytes 1986440 | tf_op jit(solution)/shard_map/dot_general | solution.py:646
  20.3 3.5 %prep.1 = (bf16[1280,384]{1,0:T(8,128)(2,1)}, bf16[1280,384]{1,0:T(8,128)(2,1)}, bf16[1280,384]{1,0:T(8,128)(2,1)S(1)}) custom-call(bf16[5,1,14,14,384]{4,3,2,1,0:T(8,128)(2,1)} %tok_hbm, bf16[5,1,14,14,384]{4,3,2,1,0:T(8,128)(2,1)} %cot_hbm, bf16[256,224]{1,0:T(8,128)(2,1)} %constant.91.clone.deal_hbm, f32[12,384]{1,0:T(8,128)} %refs_4_.1), custom_call_target="tpu_custom_call" | custom-call | flops 1000000000 | bytes 4000000 | tf_op jit(solution)/shard_map/prep/pallas_call | solution.py:158
  26.7 2.5 %collective-permute-start.15 = (bf16[4,96,384]{2,1,0:T(8,128)(2,1)S(1)}, bf16[4,96,384]{2,1,0:T(8,128)(2,1)S(1)}, u32[]{:S(2)}, u32[]{:S(2)}) collective-permute-start(bf16[4,96,384]{2,1,0:T(8,128)(2,1)S(1)} %pad_maximum_fusion.3.refs_0_), channel_id=1, source_target_pairs={{0,6},{1,7},{2,4},{3,5},{4,2},{5,3},{6,0},{7,1},{8,14},{9,15},{10,... | collective-permute-start | bytes 884744 | tf_op jit(solution)/shard_map/ppermute | solution.py:571
  30.3 7.4 %attend.1 = (bf16[1280,1152]{1,0:T(8,128)(2,1)S(1)}, bf16[5,6,256,128]{3,2,1,0:T(8,128)(2,1)S(1)}, bf16[1280,384]{1,0:T(8,128)(2,1)S(1)}, bf16[384,1152]{1,0:T(8,128)(2,1)S(1)}, bf16[384,384]{1,0:T(8,128)(2,1)S(1)}) custom-call(s32[32]{0:T(128)S(1)} %pad_add_fusion.table_ref, bf16[1280,384]{1,0:T(8,128)(2,1)S(1)} %get-tuple-element.140.n_ref, ...), custom_call_target="tpu_custom_call" | custom-call | flops 8000000000 | bytes 4000000 | tf_op jit(solution)/shard_map/attend/pallas_call | solution.py:158
  37.7 5.3 %collective-permute-done.14.refs_2_ = bf16[4,96,384]{2,1,0:T(8,128)(2,1)S(1)} collective-permute-done((bf16[4,96,384]{2,1,0:T(8,128)(2,1)S(1)}, bf16[4,96,384]{2,1,0:T(8,128)(2,1)S(1)}, u32[]{:S(2)}, u32[]{:S(2)}) %collective-permute-start.14) | collective-permute-done | bytes 294944 | tf_op jit(solution)/shard_map/ppermute | solution.py:571
  45.8 8.2 %mlp.1 = (bf16[1280,1536]{1,0:T(8,128)(2,1)S(1)}, bf16[1280,1536]{1,0:T(8,128)(2,1)S(1)}, f32[1280,384]{1,0:T(8,128)S(1)}, f32[12,384]{1,0:T(8,128)S(1)}, bf16[384,1536]{1,0:T(8,128)(2,1)S(1)}) custom-call(s32[32]{0:T(128)S(1)} %pad_add_fusion.table_ref, f32[1280,384]{1,0:T(8,128)S(1)} %get-tuple-element.158.middle_ref, ...), custom_call_target="tpu_custom_call" | custom-call | flops 10000000000 | bytes 4000000 | tf_op jit(solution)/shard_map/mlp/pallas_call | solution.py:158
  54.1 4.2 %mlp_weights.1 = (bf16[16,96,384]{2,1,0:T(8,128)(2,1)S(1)}, bf16[16,96,384]{2,1,0:T(8,128)(2,1)S(1)}) custom-call(s32[32]{0:T(128)S(1)} %pad_add_fusion.table_ref, bf16[1280,384]{1,0:T(8,128)(2,1)S(1)} %get-tuple-element.159.n_ref, bf16[1280,384]{1,0:T(8,128)(2,1)S(1)} %copy-done.25, bf16[1280,1536]{1,0:T(8,128)(2,1)S(1)} %get-tuple-element.165.hidden_ref, ...), custom_call_target="tpu_custom_call" | custom-call | flops 4000000000 | bytes 4000000 | tf_op jit(solution)/shard_map/mlp_weights/pallas_call | solution.py:158
  58.5 3.7 %output.1 = bf16[5,1,14,14,384]{4,3,2,1,0:T(8,128)(2,1)} custom-call(bf16[1280,1536]{1,0:T(8,128)(2,1)S(1)} %get-tuple-element.165.hidden_ref, bf16[384,1536]{1,0:T(8,128)(2,1)S(1)} %get-tuple-element.166.w2_ref, f32[1280,384]{1,0:T(8,128)S(1)} %get-tuple-element.158.middle_ref, f32[12,384]{1,0:T(8,128)S(1)} %copy-done.6, bf16[224,256]{1,0:T(8,128)(2,1)S(1)} %copy-done.4), custom_call_target="tpu_custom_call" | custom-call | flops 2000000000 | bytes 4000000 | tf_op jit(solution)/shard_map/output/pallas_call | solution.py:158
  66.1 7.7 %attend_back.1 = (bf16[1280,1152]{1,0:T(8,128)(2,1)S(1)}, bf16[1280,384]{1,0:T(8,128)(2,1)S(1)}, f32[3,256,128]{2,1,0:T(8,128)S(1)}, f32[2,384]{1,0:T(2,128)S(1)}) custom-call(s32[32]{0:T(128)S(1)} %pad_add_fusion.table_ref, f32[1280,384]{1,0:T(8,128)S(1)} %get-tuple-element.172.grad_ref.grad_hbm, bf16[1280,1152]{1,0:T(8,128)(2,1)S(1)} %get-tuple-element.173.packed_ref, ...), custom_call_target="tpu_custom_call" | custom-call | flops 8000000000 | bytes 4000000 | tf_op jit(solution)/shard_map/attend_back/pallas_call | solution.py:158
  73.8 3.1 %attend_weights.1 = (bf16[16,48,384]{2,1,0:T(8,128)(2,1)S(1)}, bf16[16,48,384]{2,1,0:T(8,128)(2,1)S(1)}) custom-call(s32[32]{0:T(128)S(1)} %pad_add_fusion.table_ref, bf16[1280,384]{1,0:T(8,128)(2,1)S(1)} %get-tuple-element.140.n_ref, bf16[1280,384]{1,0:T(8,128)(2,1)S(1)} %get-tuple-element.175.grad_low_ref, ...), custom_call_target="tpu_custom_call" | custom-call | flops 2000000000 | bytes 4000000 | tf_op jit(solution)/shard_map/attend_weights/pallas_call | solution.py:158
  76.9 2.5 %collective-permute-done.23.refs_2_ = bf16[4,96,384]{2,1,0:T(8,128)(2,1)S(1)} collective-permute-done((bf16[4,96,384]{2,1,0:T(8,128)(2,1)S(1)}, bf16[4,96,384]{2,1,0:T(8,128)(2,1)S(1)}, u32[]{:S(2)}, u32[]{:S(2)}) %collective-permute-start.23) | collective-permute-done | bytes 294944 | tf_op jit(solution)/shard_map/ppermute | solution.py:571
  79.4 2.0 %collective-permute-done.24.got_ref = bf16[16,48,384]{2,1,0:T(8,128)(2,1)S(1)} collective-permute-done((bf16[16,48,384]{2,1,0:T(8,128)(2,1)S(1)}, bf16[16,48,384]{2,1,0:T(8,128)(2,1)S(1)}, u32[]{:S(2)}, u32[]{:S(2)}) %collective-permute-start.24) | collective-permute-done | bytes 589856 | tf_op jit(solution)/shard_map/ppermute | solution.py:571
  85.5 2.0 %fusion = f32[36,169]{1,0:T(8,128)S(1)} fusion(bf16[4096,169]{1,0:T(8,128)(2,1)} %constant.96.clone, bf16[12,4096]{1,0:T(8,128)(2,1)S(1)} %get-tuple-element.242, bf16[12,4096]{1,0:T(8,128)(2,1)S(1)} %get-tuple-element.243, bf16[12,4096]{1,0:T(8,128)(2,1)S(1)} %get-tuple-element.241), kind=kOutput, calls=%fused_computation.7 | convolution fusion | flops 50724864 | bytes 1703696 | tf_op jit(solution)/shard_map/dot_general | solution.py:646
  90.4 7.8 %input_grad.1 = (bf16[5,1,14,14,384]{4,3,2,1,0:T(8,128)(2,1)}, f32[2,384]{1,0:T(2,128)S(1)}) custom-call(bf16[384,1152]{1,0:T(8,128)(2,1)} %copy-done.27, bf16[1280,1152]{1,0:T(8,128)(2,1)} %copy-done.23, bf16[1280,384]{1,0:T(8,128)(2,1)} %get-tuple-element.151.x_ref.x_hbm, f32[1280,384]{1,0:T(8,128)} %copy-done.26, f32[12,384]{1,0:T(8,128)S(1)} %copy-done.6, ...), custom_call_target="tpu_custom_call" | custom-call | flops 4000000000 | bytes 4000000 | tf_op jit(solution)/shard_map/input_grad/pallas_call | solution.py:158
  98.4 1.8 %collective-permute-start.33 = (bf16[1,96,384]{2,1,0:T(8,128)(2,1)S(1)}, bf16[1,96,384]{2,1,0:T(8,128)(2,1)S(1)}, u32[]{:S(2)}, u32[]{:S(2)}) collective-permute-start(bf16[1,96,384]{2,1,0:T(8,128)(2,1)S(1)} %get-tuple-element.218), channel_id=1, source_target_pairs={{0,24},{1,25},{2,26},{3,27},{4,28},{5,29},{6,30},{7,31},{8,16},{9,... | collective-permute-start | bytes 221192 | tf_op jit(solution)/shard_map/ppermute | solution.py:571
  100.7 2.3 %collective-permute-start.29 = (bf16[1,48,384]{2,1,0:T(8,128)(2,1)S(1)}, bf16[1,48,384]{2,1,0:T(8,128)(2,1)S(1)}, u32[]{:S(2)}, u32[]{:S(2)}) collective-permute-start(bf16[1,48,384]{2,1,0:T(8,128)(2,1)S(1)} %get-tuple-element.214), channel_id=1, source_target_pairs={{0,8},{1,9},{2,10},{3,11},{4,12},{5,13},{6,14},{7,15},{8,0},{9,1},... | collective-permute-start | bytes 110600 | tf_op jit(solution)/shard_map/ppermute | solution.py:571
  106.3 2.5 %collective-permute-done.30.refs_2_ = bf16[1,48,384]{2,1,0:T(8,128)(2,1)S(1)} collective-permute-done((bf16[1,48,384]{2,1,0:T(8,128)(2,1)S(1)}, bf16[1,48,384]{2,1,0:T(8,128)(2,1)S(1)}, u32[]{:S(2)}, u32[]{:S(2)}) %collective-permute-start.30) | collective-permute-done | bytes 36896 | tf_op jit(solution)/shard_map/ppermute | solution.py:571
  110.2 2.4 %collective-permute-start.37 = (f32[32,384]{1,0:T(8,128)S(1)}, f32[32,384]{1,0:T(8,128)S(1)}, u32[]{:S(2)}, u32[]{:S(2)}) collective-permute-start(f32[32,384]{1,0:T(8,128)S(1)} %add.80), channel_id=1, source_target_pairs={{0,6},{1,7},{2,4},{3,5},{4,2},{5,3},{6,0},{7,1},{8,14},{9,15},{10,... | collective-permute-start | bytes 147464 | tf_op jit(solution)/shard_map/ppermute | solution.py:571
  113.8 1.8 %collective-permute-done.37 = f32[32,384]{1,0:T(8,128)S(1)} collective-permute-done((f32[32,384]{1,0:T(8,128)S(1)}, f32[32,384]{1,0:T(8,128)S(1)}, u32[]{:S(2)}, u32[]{:S(2)}) %collective-permute-start.37) | collective-permute-done | bytes 49184 | tf_op jit(solution)/shard_map/ppermute | solution.py:571
  117.3 1.8 %collective-permute-start.40 = (f32[32,384]{1,0:T(8,128)S(1)}, f32[32,384]{1,0:T(8,128)S(1)}, u32[]{:S(2)}, u32[]{:S(2)}) collective-permute-start(f32[32,384]{1,0:T(8,128)S(1)} %add_add_fusion.1), channel_id=1, source_target_pairs={{0,24},{1,25},{2,26},{3,27},{4,28},{5,29},{6,30},{7,31},{8,16},{9,... | collective-permute-start | bytes 147464 | tf_op jit(solution)/shard_map/ppermute | solution.py:571
  119.1 2.7 %collective-permute-start.38 = (f32[32,384]{1,0:T(8,128)S(1)}, f32[32,384]{1,0:T(8,128)S(1)}, u32[]{:S(2)}, u32[]{:S(2)}) collective-permute-start(f32[32,384]{1,0:T(8,128)S(1)} %add_add_fusion.1), channel_id=1, source_target_pairs={{0,16},{1,17},{2,18},{3,19},{4,20},{5,21},{6,22},{7,23},{8,24},{9,... | collective-permute-start | bytes 147464 | tf_op jit(solution)/shard_map/ppermute | solution.py:571
  (154 shorter events, 36.2 us)
Async XLA Ops:
  1.7 9.5 %collective-permute-start.2 = (bf16[1,48,384]{2,1,0:T(8,128)(2,1)S(1)}, bf16[1,48,384]{2,1,0:T(8,128)(2,1)S(1)}, u32[]{:S(2)}, u32[]{:S(2)}) collective-permute-start(bf16[1,48,384]{2,1,0:T(8,128)(2,1)S(1)} %bitcast.47), channel_id=1, source_target_pairs={{0,24},{1,25},{2,26},{3,27},{4,28},{5,29},{6,30},{7,31},{8,16},{9,... | collective-permute-start | bytes 110600 | tf_op jit(solution)/shard_map/ppermute | solution.py:571
  6.9 5.8 %collective-permute-start = (bf16[1,48,384]{2,1,0:T(8,128)(2,1)S(1)}, bf16[1,48,384]{2,1,0:T(8,128)(2,1)S(1)}, u32[]{:S(2)}, u32[]{:S(2)}) collective-permute-start(bf16[1,48,384]{2,1,0:T(8,128)(2,1)S(1)} %bitcast.49), channel_id=1, source_target_pairs={{0,16},{1,17},{2,18},{3,19},{4,20},{5,21},{6,22},{7,23},{8,24},{9,... | collective-permute-start | bytes 110600 | tf_op jit(solution)/shard_map/ppermute | solution.py:571
  7.5 18.6 %collective-permute-start.12 = (bf16[1,96,384]{2,1,0:T(8,128)(2,1)S(1)}, bf16[1,96,384]{2,1,0:T(8,128)(2,1)S(1)}, u32[]{:S(2)}, u32[]{:S(2)}) collective-permute-start(bf16[1,96,384]{2,1,0:T(8,128)(2,1)S(1)} %bitcast.42), channel_id=1, source_target_pairs={{0,24},{1,25},{2,26},{3,27},{4,28},{5,29},{6,30},{7,31},{8,16},{9,... | collective-permute-start | bytes 221192 | tf_op jit(solution)/shard_map/ppermute | solution.py:571
  11.2 15.4 %collective-permute-start.11 = (bf16[1,96,384]{2,1,0:T(8,128)(2,1)S(1)}, bf16[1,96,384]{2,1,0:T(8,128)(2,1)S(1)}, u32[]{:S(2)}, u32[]{:S(2)}) collective-permute-start(bf16[1,96,384]{2,1,0:T(8,128)(2,1)S(1)} %bitcast.43), channel_id=1, source_target_pairs={{0,8},{1,9},{2,10},{3,11},{4,12},{5,13},{6,14},{7,15},{8,0},{9,1},... | collective-permute-start | bytes 221192 | tf_op jit(solution)/shard_map/ppermute | solution.py:571
  12.7 7.5 %collective-permute-start.5 = (bf16[4,48,384]{2,1,0:T(8,128)(2,1)S(1)}, bf16[4,48,384]{2,1,0:T(8,128)(2,1)S(1)}, u32[]{:S(2)}, u32[]{:S(2)}) collective-permute-start(bf16[4,48,384]{2,1,0:T(8,128)(2,1)S(1)} %pad_maximum_fusion.4.refs_0_), channel_id=1, source_target_pairs={{0,6},{1,7},{2,4},{3,5},{4,2},{5,3},{6,0},{7,1},{8,14},{9,15},{10,... | collective-permute-start | bytes 442376 | tf_op jit(solution)/shard_map/ppermute | solution.py:571
  15.2 8.6 %collective-permute-start.4 = (bf16[4,48,384]{2,1,0:T(8,128)(2,1)S(1)}, bf16[4,48,384]{2,1,0:T(8,128)(2,1)S(1)}, u32[]{:S(2)}, u32[]{:S(2)}) collective-permute-start(bf16[4,48,384]{2,1,0:T(8,128)(2,1)S(1)} %pad_maximum_fusion.4.refs_0_), channel_id=1, source_target_pairs={{0,4},{1,5},{2,6},{3,7},{4,0},{5,1},{6,2},{7,3},{8,12},{9,13},{10,... | collective-permute-start | bytes 442376 | tf_op jit(solution)/shard_map/ppermute | solution.py:571
  15.8 8.1 %collective-permute-start.3 = (bf16[4,48,384]{2,1,0:T(8,128)(2,1)S(1)}, bf16[4,48,384]{2,1,0:T(8,128)(2,1)S(1)}, u32[]{:S(2)}, u32[]{:S(2)}) collective-permute-start(bf16[4,48,384]{2,1,0:T(8,128)(2,1)S(1)} %pad_maximum_fusion.4.refs_0_), channel_id=1, source_target_pairs={{0,2},{1,3},{2,0},{3,1},{4,6},{5,7},{6,4},{7,5},{8,10},{9,11},{10,... | collective-permute-start | bytes 442376 | tf_op jit(solution)/shard_map/ppermute | solution.py:571
  20.3 5.3 %collective-permute-start.6 = (bf16[1,96,384]{2,1,0:T(8,128)(2,1)S(1)}, bf16[1,96,384]{2,1,0:T(8,128)(2,1)S(1)}, u32[]{:S(2)}, u32[]{:S(2)}) collective-permute-start(bf16[1,96,384]{2,1,0:T(8,128)(2,1)S(1)} %bitcast.44), channel_id=1, source_target_pairs={{0,16},{1,17},{2,18},{3,19},{4,20},{5,21},{6,22},{7,23},{8,24},{9,... | collective-permute-start | bytes 221192 | tf_op jit(solution)/shard_map/ppermute | solution.py:571
  26.7 11.0 %collective-permute-start.15 = (bf16[4,96,384]{2,1,0:T(8,128)(2,1)S(1)}, bf16[4,96,384]{2,1,0:T(8,128)(2,1)S(1)}, u32[]{:S(2)}, u32[]{:S(2)}) collective-permute-start(bf16[4,96,384]{2,1,0:T(8,128)(2,1)S(1)} %pad_maximum_fusion.3.refs_0_), channel_id=1, source_target_pairs={{0,6},{1,7},{2,4},{3,5},{4,2},{5,3},{6,0},{7,1},{8,14},{9,15},{10,... | collective-permute-start | bytes 884744 | tf_op jit(solution)/shard_map/ppermute | solution.py:571
  29.2 13.8 %collective-permute-start.14 = (bf16[4,96,384]{2,1,0:T(8,128)(2,1)S(1)}, bf16[4,96,384]{2,1,0:T(8,128)(2,1)S(1)}, u32[]{:S(2)}, u32[]{:S(2)}) collective-permute-start(bf16[4,96,384]{2,1,0:T(8,128)(2,1)S(1)} %pad_maximum_fusion.3.refs_0_), channel_id=1, source_target_pairs={{0,4},{1,5},{2,6},{3,7},{4,0},{5,1},{6,2},{7,3},{8,12},{9,13},{10,... | collective-permute-start | bytes 884744 | tf_op jit(solution)/shard_map/ppermute | solution.py:571
  29.7 13.3 %collective-permute-start.13 = (bf16[4,96,384]{2,1,0:T(8,128)(2,1)S(1)}, bf16[4,96,384]{2,1,0:T(8,128)(2,1)S(1)}, u32[]{:S(2)}, u32[]{:S(2)}) collective-permute-start(bf16[4,96,384]{2,1,0:T(8,128)(2,1)S(1)} %pad_maximum_fusion.3.refs_0_), channel_id=1, source_target_pairs={{0,2},{1,3},{2,0},{3,1},{4,6},{5,7},{6,4},{7,5},{8,10},{9,11},{10,... | collective-permute-start | bytes 884744 | tf_op jit(solution)/shard_map/ppermute | solution.py:571
  62.5 14.4 %collective-permute-start.21 = (bf16[4,96,384]{2,1,0:T(8,128)(2,1)S(1)}, bf16[4,96,384]{2,1,0:T(8,128)(2,1)S(1)}, u32[]{:S(2)}, u32[]{:S(2)}) collective-permute-start(bf16[4,96,384]{2,1,0:T(8,128)(2,1)S(1)} %get-tuple-element.181), channel_id=1, source_target_pairs={{0,2},{1,3},{2,0},{3,1},{4,6},{5,7},{6,4},{7,5},{8,10},{9,11},{10,... | collective-permute-start | bytes 884744 | tf_op jit(solution)/shard_map/ppermute | solution.py:571
  64.0 12.9 %collective-permute-start.22 = (bf16[4,96,384]{2,1,0:T(8,128)(2,1)S(1)}, bf16[4,96,384]{2,1,0:T(8,128)(2,1)S(1)}, u32[]{:S(2)}, u32[]{:S(2)}) collective-permute-start(bf16[4,96,384]{2,1,0:T(8,128)(2,1)S(1)} %get-tuple-element.182), channel_id=1, source_target_pairs={{0,4},{1,5},{2,6},{3,7},{4,0},{5,1},{6,2},{7,3},{8,12},{9,13},{10,... | collective-permute-start | bytes 884744 | tf_op jit(solution)/shard_map/ppermute | solution.py:571
  65.5 13.9 %collective-permute-start.23 = (bf16[4,96,384]{2,1,0:T(8,128)(2,1)S(1)}, bf16[4,96,384]{2,1,0:T(8,128)(2,1)S(1)}, u32[]{:S(2)}, u32[]{:S(2)}) collective-permute-start(bf16[4,96,384]{2,1,0:T(8,128)(2,1)S(1)} %get-tuple-element.183), channel_id=1, source_target_pairs={{0,6},{1,7},{2,4},{3,5},{4,2},{5,3},{6,0},{7,1},{8,14},{9,15},{10,... | collective-permute-start | bytes 884744 | tf_op jit(solution)/shard_map/ppermute | solution.py:571
  81.5 16.8 %collective-permute-start.25 = (bf16[4,48,384]{2,1,0:T(8,128)(2,1)S(1)}, bf16[4,48,384]{2,1,0:T(8,128)(2,1)S(1)}, u32[]{:S(2)}, u32[]{:S(2)}) collective-permute-start(bf16[4,48,384]{2,1,0:T(8,128)(2,1)S(1)} %get-tuple-element.197), channel_id=1, source_target_pairs={{0,2},{1,3},{2,0},{3,1},{4,6},{5,7},{6,4},{7,5},{8,10},{9,11},{10,... | collective-permute-start | bytes 442376 | tf_op jit(solution)/shard_map/ppermute | solution.py:571
  83.0 17.2 %collective-permute-start.26 = (bf16[4,48,384]{2,1,0:T(8,128)(2,1)S(1)}, bf16[4,48,384]{2,1,0:T(8,128)(2,1)S(1)}, u32[]{:S(2)}, u32[]{:S(2)}) collective-permute-start(bf16[4,48,384]{2,1,0:T(8,128)(2,1)S(1)} %get-tuple-element.198), channel_id=1, source_target_pairs={{0,4},{1,5},{2,6},{3,7},{4,0},{5,1},{6,2},{7,3},{8,12},{9,13},{10,... | collective-permute-start | bytes 442376 | tf_op jit(solution)/shard_map/ppermute | solution.py:571
  84.5 15.7 %collective-permute-start.27 = (bf16[4,48,384]{2,1,0:T(8,128)(2,1)S(1)}, bf16[4,48,384]{2,1,0:T(8,128)(2,1)S(1)}, u32[]{:S(2)}, u32[]{:S(2)}) collective-permute-start(bf16[4,48,384]{2,1,0:T(8,128)(2,1)S(1)} %get-tuple-element.199), channel_id=1, source_target_pairs={{0,6},{1,7},{2,4},{3,5},{4,2},{5,3},{6,0},{7,1},{8,14},{9,15},{10,... | collective-permute-start | bytes 442376 | tf_op jit(solution)/shard_map/ppermute | solution.py:571
  87.6 15.4 %collective-permute-start.31 = (bf16[1,96,384]{2,1,0:T(8,128)(2,1)S(1)}, bf16[1,96,384]{2,1,0:T(8,128)(2,1)S(1)}, u32[]{:S(2)}, u32[]{:S(2)}) collective-permute-start(bf16[1,96,384]{2,1,0:T(8,128)(2,1)S(1)} %get-tuple-element.216), channel_id=1, source_target_pairs={{0,16},{1,17},{2,18},{3,19},{4,20},{5,21},{6,22},{7,23},{8,24},{9,... | collective-permute-start | bytes 221192 | tf_op jit(solution)/shard_map/ppermute | solution.py:571
  88.9 15.8 %collective-permute-start.32 = (bf16[1,96,384]{2,1,0:T(8,128)(2,1)S(1)}, bf16[1,96,384]{2,1,0:T(8,128)(2,1)S(1)}, u32[]{:S(2)}, u32[]{:S(2)}) collective-permute-start(bf16[1,96,384]{2,1,0:T(8,128)(2,1)S(1)} %get-tuple-element.217), channel_id=1, source_target_pairs={{0,8},{1,9},{2,10},{3,11},{4,12},{5,13},{6,14},{7,15},{8,0},{9,1},... | collective-permute-start | bytes 221192 | tf_op jit(solution)/shard_map/ppermute | solution.py:571
  98.4 6.3 %collective-permute-start.33 = (bf16[1,96,384]{2,1,0:T(8,128)(2,1)S(1)}, bf16[1,96,384]{2,1,0:T(8,128)(2,1)S(1)}, u32[]{:S(2)}, u32[]{:S(2)}) collective-permute-start(bf16[1,96,384]{2,1,0:T(8,128)(2,1)S(1)} %get-tuple-element.218), channel_id=1, source_target_pairs={{0,24},{1,25},{2,26},{3,27},{4,28},{5,29},{6,30},{7,31},{8,16},{9,... | collective-permute-start | bytes 221192 | tf_op jit(solution)/shard_map/ppermute | solution.py:571
  100.3 6.1 %collective-permute-start.28 = (bf16[1,48,384]{2,1,0:T(8,128)(2,1)S(1)}, bf16[1,48,384]{2,1,0:T(8,128)(2,1)S(1)}, u32[]{:S(2)}, u32[]{:S(2)}) collective-permute-start(bf16[1,48,384]{2,1,0:T(8,128)(2,1)S(1)} %get-tuple-element.213), channel_id=1, source_target_pairs={{0,16},{1,17},{2,18},{3,19},{4,20},{5,21},{6,22},{7,23},{8,24},{9,... | collective-permute-start | bytes 110600 | tf_op jit(solution)/shard_map/ppermute | solution.py:571
  100.7 5.6 %collective-permute-start.29 = (bf16[1,48,384]{2,1,0:T(8,128)(2,1)S(1)}, bf16[1,48,384]{2,1,0:T(8,128)(2,1)S(1)}, u32[]{:S(2)}, u32[]{:S(2)}) collective-permute-start(bf16[1,48,384]{2,1,0:T(8,128)(2,1)S(1)} %get-tuple-element.214), channel_id=1, source_target_pairs={{0,8},{1,9},{2,10},{3,11},{4,12},{5,13},{6,14},{7,15},{8,0},{9,1},... | collective-permute-start | bytes 110600 | tf_op jit(solution)/shard_map/ppermute | solution.py:571
  103.0 5.8 %collective-permute-start.30 = (bf16[1,48,384]{2,1,0:T(8,128)(2,1)S(1)}, bf16[1,48,384]{2,1,0:T(8,128)(2,1)S(1)}, u32[]{:S(2)}, u32[]{:S(2)}) collective-permute-start(bf16[1,48,384]{2,1,0:T(8,128)(2,1)S(1)} %get-tuple-element.215), channel_id=1, source_target_pairs={{0,24},{1,25},{2,26},{3,27},{4,28},{5,29},{6,30},{7,31},{8,16},{9,... | collective-permute-start | bytes 110600 | tf_op jit(solution)/shard_map/ppermute | solution.py:571
  117.3 6.1 %collective-permute-start.40 = (f32[32,384]{1,0:T(8,128)S(1)}, f32[32,384]{1,0:T(8,128)S(1)}, u32[]{:S(2)}, u32[]{:S(2)}) collective-permute-start(f32[32,384]{1,0:T(8,128)S(1)} %add_add_fusion.1), channel_id=1, source_target_pairs={{0,24},{1,25},{2,26},{3,27},{4,28},{5,29},{6,30},{7,31},{8,16},{9,... | collective-permute-start | bytes 147464 | tf_op jit(solution)/shard_map/ppermute | solution.py:571
  (45 other events, 622.8 us)

commit v6 on v5

--- a/solution.py
+++ b/solution.py
@@ -30,6 +30,7 @@
 LANES = GROUP * HD
 BLOCKS = 32
 PIECE = 48
+EARLY = 16
 TALL, WIDE = 320, 256
 
 EPS_NORM = 1e-05
@@ -92,16 +93,16 @@
                 far = np.where(same, np.maximum(source[w][:, None], source[w][None, :]), NEVER)
                 far = np.where(np.eye(WIN, dtype=bool) & real[:, None], -1.0, far)
                 reach[pair, kind, :, side * WIN : (side + 1) * WIN] = far
-    row, col = cell // WS, cell % WS
-    offset = (row[None, :] - row[:, None] + WS - 1) * (2 * WS - 1) + col[None, :] - col[:, None] + WS - 1
-    offset = np.where(real[None, :] & real[:, None], offset, -1)
-    lookup = (offset.reshape(1, -1) == np.arange(REL)[:, None]).astype(np.float32)
+    offset = (2 * WS - 1) * (cell // WS) + cell % WS
+    shifts = [int(value) for value in offset[:CELLS]]
+    wanted = np.where(real, offset + REL // 2, -1)
+    lookup = (np.arange(256)[:, None] == np.concatenate([wanted, wanted])[None, :]).astype(np.float32)
     heads = (np.arange(LANES)[None, :] // HD == np.arange(GROUP)[:, None]).astype(np.float32)
     heads = np.repeat(np.concatenate([heads, heads], axis=1), WIN, axis=0)
-    return deal, place, reach, lookup, heads
-
-
-DEAL, PLACE, REACH, LOOKUP, HEADS = window_tables()
+    return deal, place, reach, lookup, heads, shifts
+
+
+DEAL, PLACE, REACH, LOOKUP, HEADS, SHIFTS = window_tables()
 
 
 def dot_nn(a, b):
@@ -198,10 +199,12 @@
 
 
 def pack_body(qkv_ref, proj_ref, fc1_ref, fc2_ref, near_ref, far_ref):
-    near_ref[...] = jnp.concatenate([qkv_ref[0], qkv_ref[1], qkv_ref[2], proj_ref[...]], axis=1).astype(LOW)
     depth = fc1_ref.shape[0]
-    far_ref[:depth] = fc1_ref[...].astype(LOW)
-    far_ref[depth:] = fc2_ref[...].astype(LOW)
+    early = near_ref.shape[0] - depth
+    near_ref[:depth] = jnp.concatenate([qkv_ref[0], qkv_ref[1], qkv_ref[2], proj_ref[...]], axis=1).astype(LOW)
+    near_ref[depth:] = fc1_ref[:early].astype(LOW)
+    far_ref[: depth - early] = fc1_ref[early:].astype(LOW)
+    far_ref[depth - early :] = fc2_ref[...].astype(LOW)
 
 
 def first_sum_body(keep_ref, got_ref, stays_ref, *goes_refs):
@@ -236,36 +239,86 @@
     spare[24:32] = jnp.broadcast_to(squares, (8, C))
 
 
-def prep_body(
-    tok_hbm, cot_hbm, deal_hbm, vec_hbm, x_hbm, g_hbm, n_ref, tok, cot, deal, vec, x_all, g_all, pad, sems, out_sems
-):
-    copies = [
-        pltpu.make_async_copy(source, target, sems.at[index])
-        for index, (source, target) in enumerate(((vec_hbm, vec), (deal_hbm, deal), (tok_hbm, tok), (cot_hbm, cot)))
-    ]
+def three_parts(values):
+    first = values.astype(LOW).astype(F32)
+    second = (values - first).astype(LOW).astype(F32)
+    return jnp.concatenate([first, second, values - first - second], axis=0)
+
+
+def fetch(pairs, sems):
+    copies = [pltpu.make_async_copy(source, target, sems.at[index]) for index, (source, target) in enumerate(pairs)]
     for copy in copies:
         copy.start()
+    return copies
+
+
+def deal_rows(source, deal, pad, image):
+    for r in range(GRID):
+        pad[image, 16 * r : 16 * r + GRID, :] = source[image, 0, r]
+    return dot_nn(deal[...], pad[image])
+
+
+def prep_body(
+    table_hbm, lookup_hbm, vec_hbm, deal_hbm, tok_hbm, x_hbm, unit_hbm, n_ref, bias_ref,
+    table, lookup, vec, deal, tok, x_all, unit_all, padded, pad, sems, out_sems
+):
+    copies = fetch(
+        ((table_hbm, table), (lookup_hbm, lookup), (vec_hbm, vec), (deal_hbm, deal), (tok_hbm, tok)), sems
+    )
+    padded[...] = jnp.zeros_like(padded)
+    pad[...] = jnp.zeros_like(pad)
+    bias_ref[...] = jnp.zeros_like(bias_ref)
+    copies[0].wait()
+    padded[:NH, :REL] = table[...]
+    parts = three_parts(padded[...])
+    moved = [pltpu.roll(parts, shift, 1) if shift else parts for shift in SHIFTS]
+    copies[1].wait()
+    spread = dot_nn(jnp.concatenate(moved, axis=0).astype(LOW), lookup[...])
+    for k in range(CELLS):
+        rows = spread[48 * k : 48 * k + 48]
+        bias_ref[pl.ds(k, NH, stride=WIN), :] = (rows[:16] + (rows[16:32] + rows[32:]))[:NH]
+    for copy in copies[2:]:
+        copy.wait()
+    stores, made = [], []
+    for image in range(MICRO):
+        at = slice(image * IMG, (image + 1) * IMG)
+        made.append(deal_rows(tok, deal, pad, image))
+        x_all[at, :] = made[-1].astype(LOW)
+        stores.append(pltpu.make_async_copy(x_all.at[at], x_hbm.at[at], out_sems.at[image, 0]))
+        stores[-1].start()
+    for image in range(MICRO):
+        at = slice(image * IMG, (image + 1) * IMG)
+        unit, _ = norm_parts(made[image])
+        unit_all[at, :] = unit.astype(LOW)
+        stores.append(pltpu.make_async_copy(unit_all.at[at], unit_hbm.at[at], out_sems.at[image, 1]))
+        stores[-1].start()
+        n_ref[at, :] = (unit * vec[0:1] + vec[1:2]).astype(LOW)
+    for store in stores:
+        store.wait()
+
+
+def prep_grad_body(deal_hbm, cot_hbm, g_ref, deal, cot, pad, sems):
+    copies = fetch(((deal_hbm, deal), (cot_hbm, cot)), sems)
     pad[...] = jnp.zeros_like(pad)
     for copy in copies:
         copy.wait()
     for image in range(MICRO):
-        for r in range(GRID):
-            pad[image, 0, 16 * r : 16 * r + GRID, :] = tok[image, 0, r]
-            pad[image, 1, 16 * r : 16 * r + GRID, :] = cot[image, 0, r]
-    stores, made = [], []
-    for image in range(MICRO):
-        at = slice(image * IMG, (image + 1) * IMG)
-        made.append(dot_nn(deal[...], pad[image, 0]))
-        x_all[at, :] = made[-1].astype(LOW)
-        g_all[at, :] = dot_nn(deal[...], pad[image, 1]).astype(LOW)
-        for index, (source, target) in enumerate(((x_all, x_hbm), (g_all, g_hbm))):
-            stores.append(pltpu.make_async_copy(source.at[at], target.at[at], out_sems.at[image, index]))
-            stores[-1].start()
-    for image in range(MICRO):
-        unit, _ = norm_parts(made[image])
-        n_ref[image * IMG : (image + 1) * IMG, :] = (unit * vec[0:1] + vec[1:2]).astype(LOW)
-    for store in stores:
-        store.wait()
+        g_ref[image * IMG : (image + 1) * IMG, :] = deal_rows(cot, deal, pad, image).astype(LOW)
+
+
+def table_body(sums_ref, lookup_ref, table_ref, padded):
+    padded[...] = jnp.zeros_like(padded)
+    slabs = []
+    for k in range(CELLS):
+        padded[:NH, :] = sums_ref[pl.ds(k, NH, stride=WIN), :]
+        slabs.append(three_parts(padded[...]))
+    made = dot_nt(jnp.concatenate(slabs, axis=0).astype(LOW), lookup_ref[...])
+    total = jnp.zeros((16, 256), F32)
+    for k, shift in enumerate(SHIFTS):
+        rows = made[48 * k : 48 * k + 48]
+        rows = rows[:16] + (rows[16:32] + rows[32:])
+        total = total + (pltpu.roll(rows, 256 - shift, 1) if shift else rows)
+    table_ref[...] = total[:NH, :REL]
 
 
 def put_back(rows, back_ref, target, image):
@@ -304,7 +357,7 @@
     for j in range(BLOCKS):
         at = table_ref[ME] ^ block_at(j) if direct else (j % 8) * 4 + j // 8
         row = at // 4 * PIECE if not direct else pl.multiple_of((at >> 2) * PIECE, PIECE)
-        parts[at & 3, pl.ds(row, PIECE), :] = near_refs[j // 4][j % 4]
+        parts[at & 3, pl.ds(row, PIECE), :] = near_refs[j // 4][j % 4, :PIECE]
     for w in range(3):
         wq_ref[:, w * C : (w + 1) * C] = jnp.concatenate([parts[h, :, w * 96 : (w + 1) * 96] for h in range(4)], axis=1)
     wp_ref[...] = jnp.concatenate([parts[h, :, 288:] for h in range(4)], axis=1)
@@ -359,13 +412,15 @@
 def mlp_body(
     direct, table_ref, middle_ref, n_ref, g_ref, vec_ref, *refs,
 ):
-    far_refs, (hidden_ref, grad_hidden_ref, grad_ref, sums_ref, w2_ref, w1, bias, bias_sum) = refs[:PIECES], refs[PIECES:]
+    near_refs, far_refs, refs = refs[:PIECES], refs[PIECES : 2 * PIECES], refs[2 * PIECES :]
+    (hidden_ref, grad_hidden_ref, grad_ref, sums_ref, w2_ref, w1, bias, bias_sum) = refs
     for j in range(BLOCKS):
         at = table_ref[ME] ^ block_at(j) if direct else (j % 8) * 4 + j // 8
         row = at // 4 * PIECE if not direct else pl.multiple_of((at >> 2) * PIECE, PIECE)
         col = at % 4 * C if not direct else pl.multiple_of((at & 3) * C, C)
-        w1[pl.ds(row, PIECE), pl.ds(col, C)] = far_refs[j // 4][j % 4, :PIECE]
-        w2_ref[pl.ds(row, PIECE), pl.ds(col, C)] = far_refs[j // 4][j % 4, PIECE:]
+        w1[pl.ds(row, EARLY), pl.ds(col, C)] = near_refs[j // 4][j % 4, PIECE:]
+        w1[pl.ds(row + EARLY, PIECE - EARLY), pl.ds(col, C)] = far_refs[j // 4][j % 4, : PIECE - EARLY]
+        w2_ref[pl.ds(row, PIECE), pl.ds(col, C)] = far_refs[j // 4][j % 4, PIECE - EARLY :]
     for r in range(4):
         bias[:, r * C : (r + 1) * C] = vec_ref[8 + r : 9 + r]
     sums_ref[...] = jnp.zeros_like(sums_ref)
@@ -476,13 +531,27 @@
             packed_grad_ref[rows, at : at + LANES] = (own_rows(grad_queries) * HD ** (-0.5)).astype(LOW)
             packed_grad_ref[rows, C + at : C + at + LANES] = (own_keys(grad_keys, heads_ref) * HD ** (-0.5)).astype(LOW)
             packed_grad_ref[rows, 2 * C + at : 2 * C + at + LANES] = own_keys(grad_values, heads_ref).astype(LOW)
-        sums_ref[0:1] += jnp.sum(packed_grad_ref[at_image, :C].astype(F32), axis=0, keepdims=True)
-        sums_ref[1:2] += jnp.sum(packed_grad_ref[at_image, 2 * C :].astype(F32), axis=0, keepdims=True)
-
-
-def attend_weights_body(direct, table_ref, n_ref, grad_low_ref, packed_grad_ref, attn_ref, keep_ref, send_ref, made):
-    n_turned = n_ref[...].T
-    parts = [dot_nn(n_turned, packed_grad_ref[:, w * C : (w + 1) * C]).astype(LOW) for w in range(3)]
+        sums_ref[...] += jnp.sum(packed_grad_ref[at_image, :].astype(F32), axis=0, keepdims=True)
+
+
+def attend_weights_body(
+    direct, table_ref, unit_ref, grad_low_ref, packed_grad_ref, attn_ref, wq_ref, sums_ref, vec_ref, keep_ref, send_ref, norm_ref, made
+):
+    unit_turned = unit_ref[...].T
+    turned_vec = vec_ref[...].T
+    gain, shift = turned_vec[:, 0:1], turned_vec[:, 1:2]
+    parts = []
+    gain_grad = jnp.zeros((C, 1), F32)
+    shift_grad = jnp.zeros((C, 1), F32)
+    for w in range(3):
+        cols = slice(w * C, (w + 1) * C)
+        product = dot_nn(unit_turned, packed_grad_ref[:, cols])
+        weight, sums = wq_ref[:, cols].astype(F32), sums_ref[:, cols]
+        parts.append((product * gain + shift * sums).astype(LOW))
+        gain_grad = gain_grad + jnp.sum(product * weight, axis=1, keepdims=True)
+        shift_grad = shift_grad + jnp.sum(weight * sums, axis=1, keepdims=True)
+    norm_ref[0:1] = jnp.broadcast_to(gain_grad, (C, 128)).T[0:1]
+    norm_ref[1:2] = jnp.broadcast_to(shift_grad, (C, 128)).T[0:1]
     parts.append(dot_nn(grad_low_ref[...].T, attn_ref[...]).astype(LOW))
     for h in range(4):
         block = jnp.concatenate([part[:, h * 96 : (h + 1) * 96] for part in parts], axis=1)
@@ -492,33 +561,34 @@
     send_ref[...] = made[BLOCKS // 2 :]
 
 
-def input_body(
-    wq_hbm, packed_grad_hbm, x_hbm, grad_hbm, vec_ref, back_ref, out_ref, sums_ref, wq, packed_grad, x_all, grad_all, wq_sem, sems
-):
-    sums_ref[...] = jnp.zeros_like(sums_ref)
+def input_body(first, last, *refs):
+    wq_hbm, packed_grad_hbm, x_hbm, grad_hbm = refs[:4]
+    refs = refs[4 + (first > 0) :]
+    vec_ref, back_ref, out_hbm, wq, packed_grad, x_all, grad_all, made, wq_sem, sems, out_sems = refs
+    images = range(last - first)
     whole_copy = pltpu.make_async_copy(wq_hbm, wq, wq_sem)
     whole_copy.start()
     copies = []
-    for image in range(MICRO):
+    for image in images:
+        source_at = slice((first + image) * IMG, (first + image + 1) * IMG)
         at = slice(image * IMG, (image + 1) * IMG)
         for index, (source, target) in enumerate(((packed_grad_hbm, packed_grad), (x_hbm, x_all), (grad_hbm, grad_all))):
-            copies.append(pltpu.make_async_copy(source.at[at], target.at[at], sems.at[image, index]))
+            copies.append(pltpu.make_async_copy(source.at[source_at], target.at[at], sems.at[image, index]))
             copies[-1].start()
     whole_copy.wait()
-    backs = []
-    for image in range(MICRO):
+    stores = []
+    for image in images:
+        at = slice(image * IMG, (image + 1) * IMG)
         for copy in copies[3 * image : 3 * image + 3]:
             copy.wait()
-        backs.append(dot_nt(packed_grad[image * IMG : (image + 1) * IMG, :], wq[...]))
-    made = []
-    for image, back in enumerate(backs):
-        at = slice(image * IMG, (image + 1) * IMG)
+        back = dot_nt(packed_grad[at, :], wq[...])
         unit, inverse = norm_parts(x_all[at, :].astype(F32))
-        sums_ref[0:1] += jnp.sum(back * unit, axis=0, keepdims=True)
-        sums_ref[1:2] += jnp.sum(back, axis=0, keepdims=True)
-        made.append((grad_all[at, :] + norm_back(back, unit, inverse, vec_ref[0:1])).astype(LOW))
-    for image in range(MICRO):
-        put_back(made[image], back_ref, out_ref, image)
+        rows = grad_all[at, :] + norm_back(back, unit, inverse, vec_ref[0:1])
+        put_back(rows, back_ref, made, image)
+        stores.append(pltpu.make_async_copy(made.at[image], out_hbm.at[first + image], out_sems.at[image]))
+        stores[-1].start()
+    for store in stores:
+        store.wait()
 
 
 def adam_update(weight, first, second, gradient, rate, decay):
@@ -571,17 +641,22 @@
         return lax.ppermute(rows, BOTH, [(i, i ^ mask) for i in range(devices)])
 
     depth = fc1_weight.shape[0]
+    early = depth * EARLY // PIECE
     near, far = pl.pallas_call(
-        pack_body, out_shape=(sds((depth, C), LOW), sds((2 * depth, C), LOW)), compiler_params=whole(8), name="pack"
+        pack_body, out_shape=(sds((depth + early, C), LOW), sds((2 * depth - early, C), LOW)), compiler_params=whole(8), name="pack"
     )(*streamed(qkv_weight, proj_weight.T, fc1_weight, fc2_weight.T))
 
     def gather_plain(piece):
         spread = lax.all_gather(lax.all_gather(piece, "tok", axis=0), "head", axis=0)
-        half = piece.shape[0] // depth
-        spread = spread.reshape(heads, toks, half, depth, C).transpose(0, 2, 1, 3, 4)
-        spread = spread.reshape(heads, half, 8, PIECE, C).transpose(0, 2, 1, 3, 4)
-        spread = spread.reshape(BLOCKS, half * PIECE, C)
-        return [spread[at : at + 4] for at in range(0, BLOCKS, 4)]
+        return spread.reshape(BLOCKS, PIECE, C)
+
+    def plain_pieces(near, far):
+        one = gather_plain(near[:depth])
+        two = gather_plain(jnp.concatenate([near[depth:], far[: depth - early]], axis=0))
+        three = gather_plain(far[depth - early :])
+        near = jnp.concatenate([one, two[:, :EARLY]], axis=1)
+        far = jnp.concatenate([two[:, EARLY:], three], axis=1)
+        return [[array[at : at + 4] for at in range(0, BLOCKS, 4)] for array in (near, far)]
 
     def share_plain(keep, send):
         both = jnp.concatenate([keep, send], axis=0)
@@ -614,49 +689,51 @@
     def sent(parts, masks):
         return [passed(part, mask) for part, mask in zip(parts, masks)]
 
-    def total_of(rows, masks):
-        one, two, three = spread(rows, masks)
-        return (rows + one) + (two + three)
-
     back = jnp.asarray(DEAL.T, LOW)
     deal = jnp.asarray(DEAL, LOW)
+    lookup = jnp.asarray(LOOKUP, LOW)
     place = jnp.asarray(PLACE)
     reach = jnp.asarray(REACH)
     heads_low = jnp.asarray(HEADS, LOW)
-    def prepare(tokens, cotangents):
-        image = (MICRO, 1, GRID, GRID, C)
-        return call(
+    whole_images = pltpu.VMEM((MICRO, 1, GRID, GRID, C), LOW)
+
+    def prepare(tokens, values):
+        x_rows, unit_rows, n_rows, bias = call(
             prep_body,
-            [((ROWS, C), LOW)] * 3,
-            (tokens, cotangents, deal, vectors),
+            [((ROWS, C), LOW)] * 3 + [((NH * WIN, 128), F32)],
+            (values.T, lookup, vectors, deal, tokens),
             "prep",
             scratch=[
-                pltpu.VMEM(image, LOW), pltpu.VMEM(image, LOW), pltpu.VMEM((IMG, PAD), LOW), pltpu.VMEM((12, C), F32),
-                pltpu.VMEM((ROWS, C), LOW), pltpu.VMEM((ROWS, C), LOW), pltpu.VMEM((MICRO, 2, PAD, C), LOW),
-                pltpu.SemaphoreType.DMA((4,)), pltpu.SemaphoreType.DMA((MICRO, 2)),
+                pltpu.VMEM((NH, REL), F32), pltpu.VMEM((256, 128), LOW), pltpu.VMEM((12, C), F32), pltpu.VMEM((IMG, PAD), LOW),
+                whole_images, pltpu.VMEM((ROWS, C), LOW), pltpu.VMEM((ROWS, C), LOW), pltpu.VMEM((16, 256), F32),
+                pltpu.VMEM((MICRO, PAD, C), LOW), pltpu.SemaphoreType.DMA((5,)), pltpu.SemaphoreType.DMA((MICRO, 2)),
             ],
-            fetched=4,
+            flops=1e9,
+            fetched=5,
             stored=2,
         )
-
-    def product_of(values, lookup):
-        first = lax.reduce_precision(values, 8, 7)
-        second = lax.reduce_precision(values - first, 8, 7)
-        parts = jnp.concatenate([first, second, values - first - second], axis=0).astype(LOW)
-        made = jnp.dot(parts, jnp.asarray(lookup, LOW), preferred_element_type=F32).reshape(3, values.shape[0], -1)
-        return made[0] + (made[1] + made[2])
-
-    def make_bias(values):
-        made = product_of(values.T, LOOKUP).reshape(GROUPS, GROUP * WIN, WIN)
-        return jnp.concatenate([made, made], axis=2)
+        return x_rows, unit_rows, n_rows, bias.reshape(GROUPS, GROUP * WIN, 128)
+
+    def prepare_grad(cotangents):
+        (g_rows,) = call(
+            prep_grad_body,
+            [((ROWS, C), LOW)],
+            (deal, cotangents),
+            "prep_grad",
+            limit=8,
+            scratch=[pltpu.VMEM((IMG, PAD), LOW), whole_images, pltpu.VMEM((MICRO, PAD, C), LOW), pltpu.SemaphoreType.DMA((2,))],
+            fetched=2,
+        )
+        return g_rows
 
     if direct:
         near = near[None]
         near_got, far_got = spread(near, LINE), spread(far[None], LINE)
         near_all = join(near, *near_got)
-        near_all, tokens, cotangents, extent, route, rel_bias = tie(near_all, tokens_in, cotangent, extent, route, rel_table)
         near_all = [near_all] + spread(near_all, PLANE)
-        x_rows, g_rows, n_rows = prepare(tokens, cotangents)
+        far_all = join(far[None], *far_got)
+        far_all, tokens, extent, route, rel_bias = tie(far_all, tokens_in, extent, route, rel_table)
+        x_rows, unit_rows, n_rows, bias = prepare(tokens, rel_bias)
         table = jnp.concatenate(
             [
                 jnp.stack([me, swap_bits(me)]).astype(jnp.int32),
@@ -664,14 +741,12 @@
                 lax.dynamic_index_in_dim(route, head_at, 1, False).reshape(-1),
             ]
         )
-        bias = make_bias(rel_bias)
         bias, table, n_rows, *near_all = tie(bias, table, n_rows, *near_all)
-        far_got[0], near_all[0] = tie(far_got[0], near_all[0])
-        far_all = join(far[None], *far_got)
+        far_all, near_all[0] = tie(far_all, near_all[0])
         near_all = near_all + [passed(piece, CORE) for piece in near_all]
         far_got = [far_all] + spread(far_all, PLANE)
     else:
-        x_rows, g_rows, n_rows = prepare(tokens_in, cotangent)
+        x_rows, unit_rows, n_rows, bias = prepare(tokens_in, rel_table)
         table = jnp.concatenate(
             [
                 jnp.stack([me, swap_bits(me)]).astype(jnp.int32),
@@ -679,8 +754,7 @@
                 lax.dynamic_index_in_dim(route, head_at, 1, False).reshape(-1),
             ]
         )
-        bias = make_bias(rel_table)
-        near_all, far_all = gather_plain(near), gather_plain(far)
+        near_all, far_all = plain_pieces(near, far)
 
     packed, soft, attn, w_qkv, w_proj = call(
         functools.partial(attend_body, direct),
@@ -695,21 +769,22 @@
         scalars=1,
     )
 
-    if direct:
-        attn, *far_got = tie(attn, *far_got)
-        far_core = [passed(piece, CORE) for piece in far_got]
-
     middle, n_two = call(middle_body, [((ROWS, C), F32), ((ROWS, C), LOW)], (attn, x_rows, w_proj, vectors), "middle",
         limit=4)
 
+    late = cotangent
     if direct:
-        middle, *far_core = tie(middle, *far_core)
+        middle, late, *far_got = tie(middle, late, *far_got)
+        far_core = [passed(piece, CORE) for piece in far_got]
+    g_rows = prepare_grad(late)
+    if direct:
+        g_rows, *far_core = tie(g_rows, *far_core)
         far_all = far_got + far_core
 
     hidden, grad_hidden, grad_middle, sums_mlp, w_fc2 = call(
         functools.partial(mlp_body, direct),
         [((ROWS, FF), LOW), ((ROWS, FF), LOW), ((ROWS, C), F32), ((12, C), F32), ((C, FF), LOW)],
-        (table, middle, n_two, g_rows, vectors, *far_all),
+        (table, middle, n_two, g_rows, vectors, *near_all, *far_all),
         "mlp",
         limit=8,
         scratch=[pltpu.VMEM((C, FF), LOW), pltpu.VMEM((1, FF), F32), pltpu.VMEM((1, FF), F32)],
@@ -745,7 +820,7 @@
 
     packed_grad, grad_low, bias_sum, sums_attend = call(
         attend_back_body,
-        [((ROWS, 3 * C), LOW), ((ROWS, C), LOW), ((GROUPS, GROUP * WIN, 128), F32), ((2, C), F32)],
+        [((ROWS, 3 * C), LOW), ((ROWS, C), LOW), ((GROUPS, GROUP * WIN, 128), F32), ((1, 3 * C), F32)],
         (table, grad_middle, packed, soft, w_proj, place, heads_low),
         "attend_back",
         limit=6,
@@ -753,10 +828,11 @@
         scalars=1,
     )
 
-    near_keep, near_send = call(
+    vec_square = jnp.concatenate([vectors, jnp.zeros((4, C), F32)], axis=0)
+    near_keep, near_send, sums_input = call(
         functools.partial(attend_weights_body, direct),
-        [((half, PIECE, C), LOW)] * 2,
-        (table, n_rows, grad_low, packed_grad, attn),
+        [((half, PIECE, C), LOW)] * 2 + [((2, C), F32)],
+        (table, unit_rows, grad_low, packed_grad, attn, w_qkv, sums_attend, vec_square),
         "attend_weights",
         limit=8,
         scratch=[pltpu.VMEM((BLOCKS, PIECE, C), LOW)],
@@ -768,34 +844,52 @@
         near_send, *far_got = tie(near_send, *far_got)
         near_got = passed(near_send, CORE)
         near_stays, near_goes = first_sum(near_keep, near_got)
-        near_goes[0], packed_grad, bias_sum = tie(near_goes[0], packed_grad, bias_sum)
+        near_goes[0], bias_sum = tie(near_goes[0], bias_sum)
         near_got = sent(near_goes, PLANE)
 
-    bias_sum = (bias_sum[:, :, :WIN] + bias_sum[:, :, WIN:]).reshape(NH, WIN * WIN)
-    table_grad = product_of(bias_sum, LOOKUP.T)
+    (table_grad,) = call(
+        table_body,
+        [((NH, REL), F32)],
+        (bias_sum.reshape(NH * WIN, 128), lookup),
+        "table_grad",
+        limit=8,
+        scratch=[pltpu.VMEM((16, 128), F32)],
+        flops=1e8,
+    )
     if direct:
         table_grad, *far_got = tie(table_grad, *far_got)
         far_stays, far_goes = plane_sum(far_stays, far_got)
         far_got = sent(far_goes, LINE)
 
-    grad_block, sums_input = call(
-        input_body,
-        [(tokens_in.shape, LOW), ((2, C), F32)],
-        (w_qkv, packed_grad, x_rows, grad_middle, vectors, back),
-        "input_grad",
-        scratch=[
-            pltpu.VMEM((C, 3 * C), LOW), pltpu.VMEM((ROWS, 3 * C), LOW), pltpu.VMEM((ROWS, C), LOW), pltpu.VMEM((ROWS, C), F32),
-            pltpu.SemaphoreType.DMA, pltpu.SemaphoreType.DMA((MICRO, 3)),
-        ],
-        flops=4e9,
-        fetched=4,
-    )
-
-    vec_grad = jnp.concatenate([sums_input, sums_attend, sums_mlp[4:]], axis=0)
+    def input_piece(first, last, packed_grad, grad_block):
+        count = last - first
+        sources = [pltpu.with_memory_space_constraint(array, pltpu.HBM) for array in (w_qkv, packed_grad, x_rows, grad_middle)]
+        sources += [] if grad_block is None else [pltpu.with_memory_space_constraint(grad_block, pltpu.HBM)]
+        far = pl.BlockSpec(memory_space=pltpu.HBM)
+        return pl.pallas_call(
+            functools.partial(input_body, first, last),
+            in_specs=[far] * len(sources) + [HELD] * 2,
+            out_specs=far,
+            out_shape=pltpu.HBM(tokens_in.shape, LOW),
+            input_output_aliases={} if grad_block is None else {4: 0},
+            scratch_shapes=[
+                pltpu.VMEM((C, 3 * C), LOW), pltpu.VMEM((count * IMG, 3 * C), LOW), pltpu.VMEM((count * IMG, C), LOW),
+                pltpu.VMEM((count * IMG, C), F32), pltpu.VMEM((count, 1, GRID, GRID, C), LOW),
+                pltpu.SemaphoreType.DMA, pltpu.SemaphoreType.DMA((count, 3)), pltpu.SemaphoreType.DMA((count,)),
+            ],
+            compiler_params=whole(16),
+            cost_estimate=pl.CostEstimate(flops=int(4e8 * count), bytes_accessed=2000000, transcendentals=0),
+            name="input_grad",
+        )(*sources, vectors, back)
+
+    vec_grad = jnp.concatenate([sums_input, sums_attend[:, :C], sums_attend[:, 2 * C :], sums_mlp[4:]], axis=0)
     if direct:
-        grad_block, vec_grad, table_grad, *near_got = tie(grad_block, vec_grad, table_grad, *near_got)
+        vec_grad, table_grad, far_got[0], *near_got = tie(vec_grad, table_grad, far_got[0], *near_got)
         near_stays, near_goes = plane_sum(near_stays, near_got)
+        near_goes[0], packed_grad = tie(near_goes[0], packed_grad)
         near_got = sent(near_goes, LINE)
+        grad_block = input_piece(0, 2, packed_grad, None)
+        grad_block, *near_got = tie(grad_block, *near_got)
         near_grad, far_grad, spare = pl.pallas_call(
             functools.partial(finish_body, patches),
             out_shape=[sds((depth, C), F32), sds((2 * depth, C), F32), sds((32, C), F32)],
@@ -803,9 +897,14 @@
             name="finish",
         )(near_stays, far_stays, vec_grad, table_grad, *near_got, *far_got)
         spare = spare + passed(spare, CORE)
-        spare = total_of(spare, PLANE)
-        spare = total_of(spare, LINE)
+        for masks, first, last in ((PLANE, 2, 4), (LINE, 4, 5)):
+            spare, packed_grad = tie(spare, packed_grad)
+            one, two, three = spread(spare, masks)
+            grad_block = input_piece(first, last, packed_grad, grad_block)
+            grad_block, one, two, three = tie(grad_block, one, two, three)
+            spare = (spare + one) + (two + three)
     else:
+        grad_block = input_piece(0, MICRO, packed_grad, None)
         near_grad, far_grad = share_plain(near_keep, near_send) / patches, share_plain(far_keep, far_send) / patches
         squares = jnp.sum(near_grad * near_grad) + jnp.sum(far_grad * far_grad)
         vec_grad, table_grad, squares = lax.psum((vec_grad, table_grad, squares), BOTH)

time: 126 us -> 120 us (0.952)
  waiting for transfers between devices: 24.7 us -> 10.2 us
  Pallas kernels: 49.9 us -> 58.1 us
  starting transfers between devices: 43.1 us -> 48 us
  matrix products: 3.74 us -> 0 us
    ppermute x41, waiting for transfers between devices: 24.7 us -> 10.2 us  [passed(): return lax.ppermute(rows, BOTH, [(i, i ^ mask) for i in range(devices)])]
    pallas_call x1 -> x4, Pallas kernels: 1.06 us -> 12.6 us  [the longest x3 11.5 us: input_piece(): pl.pallas_call(functools.partial(input_body, first, last), in_specs=[far]...]
    ppermute x41, starting transfers between devices: 43.1 us -> 48 us  [passed(): return lax.ppermute(rows, BOTH, [(i, i ^ mask) for i in range(devices)])]
    dot_general x2 -> x0, matrix products: 3.74 us -> none  [product_of(): jnp.dot(parts, jnp.asarray(lookup, LOW), preferred_element_type=F32)]
    pallas_call x9 -> x10, Pallas kernels: 46.7 us -> 43.5 us  [call(): pl.pallas_call(body, in_specs=[SCALARS] * scalars + [far] * fetched + [HE...]
  transfers between devices with their start and end apart: 41 -> 41, of which waited for: 15 -> 7; matrix products, arithmetic and copies ran while one was open for 5% -> 1% of each run, Pallas kernels for 27% -> 36%
where the time goes in v6:
time: 120 us; the launch traced here: 119 us
  Pallas kernels  58.1 us (48%)
  starting transfers between devices  48 us (40%)
  waiting for transfers between devices  10.2 us (8%)
  between operations  1.61 us (1%)
  local copies, waits for them, and re-layouts  1.23 us (1%)
    ppermute x41, starting transfers between devices, passed(): return lax.ppermute(rows, BOTH, [(i, i ^ mask) for i in range(devices)])  48 us
    pallas_call x10, Pallas kernels, call(): pl.pallas_call(body, in_specs=[SCALARS] * scalars + [far] * fetched + [HE...  43.5 us
    pallas_call x3, Pallas kernels, input_piece(): pl.pallas_call(functools.partial(input_body, first, last), in_specs=[far]...  11.5 us
    ppermute x41, waiting for transfers between devices, passed(): return lax.ppermute(rows, BOTH, [(i, i ^ mask) for i in range(devices)])  10.2 us
  transfers between devices with their start and end apart: 41, of which 7 were waited for; matrix products, arithmetic and copies ran while one was open for 1% of the time, Pallas kernels for 36%

profile of v6, /device:TPU:0, one launch (start us, length us, event | category | flops | bytes accessed | tf_op | source)
XLA Modules:
  0.0 119.4 jit_solution(6722133647347283910)
XLA Ops:
  1.7 4.1 %collective-permute-start.3 = (bf16[1,64,384]{2,1,0:T(8,128)(2,1)S(1)}, bf16[1,64,384]{2,1,0:T(8,128)(2,1)S(1)}, u32[]{:S(2)}, u32[]{:S(2)}) collective-permute-start(bf16[1,64,384]{2,1,0:T(8,128)(2,1)S(1)} %bitcast.41), channel_id=1, source_target_pairs={{0,16},{1,17},{2,18},{3,19},{4,20},{5,21},{6,22},{7,23},{8,24},{9,... | collective-permute-start | bytes 147464 | tf_op jit(solution)/shard_map/ppermute | solution.py:641
  7.4 1.9 %collective-permute-start = (bf16[1,80,384]{2,1,0:T(8,128)(2,1)S(1)}, bf16[1,80,384]{2,1,0:T(8,128)(2,1)S(1)}, u32[]{:S(2)}, u32[]{:S(2)}) collective-permute-start(bf16[1,80,384]{2,1,0:T(8,128)(2,1)S(1)} %bitcast.37), channel_id=1, source_target_pairs={{0,16},{1,17},{2,18},{3,19},{4,20},{5,21},{6,22},{7,23},{8,24},{9,... | collective-permute-start | bytes 184328 | tf_op jit(solution)/shard_map/ppermute | solution.py:641
  9.3 2.5 %collective-permute-start.1 = (bf16[1,80,384]{2,1,0:T(8,128)(2,1)S(1)}, bf16[1,80,384]{2,1,0:T(8,128)(2,1)S(1)}, u32[]{:S(2)}, u32[]{:S(2)}) collective-permute-start(bf16[1,80,384]{2,1,0:T(8,128)(2,1)S(1)} %bitcast.38), channel_id=1, source_target_pairs={{0,8},{1,9},{2,10},{3,11},{4,12},{5,13},{6,14},{7,15},{8,0},{9,1},... | collective-permute-start | bytes 184328 | tf_op jit(solution)/shard_map/ppermute | solution.py:641
  11.8 1.9 %collective-permute-start.2 = (bf16[1,80,384]{2,1,0:T(8,128)(2,1)S(1)}, bf16[1,80,384]{2,1,0:T(8,128)(2,1)S(1)}, u32[]{:S(2)}, u32[]{:S(2)}) collective-permute-start(bf16[1,80,384]{2,1,0:T(8,128)(2,1)S(1)} %bitcast.39), channel_id=1, source_target_pairs={{0,24},{1,25},{2,26},{3,27},{4,28},{5,29},{6,30},{7,31},{8,16},{9,... | collective-permute-start | bytes 184328 | tf_op jit(solution)/shard_map/ppermute | solution.py:641
  19.3 4.2 %prep.1 = (bf16[1280,384]{1,0:T(8,128)(2,1)}, bf16[1280,384]{1,0:T(8,128)(2,1)}, bf16[1280,384]{1,0:T(8,128)(2,1)S(1)}, f32[768,128]{1,0:T(8,128)S(1)}) custom-call(f32[12,169]{1,0:T(8,128)} %bitcast.47, bf16[256,128]{1,0:T(8,128)(2,1)} %constant.92.clone.lookup_hbm.lookup_ref, f32[12,384]{1,0:T(8,128)} %refs_4_.3, ...), custom_call_target="tpu_custom_call" | custom-call | flops 1000000000 | bytes 4000000 | tf_op jit(solution)/shard_map/prep/pallas_call | solution.py:159
  28.5 7.4 %attend.1 = (bf16[1280,1152]{1,0:T(8,128)(2,1)S(1)}, bf16[5,6,256,128]{3,2,1,0:T(8,128)(2,1)S(1)}, bf16[1280,384]{1,0:T(8,128)(2,1)S(1)}, bf16[384,1152]{1,0:T(8,128)(2,1)S(1)}, bf16[384,384]{1,0:T(8,128)(2,1)S(1)}) custom-call(s32[32]{0:T(128)S(1)} %pad_add_fusion.table_ref, bf16[1280,384]{1,0:T(8,128)(2,1)S(1)} %get-tuple-element.157.n_ref, ...), custom_call_target="tpu_custom_call" | custom-call | flops 8000000000 | bytes 4000000 | tf_op jit(solution)/shard_map/attend/pallas_call | solution.py:159
  37.2 2.4 %collective-permute-done.15.refs_11_ = bf16[4,80,384]{2,1,0:T(8,128)(2,1)S(1)} collective-permute-done((bf16[4,80,384]{2,1,0:T(8,128)(2,1)S(1)}, bf16[4,80,384]{2,1,0:T(8,128)(2,1)S(1)}, u32[]{:S(2)}, u32[]{:S(2)}) %collective-permute-start.15) | collective-permute-done | bytes 245792 | tf_op jit(solution)/shard_map/ppermute | solution.py:641
  40.6 1.8 %prep_grad.1.g_ref = bf16[1280,384]{1,0:T(8,128)(2,1)S(1)} custom-call(bf16[256,224]{1,0:T(8,128)(2,1)} %constant.91.clone.deal_hbm, bf16[5,1,14,14,384]{4,3,2,1,0:T(8,128)(2,1)} %cot_hbm), custom_call_target="tpu_custom_call" | custom-call | flops 1000000000 | bytes 4000000 | tf_op jit(solution)/shard_map/prep_grad/pallas_call | solution.py:159
  42.4 8.2 %mlp.1 = (bf16[1280,1536]{1,0:T(8,128)(2,1)S(1)}, bf16[1280,1536]{1,0:T(8,128)(2,1)S(1)}, f32[1280,384]{1,0:T(8,128)S(1)}, f32[12,384]{1,0:T(8,128)S(1)}, bf16[384,1536]{1,0:T(8,128)(2,1)S(1)}) custom-call(s32[32]{0:T(128)S(1)} %pad_add_fusion.table_ref, f32[1280,384]{1,0:T(8,128)S(1)} %get-tuple-element.170.middle_ref, ...), custom_call_target="tpu_custom_call" | custom-call | flops 10000000000 | bytes 4000000 | tf_op jit(solution)/shard_map/mlp/pallas_call | solution.py:159
  50.7 4.2 %mlp_weights.1 = (bf16[16,96,384]{2,1,0:T(8,128)(2,1)S(1)}, bf16[16,96,384]{2,1,0:T(8,128)(2,1)S(1)}) custom-call(s32[32]{0:T(128)S(1)} %pad_add_fusion.table_ref, bf16[1280,384]{1,0:T(8,128)(2,1)S(1)} %get-tuple-element.171.n_ref, bf16[1280,384]{1,0:T(8,128)(2,1)S(1)} %prep_grad.1.g_ref, bf16[1280,1536]{1,0:T(8,128)(2,1)S(1)} %get-tuple-element.182.hidden_ref, ...), custom_call_target="tpu_custom_call" | custom-call | flops 4000000000 | bytes 4000000 | tf_op jit(solution)/shard_map/mlp_weights/pallas_call | solution.py:159
  55.0 3.7 %output.1 = bf16[5,1,14,14,384]{4,3,2,1,0:T(8,128)(2,1)} custom-call(bf16[1280,1536]{1,0:T(8,128)(2,1)S(1)} %get-tuple-element.182.hidden_ref, bf16[384,1536]{1,0:T(8,128)(2,1)S(1)} %get-tuple-element.183.w2_ref, f32[1280,384]{1,0:T(8,128)S(1)} %get-tuple-element.170.middle_ref, f32[12,384]{1,0:T(8,128)S(1)} %copy-done.6, bf16[224,256]{1,0:T(8,128)(2,1)S(1)} %copy-done.5), custom_call_target="tpu_custom_call" | custom-call | flops 2000000000 | bytes 4000000 | tf_op jit(solution)/shard_map/output/pallas_call | solution.py:159
  62.6 8.0 %attend_back.1 = (bf16[1280,1152]{1,0:T(8,128)(2,1)S(1)}, bf16[1280,384]{1,0:T(8,128)(2,1)S(1)}, f32[3,256,128]{2,1,0:T(8,128)S(1)}, f32[1,1152]{1,0:T(1,128)S(1)}) custom-call(s32[32]{0:T(128)S(1)} %pad_add_fusion.table_ref, f32[1280,384]{1,0:T(8,128)S(1)} %get-tuple-element.190.grad_ref.refs_3_, bf16[1280,1152]{1,0:T(8,128)(2,1)S(1)} %get-tuple-element.191.packed_ref, ...), custom_call_target="tpu_custom_call" | custom-call | flops 8000000000 | bytes 4000000 | tf_op jit(solution)/shard_map/attend_back/pallas_call | solution.py:159
  70.6 4.1 %attend_weights.1 = (bf16[16,48,384]{2,1,0:T(8,128)(2,1)S(1)}, bf16[16,48,384]{2,1,0:T(8,128)(2,1)S(1)}, f32[2,384]{1,0:T(2,128)S(1)}) custom-call(s32[32]{0:T(128)S(1)} %pad_add_fusion.table_ref, bf16[1280,384]{1,0:T(8,128)(2,1)S(1)} %copy-done.28, bf16[1280,384]{1,0:T(8,128)(2,1)S(1)} %get-tuple-element.193.grad_low_ref, ...), custom_call_target="tpu_custom_call" | custom-call | flops 2000000000 | bytes 4000000 | tf_op jit(solution)/shard_map/attend_weights/pallas_call | solution.py:159
  76.0 2.0 %collective-permute-done.24.got_ref = bf16[16,48,384]{2,1,0:T(8,128)(2,1)S(1)} collective-permute-done((bf16[16,48,384]{2,1,0:T(8,128)(2,1)S(1)}, bf16[16,48,384]{2,1,0:T(8,128)(2,1)S(1)}, u32[]{:S(2)}, u32[]{:S(2)}) %collective-permute-start.24) | collective-permute-done | bytes 589856 | tf_op jit(solution)/shard_map/ppermute | solution.py:641
  84.0 2.5 %collective-permute-start.32 = (bf16[1,96,384]{2,1,0:T(8,128)(2,1)S(1)}, bf16[1,96,384]{2,1,0:T(8,128)(2,1)S(1)}, u32[]{:S(2)}, u32[]{:S(2)}) collective-permute-start(bf16[1,96,384]{2,1,0:T(8,128)(2,1)S(1)} %get-tuple-element.238), channel_id=1, source_target_pairs={{0,8},{1,9},{2,10},{3,11},{4,12},{5,13},{6,14},{7,15},{8,0},{9,1},... | collective-permute-start | bytes 221192 | tf_op jit(solution)/shard_map/ppermute | solution.py:641
  86.5 2.4 %collective-permute-done.25.refs_3_ = bf16[1,96,384]{2,1,0:T(8,128)(2,1)S(1)} collective-permute-done((bf16[1,96,384]{2,1,0:T(8,128)(2,1)S(1)}, bf16[1,96,384]{2,1,0:T(8,128)(2,1)S(1)}, u32[]{:S(2)}, u32[]{:S(2)}) %collective-permute-start.25) | collective-permute-done | bytes 73760 | tf_op jit(solution)/shard_map/ppermute | solution.py:641
  88.8 2.6 %collective-permute-start.33 = (bf16[1,96,384]{2,1,0:T(8,128)(2,1)S(1)}, bf16[1,96,384]{2,1,0:T(8,128)(2,1)S(1)}, u32[]{:S(2)}, u32[]{:S(2)}) collective-permute-start(bf16[1,96,384]{2,1,0:T(8,128)(2,1)S(1)} %get-tuple-element.239), channel_id=1, source_target_pairs={{0,24},{1,25},{2,26},{3,27},{4,28},{5,29},{6,30},{7,31},{8,16},{9,... | collective-permute-start | bytes 221192 | tf_op jit(solution)/shard_map/ppermute | solution.py:641
  91.6 1.7 %collective-permute-start.30 = (bf16[1,48,384]{2,1,0:T(8,128)(2,1)S(1)}, bf16[1,48,384]{2,1,0:T(8,128)(2,1)S(1)}, u32[]{:S(2)}, u32[]{:S(2)}) collective-permute-start(bf16[1,48,384]{2,1,0:T(8,128)(2,1)S(1)} %get-tuple-element.232), channel_id=1, source_target_pairs={{0,8},{1,9},{2,10},{3,11},{4,12},{5,13},{6,14},{7,15},{8,0},{9,1},... | collective-permute-start | bytes 110600 | tf_op jit(solution)/shard_map/ppermute | solution.py:641
  93.4 2.6 %collective-permute-start.31 = (bf16[1,48,384]{2,1,0:T(8,128)(2,1)S(1)}, bf16[1,48,384]{2,1,0:T(8,128)(2,1)S(1)}, u32[]{:S(2)}, u32[]{:S(2)}) collective-permute-start(bf16[1,48,384]{2,1,0:T(8,128)(2,1)S(1)} %get-tuple-element.233), channel_id=1, source_target_pairs={{0,24},{1,25},{2,26},{3,27},{4,28},{5,29},{6,30},{7,31},{8,16},{9,... | collective-permute-start | bytes 110600 | tf_op jit(solution)/shard_map/ppermute | solution.py:641
  96.0 4.2 %input_grad.3.refs_4_ = bf16[5,1,14,14,384]{4,3,2,1,0:T(8,128)(2,1)} custom-call(bf16[384,1152]{1,0:T(8,128)(2,1)} %copy-done.4, bf16[1280,1152]{1,0:T(8,128)(2,1)} %copy-done.1, bf16[1280,384]{1,0:T(8,128)(2,1)} %get-tuple-element.166.x_ref.refs_2_, f32[1280,384]{1,0:T(8,128)} %copy-done.2, f32[12,384]{1,0:T(8,128)S(1)} %copy-done.6, ...), custom_call_target="tpu_custom_call" | custom-call | flops 800000000 | bytes 2000000 | tf_op jit(solution)/shard_map/input_grad/pallas_call | solution.py:869
  105.3 4.2 %input_grad.4.refs_4_ = bf16[5,1,14,14,384]{4,3,2,1,0:T(8,128)(2,1)} custom-call(bf16[384,1152]{1,0:T(8,128)(2,1)} %copy-done.4, bf16[1280,1152]{1,0:T(8,128)(2,1)} %copy-done.1, bf16[1280,384]{1,0:T(8,128)(2,1)} %get-tuple-element.166.x_ref.refs_2_, f32[1280,384]{1,0:T(8,128)} %copy-done.2, ...), custom_call_target="tpu_custom_call", output_to_operand_aliasing={{}: (4, {})} | custom-call | flops 800000000 | bytes 2000000 | tf_op jit(solution)/shard_map/input_grad/pallas_call | solution.py:869
  109.8 2.1 %collective-permute-start.39 = (f32[32,384]{1,0:T(8,128)S(1)}, f32[32,384]{1,0:T(8,128)S(1)}, u32[]{:S(2)}, u32[]{:S(2)}) collective-permute-start(f32[32,384]{1,0:T(8,128)S(1)} %add_add_fusion.1), channel_id=1, source_target_pairs={{0,8},{1,9},{2,10},{3,11},{4,12},{5,13},{6,14},{7,15},{8,0},{9,1},... | collective-permute-start | bytes 147464 | tf_op jit(solution)/shard_map/ppermute | solution.py:641
  111.9 2.3 %collective-permute-start.40 = (f32[32,384]{1,0:T(8,128)S(1)}, f32[32,384]{1,0:T(8,128)S(1)}, u32[]{:S(2)}, u32[]{:S(2)}) collective-permute-start(f32[32,384]{1,0:T(8,128)S(1)} %add_add_fusion.1), channel_id=1, source_target_pairs={{0,24},{1,25},{2,26},{3,27},{4,28},{5,29},{6,30},{7,31},{8,16},{9,... | collective-permute-start | bytes 147464 | tf_op jit(solution)/shard_map/ppermute | solution.py:641
  114.2 3.1 %input_grad.5 = bf16[5,1,14,14,384]{4,3,2,1,0:T(8,128)(2,1)} custom-call(bf16[384,1152]{1,0:T(8,128)(2,1)} %copy-done.4, bf16[1280,1152]{1,0:T(8,128)(2,1)} %copy-done.1, bf16[1280,384]{1,0:T(8,128)(2,1)} %get-tuple-element.166.x_ref.refs_2_, f32[1280,384]{1,0:T(8,128)} %copy-done.2, ...), custom_call_target="tpu_custom_call", output_to_operand_aliasing={{}: (4, {})} | custom-call | flops 400000000 | bytes 2000000 | tf_op jit(solution)/shard_map/input_grad/pallas_call | solution.py:869
  (152 shorter events, 33.7 us)
Async XLA Ops:
  1.7 10.1 %collective-permute-start.3 = (bf16[1,64,384]{2,1,0:T(8,128)(2,1)S(1)}, bf16[1,64,384]{2,1,0:T(8,128)(2,1)S(1)}, u32[]{:S(2)}, u32[]{:S(2)}) collective-permute-start(bf16[1,64,384]{2,1,0:T(8,128)(2,1)S(1)} %bitcast.41), channel_id=1, source_target_pairs={{0,16},{1,17},{2,18},{3,19},{4,20},{5,21},{6,22},{7,23},{8,24},{9,... | collective-permute-start | bytes 147464 | tf_op jit(solution)/shard_map/ppermute | solution.py:641
  5.8 7.9 %collective-permute-start.4 = (bf16[1,64,384]{2,1,0:T(8,128)(2,1)S(1)}, bf16[1,64,384]{2,1,0:T(8,128)(2,1)S(1)}, u32[]{:S(2)}, u32[]{:S(2)}) collective-permute-start(bf16[1,64,384]{2,1,0:T(8,128)(2,1)S(1)} %bitcast.42), channel_id=1, source_target_pairs={{0,8},{1,9},{2,10},{3,11},{4,12},{5,13},{6,14},{7,15},{8,0},{9,1},... | collective-permute-start | bytes 147464 | tf_op jit(solution)/shard_map/ppermute | solution.py:641
  7.4 9.4 %collective-permute-start = (bf16[1,80,384]{2,1,0:T(8,128)(2,1)S(1)}, bf16[1,80,384]{2,1,0:T(8,128)(2,1)S(1)}, u32[]{:S(2)}, u32[]{:S(2)}) collective-permute-start(bf16[1,80,384]{2,1,0:T(8,128)(2,1)S(1)} %bitcast.37), channel_id=1, source_target_pairs={{0,16},{1,17},{2,18},{3,19},{4,20},{5,21},{6,22},{7,23},{8,24},{9,... | collective-permute-start | bytes 184328 | tf_op jit(solution)/shard_map/ppermute | solution.py:641
  9.3 8.8 %collective-permute-start.1 = (bf16[1,80,384]{2,1,0:T(8,128)(2,1)S(1)}, bf16[1,80,384]{2,1,0:T(8,128)(2,1)S(1)}, u32[]{:S(2)}, u32[]{:S(2)}) collective-permute-start(bf16[1,80,384]{2,1,0:T(8,128)(2,1)S(1)} %bitcast.38), channel_id=1, source_target_pairs={{0,8},{1,9},{2,10},{3,11},{4,12},{5,13},{6,14},{7,15},{8,0},{9,1},... | collective-permute-start | bytes 184328 | tf_op jit(solution)/shard_map/ppermute | solution.py:641
  13.8 9.8 %collective-permute-start.6 = (bf16[4,64,384]{2,1,0:T(8,128)(2,1)S(1)}, bf16[4,64,384]{2,1,0:T(8,128)(2,1)S(1)}, u32[]{:S(2)}, u32[]{:S(2)}) collective-permute-start(bf16[4,64,384]{2,1,0:T(8,128)(2,1)S(1)} %pad_maximum_fusion.1.refs_0_), channel_id=1, source_target_pairs={{0,2},{1,3},{2,0},{3,1},{4,6},{5,7},{6,4},{7,5},{8,10},{9,11},{10,... | collective-permute-start | bytes 589832 | tf_op jit(solution)/shard_map/ppermute | solution.py:641
  15.4 8.2 %collective-permute-start.7 = (bf16[4,64,384]{2,1,0:T(8,128)(2,1)S(1)}, bf16[4,64,384]{2,1,0:T(8,128)(2,1)S(1)}, u32[]{:S(2)}, u32[]{:S(2)}) collective-permute-start(bf16[4,64,384]{2,1,0:T(8,128)(2,1)S(1)} %pad_maximum_fusion.1.refs_0_), channel_id=1, source_target_pairs={{0,4},{1,5},{2,6},{3,7},{4,0},{5,1},{6,2},{7,3},{8,12},{9,13},{10,... | collective-permute-start | bytes 589832 | tf_op jit(solution)/shard_map/ppermute | solution.py:641
  16.9 7.1 %collective-permute-start.8 = (bf16[4,64,384]{2,1,0:T(8,128)(2,1)S(1)}, bf16[4,64,384]{2,1,0:T(8,128)(2,1)S(1)}, u32[]{:S(2)}, u32[]{:S(2)}) collective-permute-start(bf16[4,64,384]{2,1,0:T(8,128)(2,1)S(1)} %pad_maximum_fusion.1.refs_0_), channel_id=1, source_target_pairs={{0,6},{1,7},{2,4},{3,5},{4,2},{5,3},{6,0},{7,1},{8,14},{9,15},{10,... | collective-permute-start | bytes 589832 | tf_op jit(solution)/shard_map/ppermute | solution.py:641
  25.0 12.2 %collective-permute-start.13 = (bf16[4,80,384]{2,1,0:T(8,128)(2,1)S(1)}, bf16[4,80,384]{2,1,0:T(8,128)(2,1)S(1)}, u32[]{:S(2)}, u32[]{:S(2)}) collective-permute-start(bf16[4,80,384]{2,1,0:T(8,128)(2,1)S(1)} %pad_maximum_fusion.refs_8_), channel_id=1, source_target_pairs={{0,2},{1,3},{2,0},{3,1},{4,6},{5,7},{6,4},{7,5},{8,10},{9,11},{10,... | collective-permute-start | bytes 737288 | tf_op jit(solution)/shard_map/ppermute | solution.py:641
  26.5 10.7 %collective-permute-start.14 = (bf16[4,80,384]{2,1,0:T(8,128)(2,1)S(1)}, bf16[4,80,384]{2,1,0:T(8,128)(2,1)S(1)}, u32[]{:S(2)}, u32[]{:S(2)}) collective-permute-start(bf16[4,80,384]{2,1,0:T(8,128)(2,1)S(1)} %pad_maximum_fusion.refs_8_), channel_id=1, source_target_pairs={{0,4},{1,5},{2,6},{3,7},{4,0},{5,1},{6,2},{7,3},{8,12},{9,13},{10,... | collective-permute-start | bytes 737288 | tf_op jit(solution)/shard_map/ppermute | solution.py:641
  28.0 11.6 %collective-permute-start.15 = (bf16[4,80,384]{2,1,0:T(8,128)(2,1)S(1)}, bf16[4,80,384]{2,1,0:T(8,128)(2,1)S(1)}, u32[]{:S(2)}, u32[]{:S(2)}) collective-permute-start(bf16[4,80,384]{2,1,0:T(8,128)(2,1)S(1)} %pad_maximum_fusion.refs_8_), channel_id=1, source_target_pairs={{0,6},{1,7},{2,4},{3,5},{4,2},{5,3},{6,0},{7,1},{8,14},{9,15},{10,... | collective-permute-start | bytes 737288 | tf_op jit(solution)/shard_map/ppermute | solution.py:641
  59.0 15.7 %collective-permute-start.21 = (bf16[4,96,384]{2,1,0:T(8,128)(2,1)S(1)}, bf16[4,96,384]{2,1,0:T(8,128)(2,1)S(1)}, u32[]{:S(2)}, u32[]{:S(2)}) collective-permute-start(bf16[4,96,384]{2,1,0:T(8,128)(2,1)S(1)} %get-tuple-element.200), channel_id=1, source_target_pairs={{0,2},{1,3},{2,0},{3,1},{4,6},{5,7},{6,4},{7,5},{8,10},{9,11},{10,... | collective-permute-start | bytes 884744 | tf_op jit(solution)/shard_map/ppermute | solution.py:641
  60.3 14.4 %collective-permute-start.22 = (bf16[4,96,384]{2,1,0:T(8,128)(2,1)S(1)}, bf16[4,96,384]{2,1,0:T(8,128)(2,1)S(1)}, u32[]{:S(2)}, u32[]{:S(2)}) collective-permute-start(bf16[4,96,384]{2,1,0:T(8,128)(2,1)S(1)} %get-tuple-element.201), channel_id=1, source_target_pairs={{0,4},{1,5},{2,6},{3,7},{4,0},{5,1},{6,2},{7,3},{8,12},{9,13},{10,... | collective-permute-start | bytes 884744 | tf_op jit(solution)/shard_map/ppermute | solution.py:641
  61.8 14.2 %collective-permute-start.23 = (bf16[4,96,384]{2,1,0:T(8,128)(2,1)S(1)}, bf16[4,96,384]{2,1,0:T(8,128)(2,1)S(1)}, u32[]{:S(2)}, u32[]{:S(2)}) collective-permute-start(bf16[4,96,384]{2,1,0:T(8,128)(2,1)S(1)} %get-tuple-element.202), channel_id=1, source_target_pairs={{0,6},{1,7},{2,4},{3,5},{4,2},{5,3},{6,0},{7,1},{8,14},{9,15},{10,... | collective-permute-start | bytes 884744 | tf_op jit(solution)/shard_map/ppermute | solution.py:641
  78.1 13.4 %collective-permute-start.26 = (bf16[4,48,384]{2,1,0:T(8,128)(2,1)S(1)}, bf16[4,48,384]{2,1,0:T(8,128)(2,1)S(1)}, u32[]{:S(2)}, u32[]{:S(2)}) collective-permute-start(bf16[4,48,384]{2,1,0:T(8,128)(2,1)S(1)} %get-tuple-element.219), channel_id=1, source_target_pairs={{0,2},{1,3},{2,0},{3,1},{4,6},{5,7},{6,4},{7,5},{8,10},{9,11},{10,... | collective-permute-start | bytes 442376 | tf_op jit(solution)/shard_map/ppermute | solution.py:641
  79.4 12.1 %collective-permute-start.27 = (bf16[4,48,384]{2,1,0:T(8,128)(2,1)S(1)}, bf16[4,48,384]{2,1,0:T(8,128)(2,1)S(1)}, u32[]{:S(2)}, u32[]{:S(2)}) collective-permute-start(bf16[4,48,384]{2,1,0:T(8,128)(2,1)S(1)} %get-tuple-element.220), channel_id=1, source_target_pairs={{0,4},{1,5},{2,6},{3,7},{4,0},{5,1},{6,2},{7,3},{8,12},{9,13},{10,... | collective-permute-start | bytes 442376 | tf_op jit(solution)/shard_map/ppermute | solution.py:641
  80.9 10.6 %collective-permute-start.28 = (bf16[4,48,384]{2,1,0:T(8,128)(2,1)S(1)}, bf16[4,48,384]{2,1,0:T(8,128)(2,1)S(1)}, u32[]{:S(2)}, u32[]{:S(2)}) collective-permute-start(bf16[4,48,384]{2,1,0:T(8,128)(2,1)S(1)} %get-tuple-element.221), channel_id=1, source_target_pairs={{0,6},{1,7},{2,4},{3,5},{4,2},{5,3},{6,0},{7,1},{8,14},{9,15},{10,... | collective-permute-start | bytes 442376 | tf_op jit(solution)/shard_map/ppermute | solution.py:641
  84.0 16.3 %collective-permute-start.32 = (bf16[1,96,384]{2,1,0:T(8,128)(2,1)S(1)}, bf16[1,96,384]{2,1,0:T(8,128)(2,1)S(1)}, u32[]{:S(2)}, u32[]{:S(2)}) collective-permute-start(bf16[1,96,384]{2,1,0:T(8,128)(2,1)S(1)} %get-tuple-element.238), channel_id=1, source_target_pairs={{0,8},{1,9},{2,10},{3,11},{4,12},{5,13},{6,14},{7,15},{8,0},{9,1},... | collective-permute-start | bytes 221192 | tf_op jit(solution)/shard_map/ppermute | solution.py:641
  88.8 11.4 %collective-permute-start.33 = (bf16[1,96,384]{2,1,0:T(8,128)(2,1)S(1)}, bf16[1,96,384]{2,1,0:T(8,128)(2,1)S(1)}, u32[]{:S(2)}, u32[]{:S(2)}) collective-permute-start(bf16[1,96,384]{2,1,0:T(8,128)(2,1)S(1)} %get-tuple-element.239), channel_id=1, source_target_pairs={{0,24},{1,25},{2,26},{3,27},{4,28},{5,29},{6,30},{7,31},{8,16},{9,... | collective-permute-start | bytes 221192 | tf_op jit(solution)/shard_map/ppermute | solution.py:641
  91.6 8.7 %collective-permute-start.29 = (bf16[1,48,384]{2,1,0:T(8,128)(2,1)S(1)}, bf16[1,48,384]{2,1,0:T(8,128)(2,1)S(1)}, u32[]{:S(2)}, u32[]{:S(2)}) collective-permute-start(bf16[1,48,384]{2,1,0:T(8,128)(2,1)S(1)} %get-tuple-element.231), channel_id=1, source_target_pairs={{0,16},{1,17},{2,18},{3,19},{4,20},{5,21},{6,22},{7,23},{8,24},{9,... | collective-permute-start | bytes 110600 | tf_op jit(solution)/shard_map/ppermute | solution.py:641
  91.6 8.6 %collective-permute-start.30 = (bf16[1,48,384]{2,1,0:T(8,128)(2,1)S(1)}, bf16[1,48,384]{2,1,0:T(8,128)(2,1)S(1)}, u32[]{:S(2)}, u32[]{:S(2)}) collective-permute-start(bf16[1,48,384]{2,1,0:T(8,128)(2,1)S(1)} %get-tuple-element.232), channel_id=1, source_target_pairs={{0,8},{1,9},{2,10},{3,11},{4,12},{5,13},{6,14},{7,15},{8,0},{9,1},... | collective-permute-start | bytes 110600 | tf_op jit(solution)/shard_map/ppermute | solution.py:641
  93.4 6.9 %collective-permute-start.31 = (bf16[1,48,384]{2,1,0:T(8,128)(2,1)S(1)}, bf16[1,48,384]{2,1,0:T(8,128)(2,1)S(1)}, u32[]{:S(2)}, u32[]{:S(2)}) collective-permute-start(bf16[1,48,384]{2,1,0:T(8,128)(2,1)S(1)} %get-tuple-element.233), channel_id=1, source_target_pairs={{0,24},{1,25},{2,26},{3,27},{4,28},{5,29},{6,30},{7,31},{8,16},{9,... | collective-permute-start | bytes 110600 | tf_op jit(solution)/shard_map/ppermute | solution.py:641
  101.7 7.8 %collective-permute-start.35 = (f32[32,384]{1,0:T(8,128)S(1)}, f32[32,384]{1,0:T(8,128)S(1)}, u32[]{:S(2)}, u32[]{:S(2)}) collective-permute-start(f32[32,384]{1,0:T(8,128)S(1)} %add.55), channel_id=1, source_target_pairs={{0,2},{1,3},{2,0},{3,1},{4,6},{5,7},{6,4},{7,5},{8,10},{9,11},{10,... | collective-permute-start | bytes 147464 | tf_op jit(solution)/shard_map/ppermute | solution.py:641
  109.7 7.6 %collective-permute-start.38 = (f32[32,384]{1,0:T(8,128)S(1)}, f32[32,384]{1,0:T(8,128)S(1)}, u32[]{:S(2)}, u32[]{:S(2)}) collective-permute-start(f32[32,384]{1,0:T(8,128)S(1)} %add_add_fusion.1), channel_id=1, source_target_pairs={{0,16},{1,17},{2,18},{3,19},{4,20},{5,21},{6,22},{7,23},{8,24},{9,... | collective-permute-start | bytes 147464 | tf_op jit(solution)/shard_map/ppermute | solution.py:641
  109.8 7.5 %collective-permute-start.39 = (f32[32,384]{1,0:T(8,128)S(1)}, f32[32,384]{1,0:T(8,128)S(1)}, u32[]{:S(2)}, u32[]{:S(2)}) collective-permute-start(f32[32,384]{1,0:T(8,128)S(1)} %add_add_fusion.1), channel_id=1, source_target_pairs={{0,8},{1,9},{2,10},{3,11},{4,12},{5,13},{6,14},{7,15},{8,0},{9,1},... | collective-permute-start | bytes 147464 | tf_op jit(solution)/shard_map/ppermute | solution.py:641
  (46 other events, 353.0 us)

commit v7 on v6

--- a/solution.py
+++ b/solution.py
@@ -50,7 +50,7 @@
 MASKS = (16, 8, 2, 4, 1)
 CORE, PLANE, LINE = 1, (2, 4, 6), (16, 8, 24)
 PIECES = 8
-ME, SLOT, EXTENT, ROUTE = 0, 1, 2, 12
+ME, SLOT, IMAGE = 0, 1, 2
 
 
 def swap_bits(position):
@@ -187,12 +187,13 @@
     return [pltpu.with_memory_space_constraint(array, pltpu.HBM) for array in arrays]
 
 
-def row_mask(place_ref, table_ref, image):
+def row_mask(place_ref, table_ref, extent_ref, route_ref, image):
     parts = []
+    own = table_ref[IMAGE]
     for w in range(4):
         rows = slice(w * WIN, (w + 1) * WIN)
-        high = jnp.where(table_ref[ROUTE + 4 * image + w] >= 0, table_ref[EXTENT + 2 * image], -1).astype(F32)
-        wide = table_ref[EXTENT + 2 * image + 1].astype(F32)
+        high = jnp.where(route_ref[own, w, image] >= 0, extent_ref[own, 0, image], -1).astype(F32)
+        wide = extent_ref[own, 1, image].astype(F32)
         inside = (place_ref[0, rows] < high) & (place_ref[1, rows] < wide)
         parts.append(jnp.where(inside, 1.0, 0.0))
     return jnp.concatenate(parts, axis=0)
@@ -234,9 +235,9 @@
         target[...] = total
         squares = squares + jnp.sum(jnp.sum(total * total, axis=1, keepdims=True), axis=0, keepdims=True)
     spare[0:12] = vec_ref[...] * (1.0 / patches)
-    spare[12:24] = jnp.zeros((12, C), F32)
-    spare[12:24, :REL] = table_ref[...] * (1.0 / patches)
-    spare[24:32] = jnp.broadcast_to(squares, (8, C))
+    spare[12:24] = jnp.broadcast_to(squares, (12, C))
+    spare[12:18, :REL] = table_ref[: NH // 2] * (1.0 / patches)
+    spare[12:18, C // 2 : C // 2 + REL] = table_ref[NH // 2 :] * (1.0 / patches)
 
 
 def three_parts(values):
@@ -289,21 +290,24 @@
     for image in range(MICRO):
         at = slice(image * IMG, (image + 1) * IMG)
         unit, _ = norm_parts(made[image])
-        unit_all[at, :] = unit.astype(LOW)
-        stores.append(pltpu.make_async_copy(unit_all.at[at], unit_hbm.at[at], out_sems.at[image, 1]))
+        unit_all[:, at] = unit.astype(LOW).T
+        stores.append(pltpu.make_async_copy(unit_all.at[:, at], unit_hbm.at[:, at], out_sems.at[image, 1]))
         stores[-1].start()
         n_ref[at, :] = (unit * vec[0:1] + vec[1:2]).astype(LOW)
     for store in stores:
         store.wait()
 
 
-def prep_grad_body(deal_hbm, cot_hbm, g_ref, deal, cot, pad, sems):
+def prep_grad_body(deal_hbm, cot_hbm, g_ref, turned_ref, deal, cot, pad, sems):
     copies = fetch(((deal_hbm, deal), (cot_hbm, cot)), sems)
     pad[...] = jnp.zeros_like(pad)
     for copy in copies:
         copy.wait()
     for image in range(MICRO):
-        g_ref[image * IMG : (image + 1) * IMG, :] = deal_rows(cot, deal, pad, image).astype(LOW)
+        at = slice(image * IMG, (image + 1) * IMG)
+        rows = deal_rows(cot, deal, pad, image).astype(LOW)
+        g_ref[at, :] = rows
+        turned_ref[:, at] = rows.T
 
 
 def table_body(sums_ref, lookup_ref, table_ref, padded):
@@ -351,7 +355,7 @@
 
 
 def attend_body(
-    direct, table_ref, n_ref, vec_ref, bias_ref, reach_ref, place_ref, heads_ref, *refs,
+    direct, table_ref, extent_ref, route_ref, n_ref, vec_ref, bias_ref, reach_ref, place_ref, heads_ref, *refs,
 ):
     near_refs, (packed_ref, soft_ref, attn_ref, wq_ref, wp_ref, parts) = refs[:PIECES], refs[PIECES:]
     for j in range(BLOCKS):
@@ -369,9 +373,9 @@
         packed_ref[at_image, :C] = (made[:, :C] + vec_ref[2:3]).astype(LOW)
         packed_ref[at_image, C : 2 * C] = made[:, C : 2 * C].astype(LOW)
         packed_ref[at_image, 2 * C :] = (made[:, 2 * C :] + vec_ref[3:4]).astype(LOW)
-        mask = row_mask(place_ref, table_ref, image)
-        high = table_ref[EXTENT + 2 * image].astype(F32)
-        wide = table_ref[EXTENT + 2 * image + 1].astype(F32)
+        mask = row_mask(place_ref, table_ref, extent_ref, route_ref, image)
+        high = extent_ref[table_ref[IMAGE], 0, image].astype(F32)
+        wide = extent_ref[table_ref[IMAGE], 1, image].astype(F32)
         eye = identity()
         units = [(pair, g) for pair in range(2) for g in range(GROUPS)]
         at_pair = [pl.ds(pl.multiple_of(image * IMG + pair * 2 * WIN, 2 * WIN), 2 * WIN) for pair in range(2)]
@@ -400,13 +404,15 @@
             attn_ref[at_pair[pair], at : at + LANES] = (result * mask[rows]).astype(LOW)
 
 
-def middle_body(attn_ref, x_ref, wp_ref, vec_ref, middle_ref, n_ref):
+def middle_body(attn_ref, x_ref, wp_ref, vec_ref, middle_ref, n_ref, turned_ref):
     for image in range(MICRO):
         at = slice(image * IMG, (image + 1) * IMG)
         middle = x_ref[at, :].astype(F32) + dot_nt(attn_ref[at, :], wp_ref[...]) + vec_ref[4:5]
         middle_ref[at, :] = middle
         unit, _ = norm_parts(middle)
-        n_ref[at, :] = (unit * vec_ref[5:6] + vec_ref[6:7]).astype(LOW)
+        normed = (unit * vec_ref[5:6] + vec_ref[6:7]).astype(LOW)
+        n_ref[at, :] = normed
+        turned_ref[:, at] = normed.T
 
 
 def mlp_body(
@@ -458,9 +464,7 @@
     return table_ref[SLOT] ^ swap_bits(4 * t) ^ ((h & 1) * 16 + (h >> 1) * 4)
 
 
-def mlp_weights_body(direct, table_ref, n_ref, g_ref, hidden_ref, grad_hidden_ref, keep_ref, send_ref, n_turned, g_turned, made, first, second):
-    n_turned[...] = n_ref[...].T
-    g_turned[...] = g_ref[...].T
+def mlp_weights_body(direct, table_ref, n_turned, g_turned, hidden_ref, grad_hidden_ref, keep_ref, send_ref, made, first, second):
     for part in range(3):
         cols = slice(part * 2 * WIDE, (part + 1) * 2 * WIDE)
         first[:, cols] = dot_nn(n_turned[...], grad_hidden_ref[:, cols]).astype(LOW)
@@ -475,17 +479,23 @@
     send_ref[...] = made[BLOCKS // 2 :]
 
 
-def output_body(hidden_ref, w2_ref, middle_ref, vec_ref, back_ref, out_ref):
-    made = []
-    for image in range(MICRO):
+def output_body(first, last, hidden_ref, w2_ref, middle_ref, vec_ref, back_ref, *refs):
+    out_hbm, made, sems = refs[(first > 0) :]
+    rows = []
+    for image in range(first, last):
         at = slice(image * IMG, (image + 1) * IMG)
-        made.append((middle_ref[at, :] + dot_nt(hidden_ref[at, :], w2_ref[...]) + vec_ref[7:8]).astype(LOW))
-    for image in range(MICRO):
-        put_back(made[image], back_ref, out_ref, image)
+        rows.append((middle_ref[at, :] + dot_nt(hidden_ref[at, :], w2_ref[...]) + vec_ref[7:8]).astype(LOW))
+    stores = []
+    for index, low in enumerate(rows):
+        put_back(low, back_ref, made, index)
+        stores.append(pltpu.make_async_copy(made.at[index], out_hbm.at[first + index], sems.at[index]))
+        stores[-1].start()
+    for store in stores:
+        store.wait()
 
 
 def attend_back_body(
-    table_ref, grad_ref, packed_ref, soft_ref, wp_ref, place_ref, heads_ref,
+    table_ref, extent_ref, route_ref, grad_ref, packed_ref, soft_ref, wp_ref, place_ref, heads_ref,
     packed_grad_ref, grad_low_ref, bias_sum_ref, sums_ref,
 ):
     bias_sum_ref[...] = jnp.zeros_like(bias_sum_ref)
@@ -496,7 +506,7 @@
         at_image = image_rows(image)
         grad_low = grad_ref[at_image, :].astype(LOW)
         grad_low_ref[at_image, :] = grad_low
-        mask = row_mask(place_ref, table_ref, image)
+        mask = row_mask(place_ref, table_ref, extent_ref, route_ref, image)
         grad_attn = dot_nn(grad_low, wp_ref[...])
         grad_attn = (grad_attn * jnp.concatenate([mask] * 3, axis=1)).astype(LOW)
         eye = identity()
@@ -535,9 +545,8 @@
 
 
 def attend_weights_body(
-    direct, table_ref, unit_ref, grad_low_ref, packed_grad_ref, attn_ref, wq_ref, sums_ref, vec_ref, keep_ref, send_ref, norm_ref, made
+    direct, table_ref, unit_turned, grad_low_ref, packed_grad_ref, attn_ref, wq_ref, sums_ref, vec_ref, keep_ref, send_ref, norm_ref, made
 ):
-    unit_turned = unit_ref[...].T
     turned_vec = vec_ref[...].T
     gain, shift = turned_vec[:, 0:1], turned_vec[:, 1:2]
     parts = []
@@ -545,7 +554,7 @@
     shift_grad = jnp.zeros((C, 1), F32)
     for w in range(3):
         cols = slice(w * C, (w + 1) * C)
-        product = dot_nn(unit_turned, packed_grad_ref[:, cols])
+        product = dot_nn(unit_turned[...], packed_grad_ref[:, cols])
         weight, sums = wq_ref[:, cols].astype(F32), sums_ref[:, cols]
         parts.append((product * gain + shift * sums).astype(LOW))
         gain_grad = gain_grad + jnp.sum(product * weight, axis=1, keepdims=True)
@@ -601,9 +610,11 @@
 
 
 def adam_body(near_ref, far_ref, spare_ref, *refs):
-    olds, news = refs[:18], refs[18:]
-    vec, table = spare_ref[0:12], spare_ref[12:24, :REL]
-    total = spare_ref[24:25, 0:1]
+    olds, news, turned = refs[:18], refs[18:-1], refs[-1]
+    turned[: NH // 2] = spare_ref[12:18, :REL]
+    turned[NH // 2 :] = spare_ref[12:18, C // 2 : C // 2 + REL]
+    vec, table = spare_ref[0:12], turned[...]
+    total = spare_ref[18:19, 0:1]
     total = total + jnp.sum(jnp.sum(vec * vec, axis=1, keepdims=True), axis=0, keepdims=True)
     total = total + jnp.sum(jnp.sum(table * table, axis=1, keepdims=True), axis=0, keepdims=True)
     grad_norm = jnp.sqrt(total)
@@ -634,6 +645,9 @@
     patches = micro * devices * GRID * GRID
     head_at = lax.axis_index("head")
     me = lax.axis_index("tok") * heads + head_at
+    numbers = [me, swap_bits(me), head_at]
+    extents, routes = extent.transpose(1, 2, 0), route.transpose(1, 2, 0)
+
     def tie(*arrays):
         return lax.optimization_barrier(arrays)
 
@@ -698,33 +712,32 @@
     whole_images = pltpu.VMEM((MICRO, 1, GRID, GRID, C), LOW)
 
     def prepare(tokens, values):
-        x_rows, unit_rows, n_rows, bias = call(
+        x_rows, unit_turned, n_rows, bias = call(
             prep_body,
-            [((ROWS, C), LOW)] * 3 + [((NH * WIN, 128), F32)],
+            [((ROWS, C), LOW), ((C, ROWS), LOW), ((ROWS, C), LOW), ((NH * WIN, 128), F32)],
             (values.T, lookup, vectors, deal, tokens),
             "prep",
             scratch=[
                 pltpu.VMEM((NH, REL), F32), pltpu.VMEM((256, 128), LOW), pltpu.VMEM((12, C), F32), pltpu.VMEM((IMG, PAD), LOW),
-                whole_images, pltpu.VMEM((ROWS, C), LOW), pltpu.VMEM((ROWS, C), LOW), pltpu.VMEM((16, 256), F32),
+                whole_images, pltpu.VMEM((ROWS, C), LOW), pltpu.VMEM((C, ROWS), LOW), pltpu.VMEM((16, 256), F32),
                 pltpu.VMEM((MICRO, PAD, C), LOW), pltpu.SemaphoreType.DMA((5,)), pltpu.SemaphoreType.DMA((MICRO, 2)),
             ],
             flops=1e9,
             fetched=5,
             stored=2,
         )
-        return x_rows, unit_rows, n_rows, bias.reshape(GROUPS, GROUP * WIN, 128)
+        return x_rows, unit_turned, n_rows, bias.reshape(GROUPS, GROUP * WIN, 128)
 
     def prepare_grad(cotangents):
-        (g_rows,) = call(
+        return call(
             prep_grad_body,
-            [((ROWS, C), LOW)],
+            [((ROWS, C), LOW), ((C, ROWS), LOW)],
             (deal, cotangents),
             "prep_grad",
             limit=8,
             scratch=[pltpu.VMEM((IMG, PAD), LOW), whole_images, pltpu.VMEM((MICRO, PAD, C), LOW), pltpu.SemaphoreType.DMA((2,))],
             fetched=2,
         )
-        return g_rows
 
     if direct:
         near = near[None]
@@ -732,28 +745,16 @@
         near_all = join(near, *near_got)
         near_all = [near_all] + spread(near_all, PLANE)
         far_all = join(far[None], *far_got)
-        far_all, tokens, extent, route, rel_bias = tie(far_all, tokens_in, extent, route, rel_table)
-        x_rows, unit_rows, n_rows, bias = prepare(tokens, rel_bias)
-        table = jnp.concatenate(
-            [
-                jnp.stack([me, swap_bits(me)]).astype(jnp.int32),
-                lax.dynamic_index_in_dim(extent, head_at, 1, False).reshape(-1),
-                lax.dynamic_index_in_dim(route, head_at, 1, False).reshape(-1),
-            ]
-        )
+        far_all, tokens, rel_bias, *numbers = tie(far_all, tokens_in, rel_table, *numbers)
+        table = jnp.stack(numbers).astype(jnp.int32)
+        x_rows, unit_turned, n_rows, bias = prepare(tokens, rel_bias)
         bias, table, n_rows, *near_all = tie(bias, table, n_rows, *near_all)
         far_all, near_all[0] = tie(far_all, near_all[0])
         near_all = near_all + [passed(piece, CORE) for piece in near_all]
         far_got = [far_all] + spread(far_all, PLANE)
     else:
-        x_rows, unit_rows, n_rows, bias = prepare(tokens_in, rel_table)
-        table = jnp.concatenate(
-            [
-                jnp.stack([me, swap_bits(me)]).astype(jnp.int32),
-                lax.dynamic_index_in_dim(extent, head_at, 1, False).reshape(-1),
-                lax.dynamic_index_in_dim(route, head_at, 1, False).reshape(-1),
-            ]
-        )
+        table = jnp.stack(numbers).astype(jnp.int32)
+        x_rows, unit_turned, n_rows, bias = prepare(tokens_in, rel_table)
         near_all, far_all = plain_pieces(near, far)
 
     packed, soft, attn, w_qkv, w_proj = call(
@@ -761,22 +762,23 @@
         [
             ((ROWS, 3 * C), LOW), ((MICRO, 2 * GROUPS, GROUP * WIN, 128), LOW), ((ROWS, C), LOW), ((C, 3 * C), LOW), ((C, C), LOW),
         ],
-        (table, n_rows, vectors, bias, reach, place, heads_low, *near_all),
+        (table, extents, routes, n_rows, vectors, bias, reach, place, heads_low, *near_all),
         "attend",
         limit=8,
         scratch=[pltpu.VMEM((4, C, C), LOW)],
         flops=8e9,
-        scalars=1,
-    )
-
-    middle, n_two = call(middle_body, [((ROWS, C), F32), ((ROWS, C), LOW)], (attn, x_rows, w_proj, vectors), "middle",
-        limit=4)
+        scalars=3,
+    )
+
+    middle, n_two, n_turned = call(
+        middle_body, [((ROWS, C), F32), ((ROWS, C), LOW), ((C, ROWS), LOW)], (attn, x_rows, w_proj, vectors), "middle", limit=4
+    )
 
     late = cotangent
     if direct:
         middle, late, *far_got = tie(middle, late, *far_got)
         far_core = [passed(piece, CORE) for piece in far_got]
-    g_rows = prepare_grad(late)
+    g_rows, g_turned = prepare_grad(late)
     if direct:
         g_rows, *far_core = tie(g_rows, *far_core)
         far_all = far_got + far_core
@@ -796,12 +798,11 @@
     far_keep, far_send = call(
         functools.partial(mlp_weights_body, direct),
         [((half, 2 * PIECE, C), LOW)] * 2,
-        (table, n_two, g_rows, hidden, grad_hidden),
+        (table, n_turned, g_turned, hidden, grad_hidden),
         "mlp_weights",
         limit=14,
         scratch=[
-            pltpu.VMEM((C, ROWS), LOW), pltpu.VMEM((C, ROWS), LOW), pltpu.VMEM((BLOCKS, 2 * PIECE, C), LOW),
-            pltpu.VMEM((C, FF), LOW), pltpu.VMEM((C, FF), LOW),
+            pltpu.VMEM((BLOCKS, 2 * PIECE, C), LOW), pltpu.VMEM((C, FF), LOW), pltpu.VMEM((C, FF), LOW),
         ],
         flops=4e9,
         scalars=1,
@@ -810,29 +811,44 @@
     if direct:
         far_got = passed(far_send, CORE)
 
-    (block_out,) = call(output_body, [(tokens_in.shape, LOW)], (hidden, w_fc2, middle, vectors, back), "output",
-        limit=5, flops=2e9)
+    def output_piece(first, last, hidden, block_out):
+        far = pl.BlockSpec(memory_space=pltpu.HBM)
+        before = [] if block_out is None else [pltpu.with_memory_space_constraint(block_out, pltpu.HBM)]
+        return pl.pallas_call(
+            functools.partial(output_body, first, last),
+            in_specs=[HELD] * 5 + [far] * len(before),
+            out_specs=far,
+            out_shape=pltpu.HBM(tokens_in.shape, LOW),
+            input_output_aliases={} if block_out is None else {5: 0},
+            scratch_shapes=[pltpu.VMEM((last - first, 1, GRID, GRID, C), LOW), pltpu.SemaphoreType.DMA((last - first,))],
+            compiler_params=whole(8),
+            cost_estimate=pl.CostEstimate(flops=int(4e8 * (last - first)), bytes_accessed=2000000, transcendentals=0),
+            name="output",
+        )(hidden, w_fc2, middle, vectors, back, *before)
+
+    early_images = 3 if direct else MICRO
+    block_out = output_piece(0, early_images, hidden, None)
 
     if direct:
-        block_out, far_got, grad_middle = tie(block_out, far_got, grad_middle)
+        block_out, far_got, grad_middle, hidden = tie(block_out, far_got, grad_middle, hidden)
         far_stays, far_goes = first_sum(far_keep, far_got)
         far_got = sent(far_goes, PLANE)
 
     packed_grad, grad_low, bias_sum, sums_attend = call(
         attend_back_body,
         [((ROWS, 3 * C), LOW), ((ROWS, C), LOW), ((GROUPS, GROUP * WIN, 128), F32), ((1, 3 * C), F32)],
-        (table, grad_middle, packed, soft, w_proj, place, heads_low),
+        (table, extents, routes, grad_middle, packed, soft, w_proj, place, heads_low),
         "attend_back",
         limit=6,
         flops=8e9,
-        scalars=1,
+        scalars=3,
     )
 
     vec_square = jnp.concatenate([vectors, jnp.zeros((4, C), F32)], axis=0)
     near_keep, near_send, sums_input = call(
         functools.partial(attend_weights_body, direct),
         [((half, PIECE, C), LOW)] * 2 + [((2, C), F32)],
-        (table, unit_rows, grad_low, packed_grad, attn, w_qkv, sums_attend, vec_square),
+        (table, unit_turned, grad_low, packed_grad, attn, w_qkv, sums_attend, vec_square),
         "attend_weights",
         limit=8,
         scratch=[pltpu.VMEM((BLOCKS, PIECE, C), LOW)],
@@ -842,7 +858,10 @@
 
     if direct:
         near_send, *far_got = tie(near_send, *far_got)
+        near_send, hidden = tie(near_send, hidden)
         near_got = passed(near_send, CORE)
+        block_out = output_piece(early_images, MICRO, hidden, block_out)
+        near_got, block_out = tie(near_got, block_out)
         near_stays, near_goes = first_sum(near_keep, near_got)
         near_goes[0], bias_sum = tie(near_goes[0], bias_sum)
         near_got = sent(near_goes, PLANE)
@@ -892,7 +911,7 @@
         grad_block, *near_got = tie(grad_block, *near_got)
         near_grad, far_grad, spare = pl.pallas_call(
             functools.partial(finish_body, patches),
-            out_shape=[sds((depth, C), F32), sds((2 * depth, C), F32), sds((32, C), F32)],
+            out_shape=[sds((depth, C), F32), sds((2 * depth, C), F32), sds((24, C), F32)],
             compiler_params=whole(2),
             name="finish",
         )(near_stays, far_stays, vec_grad, table_grad, *near_got, *far_got)
@@ -908,8 +927,9 @@
         near_grad, far_grad = share_plain(near_keep, near_send) / patches, share_plain(far_keep, far_send) / patches
         squares = jnp.sum(near_grad * near_grad) + jnp.sum(far_grad * far_grad)
         vec_grad, table_grad, squares = lax.psum((vec_grad, table_grad, squares), BOTH)
-        table_grad = jnp.concatenate([table_grad, jnp.zeros((12, C - REL), F32)], axis=1)
-        spare = jnp.concatenate([vec_grad / patches, table_grad / patches, jnp.broadcast_to(squares, (8, C))], axis=0)
+        gap = jnp.zeros((6, C // 2 - REL), F32)
+        table_grad = jnp.concatenate([table_grad[:6] / patches, gap, table_grad[6:] / patches, gap], axis=1)
+        spare = jnp.concatenate([vec_grad / patches, table_grad, jnp.broadcast_to(squares, (6, C))], axis=0)
 
     olds = (
         qkv_weight, proj_weight.T, fc1_weight, fc2_weight.T, vectors, rel_table.T,
@@ -920,6 +940,7 @@
     news = pl.pallas_call(
         adam_body,
         out_shape=shapes,
+        scratch_shapes=[pltpu.VMEM((NH, REL), F32)],
         compiler_params=whole(8),
         name="adam",
     )(near_grad, far_grad, spare, *olds)

time: 120 us -> 118 us (0.983)
  starting transfers between devices: 48 us -> 46.7 us
    pallas_call x1 -> x3, Pallas kernels: 1.27 us -> 5.75 us  [the longest x2 4.42 us: output_piece(): pl.pallas_call(functools.partial(output_body, first, last), in_specs=[HEL...]
    pallas_call x10 -> x9, Pallas kernels: 43.5 us -> 40.2 us  [call(): pl.pallas_call(body, in_specs=[SCALARS] * scalars + [far] * fetched + [HE...]
    ppermute x41, starting transfers between devices: 48 us -> 46.7 us  [passed(): return lax.ppermute(rows, BOTH, [(i, i ^ mask) for i in range(devices)])]
  transfers between devices with their start and end apart: 41 -> 41, of which waited for: 7 -> 9; matrix products, arithmetic and copies ran while one was open for 1% -> 0% of each run, Pallas kernels for 36% -> 38%
where the time goes in v7:
time: 118 us; the launch traced here: 117 us
  Pallas kernels  59.3 us (50%)
  starting transfers between devices  46.7 us (40%)
  waiting for transfers between devices  9.29 us (8%)
  between operations  1.63 us (1%)
    ppermute x41, starting transfers between devices, passed(): return lax.ppermute(rows, BOTH, [(i, i ^ mask) for i in range(devices)])  46.7 us
    pallas_call x9, Pallas kernels, call(): pl.pallas_call(body, in_specs=[SCALARS] * scalars + [far] * fetched + [HE...  40.2 us
    pallas_call x3, Pallas kernels, input_piece(): pl.pallas_call(functools.partial(input_body, first, last), in_specs=[far]...  11.5 us
    ppermute x41, waiting for transfers between devices, passed(): return lax.ppermute(rows, BOTH, [(i, i ^ mask) for i in range(devices)])  9.29 us
    pallas_call x2, Pallas kernels, output_piece(): pl.pallas_call(functools.partial(output_body, first, last), in_specs=[HEL...  4.42 us
  transfers between devices with their start and end apart: 41, of which 9 were waited for; matrix products, arithmetic and copies ran while one was open for 0% of the time, Pallas kernels for 38%

profile of v7, /device:TPU:0, one launch (start us, length us, event | category | flops | bytes accessed | tf_op | source)
XLA Modules:
  0.0 117.4 jit_solution(17719906674467035763)
XLA Ops:
  1.7 5.1 %collective-permute-start.5 = (bf16[1,64,384]{2,1,0:T(8,128)(2,1)S(1)}, bf16[1,64,384]{2,1,0:T(8,128)(2,1)S(1)}, u32[]{:S(2)}, u32[]{:S(2)}) collective-permute-start(bf16[1,64,384]{2,1,0:T(8,128)(2,1)S(1)} %bitcast.40), channel_id=1, source_target_pairs={{0,24},{1,25},{2,26},{3,27},{4,28},{5,29},{6,30},{7,31},{8,16},{9,... | collective-permute-start | bytes 147464 | tf_op jit(solution)/shard_map/ppermute | solution.py:655
  7.5 3.7 %collective-permute-start.2 = (bf16[1,80,384]{2,1,0:T(8,128)(2,1)S(1)}, bf16[1,80,384]{2,1,0:T(8,128)(2,1)S(1)}, u32[]{:S(2)}, u32[]{:S(2)}) collective-permute-start(bf16[1,80,384]{2,1,0:T(8,128)(2,1)S(1)} %bitcast.36), channel_id=1, source_target_pairs={{0,24},{1,25},{2,26},{3,27},{4,28},{5,29},{6,30},{7,31},{8,16},{9,... | collective-permute-start | bytes 184328 | tf_op jit(solution)/shard_map/ppermute | solution.py:655
  12.8 1.6 %collective-permute-start.6 = (bf16[4,64,384]{2,1,0:T(8,128)(2,1)S(1)}, bf16[4,64,384]{2,1,0:T(8,128)(2,1)S(1)}, u32[]{:S(2)}, u32[]{:S(2)}) collective-permute-start(bf16[4,64,384]{2,1,0:T(8,128)(2,1)S(1)} %pad_maximum_fusion.1.refs_0_), channel_id=1, source_target_pairs={{0,2},{1,3},{2,0},{3,1},{4,6},{5,7},{6,4},{7,5},{8,10},{9,11},{10,... | collective-permute-start | bytes 589832 | tf_op jit(solution)/shard_map/ppermute | solution.py:655
  16.8 4.3 %prep.1 = (bf16[1280,384]{1,0:T(8,128)(2,1)}, bf16[384,1280]{1,0:T(8,128)(2,1)}, bf16[1280,384]{1,0:T(8,128)(2,1)S(1)}, f32[768,128]{1,0:T(8,128)S(1)}) custom-call(f32[12,169]{1,0:T(8,128)} %bitcast.46, bf16[256,128]{1,0:T(8,128)(2,1)} %constant.84.clone.lookup_hbm.lookup_ref, f32[12,384]{1,0:T(8,128)} %refs_4_.3, ...), custom_call_target="tpu_custom_call" | custom-call | flops 1000000000 | bytes 4000000 | tf_op jit(solution)/shard_map/prep/pallas_call | solution.py:159
  21.2 1.5 %collective-permute-done.8.refs_3_ = bf16[4,64,384]{2,1,0:T(8,128)(2,1)S(1)} collective-permute-done((bf16[4,64,384]{2,1,0:T(8,128)(2,1)S(1)}, bf16[4,64,384]{2,1,0:T(8,128)(2,1)S(1)}, u32[]{:S(2)}, u32[]{:S(2)}) %collective-permute-start.8) | collective-permute-done | bytes 196640 | tf_op jit(solution)/shard_map/ppermute | solution.py:655
  27.3 7.6 %attend.1 = (bf16[1280,1152]{1,0:T(8,128)(2,1)S(1)}, bf16[5,6,256,128]{3,2,1,0:T(8,128)(2,1)S(1)}, bf16[1280,384]{1,0:T(8,128)(2,1)S(1)}, bf16[384,1152]{1,0:T(8,128)(2,1)S(1)}, bf16[384,384]{1,0:T(8,128)(2,1)S(1)}) custom-call(s32[3]{0:T(128)S(1)} %pad_add_fusion.table_ref, s32[4,2,5]{2,1,0:T(2,128)S(1)} %bitcast.52, s32[4,4,5]{2,1,0:T(4,128)S(1)} %bitcast.50, ...), custom_call_target="tpu_custom_call" | custom-call | flops 8000000000 | bytes 4000000 | tf_op jit(solution)/shard_map/attend/pallas_call | solution.py:159
  36.4 1.9 %collective-permute-done.15.refs_11_ = bf16[4,80,384]{2,1,0:T(8,128)(2,1)S(1)} collective-permute-done((bf16[4,80,384]{2,1,0:T(8,128)(2,1)S(1)}, bf16[4,80,384]{2,1,0:T(8,128)(2,1)S(1)}, u32[]{:S(2)}, u32[]{:S(2)}) %collective-permute-start.15) | collective-permute-done | bytes 245792 | tf_op jit(solution)/shard_map/ppermute | solution.py:655
  39.3 1.8 %prep_grad.1 = (bf16[1280,384]{1,0:T(8,128)(2,1)S(1)}, bf16[384,1280]{1,0:T(8,128)(2,1)S(1)}) custom-call(bf16[256,224]{1,0:T(8,128)(2,1)} %constant.83.clone.deal_hbm, bf16[5,1,14,14,384]{4,3,2,1,0:T(8,128)(2,1)} %cot_hbm), custom_call_target="tpu_custom_call" | custom-call | flops 1000000000 | bytes 4000000 | tf_op jit(solution)/shard_map/prep_grad/pallas_call | solution.py:159
  41.2 8.2 %mlp.1 = (bf16[1280,1536]{1,0:T(8,128)(2,1)S(1)}, bf16[1280,1536]{1,0:T(8,128)(2,1)S(1)}, f32[1280,384]{1,0:T(8,128)S(1)}, f32[12,384]{1,0:T(8,128)S(1)}, bf16[384,1536]{1,0:T(8,128)(2,1)S(1)}) custom-call(s32[3]{0:T(128)S(1)} %pad_add_fusion.table_ref, f32[1280,384]{1,0:T(8,128)S(1)} %get-tuple-element.181.middle_ref, ...), custom_call_target="tpu_custom_call" | custom-call | flops 10000000000 | bytes 4000000 | tf_op jit(solution)/shard_map/mlp/pallas_call | solution.py:159
  49.4 4.1 %mlp_weights.1 = (bf16[16,96,384]{2,1,0:T(8,128)(2,1)S(1)}, bf16[16,96,384]{2,1,0:T(8,128)(2,1)S(1)}) custom-call(s32[3]{0:T(128)S(1)} %pad_add_fusion.table_ref, bf16[384,1280]{1,0:T(8,128)(2,1)S(1)} %get-tuple-element.196.n_turned, bf16[384,1280]{1,0:T(8,128)(2,1)S(1)} %get-tuple-element.197.g_turned, ...), custom_call_target="tpu_custom_call" | custom-call | flops 4000000000 | bytes 4000000 | tf_op jit(solution)/shard_map/mlp_weights/pallas_call | solution.py:159
  53.7 2.5 %output.2.refs_0_ = bf16[5,1,14,14,384]{4,3,2,1,0:T(8,128)(2,1)} custom-call(bf16[1280,1536]{1,0:T(8,128)(2,1)S(1)} %get-tuple-element.217.hidden_ref, bf16[384,1536]{1,0:T(8,128)(2,1)S(1)} %get-tuple-element.195.w2_ref, f32[1280,384]{1,0:T(8,128)S(1)} %get-tuple-element.181.middle_ref, f32[12,384]{1,0:T(8,128)S(1)} %copy-done.5, bf16[224,256]{1,0:T(8,128)(2,1)S(1)} %copy-done.4), custom_call_target="tpu_custom_call" | custom-call | flops 1200000000 | bytes 2000000 | tf_op jit(solution)/shard_map/output/pallas_call | solution.py:817
  60.3 8.1 %attend_back.1 = (bf16[1280,1152]{1,0:T(8,128)(2,1)S(1)}, bf16[1280,384]{1,0:T(8,128)(2,1)S(1)}, f32[3,256,128]{2,1,0:T(8,128)S(1)}, f32[1,1152]{1,0:T(1,128)S(1)}) custom-call(s32[3]{0:T(128)S(1)} %pad_add_fusion.table_ref, s32[4,2,5]{2,1,0:T(2,128)S(1)} %bitcast.53, s32[4,4,5]{2,1,0:T(4,128)S(1)} %bitcast.51, ...), custom_call_target="tpu_custom_call" | custom-call | flops 8000000000 | bytes 4000000 | tf_op jit(solution)/shard_map/attend_back/pallas_call | solution.py:159
  68.5 3.8 %attend_weights.1 = (bf16[16,48,384]{2,1,0:T(8,128)(2,1)S(1)}, bf16[16,48,384]{2,1,0:T(8,128)(2,1)S(1)}, f32[2,384]{1,0:T(2,128)S(1)}) custom-call(s32[3]{0:T(128)S(1)} %pad_add_fusion.table_ref, bf16[384,1280]{1,0:T(8,128)(2,1)S(1)} %copy-done.29, bf16[1280,384]{1,0:T(8,128)(2,1)S(1)} %get-tuple-element.204.grad_low_ref, ...), custom_call_target="tpu_custom_call" | custom-call | flops 2000000000 | bytes 4000000 | tf_op jit(solution)/shard_map/attend_weights/pallas_call | solution.py:159
  73.5 1.9 %output.3 = bf16[5,1,14,14,384]{4,3,2,1,0:T(8,128)(2,1)} custom-call(bf16[1280,1536]{1,0:T(8,128)(2,1)S(1)} %get-tuple-element.217.hidden_ref, bf16[384,1536]{1,0:T(8,128)(2,1)S(1)} %get-tuple-element.195.w2_ref, f32[1280,384]{1,0:T(8,128)S(1)} %get-tuple-element.181.middle_ref, f32[12,384]{1,0:T(8,128)S(1)} %copy-done.5, ...), custom_call_target="tpu_custom_call", output_to_operand_aliasing={{}: (5, {})} | custom-call | flops 800000000 | bytes 2000000 | tf_op jit(solution)/shard_map/output/pallas_call | solution.py:817
  80.1 2.3 %collective-permute-start.25 = (bf16[1,96,384]{2,1,0:T(8,128)(2,1)S(1)}, bf16[1,96,384]{2,1,0:T(8,128)(2,1)S(1)}, u32[]{:S(2)}, u32[]{:S(2)}) collective-permute-start(bf16[1,96,384]{2,1,0:T(8,128)(2,1)S(1)} %get-tuple-element.236), channel_id=1, source_target_pairs={{0,16},{1,17},{2,18},{3,19},{4,20},{5,21},{6,22},{7,23},{8,24},{9,... | collective-permute-start | bytes 221192 | tf_op jit(solution)/shard_map/ppermute | solution.py:655
  82.5 1.9 %collective-permute-start.32 = (bf16[1,96,384]{2,1,0:T(8,128)(2,1)S(1)}, bf16[1,96,384]{2,1,0:T(8,128)(2,1)S(1)}, u32[]{:S(2)}, u32[]{:S(2)}) collective-permute-start(bf16[1,96,384]{2,1,0:T(8,128)(2,1)S(1)} %get-tuple-element.256), channel_id=1, source_target_pairs={{0,8},{1,9},{2,10},{3,11},{4,12},{5,13},{6,14},{7,15},{8,0},{9,1},... | collective-permute-start | bytes 221192 | tf_op jit(solution)/shard_map/ppermute | solution.py:655
  84.3 1.8 %collective-permute-done.25.refs_3_ = bf16[1,96,384]{2,1,0:T(8,128)(2,1)S(1)} collective-permute-done((bf16[1,96,384]{2,1,0:T(8,128)(2,1)S(1)}, bf16[1,96,384]{2,1,0:T(8,128)(2,1)S(1)}, u32[]{:S(2)}, u32[]{:S(2)}) %collective-permute-start.25) | collective-permute-done | bytes 73760 | tf_op jit(solution)/shard_map/ppermute | solution.py:655
  86.2 3.4 %collective-permute-start.33 = (bf16[1,96,384]{2,1,0:T(8,128)(2,1)S(1)}, bf16[1,96,384]{2,1,0:T(8,128)(2,1)S(1)}, u32[]{:S(2)}, u32[]{:S(2)}) collective-permute-start(bf16[1,96,384]{2,1,0:T(8,128)(2,1)S(1)} %get-tuple-element.257), channel_id=1, source_target_pairs={{0,24},{1,25},{2,26},{3,27},{4,28},{5,29},{6,30},{7,31},{8,16},{9,... | collective-permute-start | bytes 221192 | tf_op jit(solution)/shard_map/ppermute | solution.py:655
  90.7 3.4 %collective-permute-start.31 = (bf16[1,48,384]{2,1,0:T(8,128)(2,1)S(1)}, bf16[1,48,384]{2,1,0:T(8,128)(2,1)S(1)}, u32[]{:S(2)}, u32[]{:S(2)}) collective-permute-start(bf16[1,48,384]{2,1,0:T(8,128)(2,1)S(1)} %get-tuple-element.251), channel_id=1, source_target_pairs={{0,24},{1,25},{2,26},{3,27},{4,28},{5,29},{6,30},{7,31},{8,16},{9,... | collective-permute-start | bytes 110600 | tf_op jit(solution)/shard_map/ppermute | solution.py:655
  94.2 4.2 %input_grad.3.refs_4_ = bf16[5,1,14,14,384]{4,3,2,1,0:T(8,128)(2,1)} custom-call(bf16[384,1152]{1,0:T(8,128)(2,1)} %copy-done.3, bf16[1280,1152]{1,0:T(8,128)(2,1)} %copy-done, bf16[1280,384]{1,0:T(8,128)(2,1)} %get-tuple-element.177.x_ref.refs_2_, f32[1280,384]{1,0:T(8,128)} %copy-done.1, f32[12,384]{1,0:T(8,128)S(1)} %copy-done.5, ...), custom_call_target="tpu_custom_call" | custom-call | flops 800000000 | bytes 2000000 | tf_op jit(solution)/shard_map/input_grad/pallas_call | solution.py:888
  103.3 4.2 %input_grad.4.refs_4_ = bf16[5,1,14,14,384]{4,3,2,1,0:T(8,128)(2,1)} custom-call(bf16[384,1152]{1,0:T(8,128)(2,1)} %copy-done.3, bf16[1280,1152]{1,0:T(8,128)(2,1)} %copy-done, bf16[1280,384]{1,0:T(8,128)(2,1)} %get-tuple-element.177.x_ref.refs_2_, f32[1280,384]{1,0:T(8,128)} %copy-done.1, ...), custom_call_target="tpu_custom_call", output_to_operand_aliasing={{}: (4, {})} | custom-call | flops 800000000 | bytes 2000000 | tf_op jit(solution)/shard_map/input_grad/pallas_call | solution.py:888
  107.9 2.1 %collective-permute-start.39 = (f32[24,384]{1,0:T(8,128)S(1)}, f32[24,384]{1,0:T(8,128)S(1)}, u32[]{:S(2)}, u32[]{:S(2)}) collective-permute-start(f32[24,384]{1,0:T(8,128)S(1)} %add_add_fusion.1), channel_id=1, source_target_pairs={{0,8},{1,9},{2,10},{3,11},{4,12},{5,13},{6,14},{7,15},{8,0},{9,1},... | collective-permute-start | bytes 110600 | tf_op jit(solution)/shard_map/ppermute | solution.py:655
  109.9 2.3 %collective-permute-start.40 = (f32[24,384]{1,0:T(8,128)S(1)}, f32[24,384]{1,0:T(8,128)S(1)}, u32[]{:S(2)}, u32[]{:S(2)}) collective-permute-start(f32[24,384]{1,0:T(8,128)S(1)} %add_add_fusion.1), channel_id=1, source_target_pairs={{0,24},{1,25},{2,26},{3,27},{4,28},{5,29},{6,30},{7,31},{8,16},{9,... | collective-permute-start | bytes 110600 | tf_op jit(solution)/shard_map/ppermute | solution.py:655
  112.3 3.1 %input_grad.5 = bf16[5,1,14,14,384]{4,3,2,1,0:T(8,128)(2,1)} custom-call(bf16[384,1152]{1,0:T(8,128)(2,1)} %copy-done.3, bf16[1280,1152]{1,0:T(8,128)(2,1)} %copy-done, bf16[1280,384]{1,0:T(8,128)(2,1)} %get-tuple-element.177.x_ref.refs_2_, f32[1280,384]{1,0:T(8,128)} %copy-done.1, ...), custom_call_target="tpu_custom_call", output_to_operand_aliasing={{}: (4, {})} | custom-call | flops 400000000 | bytes 2000000 | tf_op jit(solution)/shard_map/input_grad/pallas_call | solution.py:888
  (149 shorter events, 30.7 us)
Async XLA Ops:
  1.7 9.5 %collective-permute-start.5 = (bf16[1,64,384]{2,1,0:T(8,128)(2,1)S(1)}, bf16[1,64,384]{2,1,0:T(8,128)(2,1)S(1)}, u32[]{:S(2)}, u32[]{:S(2)}) collective-permute-start(bf16[1,64,384]{2,1,0:T(8,128)(2,1)S(1)} %bitcast.40), channel_id=1, source_target_pairs={{0,24},{1,25},{2,26},{3,27},{4,28},{5,29},{6,30},{7,31},{8,16},{9,... | collective-permute-start | bytes 147464 | tf_op jit(solution)/shard_map/ppermute | solution.py:655
  7.5 8.4 %collective-permute-start.2 = (bf16[1,80,384]{2,1,0:T(8,128)(2,1)S(1)}, bf16[1,80,384]{2,1,0:T(8,128)(2,1)S(1)}, u32[]{:S(2)}, u32[]{:S(2)}) collective-permute-start(bf16[1,80,384]{2,1,0:T(8,128)(2,1)S(1)} %bitcast.36), channel_id=1, source_target_pairs={{0,24},{1,25},{2,26},{3,27},{4,28},{5,29},{6,30},{7,31},{8,16},{9,... | collective-permute-start | bytes 184328 | tf_op jit(solution)/shard_map/ppermute | solution.py:655
  12.8 8.3 %collective-permute-start.6 = (bf16[4,64,384]{2,1,0:T(8,128)(2,1)S(1)}, bf16[4,64,384]{2,1,0:T(8,128)(2,1)S(1)}, u32[]{:S(2)}, u32[]{:S(2)}) collective-permute-start(bf16[4,64,384]{2,1,0:T(8,128)(2,1)S(1)} %pad_maximum_fusion.1.refs_0_), channel_id=1, source_target_pairs={{0,2},{1,3},{2,0},{3,1},{4,6},{5,7},{6,4},{7,5},{8,10},{9,11},{10,... | collective-permute-start | bytes 589832 | tf_op jit(solution)/shard_map/ppermute | solution.py:655
  14.4 6.7 %collective-permute-start.7 = (bf16[4,64,384]{2,1,0:T(8,128)(2,1)S(1)}, bf16[4,64,384]{2,1,0:T(8,128)(2,1)S(1)}, u32[]{:S(2)}, u32[]{:S(2)}) collective-permute-start(bf16[4,64,384]{2,1,0:T(8,128)(2,1)S(1)} %pad_maximum_fusion.1.refs_0_), channel_id=1, source_target_pairs={{0,4},{1,5},{2,6},{3,7},{4,0},{5,1},{6,2},{7,3},{8,12},{9,13},{10,... | collective-permute-start | bytes 589832 | tf_op jit(solution)/shard_map/ppermute | solution.py:655
  15.9 6.8 %collective-permute-start.8 = (bf16[4,64,384]{2,1,0:T(8,128)(2,1)S(1)}, bf16[4,64,384]{2,1,0:T(8,128)(2,1)S(1)}, u32[]{:S(2)}, u32[]{:S(2)}) collective-permute-start(bf16[4,64,384]{2,1,0:T(8,128)(2,1)S(1)} %pad_maximum_fusion.1.refs_0_), channel_id=1, source_target_pairs={{0,6},{1,7},{2,4},{3,5},{4,2},{5,3},{6,0},{7,1},{8,14},{9,15},{10,... | collective-permute-start | bytes 589832 | tf_op jit(solution)/shard_map/ppermute | solution.py:655
  23.7 12.7 %collective-permute-start.13 = (bf16[4,80,384]{2,1,0:T(8,128)(2,1)S(1)}, bf16[4,80,384]{2,1,0:T(8,128)(2,1)S(1)}, u32[]{:S(2)}, u32[]{:S(2)}) collective-permute-start(bf16[4,80,384]{2,1,0:T(8,128)(2,1)S(1)} %pad_maximum_fusion.refs_8_), channel_id=1, source_target_pairs={{0,2},{1,3},{2,0},{3,1},{4,6},{5,7},{6,4},{7,5},{8,10},{9,11},{10,... | collective-permute-start | bytes 737288 | tf_op jit(solution)/shard_map/ppermute | solution.py:655
  25.2 11.2 %collective-permute-start.14 = (bf16[4,80,384]{2,1,0:T(8,128)(2,1)S(1)}, bf16[4,80,384]{2,1,0:T(8,128)(2,1)S(1)}, u32[]{:S(2)}, u32[]{:S(2)}) collective-permute-start(bf16[4,80,384]{2,1,0:T(8,128)(2,1)S(1)} %pad_maximum_fusion.refs_8_), channel_id=1, source_target_pairs={{0,4},{1,5},{2,6},{3,7},{4,0},{5,1},{6,2},{7,3},{8,12},{9,13},{10,... | collective-permute-start | bytes 737288 | tf_op jit(solution)/shard_map/ppermute | solution.py:655
  26.7 11.6 %collective-permute-start.15 = (bf16[4,80,384]{2,1,0:T(8,128)(2,1)S(1)}, bf16[4,80,384]{2,1,0:T(8,128)(2,1)S(1)}, u32[]{:S(2)}, u32[]{:S(2)}) collective-permute-start(bf16[4,80,384]{2,1,0:T(8,128)(2,1)S(1)} %pad_maximum_fusion.refs_8_), channel_id=1, source_target_pairs={{0,6},{1,7},{2,4},{3,5},{4,2},{5,3},{6,0},{7,1},{8,14},{9,15},{10,... | collective-permute-start | bytes 737288 | tf_op jit(solution)/shard_map/ppermute | solution.py:655
  56.7 15.5 %collective-permute-start.21 = (bf16[4,96,384]{2,1,0:T(8,128)(2,1)S(1)}, bf16[4,96,384]{2,1,0:T(8,128)(2,1)S(1)}, u32[]{:S(2)}, u32[]{:S(2)}) collective-permute-start(bf16[4,96,384]{2,1,0:T(8,128)(2,1)S(1)} %get-tuple-element.211), channel_id=1, source_target_pairs={{0,2},{1,3},{2,0},{3,1},{4,6},{5,7},{6,4},{7,5},{8,10},{9,11},{10,... | collective-permute-start | bytes 884744 | tf_op jit(solution)/shard_map/ppermute | solution.py:655
  58.0 14.3 %collective-permute-start.22 = (bf16[4,96,384]{2,1,0:T(8,128)(2,1)S(1)}, bf16[4,96,384]{2,1,0:T(8,128)(2,1)S(1)}, u32[]{:S(2)}, u32[]{:S(2)}) collective-permute-start(bf16[4,96,384]{2,1,0:T(8,128)(2,1)S(1)} %get-tuple-element.212), channel_id=1, source_target_pairs={{0,4},{1,5},{2,6},{3,7},{4,0},{5,1},{6,2},{7,3},{8,12},{9,13},{10,... | collective-permute-start | bytes 884744 | tf_op jit(solution)/shard_map/ppermute | solution.py:655
  59.5 14.0 %collective-permute-start.23 = (bf16[4,96,384]{2,1,0:T(8,128)(2,1)S(1)}, bf16[4,96,384]{2,1,0:T(8,128)(2,1)S(1)}, u32[]{:S(2)}, u32[]{:S(2)}) collective-permute-start(bf16[4,96,384]{2,1,0:T(8,128)(2,1)S(1)} %get-tuple-element.213), channel_id=1, source_target_pairs={{0,6},{1,7},{2,4},{3,5},{4,2},{5,3},{6,0},{7,1},{8,14},{9,15},{10,... | collective-permute-start | bytes 884744 | tf_op jit(solution)/shard_map/ppermute | solution.py:655
  75.6 14.0 %collective-permute-start.26 = (bf16[4,48,384]{2,1,0:T(8,128)(2,1)S(1)}, bf16[4,48,384]{2,1,0:T(8,128)(2,1)S(1)}, u32[]{:S(2)}, u32[]{:S(2)}) collective-permute-start(bf16[4,48,384]{2,1,0:T(8,128)(2,1)S(1)} %get-tuple-element.237), channel_id=1, source_target_pairs={{0,2},{1,3},{2,0},{3,1},{4,6},{5,7},{6,4},{7,5},{8,10},{9,11},{10,... | collective-permute-start | bytes 442376 | tf_op jit(solution)/shard_map/ppermute | solution.py:655
  76.9 12.7 %collective-permute-start.27 = (bf16[4,48,384]{2,1,0:T(8,128)(2,1)S(1)}, bf16[4,48,384]{2,1,0:T(8,128)(2,1)S(1)}, u32[]{:S(2)}, u32[]{:S(2)}) collective-permute-start(bf16[4,48,384]{2,1,0:T(8,128)(2,1)S(1)} %get-tuple-element.238), channel_id=1, source_target_pairs={{0,4},{1,5},{2,6},{3,7},{4,0},{5,1},{6,2},{7,3},{8,12},{9,13},{10,... | collective-permute-start | bytes 442376 | tf_op jit(solution)/shard_map/ppermute | solution.py:655
  78.4 11.3 %collective-permute-start.28 = (bf16[4,48,384]{2,1,0:T(8,128)(2,1)S(1)}, bf16[4,48,384]{2,1,0:T(8,128)(2,1)S(1)}, u32[]{:S(2)}, u32[]{:S(2)}) collective-permute-start(bf16[4,48,384]{2,1,0:T(8,128)(2,1)S(1)} %get-tuple-element.239), channel_id=1, source_target_pairs={{0,6},{1,7},{2,4},{3,5},{4,2},{5,3},{6,0},{7,1},{8,14},{9,15},{10,... | collective-permute-start | bytes 442376 | tf_op jit(solution)/shard_map/ppermute | solution.py:655
  80.1 6.1 %collective-permute-start.25 = (bf16[1,96,384]{2,1,0:T(8,128)(2,1)S(1)}, bf16[1,96,384]{2,1,0:T(8,128)(2,1)S(1)}, u32[]{:S(2)}, u32[]{:S(2)}) collective-permute-start(bf16[1,96,384]{2,1,0:T(8,128)(2,1)S(1)} %get-tuple-element.236), channel_id=1, source_target_pairs={{0,16},{1,17},{2,18},{3,19},{4,20},{5,21},{6,22},{7,23},{8,24},{9,... | collective-permute-start | bytes 221192 | tf_op jit(solution)/shard_map/ppermute | solution.py:655
  82.5 15.9 %collective-permute-start.32 = (bf16[1,96,384]{2,1,0:T(8,128)(2,1)S(1)}, bf16[1,96,384]{2,1,0:T(8,128)(2,1)S(1)}, u32[]{:S(2)}, u32[]{:S(2)}) collective-permute-start(bf16[1,96,384]{2,1,0:T(8,128)(2,1)S(1)} %get-tuple-element.256), channel_id=1, source_target_pairs={{0,8},{1,9},{2,10},{3,11},{4,12},{5,13},{6,14},{7,15},{8,0},{9,1},... | collective-permute-start | bytes 221192 | tf_op jit(solution)/shard_map/ppermute | solution.py:655
  86.2 12.2 %collective-permute-start.33 = (bf16[1,96,384]{2,1,0:T(8,128)(2,1)S(1)}, bf16[1,96,384]{2,1,0:T(8,128)(2,1)S(1)}, u32[]{:S(2)}, u32[]{:S(2)}) collective-permute-start(bf16[1,96,384]{2,1,0:T(8,128)(2,1)S(1)} %get-tuple-element.257), channel_id=1, source_target_pairs={{0,24},{1,25},{2,26},{3,27},{4,28},{5,29},{6,30},{7,31},{8,16},{9,... | collective-permute-start | bytes 221192 | tf_op jit(solution)/shard_map/ppermute | solution.py:655
  89.7 8.7 %collective-permute-start.29 = (bf16[1,48,384]{2,1,0:T(8,128)(2,1)S(1)}, bf16[1,48,384]{2,1,0:T(8,128)(2,1)S(1)}, u32[]{:S(2)}, u32[]{:S(2)}) collective-permute-start(bf16[1,48,384]{2,1,0:T(8,128)(2,1)S(1)} %get-tuple-element.249), channel_id=1, source_target_pairs={{0,16},{1,17},{2,18},{3,19},{4,20},{5,21},{6,22},{7,23},{8,24},{9,... | collective-permute-start | bytes 110600 | tf_op jit(solution)/shard_map/ppermute | solution.py:655
  89.8 8.6 %collective-permute-start.30 = (bf16[1,48,384]{2,1,0:T(8,128)(2,1)S(1)}, bf16[1,48,384]{2,1,0:T(8,128)(2,1)S(1)}, u32[]{:S(2)}, u32[]{:S(2)}) collective-permute-start(bf16[1,48,384]{2,1,0:T(8,128)(2,1)S(1)} %get-tuple-element.250), channel_id=1, source_target_pairs={{0,8},{1,9},{2,10},{3,11},{4,12},{5,13},{6,14},{7,15},{8,0},{9,1},... | collective-permute-start | bytes 110600 | tf_op jit(solution)/shard_map/ppermute | solution.py:655
  90.7 7.7 %collective-permute-start.31 = (bf16[1,48,384]{2,1,0:T(8,128)(2,1)S(1)}, bf16[1,48,384]{2,1,0:T(8,128)(2,1)S(1)}, u32[]{:S(2)}, u32[]{:S(2)}) collective-permute-start(bf16[1,48,384]{2,1,0:T(8,128)(2,1)S(1)} %get-tuple-element.251), channel_id=1, source_target_pairs={{0,24},{1,25},{2,26},{3,27},{4,28},{5,29},{6,30},{7,31},{8,16},{9,... | collective-permute-start | bytes 110600 | tf_op jit(solution)/shard_map/ppermute | solution.py:655
  99.9 7.7 %collective-permute-start.35 = (f32[24,384]{1,0:T(8,128)S(1)}, f32[24,384]{1,0:T(8,128)S(1)}, u32[]{:S(2)}, u32[]{:S(2)}) collective-permute-start(f32[24,384]{1,0:T(8,128)S(1)} %add.48), channel_id=1, source_target_pairs={{0,2},{1,3},{2,0},{3,1},{4,6},{5,7},{6,4},{7,5},{8,10},{9,11},{10,... | collective-permute-start | bytes 110600 | tf_op jit(solution)/shard_map/ppermute | solution.py:655
  101.1 6.5 %collective-permute-start.36 = (f32[24,384]{1,0:T(8,128)S(1)}, f32[24,384]{1,0:T(8,128)S(1)}, u32[]{:S(2)}, u32[]{:S(2)}) collective-permute-start(f32[24,384]{1,0:T(8,128)S(1)} %add.48), channel_id=1, source_target_pairs={{0,4},{1,5},{2,6},{3,7},{4,0},{5,1},{6,2},{7,3},{8,12},{9,13},{10,... | collective-permute-start | bytes 110600 | tf_op jit(solution)/shard_map/ppermute | solution.py:655
  107.8 7.6 %collective-permute-start.38 = (f32[24,384]{1,0:T(8,128)S(1)}, f32[24,384]{1,0:T(8,128)S(1)}, u32[]{:S(2)}, u32[]{:S(2)}) collective-permute-start(f32[24,384]{1,0:T(8,128)S(1)} %add_add_fusion.1), channel_id=1, source_target_pairs={{0,16},{1,17},{2,18},{3,19},{4,20},{5,21},{6,22},{7,23},{8,24},{9,... | collective-permute-start | bytes 110600 | tf_op jit(solution)/shard_map/ppermute | solution.py:655
  107.9 7.5 %collective-permute-start.39 = (f32[24,384]{1,0:T(8,128)S(1)}, f32[24,384]{1,0:T(8,128)S(1)}, u32[]{:S(2)}, u32[]{:S(2)}) collective-permute-start(f32[24,384]{1,0:T(8,128)S(1)} %add_add_fusion.1), channel_id=1, source_target_pairs={{0,8},{1,9},{2,10},{3,11},{4,12},{5,13},{6,14},{7,15},{8,0},{9,1},... | collective-permute-start | bytes 110600 | tf_op jit(solution)/shard_map/ppermute | solution.py:655
  (47 other events, 338.6 us)

commit v8 on v7

--- a/solution.py
+++ b/solution.py
@@ -464,7 +464,7 @@
     return table_ref[SLOT] ^ swap_bits(4 * t) ^ ((h & 1) * 16 + (h >> 1) * 4)
 
 
-def mlp_weights_body(direct, table_ref, n_turned, g_turned, hidden_ref, grad_hidden_ref, keep_ref, send_ref, made, first, second):
+def mlp_weights_body(direct, table_ref, n_turned, g_turned, hidden_ref, grad_hidden_ref, keep_ref, send_ref, early_ref, made, first, second):
     for part in range(3):
         cols = slice(part * 2 * WIDE, (part + 1) * 2 * WIDE)
         first[:, cols] = dot_nn(n_turned[...], grad_hidden_ref[:, cols]).astype(LOW)
@@ -473,8 +473,9 @@
         cols = slice(h * C, (h + 1) * C)
         for t in range(8):
             at = place_of(direct, table_ref, t, h)
-            made[at, :PIECE] = first[t * PIECE : (t + 1) * PIECE, cols]
-            made[at, PIECE:] = second[t * PIECE : (t + 1) * PIECE, cols]
+            early_ref[at] = first[t * PIECE : t * PIECE + EARLY, cols]
+            made[at, : PIECE - EARLY] = first[t * PIECE + EARLY : (t + 1) * PIECE, cols]
+            made[at, PIECE - EARLY :] = second[t * PIECE : (t + 1) * PIECE, cols]
     keep_ref[...] = made[: BLOCKS // 2]
     send_ref[...] = made[BLOCKS // 2 :]
 
@@ -501,7 +502,7 @@
     bias_sum_ref[...] = jnp.zeros_like(bias_sum_ref)
     sums_ref[...] = jnp.zeros_like(sums_ref)
 
-    @pl.loop(0, MICRO)
+    @pl.loop(0, MICRO, unroll=True)
     def _(image):
         at_image = image_rows(image)
         grad_low = grad_ref[at_image, :].astype(LOW)
@@ -545,7 +546,8 @@
 
 
 def attend_weights_body(
-    direct, table_ref, unit_turned, grad_low_ref, packed_grad_ref, attn_ref, wq_ref, sums_ref, vec_ref, keep_ref, send_ref, norm_ref, made
+    direct, table_ref, unit_turned, grad_low_ref, packed_grad_ref, attn_ref, wq_ref, sums_ref, vec_ref, early_ref,
+    keep_ref, send_ref, norm_ref, made,
 ):
     turned_vec = vec_ref[...].T
     gain, shift = turned_vec[:, 0:1], turned_vec[:, 1:2]
@@ -565,7 +567,9 @@
     for h in range(4):
         block = jnp.concatenate([part[:, h * 96 : (h + 1) * 96] for part in parts], axis=1)
         for t in range(8):
-            made[place_of(direct, table_ref, t, h)] = block[t * PIECE : (t + 1) * PIECE]
+            at = place_of(direct, table_ref, t, h)
+            made[at, :PIECE] = block[t * PIECE : (t + 1) * PIECE]
+            made[at, PIECE:] = early_ref[at]
     keep_ref[...] = made[: BLOCKS // 2]
     send_ref[...] = made[BLOCKS // 2 :]
 
@@ -610,7 +614,11 @@
 
 
 def adam_body(near_ref, far_ref, spare_ref, *refs):
-    olds, news, turned = refs[:18], refs[18:-1], refs[-1]
+    olds, news, turned, hidden_grad = refs[:18], refs[18:-2], refs[-2], refs[-1]
+    depth = hidden_grad.shape[0]
+    early = near_ref.shape[0] - depth
+    hidden_grad[:early] = near_ref[depth:]
+    hidden_grad[early:] = far_ref[: depth - early]
     turned[: NH // 2] = spare_ref[12:18, :REL]
     turned[NH // 2 :] = spare_ref[12:18, C // 2 : C // 2 + REL]
     vec, table = spare_ref[0:12], turned[...]
@@ -620,14 +628,13 @@
     grad_norm = jnp.sqrt(total)
     factor = jnp.minimum(1.0, CLIP_NORM / (grad_norm + 1e-06))
     news[0][...] = grad_norm
-    depth = far_ref.shape[0] // 2
-    grads = [None, near_ref[:, 288:], far_ref[:depth], far_ref[depth:], vec, table]
+    grads = [None, near_ref[:depth, 288:], hidden_grad[...], far_ref[depth - early :], vec, table]
     for index in range(6):
         weight, first, second = olds[index], olds[6 + index], olds[12 + index]
         rate, decay = (RATE_MATRIX, DECAY_MATRIX) if index < 4 else (RATE_VECTOR, 0.0)
         for w in range(3 if index == 0 else 1):
             pick = (w,) if index == 0 else (Ellipsis,)
-            gradient = near_ref[:, w * 96 : (w + 1) * 96] if index == 0 else grads[index]
+            gradient = near_ref[:depth, w * 96 : (w + 1) * 96] if index == 0 else grads[index]
             made = adam_update(weight[pick], first[pick], second[pick], gradient * factor, rate, decay)
             for kind in range(3):
                 news[1 + 3 * index + kind][pick] = made[kind]
@@ -672,13 +679,16 @@
         far = jnp.concatenate([two[:, EARLY:], three], axis=1)
         return [[array[at : at + 4] for at in range(0, BLOCKS, 4)] for array in (near, far)]
 
-    def share_plain(keep, send):
-        both = jnp.concatenate([keep, send], axis=0)
-        half = both.shape[1] // PIECE
-        both = both.reshape(heads, 8, half, PIECE, C).transpose(0, 2, 1, 3, 4)
-        both = both.reshape(heads, half, toks, depth, C).transpose(0, 2, 1, 3, 4).reshape(devices, half * depth, C)
-        both = lax.psum_scatter(both.astype(F32), "head", scatter_dimension=0, tiled=True)
-        return lax.psum_scatter(both, "tok", scatter_dimension=0, tiled=True)[0]
+    def share_plain(blocks):
+        blocks = blocks.reshape(devices, depth, C).astype(F32)
+        part = lax.psum_scatter(blocks, "head", scatter_dimension=0, tiled=True)
+        return lax.psum_scatter(part, "tok", scatter_dimension=0, tiled=True)[0]
+
+    def plain_shares(near, far):
+        one, three = share_plain(near[:, :PIECE]), share_plain(far[:, PIECE - EARLY :])
+        two = share_plain(jnp.concatenate([near[:, PIECE:], far[:, : PIECE - EARLY]], axis=1))
+        near = jnp.concatenate([one, two[:early]], axis=0) / patches
+        return near, jnp.concatenate([two[early:], three], axis=0) / patches
 
     def join(*arrays):
         return jnp.concatenate(arrays, axis=0)
@@ -795,14 +805,14 @@
     )
 
     half = BLOCKS // 2
-    far_keep, far_send = call(
+    far_keep, far_send, early_grad = call(
         functools.partial(mlp_weights_body, direct),
-        [((half, 2 * PIECE, C), LOW)] * 2,
+        [((half, 2 * PIECE - EARLY, C), LOW)] * 2 + [((BLOCKS, EARLY, C), LOW)],
         (table, n_turned, g_turned, hidden, grad_hidden),
         "mlp_weights",
         limit=14,
         scratch=[
-            pltpu.VMEM((BLOCKS, 2 * PIECE, C), LOW), pltpu.VMEM((C, FF), LOW), pltpu.VMEM((C, FF), LOW),
+            pltpu.VMEM((BLOCKS, 2 * PIECE - EARLY, C), LOW), pltpu.VMEM((C, FF), LOW), pltpu.VMEM((C, FF), LOW),
         ],
         flops=4e9,
         scalars=1,
@@ -847,11 +857,11 @@
     vec_square = jnp.concatenate([vectors, jnp.zeros((4, C), F32)], axis=0)
     near_keep, near_send, sums_input = call(
         functools.partial(attend_weights_body, direct),
-        [((half, PIECE, C), LOW)] * 2 + [((2, C), F32)],
-        (table, unit_turned, grad_low, packed_grad, attn, w_qkv, sums_attend, vec_square),
+        [((half, PIECE + EARLY, C), LOW)] * 2 + [((2, C), F32)],
+        (table, unit_turned, grad_low, packed_grad, attn, w_qkv, sums_attend, vec_square, early_grad),
         "attend_weights",
         limit=8,
-        scratch=[pltpu.VMEM((BLOCKS, PIECE, C), LOW)],
+        scratch=[pltpu.VMEM((BLOCKS, PIECE + EARLY, C), LOW)],
         flops=2e9,
         scalars=1,
     )
@@ -911,7 +921,7 @@
         grad_block, *near_got = tie(grad_block, *near_got)
         near_grad, far_grad, spare = pl.pallas_call(
             functools.partial(finish_body, patches),
-            out_shape=[sds((depth, C), F32), sds((2 * depth, C), F32), sds((24, C), F32)],
+            out_shape=[sds((depth + early, C), F32), sds((2 * depth - early, C), F32), sds((24, C), F32)],
             compiler_params=whole(2),
             name="finish",
         )(near_stays, far_stays, vec_grad, table_grad, *near_got, *far_got)
@@ -924,7 +934,7 @@
             spare = (spare + one) + (two + three)
     else:
         grad_block = input_piece(0, MICRO, packed_grad, None)
-        near_grad, far_grad = share_plain(near_keep, near_send) / patches, share_plain(far_keep, far_send) / patches
+        near_grad, far_grad = plain_shares(join(near_keep, near_send), join(far_keep, far_send))
         squares = jnp.sum(near_grad * near_grad) + jnp.sum(far_grad * far_grad)
         vec_grad, table_grad, squares = lax.psum((vec_grad, table_grad, squares), BOTH)
         gap = jnp.zeros((6, C // 2 - REL), F32)
@@ -940,7 +950,7 @@
     news = pl.pallas_call(
         adam_body,
         out_shape=shapes,
-        scratch_shapes=[pltpu.VMEM((NH, REL), F32)],
+        scratch_shapes=[pltpu.VMEM((NH, REL), F32), pltpu.VMEM((depth, C), F32)],
         compiler_params=whole(8),
         name="adam",
     )(near_grad, far_grad, spare, *olds)

time: 118 us -> 116 us (0.983)
  transfers between devices with their start and end apart: 41 -> 41, of which waited for: 9 -> 8; matrix products, arithmetic and copies ran while one was open for 0% -> 0% of each run, Pallas kernels for 38% -> 37%
where the time goes in v8:
time: 116 us
  Pallas kernels  58.4 us (50%)
  starting transfers between devices  47.1 us (41%)
  waiting for transfers between devices  8.56 us (7%)
  between operations  1.66 us (1%)
    ppermute x41, starting transfers between devices, passed(): return lax.ppermute(rows, BOTH, [(i, i ^ mask) for i in range(devices)])  47.1 us
    pallas_call x9, Pallas kernels, call(): pl.pallas_call(body, in_specs=[SCALARS] * scalars + [far] * fetched + [HE...  39.2 us
    pallas_call x3, Pallas kernels, input_piece(): pl.pallas_call(functools.partial(input_body, first, last), in_specs=[far]...  11.5 us
    ppermute x41, waiting for transfers between devices, passed(): return lax.ppermute(rows, BOTH, [(i, i ^ mask) for i in range(devices)])  8.56 us
    pallas_call x2, Pallas kernels, output_piece(): pl.pallas_call(functools.partial(output_body, first, last), in_specs=[HEL...  4.42 us
  transfers between devices with their start and end apart: 41, of which 8 were waited for; matrix products, arithmetic and copies ran while one was open for 0% of the time, Pallas kernels for 37%

profile of v8, /device:TPU:0, one launch (start us, length us, event | category | flops | bytes accessed | tf_op | source)
XLA Modules:
  0.0 116.1 jit_solution(17282504769923470239)
XLA Ops:
  1.9 5.1 %collective-permute-start.5 = (bf16[1,64,384]{2,1,0:T(8,128)(2,1)S(1)}, bf16[1,64,384]{2,1,0:T(8,128)(2,1)S(1)}, u32[]{:S(2)}, u32[]{:S(2)}) collective-permute-start(bf16[1,64,384]{2,1,0:T(8,128)(2,1)S(1)} %bitcast.40), channel_id=1, source_target_pairs={{0,24},{1,25},{2,26},{3,27},{4,28},{5,29},{6,30},{7,31},{8,16},{9,... | collective-permute-start | bytes 147464 | tf_op jit(solution)/shard_map/ppermute | solution.py:662
  7.6 3.7 %collective-permute-start.2 = (bf16[1,80,384]{2,1,0:T(8,128)(2,1)S(1)}, bf16[1,80,384]{2,1,0:T(8,128)(2,1)S(1)}, u32[]{:S(2)}, u32[]{:S(2)}) collective-permute-start(bf16[1,80,384]{2,1,0:T(8,128)(2,1)S(1)} %bitcast.36), channel_id=1, source_target_pairs={{0,24},{1,25},{2,26},{3,27},{4,28},{5,29},{6,30},{7,31},{8,16},{9,... | collective-permute-start | bytes 184328 | tf_op jit(solution)/shard_map/ppermute | solution.py:662
  13.0 1.6 %collective-permute-start.6 = (bf16[4,64,384]{2,1,0:T(8,128)(2,1)S(1)}, bf16[4,64,384]{2,1,0:T(8,128)(2,1)S(1)}, u32[]{:S(2)}, u32[]{:S(2)}) collective-permute-start(bf16[4,64,384]{2,1,0:T(8,128)(2,1)S(1)} %pad_maximum_fusion.1.refs_0_), channel_id=1, source_target_pairs={{0,2},{1,3},{2,0},{3,1},{4,6},{5,7},{6,4},{7,5},{8,10},{9,11},{10,... | collective-permute-start | bytes 589832 | tf_op jit(solution)/shard_map/ppermute | solution.py:662
  16.8 4.3 %prep.1 = (bf16[1280,384]{1,0:T(8,128)(2,1)}, bf16[384,1280]{1,0:T(8,128)(2,1)}, bf16[1280,384]{1,0:T(8,128)(2,1)S(1)}, f32[768,128]{1,0:T(8,128)S(1)}) custom-call(f32[12,169]{1,0:T(8,128)} %bitcast.46, bf16[256,128]{1,0:T(8,128)(2,1)} %constant.84.clone.lookup_hbm.lookup_ref, f32[12,384]{1,0:T(8,128)} %refs_4_.3, ...), custom_call_target="tpu_custom_call" | custom-call | flops 1000000000 | bytes 4000000 | tf_op jit(solution)/shard_map/prep/pallas_call | solution.py:159
  21.2 1.6 %collective-permute-done.8.refs_3_ = bf16[4,64,384]{2,1,0:T(8,128)(2,1)S(1)} collective-permute-done((bf16[4,64,384]{2,1,0:T(8,128)(2,1)S(1)}, bf16[4,64,384]{2,1,0:T(8,128)(2,1)S(1)}, u32[]{:S(2)}, u32[]{:S(2)}) %collective-permute-start.8) | collective-permute-done | bytes 196640 | tf_op jit(solution)/shard_map/ppermute | solution.py:662
  27.4 7.6 %attend.1 = (bf16[1280,1152]{1,0:T(8,128)(2,1)S(1)}, bf16[5,6,256,128]{3,2,1,0:T(8,128)(2,1)S(1)}, bf16[1280,384]{1,0:T(8,128)(2,1)S(1)}, bf16[384,1152]{1,0:T(8,128)(2,1)S(1)}, bf16[384,384]{1,0:T(8,128)(2,1)S(1)}) custom-call(s32[3]{0:T(128)S(1)} %pad_add_fusion.table_ref, s32[4,2,5]{2,1,0:T(2,128)S(1)} %bitcast.52, s32[4,4,5]{2,1,0:T(4,128)S(1)} %bitcast.50, ...), custom_call_target="tpu_custom_call" | custom-call | flops 8000000000 | bytes 4000000 | tf_op jit(solution)/shard_map/attend/pallas_call | solution.py:159
  36.5 1.9 %collective-permute-done.15.refs_11_ = bf16[4,80,384]{2,1,0:T(8,128)(2,1)S(1)} collective-permute-done((bf16[4,80,384]{2,1,0:T(8,128)(2,1)S(1)}, bf16[4,80,384]{2,1,0:T(8,128)(2,1)S(1)}, u32[]{:S(2)}, u32[]{:S(2)}) %collective-permute-start.15) | collective-permute-done | bytes 245792 | tf_op jit(solution)/shard_map/ppermute | solution.py:662
  39.4 1.8 %prep_grad.1 = (bf16[1280,384]{1,0:T(8,128)(2,1)S(1)}, bf16[384,1280]{1,0:T(8,128)(2,1)S(1)}) custom-call(bf16[256,224]{1,0:T(8,128)(2,1)} %constant.83.clone.deal_hbm, bf16[5,1,14,14,384]{4,3,2,1,0:T(8,128)(2,1)} %cot_hbm), custom_call_target="tpu_custom_call" | custom-call | flops 1000000000 | bytes 4000000 | tf_op jit(solution)/shard_map/prep_grad/pallas_call | solution.py:159
  41.3 8.2 %mlp.1 = (bf16[1280,1536]{1,0:T(8,128)(2,1)S(1)}, bf16[1280,1536]{1,0:T(8,128)(2,1)S(1)}, f32[1280,384]{1,0:T(8,128)S(1)}, f32[12,384]{1,0:T(8,128)S(1)}, bf16[384,1536]{1,0:T(8,128)(2,1)S(1)}) custom-call(s32[3]{0:T(128)S(1)} %pad_add_fusion.table_ref, f32[1280,384]{1,0:T(8,128)S(1)} %get-tuple-element.182.middle_ref, ...), custom_call_target="tpu_custom_call" | custom-call | flops 10000000000 | bytes 4000000 | tf_op jit(solution)/shard_map/mlp/pallas_call | solution.py:159
  49.5 4.1 %mlp_weights.1 = (bf16[16,80,384]{2,1,0:T(8,128)(2,1)S(1)}, bf16[16,80,384]{2,1,0:T(8,128)(2,1)S(1)}, bf16[32,16,384]{2,1,0:T(8,128)(2,1)S(1)}) custom-call(s32[3]{0:T(128)S(1)} %pad_add_fusion.table_ref, bf16[384,1280]{1,0:T(8,128)(2,1)S(1)} %get-tuple-element.197.n_turned, bf16[384,1280]{1,0:T(8,128)(2,1)S(1)} %get-tuple-element.198.g_turned, ...), custom_call_target="tpu_custom_call" | custom-call | flops 4000000000 | bytes 4000000 | tf_op jit(solution)/shard_map/mlp_weights/pallas_call | solution.py:159
  53.8 2.5 %output.2.refs_0_ = bf16[5,1,14,14,384]{4,3,2,1,0:T(8,128)(2,1)} custom-call(bf16[1280,1536]{1,0:T(8,128)(2,1)S(1)} %get-tuple-element.219.hidden_ref, bf16[384,1536]{1,0:T(8,128)(2,1)S(1)} %get-tuple-element.196.w2_ref, f32[1280,384]{1,0:T(8,128)S(1)} %get-tuple-element.182.middle_ref, f32[12,384]{1,0:T(8,128)S(1)} %copy-done.5, bf16[224,256]{1,0:T(8,128)(2,1)S(1)} %copy-done.4), custom_call_target="tpu_custom_call" | custom-call | flops 1200000000 | bytes 2000000 | tf_op jit(solution)/shard_map/output/pallas_call | solution.py:827
  60.1 6.9 %attend_back.1 = (bf16[1280,1152]{1,0:T(8,128)(2,1)S(1)}, bf16[1280,384]{1,0:T(8,128)(2,1)S(1)}, f32[3,256,128]{2,1,0:T(8,128)S(1)}, f32[1,1152]{1,0:T(1,128)S(1)}) custom-call(s32[3]{0:T(128)S(1)} %pad_add_fusion.table_ref, s32[4,2,5]{2,1,0:T(2,128)S(1)} %bitcast.53, s32[4,4,5]{2,1,0:T(4,128)S(1)} %bitcast.51, ...), custom_call_target="tpu_custom_call" | custom-call | flops 8000000000 | bytes 4000000 | tf_op jit(solution)/shard_map/attend_back/pallas_call | solution.py:159
  67.1 3.8 %attend_weights.1 = (bf16[16,64,384]{2,1,0:T(8,128)(2,1)S(1)}, bf16[16,64,384]{2,1,0:T(8,128)(2,1)S(1)}, f32[2,384]{1,0:T(2,128)S(1)}) custom-call(s32[3]{0:T(128)S(1)} %pad_add_fusion.table_ref, bf16[384,1280]{1,0:T(8,128)(2,1)S(1)} %copy-done.29, bf16[1280,384]{1,0:T(8,128)(2,1)S(1)} %get-tuple-element.205.grad_low_ref, ...), custom_call_target="tpu_custom_call" | custom-call | flops 2000000000 | bytes 4000000 | tf_op jit(solution)/shard_map/attend_weights/pallas_call | solution.py:159
  71.5 1.9 %output.3 = bf16[5,1,14,14,384]{4,3,2,1,0:T(8,128)(2,1)} custom-call(bf16[1280,1536]{1,0:T(8,128)(2,1)S(1)} %get-tuple-element.219.hidden_ref, bf16[384,1536]{1,0:T(8,128)(2,1)S(1)} %get-tuple-element.196.w2_ref, f32[1280,384]{1,0:T(8,128)S(1)} %get-tuple-element.182.middle_ref, f32[12,384]{1,0:T(8,128)S(1)} %copy-done.5, ...), custom_call_target="tpu_custom_call", output_to_operand_aliasing={{}: (5, {})} | custom-call | flops 800000000 | bytes 2000000 | tf_op jit(solution)/shard_map/output/pallas_call | solution.py:827
  78.6 2.3 %collective-permute-start.25 = (bf16[1,80,384]{2,1,0:T(8,128)(2,1)S(1)}, bf16[1,80,384]{2,1,0:T(8,128)(2,1)S(1)}, u32[]{:S(2)}, u32[]{:S(2)}) collective-permute-start(bf16[1,80,384]{2,1,0:T(8,128)(2,1)S(1)} %get-tuple-element.238), channel_id=1, source_target_pairs={{0,16},{1,17},{2,18},{3,19},{4,20},{5,21},{6,22},{7,23},{8,24},{9,... | collective-permute-start | bytes 184328 | tf_op jit(solution)/shard_map/ppermute | solution.py:662
  81.0 1.9 %collective-permute-start.32 = (bf16[1,80,384]{2,1,0:T(8,128)(2,1)S(1)}, bf16[1,80,384]{2,1,0:T(8,128)(2,1)S(1)}, u32[]{:S(2)}, u32[]{:S(2)}) collective-permute-start(bf16[1,80,384]{2,1,0:T(8,128)(2,1)S(1)} %get-tuple-element.258), channel_id=1, source_target_pairs={{0,8},{1,9},{2,10},{3,11},{4,12},{5,13},{6,14},{7,15},{8,0},{9,1},... | collective-permute-start | bytes 184328 | tf_op jit(solution)/shard_map/ppermute | solution.py:662
  84.1 3.8 %collective-permute-start.33 = (bf16[1,80,384]{2,1,0:T(8,128)(2,1)S(1)}, bf16[1,80,384]{2,1,0:T(8,128)(2,1)S(1)}, u32[]{:S(2)}, u32[]{:S(2)}) collective-permute-start(bf16[1,80,384]{2,1,0:T(8,128)(2,1)S(1)} %get-tuple-element.259), channel_id=1, source_target_pairs={{0,24},{1,25},{2,26},{3,27},{4,28},{5,29},{6,30},{7,31},{8,16},{9,... | collective-permute-start | bytes 184328 | tf_op jit(solution)/shard_map/ppermute | solution.py:662
  88.8 1.8 %collective-permute-start.30 = (bf16[1,64,384]{2,1,0:T(8,128)(2,1)S(1)}, bf16[1,64,384]{2,1,0:T(8,128)(2,1)S(1)}, u32[]{:S(2)}, u32[]{:S(2)}) collective-permute-start(bf16[1,64,384]{2,1,0:T(8,128)(2,1)S(1)} %get-tuple-element.252), channel_id=1, source_target_pairs={{0,8},{1,9},{2,10},{3,11},{4,12},{5,13},{6,14},{7,15},{8,0},{9,1},... | collective-permute-start | bytes 147464 | tf_op jit(solution)/shard_map/ppermute | solution.py:662
  90.6 1.9 %collective-permute-start.31 = (bf16[1,64,384]{2,1,0:T(8,128)(2,1)S(1)}, bf16[1,64,384]{2,1,0:T(8,128)(2,1)S(1)}, u32[]{:S(2)}, u32[]{:S(2)}) collective-permute-start(bf16[1,64,384]{2,1,0:T(8,128)(2,1)S(1)} %get-tuple-element.253), channel_id=1, source_target_pairs={{0,24},{1,25},{2,26},{3,27},{4,28},{5,29},{6,30},{7,31},{8,16},{9,... | collective-permute-start | bytes 147464 | tf_op jit(solution)/shard_map/ppermute | solution.py:662
  92.4 4.2 %input_grad.3.refs_4_ = bf16[5,1,14,14,384]{4,3,2,1,0:T(8,128)(2,1)} custom-call(bf16[384,1152]{1,0:T(8,128)(2,1)} %copy-done.3, bf16[1280,1152]{1,0:T(8,128)(2,1)} %copy-done, bf16[1280,384]{1,0:T(8,128)(2,1)} %get-tuple-element.178.x_ref.refs_2_, f32[1280,384]{1,0:T(8,128)} %copy-done.1, f32[12,384]{1,0:T(8,128)S(1)} %copy-done.5, ...), custom_call_target="tpu_custom_call" | custom-call | flops 800000000 | bytes 2000000 | tf_op jit(solution)/shard_map/input_grad/pallas_call | solution.py:898
  101.6 4.2 %input_grad.4.refs_4_ = bf16[5,1,14,14,384]{4,3,2,1,0:T(8,128)(2,1)} custom-call(bf16[384,1152]{1,0:T(8,128)(2,1)} %copy-done.3, bf16[1280,1152]{1,0:T(8,128)(2,1)} %copy-done, bf16[1280,384]{1,0:T(8,128)(2,1)} %get-tuple-element.178.x_ref.refs_2_, f32[1280,384]{1,0:T(8,128)} %copy-done.1, ...), custom_call_target="tpu_custom_call", output_to_operand_aliasing={{}: (4, {})} | custom-call | flops 800000000 | bytes 2000000 | tf_op jit(solution)/shard_map/input_grad/pallas_call | solution.py:898
  106.2 2.5 %collective-permute-start.39 = (f32[24,384]{1,0:T(8,128)S(1)}, f32[24,384]{1,0:T(8,128)S(1)}, u32[]{:S(2)}, u32[]{:S(2)}) collective-permute-start(f32[24,384]{1,0:T(8,128)S(1)} %add_add_fusion.1), channel_id=1, source_target_pairs={{0,8},{1,9},{2,10},{3,11},{4,12},{5,13},{6,14},{7,15},{8,0},{9,1},... | collective-permute-start | bytes 110600 | tf_op jit(solution)/shard_map/ppermute | solution.py:662
  108.7 1.9 %collective-permute-start.40 = (f32[24,384]{1,0:T(8,128)S(1)}, f32[24,384]{1,0:T(8,128)S(1)}, u32[]{:S(2)}, u32[]{:S(2)}) collective-permute-start(f32[24,384]{1,0:T(8,128)S(1)} %add_add_fusion.1), channel_id=1, source_target_pairs={{0,24},{1,25},{2,26},{3,27},{4,28},{5,29},{6,30},{7,31},{8,16},{9,... | collective-permute-start | bytes 110600 | tf_op jit(solution)/shard_map/ppermute | solution.py:662
  110.6 3.1 %input_grad.5 = bf16[5,1,14,14,384]{4,3,2,1,0:T(8,128)(2,1)} custom-call(bf16[384,1152]{1,0:T(8,128)(2,1)} %copy-done.3, bf16[1280,1152]{1,0:T(8,128)(2,1)} %copy-done, bf16[1280,384]{1,0:T(8,128)(2,1)} %get-tuple-element.178.x_ref.refs_2_, f32[1280,384]{1,0:T(8,128)} %copy-done.1, ...), custom_call_target="tpu_custom_call", output_to_operand_aliasing={{}: (4, {})} | custom-call | flops 400000000 | bytes 2000000 | tf_op jit(solution)/shard_map/input_grad/pallas_call | solution.py:898
  (149 shorter events, 31.8 us)
Async XLA Ops:
  1.9 9.5 %collective-permute-start.5 = (bf16[1,64,384]{2,1,0:T(8,128)(2,1)S(1)}, bf16[1,64,384]{2,1,0:T(8,128)(2,1)S(1)}, u32[]{:S(2)}, u32[]{:S(2)}) collective-permute-start(bf16[1,64,384]{2,1,0:T(8,128)(2,1)S(1)} %bitcast.40), channel_id=1, source_target_pairs={{0,24},{1,25},{2,26},{3,27},{4,28},{5,29},{6,30},{7,31},{8,16},{9,... | collective-permute-start | bytes 147464 | tf_op jit(solution)/shard_map/ppermute | solution.py:662
  7.0 6.0 %collective-permute-start.3 = (bf16[1,64,384]{2,1,0:T(8,128)(2,1)S(1)}, bf16[1,64,384]{2,1,0:T(8,128)(2,1)S(1)}, u32[]{:S(2)}, u32[]{:S(2)}) collective-permute-start(bf16[1,64,384]{2,1,0:T(8,128)(2,1)S(1)} %bitcast.42), channel_id=1, source_target_pairs={{0,16},{1,17},{2,18},{3,19},{4,20},{5,21},{6,22},{7,23},{8,24},{9,... | collective-permute-start | bytes 147464 | tf_op jit(solution)/shard_map/ppermute | solution.py:662
  7.6 8.4 %collective-permute-start.2 = (bf16[1,80,384]{2,1,0:T(8,128)(2,1)S(1)}, bf16[1,80,384]{2,1,0:T(8,128)(2,1)S(1)}, u32[]{:S(2)}, u32[]{:S(2)}) collective-permute-start(bf16[1,80,384]{2,1,0:T(8,128)(2,1)S(1)} %bitcast.36), channel_id=1, source_target_pairs={{0,24},{1,25},{2,26},{3,27},{4,28},{5,29},{6,30},{7,31},{8,16},{9,... | collective-permute-start | bytes 184328 | tf_op jit(solution)/shard_map/ppermute | solution.py:662
  13.0 8.2 %collective-permute-start.6 = (bf16[4,64,384]{2,1,0:T(8,128)(2,1)S(1)}, bf16[4,64,384]{2,1,0:T(8,128)(2,1)S(1)}, u32[]{:S(2)}, u32[]{:S(2)}) collective-permute-start(bf16[4,64,384]{2,1,0:T(8,128)(2,1)S(1)} %pad_maximum_fusion.1.refs_0_), channel_id=1, source_target_pairs={{0,2},{1,3},{2,0},{3,1},{4,6},{5,7},{6,4},{7,5},{8,10},{9,11},{10,... | collective-permute-start | bytes 589832 | tf_op jit(solution)/shard_map/ppermute | solution.py:662
  14.6 6.6 %collective-permute-start.7 = (bf16[4,64,384]{2,1,0:T(8,128)(2,1)S(1)}, bf16[4,64,384]{2,1,0:T(8,128)(2,1)S(1)}, u32[]{:S(2)}, u32[]{:S(2)}) collective-permute-start(bf16[4,64,384]{2,1,0:T(8,128)(2,1)S(1)} %pad_maximum_fusion.1.refs_0_), channel_id=1, source_target_pairs={{0,4},{1,5},{2,6},{3,7},{4,0},{5,1},{6,2},{7,3},{8,12},{9,13},{10,... | collective-permute-start | bytes 589832 | tf_op jit(solution)/shard_map/ppermute | solution.py:662
  16.1 6.8 %collective-permute-start.8 = (bf16[4,64,384]{2,1,0:T(8,128)(2,1)S(1)}, bf16[4,64,384]{2,1,0:T(8,128)(2,1)S(1)}, u32[]{:S(2)}, u32[]{:S(2)}) collective-permute-start(bf16[4,64,384]{2,1,0:T(8,128)(2,1)S(1)} %pad_maximum_fusion.1.refs_0_), channel_id=1, source_target_pairs={{0,6},{1,7},{2,4},{3,5},{4,2},{5,3},{6,0},{7,1},{8,14},{9,15},{10,... | collective-permute-start | bytes 589832 | tf_op jit(solution)/shard_map/ppermute | solution.py:662
  23.8 12.7 %collective-permute-start.13 = (bf16[4,80,384]{2,1,0:T(8,128)(2,1)S(1)}, bf16[4,80,384]{2,1,0:T(8,128)(2,1)S(1)}, u32[]{:S(2)}, u32[]{:S(2)}) collective-permute-start(bf16[4,80,384]{2,1,0:T(8,128)(2,1)S(1)} %pad_maximum_fusion.refs_8_), channel_id=1, source_target_pairs={{0,2},{1,3},{2,0},{3,1},{4,6},{5,7},{6,4},{7,5},{8,10},{9,11},{10,... | collective-permute-start | bytes 737288 | tf_op jit(solution)/shard_map/ppermute | solution.py:662
  25.3 11.2 %collective-permute-start.14 = (bf16[4,80,384]{2,1,0:T(8,128)(2,1)S(1)}, bf16[4,80,384]{2,1,0:T(8,128)(2,1)S(1)}, u32[]{:S(2)}, u32[]{:S(2)}) collective-permute-start(bf16[4,80,384]{2,1,0:T(8,128)(2,1)S(1)} %pad_maximum_fusion.refs_8_), channel_id=1, source_target_pairs={{0,4},{1,5},{2,6},{3,7},{4,0},{5,1},{6,2},{7,3},{8,12},{9,13},{10,... | collective-permute-start | bytes 737288 | tf_op jit(solution)/shard_map/ppermute | solution.py:662
  26.8 11.6 %collective-permute-start.15 = (bf16[4,80,384]{2,1,0:T(8,128)(2,1)S(1)}, bf16[4,80,384]{2,1,0:T(8,128)(2,1)S(1)}, u32[]{:S(2)}, u32[]{:S(2)}) collective-permute-start(bf16[4,80,384]{2,1,0:T(8,128)(2,1)S(1)} %pad_maximum_fusion.refs_8_), channel_id=1, source_target_pairs={{0,6},{1,7},{2,4},{3,5},{4,2},{5,3},{6,0},{7,1},{8,14},{9,15},{10,... | collective-permute-start | bytes 737288 | tf_op jit(solution)/shard_map/ppermute | solution.py:662
  56.6 14.3 %collective-permute-start.21 = (bf16[4,80,384]{2,1,0:T(8,128)(2,1)S(1)}, bf16[4,80,384]{2,1,0:T(8,128)(2,1)S(1)}, u32[]{:S(2)}, u32[]{:S(2)}) collective-permute-start(bf16[4,80,384]{2,1,0:T(8,128)(2,1)S(1)} %get-tuple-element.213), channel_id=1, source_target_pairs={{0,2},{1,3},{2,0},{3,1},{4,6},{5,7},{6,4},{7,5},{8,10},{9,11},{10,... | collective-permute-start | bytes 737288 | tf_op jit(solution)/shard_map/ppermute | solution.py:662
  57.8 13.1 %collective-permute-start.22 = (bf16[4,80,384]{2,1,0:T(8,128)(2,1)S(1)}, bf16[4,80,384]{2,1,0:T(8,128)(2,1)S(1)}, u32[]{:S(2)}, u32[]{:S(2)}) collective-permute-start(bf16[4,80,384]{2,1,0:T(8,128)(2,1)S(1)} %get-tuple-element.214), channel_id=1, source_target_pairs={{0,4},{1,5},{2,6},{3,7},{4,0},{5,1},{6,2},{7,3},{8,12},{9,13},{10,... | collective-permute-start | bytes 737288 | tf_op jit(solution)/shard_map/ppermute | solution.py:662
  59.3 12.1 %collective-permute-start.23 = (bf16[4,80,384]{2,1,0:T(8,128)(2,1)S(1)}, bf16[4,80,384]{2,1,0:T(8,128)(2,1)S(1)}, u32[]{:S(2)}, u32[]{:S(2)}) collective-permute-start(bf16[4,80,384]{2,1,0:T(8,128)(2,1)S(1)} %get-tuple-element.215), channel_id=1, source_target_pairs={{0,6},{1,7},{2,4},{3,5},{4,2},{5,3},{6,0},{7,1},{8,14},{9,15},{10,... | collective-permute-start | bytes 737288 | tf_op jit(solution)/shard_map/ppermute | solution.py:662
  73.9 14.0 %collective-permute-start.26 = (bf16[4,64,384]{2,1,0:T(8,128)(2,1)S(1)}, bf16[4,64,384]{2,1,0:T(8,128)(2,1)S(1)}, u32[]{:S(2)}, u32[]{:S(2)}) collective-permute-start(bf16[4,64,384]{2,1,0:T(8,128)(2,1)S(1)} %get-tuple-element.239), channel_id=1, source_target_pairs={{0,2},{1,3},{2,0},{3,1},{4,6},{5,7},{6,4},{7,5},{8,10},{9,11},{10,... | collective-permute-start | bytes 589832 | tf_op jit(solution)/shard_map/ppermute | solution.py:662
  75.2 12.7 %collective-permute-start.27 = (bf16[4,64,384]{2,1,0:T(8,128)(2,1)S(1)}, bf16[4,64,384]{2,1,0:T(8,128)(2,1)S(1)}, u32[]{:S(2)}, u32[]{:S(2)}) collective-permute-start(bf16[4,64,384]{2,1,0:T(8,128)(2,1)S(1)} %get-tuple-element.240), channel_id=1, source_target_pairs={{0,4},{1,5},{2,6},{3,7},{4,0},{5,1},{6,2},{7,3},{8,12},{9,13},{10,... | collective-permute-start | bytes 589832 | tf_op jit(solution)/shard_map/ppermute | solution.py:662
  76.7 11.2 %collective-permute-start.28 = (bf16[4,64,384]{2,1,0:T(8,128)(2,1)S(1)}, bf16[4,64,384]{2,1,0:T(8,128)(2,1)S(1)}, u32[]{:S(2)}, u32[]{:S(2)}) collective-permute-start(bf16[4,64,384]{2,1,0:T(8,128)(2,1)S(1)} %get-tuple-element.241), channel_id=1, source_target_pairs={{0,6},{1,7},{2,4},{3,5},{4,2},{5,3},{6,0},{7,1},{8,14},{9,15},{10,... | collective-permute-start | bytes 589832 | tf_op jit(solution)/shard_map/ppermute | solution.py:662
  81.0 15.7 %collective-permute-start.32 = (bf16[1,80,384]{2,1,0:T(8,128)(2,1)S(1)}, bf16[1,80,384]{2,1,0:T(8,128)(2,1)S(1)}, u32[]{:S(2)}, u32[]{:S(2)}) collective-permute-start(bf16[1,80,384]{2,1,0:T(8,128)(2,1)S(1)} %get-tuple-element.258), channel_id=1, source_target_pairs={{0,8},{1,9},{2,10},{3,11},{4,12},{5,13},{6,14},{7,15},{8,0},{9,1},... | collective-permute-start | bytes 184328 | tf_op jit(solution)/shard_map/ppermute | solution.py:662
  84.1 12.6 %collective-permute-start.33 = (bf16[1,80,384]{2,1,0:T(8,128)(2,1)S(1)}, bf16[1,80,384]{2,1,0:T(8,128)(2,1)S(1)}, u32[]{:S(2)}, u32[]{:S(2)}) collective-permute-start(bf16[1,80,384]{2,1,0:T(8,128)(2,1)S(1)} %get-tuple-element.259), channel_id=1, source_target_pairs={{0,24},{1,25},{2,26},{3,27},{4,28},{5,29},{6,30},{7,31},{8,16},{9,... | collective-permute-start | bytes 184328 | tf_op jit(solution)/shard_map/ppermute | solution.py:662
  88.0 8.7 %collective-permute-start.29 = (bf16[1,64,384]{2,1,0:T(8,128)(2,1)S(1)}, bf16[1,64,384]{2,1,0:T(8,128)(2,1)S(1)}, u32[]{:S(2)}, u32[]{:S(2)}) collective-permute-start(bf16[1,64,384]{2,1,0:T(8,128)(2,1)S(1)} %get-tuple-element.251), channel_id=1, source_target_pairs={{0,16},{1,17},{2,18},{3,19},{4,20},{5,21},{6,22},{7,23},{8,24},{9,... | collective-permute-start | bytes 147464 | tf_op jit(solution)/shard_map/ppermute | solution.py:662
  88.8 7.9 %collective-permute-start.30 = (bf16[1,64,384]{2,1,0:T(8,128)(2,1)S(1)}, bf16[1,64,384]{2,1,0:T(8,128)(2,1)S(1)}, u32[]{:S(2)}, u32[]{:S(2)}) collective-permute-start(bf16[1,64,384]{2,1,0:T(8,128)(2,1)S(1)} %get-tuple-element.252), channel_id=1, source_target_pairs={{0,8},{1,9},{2,10},{3,11},{4,12},{5,13},{6,14},{7,15},{8,0},{9,1},... | collective-permute-start | bytes 147464 | tf_op jit(solution)/shard_map/ppermute | solution.py:662
  90.6 6.1 %collective-permute-start.31 = (bf16[1,64,384]{2,1,0:T(8,128)(2,1)S(1)}, bf16[1,64,384]{2,1,0:T(8,128)(2,1)S(1)}, u32[]{:S(2)}, u32[]{:S(2)}) collective-permute-start(bf16[1,64,384]{2,1,0:T(8,128)(2,1)S(1)} %get-tuple-element.253), channel_id=1, source_target_pairs={{0,24},{1,25},{2,26},{3,27},{4,28},{5,29},{6,30},{7,31},{8,16},{9,... | collective-permute-start | bytes 147464 | tf_op jit(solution)/shard_map/ppermute | solution.py:662
  98.2 7.7 %collective-permute-start.35 = (f32[24,384]{1,0:T(8,128)S(1)}, f32[24,384]{1,0:T(8,128)S(1)}, u32[]{:S(2)}, u32[]{:S(2)}) collective-permute-start(f32[24,384]{1,0:T(8,128)S(1)} %add.48), channel_id=1, source_target_pairs={{0,2},{1,3},{2,0},{3,1},{4,6},{5,7},{6,4},{7,5},{8,10},{9,11},{10,... | collective-permute-start | bytes 110600 | tf_op jit(solution)/shard_map/ppermute | solution.py:662
  99.3 6.5 %collective-permute-start.36 = (f32[24,384]{1,0:T(8,128)S(1)}, f32[24,384]{1,0:T(8,128)S(1)}, u32[]{:S(2)}, u32[]{:S(2)}) collective-permute-start(f32[24,384]{1,0:T(8,128)S(1)} %add.48), channel_id=1, source_target_pairs={{0,4},{1,5},{2,6},{3,7},{4,0},{5,1},{6,2},{7,3},{8,12},{9,13},{10,... | collective-permute-start | bytes 110600 | tf_op jit(solution)/shard_map/ppermute | solution.py:662
  106.1 7.6 %collective-permute-start.38 = (f32[24,384]{1,0:T(8,128)S(1)}, f32[24,384]{1,0:T(8,128)S(1)}, u32[]{:S(2)}, u32[]{:S(2)}) collective-permute-start(f32[24,384]{1,0:T(8,128)S(1)} %add_add_fusion.1), channel_id=1, source_target_pairs={{0,16},{1,17},{2,18},{3,19},{4,20},{5,21},{6,22},{7,23},{8,24},{9,... | collective-permute-start | bytes 110600 | tf_op jit(solution)/shard_map/ppermute | solution.py:662
  106.2 7.5 %collective-permute-start.39 = (f32[24,384]{1,0:T(8,128)S(1)}, f32[24,384]{1,0:T(8,128)S(1)}, u32[]{:S(2)}, u32[]{:S(2)}) collective-permute-start(f32[24,384]{1,0:T(8,128)S(1)} %add_add_fusion.1), channel_id=1, source_target_pairs={{0,8},{1,9},{2,10},{3,11},{4,12},{5,13},{6,14},{7,15},{8,0},{9,1},... | collective-permute-start | bytes 110600 | tf_op jit(solution)/shard_map/ppermute | solution.py:662
  (47 other events, 439.7 us)
